TPU v7x, 128 devices: a whole 4x4x4 slice. The times are simulated.
128 devices in a mesh: ctx: 32 (over y, x_hi, z), seq: 4 (over x_lo, core).
Axes of the slice: x: 4 (x_hi: 2, x_lo: 2; x = x_hi * 2 + x_lo), y: 4, z: 4, core: 2. Of those that a mesh axis runs over, the one named last changes fastest.
Arguments:
- tokens: bfloat16 [131072, 1024], P(('ctx', 'seq')), may hold values from -24 to 24
- w_query: bfloat16 [1024, 128], P(('ctx', 'seq')), may hold values from -0.1875 to 0.1875
- w_key: bfloat16 [1024, 128], P(('ctx', 'seq')), may hold values from -0.1875 to 0.1875
- w_value: bfloat16 [1024, 1024], P(('ctx', 'seq')), may hold values from -2 to 2
- w_out: bfloat16 [1024, 1024], P(('ctx', 'seq')), may hold values from -2 to 2
- cotangent: bfloat16 [131072, 1024], P(('ctx', 'seq')), may hold values from -6 to 6
Outputs:
- mixed: bfloat16 [131072, 1024], P(('ctx', 'seq'))
- grad_tokens: bfloat16 [131072, 1024], P(('ctx', 'seq'))
- grad_query: float32 [1024, 128], P(('ctx', 'seq'))
- grad_key: float32 [1024, 128], P(('ctx', 'seq'))
- grad_value: float32 [1024, 1024], P(('ctx', 'seq'))
- grad_out: float32 [1024, 1024], P(('ctx', 'seq'))
All inputs are finite; a program needn't handle non-finite values.
Results may differ from a plain program's by a relative error of at most 0.013.
Values may be sent and summed in bfloat16 or wider, within the bound.
No kernel may reach another device: no remote copies, remote signals or barrier semaphores. Data moves between devices by JAX's collectives and lax.ppermute only.
A program may use at most 128 MiB of HBM per device.

v0:
```python
import jax
import jax.numpy as jnp
from jax import lax
from jax.sharding import PartitionSpec as P

H = 8


def features(projected, head_count):
    tok_rows = projected.shape[0]
    head_dim = projected.shape[1] // head_count
    per_head = jnp.transpose(projected.reshape(tok_rows, head_count, head_dim), (1, 2, 0))
    linear = per_head * head_dim ** (-0.25)
    square = (per_head[:, :, None, :] * per_head[:, None, :, :]).reshape(
        head_count, head_dim * head_dim, tok_rows
    )
    square = square * (2.0 * head_dim) ** (-0.5)
    ones_row = jnp.ones((head_count, 1, tok_rows), jnp.float32)
    return jnp.concatenate([ones_row, linear, square], axis=1)


def per_device(tokens, w_query, w_key, w_value, w_out, cotangent):
    highest = lax.Precision.HIGHEST
    high = lax.Precision.HIGH
    contract_last = (((1,), (1,)), ((), ()))
    contract_first = (((0,), (0,)), ((), ()))
    tok_rows = tokens.shape[0]
    qk_cols = w_query.shape[1]
    value_cols = w_value.shape[1]
    head_count = H
    value_dim = value_cols // head_count
    w_joined = jnp.concatenate([w_query, w_key, w_value], axis=1)
    joined_full, out_full = (
        lax.all_gather(w_joined, ("ctx", "seq"), axis=0, tiled=True),
        lax.all_gather(w_out, ("ctx", "seq"), axis=0, tiled=True),
    )
    mixed_qkv = jnp.dot(tokens, joined_full, preferred_element_type=jnp.float32)
    qkv_bf = mixed_qkv.astype(jnp.bfloat16)
    query_bf = qkv_bf[:, :qk_cols]
    key_bf = qkv_bf[:, qk_cols : 2 * qk_cols]
    value_bf = qkv_bf[:, 2 * qk_cols :]
    query_feat = features(query_bf.astype(jnp.float32), head_count).astype(jnp.bfloat16)
    key_feat = features(key_bf.astype(jnp.float32), head_count).astype(jnp.bfloat16)
    value_heads = value_bf.reshape(tok_rows, head_count, value_dim)
    state_part = jnp.einsum(
        "hft,the->hfe", key_feat, value_heads, preferred_element_type=jnp.float32
    )
    norm_part = jnp.einsum(
        "hft,t->hf",
        key_feat,
        jnp.ones((tok_rows,), jnp.bfloat16),
        preferred_element_type=jnp.float32,
    )
    state_sum, norm_sum = lax.psum((state_part, norm_part), ("ctx", "seq"))
    query_wide = query_feat.astype(jnp.float32)
    numerator = jnp.einsum("hft,hfe->the", query_wide, state_sum, precision=high)
    denominator = jnp.einsum("hft,hf->th", query_wide, norm_sum, precision=high)
    attended = numerator / denominator[:, :, None]
    attended_bf = attended.reshape(tok_rows, value_cols).astype(jnp.bfloat16)
    mixed_wide = jnp.dot(attended_bf, out_full, preferred_element_type=jnp.float32)
    upstream = lax.dot_general(
        cotangent, out_full, contract_last, preferred_element_type=jnp.float32
    )
    mixed = mixed_wide.astype(jnp.bfloat16)
    upstream = upstream.reshape(tok_rows, head_count, value_dim)
    grad_num = upstream / denominator[:, :, None]
    grad_den = -jnp.sum(grad_num * attended, axis=2)
    state_gpart = jnp.einsum("hft,the->hfe", query_wide, grad_num, precision=high)
    norm_gpart = jnp.einsum("hft,th->hf", query_wide, grad_den, precision=high)
    state_grad, norm_grad = lax.psum((state_gpart, norm_gpart), ("ctx", "seq"))
    query_fgrad = jnp.einsum("the,hfe->hft", grad_num, state_sum, precision=highest)
    query_fgrad = query_fgrad + jnp.einsum("th,hf->hft", grad_den, norm_sum, precision=highest)
    key_fgrad = jnp.einsum(
        "the,hfe->hft", value_heads.astype(jnp.float32), state_grad, precision=high
    )
    key_fgrad = key_fgrad + norm_grad[:, :, None]
    key_wide = key_feat.astype(jnp.float32)
    value_grad = jnp.einsum("hft,hfe->the", key_wide, state_grad, precision=high)
    value_grad = value_grad.reshape(tok_rows, value_cols).astype(jnp.bfloat16)
    ignored_q, query_back = jax.vjp(
        lambda projected: features(projected, head_count), query_bf.astype(jnp.float32)
    )
    ignored_k, key_back = jax.vjp(
        lambda projected: features(projected, head_count), key_bf.astype(jnp.float32)
    )
    query_grad = query_back(query_fgrad)[0].astype(jnp.bfloat16)
    key_grad = key_back(key_fgrad)[0].astype(jnp.bfloat16)
    joined_grad = jnp.concatenate([query_grad, key_grad, value_grad], axis=1)
    tok_wide = lax.dot_general(
        joined_grad, joined_full, contract_last, preferred_element_type=jnp.float32
    )
    grad_tokens = tok_wide.astype(jnp.bfloat16)
    columns = tokens
    joined_wgrad = lax.psum_scatter(
        lax.dot_general(columns, joined_grad, contract_first, preferred_element_type=jnp.float32),
        ("ctx", "seq"),
        scatter_dimension=0,
        tiled=True,
    )
    columns = attended_bf
    out_wgrad = lax.psum_scatter(
        lax.dot_general(columns, cotangent, contract_first, preferred_element_type=jnp.float32),
        ("ctx", "seq"),
        scatter_dimension=0,
        tiled=True,
    )
    scale_factor = (tok_rows * lax.axis_size(("ctx", "seq"))) ** (-0.5)
    joined_wgrad = joined_wgrad * scale_factor
    grad_query = joined_wgrad[:, :qk_cols]
    grad_key = joined_wgrad[:, qk_cols : 2 * qk_cols]
    grad_value = joined_wgrad[:, 2 * qk_cols :]
    grad_out = out_wgrad * scale_factor
    return (mixed, grad_tokens, grad_query, grad_key, grad_value, grad_out)


def solution(mesh):
    placed = (
        P(("ctx", "seq"), None),
        P(("ctx", "seq"), None),
        P(("ctx", "seq"), None),
        P(("ctx", "seq"), None),
        P(("ctx", "seq"), None),
        P(("ctx", "seq"), None),
    )
    return jax.shard_map(
        per_device,
        mesh=mesh,
        in_specs=placed,
        out_specs=(
            P(("ctx", "seq"), None),
            P(("ctx", "seq"), None),
            P(("ctx", "seq"), None),
            P(("ctx", "seq"), None),
            P(("ctx", "seq"), None),
            P(("ctx", "seq"), None),
        ),
        check_vma=False,
    )
```

profile of v0, /device:TPU:1, one launch (start us, length us, event | category | flops | bytes accessed | tf_op | source)
XLA Modules:
  0.0 1941.2 jit_solution(11607639361990967095)
XLA Ops:
  7.2 0.0 copy-start
  7.2 0.0 all-gather.5.cloned.1.call-start
  7.2 0.7 all-gather.5.cloned.1.call-update
  7.9 0.0 all-gather.3.cloned.1.call-start
  8.0 1.3 pad_maximum_fusion.5
  9.3 0.0 all-gather.3.cloned.1.call-update
  9.3 0.0 all-reduce.3.cloned.1.call-start
  9.4 197.6 %all-gather.5.cloned.1.call-done = bf16[1024,1024]{1,0:T(8,128)(2,1)} async-done(((bf16[8,1024]{1,0:T(8,128)(2,1)}), bf16[1024,1024]{1,0:T(8,128)(2,1)}) %all-gather.5.cloned.1.call-update) | async-done | bytes 2097168 | tf_op jit(solution)/shard_map/all_gather | solution.py:35
  207.0 6.6 fusion.18
  213.6 190.5 %all-gather.3.cloned.1.call-done = bf16[1024,1280]{1,0:T(8,128)(2,1)} async-done(((bf16[8,1280]{1,0:T(8,128)(2,1)}), bf16[1024,1280]{1,0:T(8,128)(2,1)}) %all-gather.3.cloned.1.call-update) | async-done | bytes 2621456 | tf_op jit(solution)/shard_map/all_gather | solution.py:34
  404.1 0.0 copy-done
  404.1 4.9 fusion
  409.2 0.1 multiply_convert_fusion.3
  409.3 0.0 copy-start.7
  409.3 1.5 slice.25
  410.8 3.2 multiply_convert_fusion
  414.0 1.3 multiply_convert_fusion.1
  415.4 1.7 fusion.9
  417.0 0.3 copy-done.3
  417.3 63.7 %psum.29 = f32[8,273]{1,0:T(8,128)S(1)} all-reduce(f32[8,273]{1,0:T(8,128)S(1)} %bitcast.91), channel_id=1, replica_groups=mesh['ctx'=32,'seq'=4] {'ctx','seq'}, use_global_device_ids=true, to_apply=%region_1.0 | all-reduce | flops 2184 | bytes 17472 | tf_op jit(solution)/shard_map/psum | solution.py:54
  481.0 3.9 pad_maximum_fusion.1
  485.0 0.0 copy-start.2
  485.0 0.0 copy-start.8
  485.0 1.7 fusion.7
  486.7 1.4 copy-done.2
  488.1 0.1 copy-done.8
  488.2 2.7 fusion.15
  490.9 0.0 copy-done.12
  490.9 3.7 fusion.14
  494.6 0.0 all-reduce.3.cloned.1.call-update
  494.6 0.3 reduce-scatter.5.cloned.1.call-start
  494.8 147.8 %all-reduce.3.cloned.1.call-done = (f32[8,273,128]{2,1,0:T(8,128)}, f32[8,273,128]{2,1,0:T(8,128)}) async-done(((f32[8,273,128]{2,1,0:T(8,128)}, f32[8,273,128]{2,1,0:T(8,128)}), (f32[8,273,128]{2,1,0:T(8,128)}, f32[8,273,128]{2,1,0:T(8,128)})) %all-reduce.3.cloned.1.call-update) | async-done | bytes 2236432 | tf_op jit(solution)/shard_map/psum | solution.py:54
  642.7 6.8 multiply_reduce_fusion.4
  649.5 1.4 copy-done.14
  650.9 4.4 fusion.19
  655.3 0.0 reduce-scatter.5.cloned.1.call-update
  655.3 0.0 reduce-scatter.7.cloned.1.call-start
  655.4 4.8 fusion.5
  660.2 65.0 %psum.31 = f32[8,273]{1,0:T(8,128)S(1)} all-reduce(f32[8,273]{1,0:T(8,128)S(1)} %bitcast.92), channel_id=1, replica_groups=mesh['ctx'=32,'seq'=4] {'ctx','seq'}, use_global_device_ids=true, to_apply=%region_6.0 | all-reduce | flops 2184 | bytes 17472 | tf_op jit(solution)/shard_map/psum | solution.py:70
  725.2 4.6 broadcast_add_fusion
  729.8 2.1 slice_multiply_fusion
  731.9 5.4 multiply_reduce_fusion
  737.3 0.2 fusion.2
  737.5 8.4 multiply_add_fusion
  745.9 2.1 slice_multiply_fusion.1
  747.9 5.1 multiply_reduce_fusion.2
  753.1 0.2 fusion.4
  753.3 3.0 convolution_convert_fusion.2
  756.3 0.0 copy-start.15
  756.3 1.3 copy-done.15
  757.6 5.2 convolution_bitcast_fusion
  762.8 5.9 copy.35
  768.7 0.0 reduce-scatter.7.cloned.1.call-update
  768.8 0.0 copy-start.16
  768.8 6.1 convolution_convert_fusion.3
  774.9 4.1 convolution_convert_fusion.1
  779.0 510.8 %reduce-scatter.5.cloned.1.call-done = f32[8,1024]{1,0:T(8,128)} async-done(((f32[1024,1024]{1,0:T(8,128)}), f32[8,1024]{1,0:T(8,128)}) %reduce-scatter.5.cloned.1.call-update) | async-done | bytes 32784 | tf_op jit(solution)/shard_map/reduce_scatter | solution.py:101
  1289.8 1.4 broadcast_multiply_fusion.1
  1291.2 640.0 %reduce-scatter.7.cloned.1.call-done = f32[8,1280]{1,0:T(8,128)} async-done(((f32[1024,1280]{1,0:T(8,128)}), f32[8,1280]{1,0:T(8,128)}) %reduce-scatter.7.cloned.1.call-update) | async-done | bytes 40976
  1931.2 1.0 copy.36
  1932.2 0.1 broadcast_multiply_fusion
  1932.4 0.7 copy.23
  1933.0 0.7 copy.24
  1933.7 0.8 copy.25
  (32 shorter events, 0.3 us)
Async XLA Ops:
  7.2 396.9 %copy-start = (bf16[1024,1024]{1,0:T(8,128)(2,1)S(1)}, bf16[1024,1024]{1,0:T(8,128)(2,1)}, u32[]{:S(2)}) copy-start(bf16[1024,1024]{1,0:T(8,128)(2,1)} %param.6) | copy-start | bytes 6291460
  7.2 199.8 %all-gather.5.cloned.1.call-start = ((), (), s32[]{:S(2)}) async-start(), calls=%async_computation.3 | async-start | bytes 2113536 | tf_op jit(solution)/shard_map/all_gather | solution.py:35
  7.9 396.2 %all-gather.3.cloned.1.call-start = ((), (), s32[]{:S(2)}) async-start(), calls=%async_computation.2 | async-start | bytes 2641920 | tf_op jit(solution)/shard_map/all_gather | solution.py:34
  9.3 633.3 %all-reduce.3.cloned.1.call-start = ((), (), s32[]{:S(2)}) async-start(), calls=%async_computation.6 | async-start | bytes 4587520 | tf_op jit(solution)/shard_map/psum | solution.py:54
  409.3 6.1 copy-start.7
  415.3 2.0 copy-start.3
  481.0 5.7 copy-start.4
  485.0 5.9 copy-start.1
  485.0 3.2 copy-start.2
  485.0 3.2 copy-start.8
  488.2 2.7 copy-start.12
  494.6 795.2 %reduce-scatter.5.cloned.1.call-start = ((), (), s32[]{:S(2)}) async-start(), calls=%async_computation.4 | async-start | bytes 4227072 | tf_op jit(solution)/shard_map/reduce_scatter | solution.py:101
  642.7 8.2 copy-start.10
  649.5 1.4 copy-start.14
  655.3 1275.9 %reduce-scatter.7.cloned.1.call-start = ((), (), s32[]{:S(2)}) async-start(), calls=%async_computation.5 | async-start | bytes 5283840
  731.9 5.6 copy-start.11
  731.9 5.6 copy-start.13
  747.9 5.3 copy-start.5
  747.9 5.3 copy-start.6
  756.3 1.3 copy-start.15
  768.8 6.1 copy-start.9
  768.8 6.1 copy-start.16
Sparse Core Ops, SparseCore 0:
  9.7 197.2 all-gather.4
  209.3 194.7 all-gather.2
  494.7 147.9 all-reduce.2
  655.4 634.3 reduce-scatter.4
  1292.0 639.1 reduce-scatter.6
where the time goes:
time: 1950 us; the launch traced here: 1940 us
  waiting for transfers between devices  1690 us (87%)
  blocking collectives  129 us (7%)
  matrix products  68.6 us (4%)
  other arithmetic  26.4 us (1%)
    unnamed x6, waiting for transfers between devices  641 us
    reduce_scatter x1, waiting for transfers between devices, per_device(): lax.psum_scatter(lax.dot_general(columns, cotangent, contract_first, pref...  511 us
    all_gather x1, waiting for transfers between devices, per_device(): lax.all_gather(w_out, ('ctx', 'seq'), axis=0, tiled=True)  198 us
    all_gather x1, waiting for transfers between devices, per_device(): lax.all_gather(w_joined, ('ctx', 'seq'), axis=0, tiled=True)  191 us
    psum x1, waiting for transfers between devices, per_device(): state_sum, norm_sum = lax.psum((state_part, norm_part), ('ctx', 'seq'))  148 us
    psum x1, blocking collectives, per_device(): state_grad, norm_grad = lax.psum((state_gpart, norm_gpart), ('ctx', 'seq'))  65 us
    psum x1, blocking collectives, per_device(): state_sum, norm_sum = lax.psum((state_part, norm_part), ('ctx', 'seq'))  63.7 us
  transfers between devices with their start and end apart: 5, of which 5 were waited for; matrix products, arithmetic and copies ran while one was open for 3% of the time, Pallas kernels for 0%

commit v1 on v0

v1 whole, which is shorter than its diff:
```python
import jax
import jax.numpy as jnp
from jax import lax
from jax.sharding import PartitionSpec as P

H = 8
DK = 16
DV = 128
BANDS = DK // 2 + 1
FPAD = (BANDS + 2) * DK
AXES = ("ctx", "seq")
BF = jnp.bfloat16
F32 = jnp.float32
SQUARE = (2.0 * DK) ** (-0.5)
LINEAR = DK ** (-0.25)


def dot(a, b, contract):
    return lax.dot_general(a, b, ((contract[:1], contract[1:]), ((), ())), preferred_element_type=F32)


def band_weight():
    row = jnp.arange(FPAD)
    twice = (row >= DK) & (row < (BANDS - 1) * DK)
    return jnp.where(twice, 2.0, 1.0).astype(F32)


def shifted(u, d):
    return jnp.concatenate([u[d:], u[:d]], axis=0) if d else u


def features(u):
    tok = u.shape[1]
    bands = [u * shifted(u, d) * SQUARE for d in range(BANDS)]
    first = lax.broadcasted_iota(jnp.int32, (DK, tok), 0) == 0
    return jnp.concatenate(bands + [u * LINEAR, jnp.where(first, 1.0, 0.0)], axis=0).astype(BF)


def features_back(u, fgrad):
    def band(d):
        return fgrad[d * DK : (d + 1) * DK]

    total = band(0) * u + band(BANDS - 1) * shifted(u, BANDS - 1)
    for d in range(1, BANDS - 1):
        total = total + band(d) * shifted(u, d) + shifted(band(d) * u, DK - d)
    return total * (2.0 * SQUARE) + band(BANDS) * LINEAR


def head_rows(array, head, size):
    return array[head * size : (head + 1) * size]


def keys_phase(tokens, w_qkv, heads):
    qk = heads * DK
    qk_t = dot(w_qkv[:, : 2 * qk], tokens, (0, 1)).astype(BF)
    value = dot(tokens, w_qkv[:, 2 * qk :], (1, 0)).astype(BF)
    states, norms, feats = [], [], []
    for head in range(heads):
        feat = features(head_rows(qk_t[qk:], head, DK).astype(F32))
        states.append(dot(feat, value[:, head * DV : (head + 1) * DV], (1, 0)))
        norms.append(jnp.sum(feat.astype(F32), axis=1))
        feats.append(feat)
    return qk_t, value, jnp.concatenate(feats), jnp.concatenate(states).astype(BF), jnp.concatenate(norms)


def query_phase(qk_t, up_t, norm, heads):
    weight = band_weight()
    sgrads, feats, scales = [], [], []
    for head in range(heads):
        feat = features(head_rows(qk_t, head, DK).astype(F32))
        weighted = weight * head_rows(norm, head, FPAD)
        scale = 1.0 / jnp.sum(feat.astype(F32) * weighted[:, None], axis=0, keepdims=True)
        grad_num = (head_rows(up_t, head, DV) * scale).astype(BF)
        sgrads.append(dot(feat, grad_num, (1, 1)))
        feats.append(feat)
        scales.append(scale)
    return jnp.concatenate(feats), jnp.concatenate(scales), jnp.concatenate(sgrads).astype(BF)


def attend_phase(qk_t, feats, scales, up_t, state, norm, heads):
    weight = band_weight()
    attended, qgrads, ngrads = [], [], []
    for head in range(heads):
        feat = head_rows(feats, head, FPAD)
        scale = scales[head : head + 1]
        head_state = head_rows(state, head, FPAD)
        weighted = (head_state.astype(F32) * weight[:, None]).astype(BF)
        att = dot(weighted, feat, (0, 0)) * scale
        grad_num = head_rows(up_t, head, DV) * scale
        grad_den = -jnp.sum(grad_num * att, axis=0, keepdims=True)
        ngrads.append(jnp.sum(feat.astype(F32) * grad_den, axis=1))
        fgrad = dot(head_state, grad_num.astype(BF), (1, 0))
        fgrad = fgrad + head_rows(norm, head, FPAD)[:, None] * grad_den
        u = head_rows(qk_t, head, DK).astype(F32)
        qgrads.append(features_back(u, fgrad).astype(BF))
        attended.append(att.astype(BF))
    return jnp.concatenate(attended), jnp.concatenate(qgrads), jnp.concatenate(ngrads)


def back_phase(qk_t, value, feats, sgrad, ngrad, heads):
    weight = band_weight()
    kgrads, vgrads = [], []
    for head in range(heads):
        head_sgrad = head_rows(sgrad, head, FPAD)
        fgrad = dot(head_sgrad, value[:, head * DV : (head + 1) * DV], (1, 1))
        fgrad = fgrad + head_rows(ngrad, head, FPAD)[:, None]
        u = head_rows(qk_t[heads * DK :], head, DK).astype(F32)
        kgrads.append(features_back(u, fgrad).astype(BF))
        weighted = (head_sgrad.astype(F32) * weight[:, None]).astype(BF)
        vgrads.append(dot(weighted, head_rows(feats, head, FPAD), (0, 0)).astype(BF))
    return jnp.concatenate(kgrads), jnp.concatenate(vgrads)


def per_device(chips, tokens, w_query, w_key, w_value, w_out, cotangent):
    n = 2 * chips
    heads = H // 2
    core = lax.axis_index("seq") % 2
    same_core = [[2 * p + c for p in range(chips)] for c in range(2)]
    swap = [(i, i ^ 1) for i in range(n)]
    scale_factor = (tokens.shape[0] * n) ** (-0.5)

    def exchange(x):
        return lax.ppermute(x, AXES, swap)

    def spread(x):
        return lax.all_to_all(x, AXES, 0, 0, axis_index_groups=same_core, tiled=True)

    def sum_small(x):
        row = jnp.pad(x, (0, -x.shape[0] % 1024)).reshape(1, -1, 128)
        every = spread(jnp.broadcast_to(row, (chips,) + row.shape[1:]))
        return jnp.sum(every, axis=0).reshape(-1)[: x.shape[0]]

    def sum_state(x):
        rows, cols = x.shape
        part = rows // chips
        own = jnp.sum(spread(x.reshape(chips, part, cols)).astype(F32), axis=0).astype(BF)
        return spread(jnp.broadcast_to(own[None], (chips, part, cols))).reshape(rows, cols)

    halves = [
        jnp.concatenate(
            [
                w_query[:, c * heads * DK : (c + 1) * heads * DK],
                w_key[:, c * heads * DK : (c + 1) * heads * DK],
                w_value[:, c * heads * DV : (c + 1) * heads * DV],
            ],
            axis=1,
        )
        for c in range(2)
    ]
    to_send = jnp.broadcast_to(jnp.stack(halves)[None], (chips, 2) + halves[0].shape)
    w_qkv = lax.all_to_all(to_send.reshape((n,) + halves[0].shape), AXES, 0, 0, tiled=True)
    w_qkv = w_qkv.reshape(-1, halves[0].shape[1])
    out_rows = lax.ppermute(w_out, AXES, [(c * chips + p, 2 * p + c) for p in range(chips) for c in range(2)])
    w_out_half = spread(jnp.broadcast_to(out_rows[None], (chips,) + out_rows.shape)).reshape(-1, out_rows.shape[1])

    tok = jnp.concatenate([tokens, exchange(tokens)])
    cot = jnp.concatenate([cotangent, exchange(cotangent)])
    own = tokens.shape[0]

    qk_t, value, key_feat, state_part, norm_part = keys_phase(tok, w_qkv, heads)
    norm = sum_small(norm_part)
    state = sum_state(state_part)
    up_t = dot(w_out_half, cot, (1, 1))
    query_feat, scales, sgrad_part = query_phase(qk_t, up_t, norm, heads)
    sgrad = sum_state(sgrad_part)
    moments = dot(tok, key_feat, (0, 1))

    attended_t, qgrad_t, ngrad_part = attend_phase(qk_t, query_feat, scales, up_t, state, norm, heads)
    ngrad = sum_small(ngrad_part)
    mixed_part = dot(attended_t, w_out_half, (0, 0)).astype(BF)
    mixed_other = exchange(mixed_part[own:])
    mixed = (mixed_part[:own].astype(F32) + mixed_other.astype(F32)).astype(BF)

    early = jnp.concatenate([moments, dot(tok, qgrad_t, (0, 1))], axis=1).astype(BF)
    early = jnp.sum(spread(early.reshape(chips, -1, early.shape[1])).astype(F32), axis=0)
    out_part = dot(attended_t, cot, (1, 0)).astype(BF)
    out_sum = jnp.sum(spread(out_part.reshape(chips, -1, out_part.shape[1])).astype(F32), axis=0)
    grad_out = lax.ppermute(out_sum, AXES, [(2 * p + c, c * chips + p) for p in range(chips) for c in range(2)])

    kgrad_t, vgrad_t = back_phase(qk_t, value, key_feat, sgrad, ngrad, heads)
    kgrad_part = dot(tok, kgrad_t, (0, 1)).astype(BF)
    kgrad_all = lax.all_to_all(kgrad_part.reshape(n, -1, kgrad_part.shape[1]), AXES, 0, 0, tiled=True)
    kgrad_sum = jnp.sum(kgrad_all.reshape((chips, 2) + kgrad_all.shape[1:]).astype(F32), axis=0)
    joined_t = jnp.concatenate([qgrad_t, kgrad_t, vgrad_t])
    gtok_part = dot(joined_t, w_qkv, (0, 1)).astype(BF)
    gtok_other = exchange(gtok_part[own:])
    grad_tokens = (gtok_part[:own].astype(F32) + gtok_other.astype(F32)).astype(BF)

    weight = band_weight()
    gvalue = jnp.concatenate(
        [
            jnp.dot(
                early[:, h * FPAD : (h + 1) * FPAD] * weight,
                head_rows(sgrad, h, FPAD).astype(F32),
                precision=lax.Precision.HIGH,
            )
            for h in range(heads)
        ],
        axis=1,
    )
    mine = jnp.concatenate([early[:, heads * FPAD :], gvalue], axis=1)
    rows = mine.shape[0] // 2
    got = exchange(lax.dynamic_slice_in_dim(mine, (1 - core) * rows, rows, 0))
    kept = lax.dynamic_slice_in_dim(mine, core * rows, rows, 0)
    low, high = jnp.where(core == 0, kept, got), jnp.where(core == 0, got, kept)
    qk = heads * DK
    grad_query = jnp.concatenate([low[:, :qk], high[:, :qk]], axis=1) * scale_factor
    grad_value = jnp.concatenate([low[:, qk:], high[:, qk:]], axis=1) * scale_factor
    grad_key = jnp.concatenate([kgrad_sum[0], kgrad_sum[1]], axis=1) * scale_factor
    return (mixed, grad_tokens, grad_query, grad_key, grad_value, grad_out * scale_factor)


def solution(mesh):
    chips = mesh.size // 2
    placed = P(AXES, None)
    return jax.shard_map(
        lambda *args: per_device(chips, *args),
        mesh=mesh,
        in_specs=(placed,) * 6,
        out_specs=(placed,) * 6,
        check_vma=False,
    )
```

time: 1950 us -> 343 us (0.18)
  waiting for transfers between devices: 1690 us -> 39 us
  blocking collectives: 129 us -> 0 us
  starting transfers between devices: 0.41 us -> 105 us
  local copies, waits for them, and re-layouts: 15.2 us -> 63.8 us
  other arithmetic: 26.4 us -> 60.4 us
    unnamed x6 -> x0, waiting for transfers between devices: 641 us -> none
    reduce_scatter x1 -> x0, waiting for transfers between devices: 511 us -> none  [per_device(): lax.psum_scatter(lax.dot_general(columns, cotangent, contract_first, pref...]
    all_gather x2 -> x0, waiting for transfers between devices: 388 us -> none  [the longest x1 198 us: per_device(): lax.all_gather(w_out, ('ctx', 'seq'), axis=0, tiled=True)]
    psum x1 -> x0, waiting for transfers between devices: 148 us -> none  [per_device(): state_sum, norm_sum = lax.psum((state_part, norm_part), ('ctx', 'seq'))]
    psum x2 -> x0, blocking collectives: 129 us -> none  [the longest x1 65 us: per_device(): state_grad, norm_grad = lax.psum((state_gpart, norm_gpart), ('ctx', 'seq'))]
    all_to_all x0 -> x11, starting transfers between devices: none -> 88.9 us  [the longest x9 68.9 us: spread(): lax.all_to_all(x, AXES, 0, 0, axis_index_groups=same_core, tiled=True)]
    all_to_all x0 -> x11, waiting for transfers between devices: none -> 35.6 us  [the longest x9 21.1 us: spread(): lax.all_to_all(x, AXES, 0, 0, axis_index_groups=same_core, tiled=True)]
    slice x4 -> x197, local copies, waits for them, and re-layouts: 1.57 us -> 32.4 us  [the longest x176 17.7 us: shifted(): return jnp.concatenate([u[d:], u[:d]], axis=0) if d else u]
  transfers between devices with their start and end apart: 5 -> 18, of which waited for: 5 -> 10; matrix products, arithmetic and copies ran while one was open for 3% -> 46% of each run, Pallas kernels for 0% -> 0%
where the time goes in v1:
time: 343 us; the launch traced here: 336 us
  starting transfers between devices  105 us (31%)
  local copies, waits for them, and re-layouts  63.8 us (19%)
  matrix products  61 us (18%)
  other arithmetic  60.4 us (18%)
  waiting for transfers between devices  39 us (11%)
  between operations  6.67 us (2%)
    all_to_all x9, starting transfers between devices, spread(): lax.all_to_all(x, AXES, 0, 0, axis_index_groups=same_core, tiled=True)  68.9 us
    dot_general x33, matrix products, dot(): lax.dot_general(a, b, ((contract[:1], contract[1:]), ((), ())), preferred...  60.3 us
    unnamed x55, other arithmetic  29.2 us
    all_to_all x9, waiting for transfers between devices, spread(): lax.all_to_all(x, AXES, 0, 0, axis_index_groups=same_core, tiled=True)  21.1 us
    slice x176, local copies, waits for them, and re-layouts, shifted(): return jnp.concatenate([u[d:], u[:d]], axis=0) if d else u  17.7 us
    unnamed x589, local copies, waits for them, and re-layouts  12.7 us
    all_to_all x1, starting transfers between devices, per_device(): lax.all_to_all(to_send.reshape((n,) + halves[0].shape), AXES, 0, 0, tiled...  10.2 us
    all_to_all x1, starting transfers between devices, per_device(): lax.all_to_all(kgrad_part.reshape(n, -1, kgrad_part.shape[1]), AXES, 0, 0...  9.73 us
  transfers between devices with their start and end apart: 18, of which 10 were waited for; matrix products, arithmetic and copies ran while one was open for 46% of the time, Pallas kernels for 0%

profile of v1, /device:TPU:1, one launch (start us, length us, event | category | flops | bytes accessed | tf_op | source)
XLA Modules:
  0.0 336.3 jit_solution(56554401210706348)
XLA Ops:
  0.7 1.5 collective-permute-start
  5.8 10.2 %all-to-all-start = ((bf16[128,8,640]{2,1,0:T(8,128)(2,1)}), bf16[128,8,640]{2,1,0:T(8,128)(2,1)S(1)}, u32[]{:S(2)}, u32[]{:S(2)}) async-start(bf16[128,8,640]{2,1,0:T(8,128)(2,1)} %bitcast.2), calls=%async_computation | async-start | bytes 2621440 | tf_op jit(solution)/shard_map/all_to_all | solution.py:151
  16.0 3.5 %collective-permute-start.1 = (bf16[8,1024]{1,0:T(8,128)(2,1)S(1)}, bf16[8,1024]{1,0:T(8,128)(2,1)S(1)}, u32[]{:S(2)}, u32[]{:S(2)}) collective-permute-start(bf16[8,1024]{1,0:T(8,128)(2,1)S(1)} %copy-done.276), channel_id=1, source_target_pairs={{0,0},{64,1},{1,2},{65,3},{2,4},{66,5},{3,6},{67,7},{4,8},{68,9},{... | collective-permute-start | bytes 49160 | tf_op jit(solution)/shard_map/ppermute | solution.py:153
  20.3 1.6 constant_dynamic-update-slice_fusion.1
  21.9 1.5 constant_dynamic-update-slice_fusion.91
  23.4 3.1 constant_dynamic-update-slice_fusion
  26.5 3.2 collective-permute-done.1
  29.6 8.3 %all-to-all-done = bf16[128,8,640]{2,1,0:T(8,128)(2,1)S(1)} async-done(((bf16[128,8,640]{2,1,0:T(8,128)(2,1)}), bf16[128,8,640]{2,1,0:T(8,128)(2,1)S(1)}, u32[]{:S(2)}, u32[]{:S(2)}) %all-to-all-start) | async-done | bytes 1310752 | tf_op jit(solution)/shard_map/all_to_all | solution.py:151
  39.2 5.8 %all-to-all-start.4 = ((bf16[64,8,1024]{2,1,0:T(8,128)(2,1)}), bf16[64,8,1024]{2,1,0:T(8,128)(2,1)}, u32[]{:S(2)}, u32[]{:S(2)}) async-start(bf16[64,8,1024]{2,1,0:T(8,128)(2,1)} %broadcast_in_dim.60), calls=%async_computation.4 | async-start | bytes 2097152 | tf_op jit(solution)/shard_map/all_to_all | solution.py:126
  45.0 3.7 %convolution_convert_fusion.7 = bf16[128,2048]{1,0:T(8,128)(2,1)S(1)} fusion(bf16[2048,1024]{1,0:T(8,128)(2,1)} %constant_dynamic-update-slice_fusion, bf16[1024,640]{1,0:T(8,128)(2,1)S(1)} %bitcast.126), kind=kOutput, calls=%fused_computation.27 | convolution fusion | flops 537133056 | bytes 4980736 | tf_op jit(solution)/shard_map/dot_general | solution.py:19
  54.7 4.6 %convolution_convert_fusion.2 = bf16[2048,512]{1,0:T(8,128)(2,1)S(1)} fusion(bf16[2048,1024]{1,0:T(8,128)(2,1)} %constant_dynamic-update-slice_fusion, bf16[1024,640]{1,0:T(8,128)(2,1)S(1)} %bitcast.127), kind=kOutput, calls=%fused_computation.6 | convolution fusion | flops 2148532224 | bytes 7340032 | tf_op jit(solution)/shard_map/dot_general | solution.py:19
  85.5 1.7 convert_element_type.257
  87.2 1.4 convert_reduce_fusion.4
  91.2 1.9 convert_reduce_fusion.5
  93.1 6.5 %convolution_convert_fusion.8 = bf16[1024,704]{0,1:T(8,128)(2,1)} fusion(bf16[704,2048]{1,0:T(8,128)(2,1)S(1)} %copy-done.275, bf16[2048,1024]{1,0:T(8,128)(2,1)} %constant_dynamic-update-slice_fusion), kind=kOutput, calls=%fused_computation.38 | convolution fusion | flops 2953510912 | bytes 8519680 | tf_op jit(solution)/shard_map/dot_general | solution.py:19
  99.6 10.7 %all-to-all-start.1 = ((bf16[64,11,128]{2,1,0:T(8,128)(2,1)}), bf16[64,11,128]{2,1,0:T(8,128)(2,1)}, u32[]{:S(2)}, u32[]{:S(2)}) async-start(bf16[64,11,128]{2,1,0:T(8,128)(2,1)} %convert_element_type.257), calls=%async_computation.1 | async-start | bytes 524288 | tf_op jit(solution)/shard_map/all_to_all | solution.py:126
  111.0 3.1 constant_dynamic-update-slice_fusion.90
  114.2 5.3 %all-to-all-done.1 = bf16[64,11,128]{2,1,0:T(8,128)(2,1)} async-done(((bf16[64,11,128]{2,1,0:T(8,128)(2,1)}), bf16[64,11,128]{2,1,0:T(8,128)(2,1)}, u32[]{:S(2)}, u32[]{:S(2)}) %all-to-all-start.1) | async-done | bytes 180256 | tf_op jit(solution)/shard_map/all_to_all | solution.py:126
  120.2 5.4 %all-to-all-start.3 = ((f32[64,8,128]{2,1,0:T(8,128)}), f32[64,8,128]{2,1,0:T(8,128)}, u32[]{:S(2)}, u32[]{:S(2)}) async-start(f32[64,8,128]{2,1,0:T(8,128)} %broadcast_in_dim.59), calls=%async_computation.3 | async-start | bytes 524288 | tf_op jit(solution)/shard_map/all_to_all | solution.py:126
  125.6 6.8 %convolution_bitcast_fusion = f32[512,2048]{1,0:T(8,128)} fusion(bf16[2048,1024]{1,0:T(8,128)(2,1)} %constant_dynamic-update-slice_fusion.90, bf16[64,8,1024]{2,1,0:T(8,128)(2,1)} %all-to-all-done.4), kind=kOutput, calls=%fused_computation.4 | convolution fusion | flops 2147483648 | bytes 9437184 | tf_op jit(solution)/shard_map/dot_general | solution.py:19
  132.4 2.6 copy.15
  136.8 10.0 %all-to-all-start.2 = ((bf16[64,11,128]{2,1,0:T(8,128)(2,1)}), bf16[64,11,128]{2,1,0:T(8,128)(2,1)}, u32[]{:S(2)}, u32[]{:S(2)}) async-start(bf16[64,11,128]{2,1,0:T(8,128)(2,1)} %broadcast_in_dim.55), calls=%async_computation.2 | async-start | bytes 524288 | tf_op jit(solution)/shard_map/all_to_all | solution.py:126
  150.0 1.6 convolution_convert_fusion.12
  153.4 1.7 convert_element_type.294
  155.9 9.3 %all-to-all-start.5 = ((bf16[64,11,128]{2,1,0:T(8,128)(2,1)}), bf16[64,11,128]{2,1,0:T(8,128)(2,1)}, u32[]{:S(2)}, u32[]{:S(2)}) async-start(bf16[64,11,128]{2,1,0:T(8,128)(2,1)} %convert_element_type.294), calls=%async_computation.5 | async-start | bytes 524288 | tf_op jit(solution)/shard_map/all_to_all | solution.py:126
  165.2 1.7 fusion.412
  166.9 1.5 slice.1460
  168.4 1.5 slice.1520
  169.9 1.5 slice.1500
  171.4 1.5 slice.1480
  182.2 1.6 copy-done.130
  183.9 3.3 fusion.12
  187.5 2.2 constant_dynamic-update-slice_fusion.99
  189.9 2.1 constant_dynamic-update-slice_fusion.98
  192.1 2.0 constant_dynamic-update-slice_fusion.97
  197.0 9.9 %all-to-all-start.6 = ((bf16[64,11,128]{2,1,0:T(8,128)(2,1)}), bf16[64,11,128]{2,1,0:T(8,128)(2,1)S(1)}, u32[]{:S(2)}, u32[]{:S(2)}) async-start(bf16[64,11,128]{2,1,0:T(8,128)(2,1)} %broadcast_in_dim.61), calls=%async_computation.6 | async-start | bytes 524288 | tf_op jit(solution)/shard_map/all_to_all | solution.py:126
  213.8 2.4 all-to-all-done.6
  216.9 7.6 %all-to-all-start.7 = ((f32[64,8,128]{2,1,0:T(8,128)}), f32[64,8,128]{2,1,0:T(8,128)S(1)}, u32[]{:S(2)}, u32[]{:S(2)}) async-start(f32[64,8,128]{2,1,0:T(8,128)} %broadcast_in_dim.117), calls=%async_computation.7 | async-start | bytes 524288 | tf_op jit(solution)/shard_map/all_to_all | solution.py:126
  224.6 2.7 constant_dynamic-update-slice_fusion.96
  228.8 5.0 %all-to-all-done.7 = f32[64,8,128]{2,1,0:T(8,128)S(1)} async-done(((f32[64,8,128]{2,1,0:T(8,128)}), f32[64,8,128]{2,1,0:T(8,128)S(1)}, u32[]{:S(2)}, u32[]{:S(2)}) %all-to-all-start.7) | async-done | bytes 262176 | tf_op jit(solution)/shard_map/all_to_all | solution.py:126
  234.0 1.4 convolution_add_fusion.3
  235.6 1.5 convolution_add_fusion.2
  240.4 2.0 constant_dynamic-update-slice_fusion.94
  242.7 2.0 constant_dynamic-update-slice_fusion.93
  244.8 1.9 constant_dynamic-update-slice_fusion.92
  246.7 3.1 convolution_convert_fusion.10
  250.8 9.7 %all-to-all-start.9 = ((bf16[128,2,256]{2,1,0:T(2,128)(2,1)}), bf16[128,2,256]{2,1,0:T(2,128)(2,1)S(1)}, u32[]{:S(2)}, u32[]{:S(2)}) async-start(bf16[128,2,256]{2,1,0:T(2,128)(2,1)} %reshape.133), calls=%async_computation.9 | async-start | bytes 262144 | tf_op jit(solution)/shard_map/all_to_all | solution.py:182
  260.6 3.2 convolution_convert_fusion.11
  264.6 6.2 %all-to-all-done.9 = bf16[128,2,256]{2,1,0:T(2,128)(2,1)S(1)} async-done(((bf16[128,2,256]{2,1,0:T(2,128)(2,1)}), bf16[128,2,256]{2,1,0:T(2,128)(2,1)S(1)}, u32[]{:S(2)}, u32[]{:S(2)}) %all-to-all-start.9) | async-done | bytes 131104 | tf_op jit(solution)/shard_map/all_to_all | solution.py:182
  271.5 4.7 %all-to-all-start.10 = ((bf16[64,8,1024]{2,1,0:T(8,128)(2,1)}), bf16[64,8,1024]{2,1,0:T(8,128)(2,1)S(1)}, u32[]{:S(2)}, u32[]{:S(2)}) async-start(bf16[64,8,1024]{2,1,0:T(8,128)(2,1)} %fusion.12), calls=%async_computation.10 | async-start | bytes 2097152 | tf_op jit(solution)/shard_map/all_to_all | solution.py:126
  276.3 3.6 %convolution_convert_fusion.1 = bf16[2048,1024]{1,0:T(8,128)(2,1)S(1)} fusion(bf16[64,8,1024]{2,1,0:T(8,128)(2,1)} %all-to-all-done.4, bf16[128,2048]{1,0:T(8,128)(2,1)S(1)} %copy-done.211, bf16[128,2048]{1,0:T(8,128)(2,1)S(1)} %copy-done.209, bf16[128,2048]{1,0:T(8,128)(2,1)S(1)} %copy-done.207, bf16[128,2048]{1,0:T(8,128)(2,1)S(1)} %copy-done.205), kind=kOutput, calls=%fused_computation.3 | convolution fusion | flops 2157969408 | bytes 7340032 | tf_op jit(solution)/shard_map/dot_general | solution.py:19
  279.9 1.5 slice.1909
  282.6 1.4 pad_maximum_fusion.1
  286.4 7.0 %all-to-all-done.10 = bf16[64,8,1024]{2,1,0:T(8,128)(2,1)S(1)} async-done(((bf16[64,8,1024]{2,1,0:T(8,128)(2,1)}), bf16[64,8,1024]{2,1,0:T(8,128)(2,1)S(1)}, u32[]{:S(2)}, u32[]{:S(2)}) %all-to-all-start.10) | async-done | bytes 1048608 | tf_op jit(solution)/shard_map/all_to_all | solution.py:126
  293.4 5.5 %all-to-all-start.8 = ((bf16[64,16,768]{2,1,0:T(8,128)(2,1)}), bf16[64,16,768]{2,1,0:T(8,128)(2,1)S(1)}, u32[]{:S(2)}, u32[]{:S(2)}) async-start(bf16[64,16,768]{2,1,0:T(8,128)(2,1)} %pad_maximum_fusion.1), calls=%async_computation.8 | async-start | bytes 3145728 | tf_op jit(solution)/shard_map/all_to_all | solution.py:126
  298.9 2.4 fusion.1
  302.6 5.6 %convolution_convert_fusion = bf16[2048,1024]{1,0:T(8,128)(2,1)S(1)} fusion(bf16[640,2048]{1,0:T(8,128)(2,1)} %fusion, bf16[128,8,640]{2,1,0:T(8,128)(2,1)} %copy-done.18), kind=kOutput, calls=%fused_computation.2 | convolution fusion | flops 2686451712 | bytes 8126464 | tf_op jit(solution)/shard_map/dot_general | solution.py:19
  308.2 1.9 copy-done.5
  310.1 1.5 slice.2111
  311.6 2.1 collective-permute-start.4
  314.8 4.7 %collective-permute-start.6 = (f32[8,1024]{1,0:T(8,128)S(1)}, f32[8,1024]{1,0:T(8,128)S(1)}, u32[]{:S(2)}, u32[]{:S(2)}) collective-permute-start(f32[8,1024]{1,0:T(8,128)S(1)} %convert_reduce_fusion.1), channel_id=1, source_target_pairs={{0,0},{1,64},{2,1},{3,65},{4,2},{5,66},{6,3},{7,67},{8,4},{9,68},{... | collective-permute-start | bytes 98312 | tf_op jit(solution)/shard_map/ppermute | solution.py:178
  321.2 4.0 %collective-permute-start.5 = (f32[8,576]{1,0:T(8,128)S(1)}, f32[8,576]{1,0:T(8,128)S(1)}, u32[]{:S(2)}, u32[]{:S(2)}) collective-permute-start(f32[8,576]{1,0:T(8,128)S(1)} %constant_dynamic-slice_fusion), channel_id=1, source_target_pairs={{0,1},{1,0},{2,3},{3,2},{4,5},{5,4},{6,7},{7,6},{8,9},{9,8},{10,11... | collective-permute-start | bytes 55304 | tf_op jit(solution)/shard_map/ppermute | solution.py:123
  327.5 4.7 %add_convert_fusion.1 = bf16[1024,1024]{1,0:T(8,128)(2,1)} fusion(bf16[1024,1024]{1,0:T(8,128)(2,1)} %collective-permute-done.2, bf16[2048,1024]{1,0:T(8,128)(2,1)} %copy-done.4), kind=kLoop, calls=%fused_computation.1 | loop fusion | flops 4194304 | bytes 6291456 | tf_op jit(solution)/shard_map/convert_element_type | solution.py:172
  332.1 3.9 %add_convert_fusion = bf16[1024,1024]{1,0:T(8,128)(2,1)} fusion(bf16[1024,1024]{1,0:T(8,128)(2,1)} %collective-permute-done.4, bf16[2048,1024]{1,0:T(8,128)(2,1)S(1)} %copy-done.6), kind=kLoop, calls=%fused_computation | loop fusion | flops 4194304 | bytes 6291456 | tf_op jit(solution)/shard_map/convert_element_type | solution.py:187
  (921 shorter events, 82.9 us)
Async XLA Ops:
  0.6 19.6 %copy-start.16 = (bf16[1024,1024]{1,0:T(8,128)(2,1)S(1)}, bf16[1024,1024]{1,0:T(8,128)(2,1)}, u32[]{:S(2)}) copy-start(bf16[1024,1024]{1,0:T(8,128)(2,1)} %param.6) | copy-start | bytes 6291460
  0.6 15.4 %copy-start.276 = (bf16[8,1024]{1,0:T(8,128)(2,1)S(1)}, bf16[8,1024]{1,0:T(8,128)(2,1)}, u32[]{:S(2)}) copy-start(bf16[8,1024]{1,0:T(8,128)(2,1)} %param.10) | copy-start | bytes 49156
  0.7 22.7 %collective-permute-start = (bf16[1024,1024]{1,0:T(8,128)(2,1)}, bf16[1024,1024]{1,0:T(8,128)(2,1)}, u32[]{:S(2)}, u32[]{:S(2)}) collective-permute-start(bf16[1024,1024]{1,0:T(8,128)(2,1)} %param.6), channel_id=1, source_target_pairs={{0,1},{1,0},{2,3},{3,2},{4,5},{5,4},{6,7},{7,6},{8,9},{9,8},{10,11... | collective-permute-start | bytes 6291464 | tf_op jit(solution)/shard_map/ppermute | solution.py:123
  5.8 32.2 %all-to-all-start = ((bf16[128,8,640]{2,1,0:T(8,128)(2,1)}), bf16[128,8,640]{2,1,0:T(8,128)(2,1)S(1)}, u32[]{:S(2)}, u32[]{:S(2)}) async-start(bf16[128,8,640]{2,1,0:T(8,128)(2,1)} %bitcast.2), calls=%async_computation | async-start | bytes 2621440 | tf_op jit(solution)/shard_map/all_to_all | solution.py:151
  16.0 13.6 %collective-permute-start.1 = (bf16[8,1024]{1,0:T(8,128)(2,1)S(1)}, bf16[8,1024]{1,0:T(8,128)(2,1)S(1)}, u32[]{:S(2)}, u32[]{:S(2)}) collective-permute-start(bf16[8,1024]{1,0:T(8,128)(2,1)S(1)} %copy-done.276), channel_id=1, source_target_pairs={{0,0},{64,1},{1,2},{65,3},{2,4},{66,5},{3,6},{67,7},{4,8},{68,9},{... | collective-permute-start | bytes 49160 | tf_op jit(solution)/shard_map/ppermute | solution.py:153
  19.6 91.5 %collective-permute-start.3 = (bf16[1024,1024]{1,0:T(8,128)(2,1)}, bf16[1024,1024]{1,0:T(8,128)(2,1)}, u32[]{:S(2)}, u32[]{:S(2)}) collective-permute-start(bf16[1024,1024]{1,0:T(8,128)(2,1)} %param.11), channel_id=1, source_target_pairs={{0,1},{1,0},{2,3},{3,2},{4,5},{5,4},{6,7},{7,6},{8,9},{9,8},{10,11... | collective-permute-start | bytes 6291464 | tf_op jit(solution)/shard_map/ppermute | solution.py:123
  39.2 60.4 %all-to-all-start.4 = ((bf16[64,8,1024]{2,1,0:T(8,128)(2,1)}), bf16[64,8,1024]{2,1,0:T(8,128)(2,1)}, u32[]{:S(2)}, u32[]{:S(2)}) async-start(bf16[64,8,1024]{2,1,0:T(8,128)(2,1)} %broadcast_in_dim.60), calls=%async_computation.4 | async-start | bytes 2097152 | tf_op jit(solution)/shard_map/all_to_all | solution.py:126
  52.2 13.2 %copy-start.104 = (f32[9,2048]{1,0:T(8,128)}, f32[9,2048]{1,0:T(8,128)S(1)}, u32[]{:S(2)}) copy-start(f32[9,2048]{1,0:T(8,128)S(1)} %slice.1850) | copy-start | bytes 221188
  59.3 24.1 %copy-start.14 = (bf16[2048,512]{1,0:T(8,128)(2,1)}, bf16[2048,512]{1,0:T(8,128)(2,1)S(1)}, u32[]{:S(2)}) copy-start(bf16[2048,512]{1,0:T(8,128)(2,1)S(1)} %convolution_convert_fusion.2) | copy-start | bytes 6291460
  64.1 14.3 %copy-start.149 = (f32[7,2048]{1,0:T(8,128)}, f32[7,2048]{1,0:T(8,128)S(1)}, u32[]{:S(2)}) copy-start(f32[7,2048]{1,0:T(8,128)S(1)} %slice.1905) | copy-start | bytes 172036
  64.9 11.6 %copy-start.110 = (f32[11,2048]{1,0:T(8,128)}, f32[11,2048]{1,0:T(8,128)S(1)}, u32[]{:S(2)}) copy-start(f32[11,2048]{1,0:T(8,128)S(1)} %slice.1900) | copy-start | bytes 270340
  64.9 10.7 %copy-start.112 = (f32[12,2048]{1,0:T(8,128)}, f32[12,2048]{1,0:T(8,128)S(1)}, u32[]{:S(2)}) copy-start(f32[12,2048]{1,0:T(8,128)S(1)} %slice.1898) | copy-start | bytes 294916
  64.9 13.5 %copy-start.54 = (f32[9,2048]{1,0:T(8,128)}, f32[9,2048]{1,0:T(8,128)S(1)}, u32[]{:S(2)}) copy-start(f32[9,2048]{1,0:T(8,128)S(1)} %slice.1904) | copy-start | bytes 221188
  65.0 9.8 %copy-start.56 = (f32[13,2048]{1,0:T(8,128)}, f32[13,2048]{1,0:T(8,128)S(1)}, u32[]{:S(2)}) copy-start(f32[13,2048]{1,0:T(8,128)S(1)} %slice.1896) | copy-start | bytes 319492
  65.0 8.9 %copy-start.58 = (f32[14,2048]{1,0:T(8,128)}, f32[14,2048]{1,0:T(8,128)S(1)}, u32[]{:S(2)}) copy-start(f32[14,2048]{1,0:T(8,128)S(1)} %slice.1894) | copy-start | bytes 344068
  65.1 12.4 %copy-start.114 = (f32[10,2048]{1,0:T(8,128)}, f32[10,2048]{1,0:T(8,128)S(1)}, u32[]{:S(2)}) copy-start(f32[10,2048]{1,0:T(8,128)S(1)} %slice.1902) | copy-start | bytes 245764
  65.1 17.0 %copy-start.163 = (f32[8,2048]{1,0:T(8,128)}, f32[8,2048]{1,0:T(8,128)S(1)}, u32[]{:S(2)}) copy-start(f32[8,2048]{1,0:T(8,128)S(1)} %get-tuple-element.230) | copy-start | bytes 196612
  65.1 17.0 %copy-start.165 = (f32[8,2048]{1,0:T(8,128)}, f32[8,2048]{1,0:T(8,128)S(1)}, u32[]{:S(2)}) copy-start(f32[8,2048]{1,0:T(8,128)S(1)} %get-tuple-element.231) | copy-start | bytes 196612
  71.5 10.3 %copy-start.176 = (f32[5,2048]{1,0:T(8,128)}, f32[5,2048]{1,0:T(8,128)S(1)}, u32[]{:S(2)}) copy-start(f32[5,2048]{1,0:T(8,128)S(1)} %slice.1828) | copy-start | bytes 122884
  71.6 10.4 %copy-start.178 = (f32[7,2048]{1,0:T(8,128)}, f32[7,2048]{1,0:T(8,128)S(1)}, u32[]{:S(2)}) copy-start(f32[7,2048]{1,0:T(8,128)S(1)} %slice.1832) | copy-start | bytes 172036
  71.6 10.3 %copy-start.180 = (f32[6,2048]{1,0:T(8,128)}, f32[6,2048]{1,0:T(8,128)S(1)}, u32[]{:S(2)}) copy-start(f32[6,2048]{1,0:T(8,128)S(1)} %slice.1830) | copy-start | bytes 147460
  71.7 10.2 %copy-start.32 = (f32[11,2048]{1,0:T(8,128)}, f32[11,2048]{1,0:T(8,128)S(1)}, u32[]{:S(2)}) copy-start(f32[11,2048]{1,0:T(8,128)S(1)} %slice.1827) | copy-start | bytes 270340
  71.7 9.3 %copy-start.78 = (f32[12,2048]{1,0:T(8,128)}, f32[12,2048]{1,0:T(8,128)S(1)}, u32[]{:S(2)}) copy-start(f32[12,2048]{1,0:T(8,128)S(1)} %slice.1825) | copy-start | bytes 294916
  71.7 10.2 %copy-start.34 = (f32[9,2048]{1,0:T(8,128)}, f32[9,2048]{1,0:T(8,128)S(1)}, u32[]{:S(2)}) copy-start(f32[9,2048]{1,0:T(8,128)S(1)} %slice.1831) | copy-start | bytes 221188
  71.8 8.4 %copy-start.80 = (f32[13,2048]{1,0:T(8,128)}, f32[13,2048]{1,0:T(8,128)S(1)}, u32[]{:S(2)}) copy-start(f32[13,2048]{1,0:T(8,128)S(1)} %slice.1823) | copy-start | bytes 319492
  71.9 10.0 %copy-start.36 = (f32[10,2048]{1,0:T(8,128)}, f32[10,2048]{1,0:T(8,128)S(1)}, u32[]{:S(2)}) copy-start(f32[10,2048]{1,0:T(8,128)S(1)} %slice.1829) | copy-start | bytes 245764
  71.9 10.2 %copy-start.155 = (f32[8,2048]{1,0:T(8,128)}, f32[8,2048]{1,0:T(8,128)S(1)}, u32[]{:S(2)}) copy-start(f32[8,2048]{1,0:T(8,128)S(1)} %get-tuple-element.222) | copy-start | bytes 196612
  71.9 10.2 %copy-start.157 = (f32[8,2048]{1,0:T(8,128)}, f32[8,2048]{1,0:T(8,128)S(1)}, u32[]{:S(2)}) copy-start(f32[8,2048]{1,0:T(8,128)S(1)} %get-tuple-element.223) | copy-start | bytes 196612
  99.6 19.9 %all-to-all-start.1 = ((bf16[64,11,128]{2,1,0:T(8,128)(2,1)}), bf16[64,11,128]{2,1,0:T(8,128)(2,1)}, u32[]{:S(2)}, u32[]{:S(2)}) async-start(bf16[64,11,128]{2,1,0:T(8,128)(2,1)} %convert_element_type.257), calls=%async_computation.1 | async-start | bytes 524288 | tf_op jit(solution)/shard_map/all_to_all | solution.py:126
  120.2 15.9 %all-to-all-start.3 = ((f32[64,8,128]{2,1,0:T(8,128)}), f32[64,8,128]{2,1,0:T(8,128)}, u32[]{:S(2)}, u32[]{:S(2)}) async-start(f32[64,8,128]{2,1,0:T(8,128)} %broadcast_in_dim.59), calls=%async_computation.3 | async-start | bytes 524288 | tf_op jit(solution)/shard_map/all_to_all | solution.py:126
  136.8 19.2 %all-to-all-start.2 = ((bf16[64,11,128]{2,1,0:T(8,128)(2,1)}), bf16[64,11,128]{2,1,0:T(8,128)(2,1)}, u32[]{:S(2)}, u32[]{:S(2)}) async-start(bf16[64,11,128]{2,1,0:T(8,128)(2,1)} %broadcast_in_dim.55), calls=%async_computation.2 | async-start | bytes 524288 | tf_op jit(solution)/shard_map/all_to_all | solution.py:126
  155.9 39.3 %all-to-all-start.5 = ((bf16[64,11,128]{2,1,0:T(8,128)(2,1)}), bf16[64,11,128]{2,1,0:T(8,128)(2,1)}, u32[]{:S(2)}, u32[]{:S(2)}) async-start(bf16[64,11,128]{2,1,0:T(8,128)(2,1)} %convert_element_type.294), calls=%async_computation.5 | async-start | bytes 524288 | tf_op jit(solution)/shard_map/all_to_all | solution.py:126
  192.1 14.7 %copy-start.265 = (f32[2048]{0:T(1024)S(1)}, f32[2048]{0:T(1024)}, u32[]{:S(2)}) copy-start(f32[2048]{0:T(1024)} %copy-done.264) | copy-start | bytes 24580
  194.1 18.9 %copy-start.273 = (f32[176]{0:T(256)S(1)}, f32[176]{0:T(256)}, u32[]{:S(2)}) copy-start(f32[176]{0:T(256)} %fusion.11) | copy-start | bytes 2116
  194.1 30.4 %copy-start.55 = (f32[9,2048]{1,0:T(8,128)S(1)}, f32[9,2048]{1,0:T(8,128)}, u32[]{:S(2)}) copy-start(f32[9,2048]{1,0:T(8,128)} %copy-done.54) | copy-start | bytes 221188
  194.1 30.4 %copy-start.57 = (f32[13,2048]{1,0:T(8,128)S(1)}, f32[13,2048]{1,0:T(8,128)}, u32[]{:S(2)}) copy-start(f32[13,2048]{1,0:T(8,128)} %copy-done.56) | copy-start | bytes 319492
  194.1 30.4 %copy-start.59 = (f32[14,2048]{1,0:T(8,128)S(1)}, f32[14,2048]{1,0:T(8,128)}, u32[]{:S(2)}) copy-start(f32[14,2048]{1,0:T(8,128)} %copy-done.58) | copy-start | bytes 344068
  194.1 30.5 %copy-start.61 = (f32[15,2048]{1,0:T(8,128)S(1)}, f32[15,2048]{1,0:T(8,128)}, u32[]{:S(2)}) copy-start(f32[15,2048]{1,0:T(8,128)} %copy-done.60) | copy-start | bytes 368644
  194.1 30.5 %copy-start.111 = (f32[11,2048]{1,0:T(8,128)S(1)}, f32[11,2048]{1,0:T(8,128)}, u32[]{:S(2)}) copy-start(f32[11,2048]{1,0:T(8,128)} %copy-done.110) | copy-start | bytes 270340
  194.1 30.5 %copy-start.150 = (f32[7,2048]{1,0:T(8,128)S(1)}, f32[7,2048]{1,0:T(8,128)}, u32[]{:S(2)}) copy-start(f32[7,2048]{1,0:T(8,128)} %copy-done.149) | copy-start | bytes 172036
  194.4 30.2 %copy-start.113 = (f32[12,2048]{1,0:T(8,128)S(1)}, f32[12,2048]{1,0:T(8,128)}, u32[]{:S(2)}) copy-start(f32[12,2048]{1,0:T(8,128)} %copy-done.112) | copy-start | bytes 294916
  194.4 30.2 %copy-start.115 = (f32[10,2048]{1,0:T(8,128)S(1)}, f32[10,2048]{1,0:T(8,128)}, u32[]{:S(2)}) copy-start(f32[10,2048]{1,0:T(8,128)} %copy-done.114) | copy-start | bytes 245764
  194.4 30.2 %copy-start.132 = (f32[16,2048]{1,0:T(8,128)S(1)}, f32[16,2048]{1,0:T(8,128)}, u32[]{:S(2)}) copy-start(f32[16,2048]{1,0:T(8,128)} %get-tuple-element.111) | copy-start | bytes 393220
  194.4 30.2 %copy-start.164 = (f32[8,2048]{1,0:T(8,128)S(1)}, f32[8,2048]{1,0:T(8,128)}, u32[]{:S(2)}) copy-start(f32[8,2048]{1,0:T(8,128)} %copy-done.163) | copy-start | bytes 196612
  197.0 19.2 %all-to-all-start.6 = ((bf16[64,11,128]{2,1,0:T(8,128)(2,1)}), bf16[64,11,128]{2,1,0:T(8,128)(2,1)S(1)}, u32[]{:S(2)}, u32[]{:S(2)}) async-start(bf16[64,11,128]{2,1,0:T(8,128)(2,1)} %broadcast_in_dim.61), calls=%async_computation.6 | async-start | bytes 524288 | tf_op jit(solution)/shard_map/all_to_all | solution.py:126
  216.9 16.9 %all-to-all-start.7 = ((f32[64,8,128]{2,1,0:T(8,128)}), f32[64,8,128]{2,1,0:T(8,128)S(1)}, u32[]{:S(2)}, u32[]{:S(2)}) async-start(f32[64,8,128]{2,1,0:T(8,128)} %broadcast_in_dim.117), calls=%async_computation.7 | async-start | bytes 524288 | tf_op jit(solution)/shard_map/all_to_all | solution.py:126
  246.6 13.9 %copy-start.239 = (bf16[16,2048]{1,0:T(8,128)(2,1)S(1)}, bf16[16,2048]{1,0:T(8,128)(2,1)}, u32[]{:S(2)}) copy-start(bf16[16,2048]{1,0:T(8,128)(2,1)} %get-tuple-element.81) | copy-start | bytes 196612
  246.6 13.9 %copy-start.240 = (bf16[16,2048]{1,0:T(8,128)(2,1)S(1)}, bf16[16,2048]{1,0:T(8,128)(2,1)}, u32[]{:S(2)}) copy-start(bf16[16,2048]{1,0:T(8,128)(2,1)} %get-tuple-element.79) | copy-start | bytes 196612
  246.6 13.9 %copy-start.241 = (bf16[16,2048]{1,0:T(8,128)(2,1)S(1)}, bf16[16,2048]{1,0:T(8,128)(2,1)}, u32[]{:S(2)}) copy-start(bf16[16,2048]{1,0:T(8,128)(2,1)} %get-tuple-element.77) | copy-start | bytes 196612
  246.6 13.9 %copy-start.242 = (bf16[16,2048]{1,0:T(8,128)(2,1)S(1)}, bf16[16,2048]{1,0:T(8,128)(2,1)}, u32[]{:S(2)}) copy-start(bf16[16,2048]{1,0:T(8,128)(2,1)} %get-tuple-element.75) | copy-start | bytes 196612
  250.8 20.0 %all-to-all-start.9 = ((bf16[128,2,256]{2,1,0:T(2,128)(2,1)}), bf16[128,2,256]{2,1,0:T(2,128)(2,1)S(1)}, u32[]{:S(2)}, u32[]{:S(2)}) async-start(bf16[128,2,256]{2,1,0:T(2,128)(2,1)} %reshape.133), calls=%async_computation.9 | async-start | bytes 262144 | tf_op jit(solution)/shard_map/all_to_all | solution.py:182
  260.6 15.6 %copy-start.205 = (bf16[128,2048]{1,0:T(8,128)(2,1)S(1)}, bf16[128,2048]{1,0:T(8,128)(2,1)}, u32[]{:S(2)}) copy-start(bf16[128,2048]{1,0:T(8,128)(2,1)} %copy-done.204) | copy-start | bytes 1572868
  260.6 15.6 %copy-start.207 = (bf16[128,2048]{1,0:T(8,128)(2,1)S(1)}, bf16[128,2048]{1,0:T(8,128)(2,1)}, u32[]{:S(2)}) copy-start(bf16[128,2048]{1,0:T(8,128)(2,1)} %copy-done.206) | copy-start | bytes 1572868
  260.6 15.6 %copy-start.209 = (bf16[128,2048]{1,0:T(8,128)(2,1)S(1)}, bf16[128,2048]{1,0:T(8,128)(2,1)}, u32[]{:S(2)}) copy-start(bf16[128,2048]{1,0:T(8,128)(2,1)} %copy-done.208) | copy-start | bytes 1572868
  260.6 15.6 %copy-start.211 = (bf16[128,2048]{1,0:T(8,128)(2,1)S(1)}, bf16[128,2048]{1,0:T(8,128)(2,1)}, u32[]{:S(2)}) copy-start(bf16[128,2048]{1,0:T(8,128)(2,1)} %copy-done.210) | copy-start | bytes 1572868
  271.5 22.0 %all-to-all-start.10 = ((bf16[64,8,1024]{2,1,0:T(8,128)(2,1)}), bf16[64,8,1024]{2,1,0:T(8,128)(2,1)S(1)}, u32[]{:S(2)}, u32[]{:S(2)}) async-start(bf16[64,8,1024]{2,1,0:T(8,128)(2,1)} %fusion.12), calls=%async_computation.10 | async-start | bytes 2097152 | tf_op jit(solution)/shard_map/all_to_all | solution.py:126
  281.4 46.0 %collective-permute-start.2 = (bf16[1024,1024]{1,0:T(8,128)(2,1)}, bf16[1024,1024]{1,0:T(8,128)(2,1)}, u32[]{:S(2)}, u32[]{:S(2)}) collective-permute-start(bf16[1024,1024]{1,0:T(8,128)(2,1)} %slice.1909), channel_id=1, source_target_pairs={{0,1},{1,0},{2,3},{3,2},{4,5},{5,4},{6,7},{7,6},{8,9},{9,8},{10,11... | collective-permute-start | bytes 6291464 | tf_op jit(solution)/shard_map/ppermute | solution.py:123
  284.0 14.9 %copy-start.136 = (bf16[176,128]{1,0:T(8,128)(2,1)S(1)}, bf16[176,128]{1,0:T(8,128)(2,1)}, u32[]{:S(2)}) copy-start(bf16[176,128]{1,0:T(8,128)(2,1)} %slice.1696) | copy-start | bytes 135172
  285.2 16.1 %copy-start.10 = (bf16[176,2048]{1,0:T(8,128)(2,1)S(1)}, bf16[176,2048]{1,0:T(8,128)(2,1)}, u32[]{:S(2)}) copy-start(bf16[176,2048]{1,0:T(8,128)(2,1)} %copy-done.9) | copy-start | bytes 2162692
  285.2 16.1 %copy-start.134 = (bf16[176,128]{1,0:T(8,128)(2,1)S(1)}, bf16[176,128]{1,0:T(8,128)(2,1)}, u32[]{:S(2)}) copy-start(bf16[176,128]{1,0:T(8,128)(2,1)} %slice.1723) | copy-start | bytes 135172
  293.4 26.6 %all-to-all-start.8 = ((bf16[64,16,768]{2,1,0:T(8,128)(2,1)}), bf16[64,16,768]{2,1,0:T(8,128)(2,1)S(1)}, u32[]{:S(2)}, u32[]{:S(2)}) async-start(bf16[64,16,768]{2,1,0:T(8,128)(2,1)} %pad_maximum_fusion.1), calls=%async_computation.8 | async-start | bytes 3145728 | tf_op jit(solution)/shard_map/all_to_all | solution.py:126
  311.6 20.5 %collective-permute-start.4 = (bf16[1024,1024]{1,0:T(8,128)(2,1)}, bf16[1024,1024]{1,0:T(8,128)(2,1)}, u32[]{:S(2)}, u32[]{:S(2)}) collective-permute-start(bf16[1024,1024]{1,0:T(8,128)(2,1)} %slice.2111), channel_id=1, source_target_pairs={{0,1},{1,0},{2,3},{3,2},{4,5},{5,4},{6,7},{7,6},{8,9},{9,8},{10,11... | collective-permute-start | bytes 6291464 | tf_op jit(solution)/shard_map/ppermute | solution.py:123
  314.8 10.3 %collective-permute-start.6 = (f32[8,1024]{1,0:T(8,128)S(1)}, f32[8,1024]{1,0:T(8,128)S(1)}, u32[]{:S(2)}, u32[]{:S(2)}) collective-permute-start(f32[8,1024]{1,0:T(8,128)S(1)} %convert_reduce_fusion.1), channel_id=1, source_target_pairs={{0,0},{1,64},{2,1},{3,65},{4,2},{5,66},{6,3},{7,67},{8,4},{9,68},{... | collective-permute-start | bytes 98312 | tf_op jit(solution)/shard_map/ppermute | solution.py:178
  321.2 4.8 %collective-permute-start.5 = (f32[8,576]{1,0:T(8,128)S(1)}, f32[8,576]{1,0:T(8,128)S(1)}, u32[]{:S(2)}, u32[]{:S(2)}) collective-permute-start(f32[8,576]{1,0:T(8,128)S(1)} %constant_dynamic-slice_fusion), channel_id=1, source_target_pairs={{0,1},{1,0},{2,3},{3,2},{4,5},{5,4},{6,7},{7,6},{8,9},{9,8},{10,11... | collective-permute-start | bytes 55304 | tf_op jit(solution)/shard_map/ppermute | solution.py:123
  (231 other events, 726.7 us)

commit v2 on v1

v2 whole, which is shorter than its diff:
```python
import jax
import jax.numpy as jnp
from jax import lax
from jax.experimental import pallas as pl
from jax.experimental.pallas import tpu as pltpu
from jax.sharding import PartitionSpec as P

H = 8
DK = 16
DV = 128
BANDS = DK // 2 + 1
FPAD = (BANDS + 2) * DK
SPAD = 256
AXES = ("ctx", "seq")
BF = jnp.bfloat16
F32 = jnp.float32
SQUARE = (2.0 * DK) ** (-0.5)
LINEAR = DK ** (-0.25)


def dot(a, b, contract):
    return lax.dot_general(a, b, ((contract[:1], contract[1:]), ((), ())), preferred_element_type=F32)


def band_weight(shape, dim):
    row = lax.broadcasted_iota(jnp.int32, shape, dim)
    twice = (row >= DK) & (row < (BANDS - 1) * DK)
    return jnp.where(twice, 2.0, 1.0).astype(F32)


def shifted(u, d):
    return pltpu.roll(u, DK - d, 0) if d else u


def features(u):
    bands = [u * shifted(u, d) * SQUARE for d in range(BANDS)]
    first = lax.broadcasted_iota(jnp.int32, u.shape, 0) == 0
    return jnp.concatenate(bands + [u * LINEAR, jnp.where(first, 1.0, 0.0)], axis=0).astype(BF)


def features_back(u, fgrad):
    def band(d):
        return fgrad[d * DK : (d + 1) * DK]

    total = band(0) * u + band(BANDS - 1) * shifted(u, BANDS - 1)
    for d in range(1, BANDS - 1):
        total = total + band(d) * shifted(u, d) + shifted(band(d) * u, DK - d)
    return total * (2.0 * SQUARE) + band(BANDS) * LINEAR


def in_parts(row):
    high = row.astype(BF).astype(F32)
    rest = row - high
    mid = rest.astype(BF).astype(F32)
    at = lax.broadcasted_iota(jnp.int32, (16, row.shape[1]), 0)
    low = jnp.where(at == 2, rest - mid, 0.0)
    return jnp.where(at == 0, high, jnp.where(at == 1, mid, low)).astype(BF)


def rows_of(array, head, size):
    return array[head * size : (head + 1) * size]


def column(rows, head):
    return rows.T[:FPAD, head : head + 1]


def call(body, tok_count, ins, in_kinds, outs, out_kinds, scratch, flops):
    block = min(512, tok_count)

    def spec(shape, kind):
        if kind is None:
            return pl.BlockSpec(shape, lambda i: (0,) * len(shape))
        if kind == 0:
            return pl.BlockSpec((block, shape[1]), lambda i: (i, 0))
        return pl.BlockSpec((shape[0], block), lambda i: (0, i))

    nbytes = sum(x.size * x.dtype.itemsize for x in list(ins) + list(outs))
    return pl.pallas_call(
        body,
        grid=(tok_count // block,),
        in_specs=[spec(x.shape, k) for x, k in zip(ins, in_kinds)],
        out_specs=[spec(x.shape, k) for x, k in zip(outs, out_kinds)],
        out_shape=outs,
        scratch_shapes=scratch,
        compiler_params=pltpu.CompilerParams(
            dimension_semantics=("arbitrary",), vmem_limit_bytes=48 * 2**20
        ),
        cost_estimate=pl.CostEstimate(flops=flops, bytes_accessed=nbytes, transcendentals=0),
    )(*ins)


def shape(dims, dtype):
    return jax.ShapeDtypeStruct(dims, dtype)


def clear_at_first(*refs):
    @pl.when(pl.program_id(0) == 0)
    def _():
        for ref in refs:
            ref[...] = jnp.zeros(ref.shape, ref.dtype)


def at_last(fn):
    pl.when(pl.program_id(0) == pl.num_programs(0) - 1)(fn)


def keys_phase(tokens, w_qkv, heads):
    qk = heads * DK

    def body(tok_ref, w_ref, qk_ref, value_ref, feat_ref, state_ref, norm_ref, state_acc, norm_acc):
        clear_at_first(state_acc, norm_acc)
        joined = dot(tok_ref[...], w_ref[...], (1, 0))
        qk_t = joined[:, : 2 * qk].T.astype(BF)
        value = joined[:, 2 * qk :].astype(BF)
        qk_ref[...] = qk_t
        value_ref[...] = value
        keys = qk_t.astype(F32)[qk:]
        ones = jnp.ones((16, value.shape[0]), BF)
        for head in range(heads):
            feat = features(rows_of(keys, head, DK))
            feat_ref[head * FPAD : (head + 1) * FPAD, :] = feat
            state_acc[head, :FPAD, :] += dot(feat, value[:, head * DV : (head + 1) * DV], (1, 0))
            norm_acc[head, :, :FPAD] += dot(ones, feat, (1, 1))

        @at_last
        def _():
            norm_ref[...] = jnp.zeros(norm_ref.shape, F32)
            for head in range(heads):
                state_ref[head * SPAD : (head + 1) * SPAD, :] = state_acc[head].astype(BF)
                norm_ref[head : head + 1, :] = norm_acc[head, :1, :]

    count = tokens.shape[0]
    return call(
        body,
        count,
        (tokens, w_qkv),
        (0, None),
        (
            shape((2 * qk, count), BF),
            shape((count, heads * DV), BF),
            shape((heads * FPAD, count), BF),
            shape((heads * SPAD, DV), BF),
            shape((8, SPAD), F32),
        ),
        (1, 0, 1, None, None),
        [pltpu.VMEM((heads, SPAD, DV), F32), pltpu.VMEM((heads, 16, SPAD), F32)],
        2 * count * (tokens.shape[1] * w_qkv.shape[1] + heads * FPAD * DV * 2),
    )


def upstream_phase(qk_t, cot, w_out_half, heads):
    count = cot.shape[0]

    def body(qk_ref, cot_ref, w_ref, up_ref, feat_ref):
        up_ref[...] = dot(w_ref[...], cot_ref[...], (1, 1))
        query = qk_ref[...].astype(F32)
        for head in range(heads):
            feat_ref[head * FPAD : (head + 1) * FPAD, :] = features(rows_of(query, head, DK))

    return call(
        body,
        count,
        (qk_t, cot, w_out_half),
        (1, 0, None),
        (shape((heads * DV, count), F32), shape((heads * FPAD, count), BF)),
        (1, 1),
        [],
        2 * count * cot.shape[1] * heads * DV,
    )


def query_phase(feats, up_t, norm, heads):
    count = up_t.shape[1]

    def body(feat_ref, up_ref, norm_ref, scale_ref, sgrad_ref, acc):
        clear_at_first(acc)
        weighted = norm_ref[...] * band_weight((8, SPAD), 1)
        at = lax.broadcasted_iota(jnp.int32, scale_ref.shape, 0)
        scales = jnp.zeros(scale_ref.shape, F32)
        for head in range(heads):
            feat = feat_ref[head * FPAD : (head + 1) * FPAD, :]
            parts = in_parts(weighted[head : head + 1, :])[:, :FPAD]
            scale = 1.0 / jnp.sum(dot(parts, feat, (1, 0)), axis=0, keepdims=True)
            grad_num = (up_ref[head * DV : (head + 1) * DV, :] * scale).astype(BF)
            acc[head, :FPAD, :] += dot(feat, grad_num, (1, 1))
            scales = jnp.where(at == head, scale, scales)
        scale_ref[...] = scales

        @at_last
        def _():
            for head in range(heads):
                sgrad_ref[head * SPAD : (head + 1) * SPAD, :] = acc[head].astype(BF)

    return call(
        body,
        count,
        (feats, up_t, norm),
        (1, 1, None),
        (shape((8, count), F32), shape((heads * SPAD, DV), BF)),
        (1, None),
        [pltpu.VMEM((heads, SPAD, DV), F32)],
        2 * count * heads * FPAD * DV * 2,
    )


def attend_phase(qk_t, feats, scales, up_t, state, norm, heads):
    count = up_t.shape[1]

    def body(qk_ref, feat_ref, scale_ref, up_ref, state_ref, norm_ref, att_ref, qgrad_ref, ngrad_ref, turned, acc):
        clear_at_first(acc)

        @pl.when(pl.program_id(0) == 0)
        def _():
            for head in range(heads):
                whole = state_ref[head * SPAD : (head + 1) * SPAD, :].astype(F32)
                turned[head] = (whole * band_weight((SPAD, DV), 0)).T.astype(BF)

        query = qk_ref[...].astype(F32)
        norms = norm_ref[...]
        for head in range(heads):
            feat = feat_ref[head * FPAD : (head + 1) * FPAD, :]
            scale = scale_ref[head : head + 1, :]
            att = dot(turned[head, :, :FPAD], feat, (1, 0)) * scale
            grad_num = up_ref[head * DV : (head + 1) * DV, :] * scale
            grad_den = -jnp.sum(grad_num * att, axis=0, keepdims=True)
            acc[head, :, :FPAD] += dot(in_parts(grad_den), feat, (1, 1))
            fgrad = dot(state_ref[head * SPAD : head * SPAD + FPAD, :], grad_num.astype(BF), (1, 0))
            fgrad = fgrad + column(norms, head) * grad_den
            qgrad_ref[head * DK : (head + 1) * DK, :] = features_back(rows_of(query, head, DK), fgrad).astype(BF)
            att_ref[head * DV : (head + 1) * DV, :] = att.astype(BF)

        @at_last
        def _():
            ngrad_ref[...] = jnp.zeros(ngrad_ref.shape, F32)
            for head in range(heads):
                ngrad_ref[head : head + 1, :] = jnp.sum(acc[head], axis=0, keepdims=True)

    return call(
        body,
        count,
        (qk_t, feats, scales, up_t, state, norm),
        (1, 1, 1, 1, None, None),
        (shape((heads * DV, count), BF), shape((heads * DK, count), BF), shape((8, SPAD), F32)),
        (1, 1, None),
        [pltpu.VMEM((heads, DV, SPAD), BF), pltpu.VMEM((heads, 16, SPAD), F32)],
        2 * count * heads * FPAD * DV * 4,
    )


def back_phase(qk_t, value, feats, sgrad, heads):
    count = value.shape[0]
    qk = heads * DK

    def body(qk_ref, value_ref, feat_ref, sgrad_ref, kgrad_ref, vgrad_ref, turned):
        @pl.when(pl.program_id(0) == 0)
        def _():
            for head in range(heads):
                whole = sgrad_ref[head * SPAD : (head + 1) * SPAD, :].astype(F32)
                turned[head] = (whole * band_weight((SPAD, DV), 0)).T.astype(BF)

        keys = qk_ref[...].astype(F32)[qk:]
        for head in range(heads):
            fgrad = dot(
                sgrad_ref[head * SPAD : head * SPAD + FPAD, :],
                value_ref[:, head * DV : (head + 1) * DV],
                (1, 1),
            )
            kgrad_ref[head * DK : (head + 1) * DK, :] = features_back(rows_of(keys, head, DK), fgrad)
            feat = feat_ref[head * FPAD : (head + 1) * FPAD, :]
            vgrad_ref[head * DV : (head + 1) * DV, :] = dot(turned[head, :, :FPAD], feat, (1, 0)).astype(BF)

    return call(
        body,
        count,
        (qk_t, value, feats, sgrad),
        (1, 0, 1, None),
        (shape((qk, count), F32), shape((heads * DV, count), BF)),
        (1, 1),
        [pltpu.VMEM((heads, DV, SPAD), BF)],
        2 * count * heads * FPAD * DV * 3,
    )


def key_phase(qk_t, partial, ngrad, tokens, heads):
    count, width = tokens.shape
    qk = heads * DK

    def body(qk_ref, partial_ref, ngrad_ref, tok_ref, kgrad_ref, wgrad_ref, acc):
        clear_at_first(acc)
        keys = qk_ref[...].astype(F32)[qk:]
        rows = ngrad_ref[...]
        whole = []
        for head in range(heads):
            key = rows_of(keys, head, DK)
            fgrad = jnp.broadcast_to(column(rows, head), (FPAD, key.shape[1]))
            whole.append(rows_of(partial_ref[...], head, DK) + features_back(key, fgrad))
        kgrad = jnp.concatenate(whole, axis=0).astype(BF)
        kgrad_ref[...] = kgrad
        acc[...] += dot(kgrad, tok_ref[...], (1, 0))

        @at_last
        def _():
            wgrad_ref[...] = acc[...].T.astype(BF)

    return call(
        body,
        count,
        (qk_t, partial, ngrad, tokens),
        (1, 1, None, 0),
        (shape((qk, count), BF), shape((width, qk), BF)),
        (1, None),
        [pltpu.VMEM((qk, width), F32)],
        2 * count * width * qk,
    )


def per_device(chips, tokens, w_query, w_key, w_value, w_out, cotangent):
    n = 2 * chips
    heads = H // 2
    core = lax.axis_index("seq") % 2
    same_core = [[2 * p + c for p in range(chips)] for c in range(2)]
    swap = [(i, i ^ 1) for i in range(n)]
    scale_factor = (tokens.shape[0] * n) ** (-0.5)

    def exchange(x):
        return lax.ppermute(x, AXES, swap)

    def spread(x):
        return lax.all_to_all(x, AXES, 0, 0, axis_index_groups=same_core, tiled=True)

    def sum_small(x):
        return jnp.sum(spread(jnp.broadcast_to(x[None], (chips,) + x.shape)), axis=0)

    def sum_state(x):
        rows, cols = x.shape
        part = rows // chips
        own = jnp.sum(spread(x.reshape(chips, part, cols)).astype(F32), axis=0).astype(BF)
        return spread(jnp.broadcast_to(own[None], (chips, part, cols))).reshape(rows, cols)

    halves = [
        jnp.concatenate(
            [
                w_query[:, c * heads * DK : (c + 1) * heads * DK],
                w_key[:, c * heads * DK : (c + 1) * heads * DK],
                w_value[:, c * heads * DV : (c + 1) * heads * DV],
            ],
            axis=1,
        )
        for c in range(2)
    ]
    to_send = jnp.broadcast_to(jnp.stack(halves)[None], (chips, 2) + halves[0].shape)
    w_qkv = lax.all_to_all(to_send.reshape((n,) + halves[0].shape), AXES, 0, 0, tiled=True)
    w_qkv = w_qkv.reshape(-1, halves[0].shape[1])
    out_rows = lax.ppermute(w_out, AXES, [(c * chips + p, 2 * p + c) for p in range(chips) for c in range(2)])
    w_out_half = spread(jnp.broadcast_to(out_rows[None], (chips,) + out_rows.shape)).reshape(-1, out_rows.shape[1])

    tok = jnp.concatenate([tokens, exchange(tokens)])
    cot = jnp.concatenate([cotangent, exchange(cotangent)])
    own = tokens.shape[0]

    qk_t, value, key_feat, state_part, norm_part = keys_phase(tok, w_qkv, heads)
    norm = sum_small(norm_part)
    state = sum_state(state_part)
    up_t, query_feat = upstream_phase(qk_t, cot, w_out_half, heads)
    scales, sgrad_part = query_phase(query_feat, up_t, norm, heads)
    sgrad = sum_state(sgrad_part)
    moments = dot(tok, key_feat, (0, 1))

    attended_t, qgrad_t, ngrad_part = attend_phase(qk_t, query_feat, scales, up_t, state, norm, heads)
    ngrad = sum_small(ngrad_part)
    mixed_part = dot(attended_t, w_out_half, (0, 0)).astype(BF)
    mixed_other = exchange(mixed_part[own:])
    mixed = (mixed_part[:own].astype(F32) + mixed_other.astype(F32)).astype(BF)

    early = jnp.concatenate([moments, dot(tok, qgrad_t, (0, 1))], axis=1).astype(BF)
    early = jnp.sum(spread(early.reshape(chips, -1, early.shape[1])).astype(F32), axis=0)
    out_part = dot(attended_t, cot, (1, 0)).astype(BF)
    out_sum = jnp.sum(spread(out_part.reshape(chips, -1, out_part.shape[1])).astype(F32), axis=0)
    grad_out = lax.ppermute(out_sum, AXES, [(2 * p + c, c * chips + p) for p in range(chips) for c in range(2)])

    kgrad_rest, vgrad_t = back_phase(qk_t, value, key_feat, sgrad, heads)
    kgrad_t, kgrad_part = key_phase(qk_t, kgrad_rest, ngrad, tok, heads)
    kgrad_all = lax.all_to_all(kgrad_part.reshape(n, -1, kgrad_part.shape[1]), AXES, 0, 0, tiled=True)
    kgrad_sum = jnp.sum(kgrad_all.reshape((chips, 2) + kgrad_all.shape[1:]).astype(F32), axis=0)
    joined_t = jnp.concatenate([qgrad_t, kgrad_t, vgrad_t])
    gtok_part = dot(joined_t, w_qkv, (0, 1)).astype(BF)
    gtok_other = exchange(gtok_part[own:])
    grad_tokens = (gtok_part[:own].astype(F32) + gtok_other.astype(F32)).astype(BF)

    weight = band_weight((1, FPAD), 1)
    gvalue = jnp.concatenate(
        [
            jnp.dot(
                early[:, h * FPAD : (h + 1) * FPAD] * weight,
                sgrad[h * SPAD : h * SPAD + FPAD].astype(F32),
                precision=lax.Precision.HIGH,
            )
            for h in range(heads)
        ],
        axis=1,
    )
    mine = jnp.concatenate([early[:, heads * FPAD :], gvalue], axis=1)
    rows = mine.shape[0] // 2
    got = exchange(lax.dynamic_slice_in_dim(mine, (1 - core) * rows, rows, 0))
    kept = lax.dynamic_slice_in_dim(mine, core * rows, rows, 0)
    low, high = jnp.where(core == 0, kept, got), jnp.where(core == 0, got, kept)
    qk = heads * DK
    grad_query = jnp.concatenate([low[:, :qk], high[:, :qk]], axis=1) * scale_factor
    grad_value = jnp.concatenate([low[:, qk:], high[:, qk:]], axis=1) * scale_factor
    grad_key = jnp.concatenate([kgrad_sum[0], kgrad_sum[1]], axis=1) * scale_factor
    return (mixed, grad_tokens, grad_query, grad_key, grad_value, grad_out * scale_factor)


def solution(mesh):
    chips = mesh.size // 2
    placed = P(AXES, None)
    return jax.shard_map(
        lambda *args: per_device(chips, *args),
        mesh=mesh,
        in_specs=(placed,) * 6,
        out_specs=(placed,) * 6,
        check_vma=False,
    )
```

time: 343 us -> 276 us (0.80); the launches traced: 336 us -> 273 us
  other arithmetic: 60.4 us -> 19.9 us
  matrix products: 61 us -> 22.8 us
  Pallas kernels: 0 us -> 35.2 us
  local copies, waits for them, and re-layouts: 63.8 us -> 43.5 us
  waiting for transfers between devices: 39 us -> 50 us
  between operations: 6.67 us -> 1.05 us
  starting transfers between devices: 105 us -> 100 us
    dot_general x33 -> x5, matrix products: 60.3 us -> 22.1 us  [dot(): lax.dot_general(a, b, ((contract[:1], contract[1:]), ((), ())), preferred...]
    pallas_call x0 -> x6, Pallas kernels: none -> 35.2 us  [call(): pl.pallas_call(body, grid=(tok_count // block,), in_specs=[spec(x.shape,...]
    unnamed x55 -> x0, other arithmetic: 29.2 us -> none
    slice x187 -> x1, local copies, waits for them, and re-layouts: 26.8 us -> 0.87 us  [per_device(): sgrad[h * SPAD:h * SPAD + FPAD].astype(F32)]
    unnamed x589 -> x50, local copies, waits for them, and re-layouts: 12.7 us -> 23 us
    reduce_sum x14 -> x2, other arithmetic: 10.1 us -> 1.18 us  [sum_small(): jnp.sum(spread(jnp.broadcast_to(x[None], (chips,) + x.shape)), axis=0)]
    ppermute x1, waiting for transfers between devices: 3.17 us -> 9.87 us  [per_device(): lax.ppermute(w_out, AXES, [(c * chips + p, 2 * p + c) for p in range(chip...]
    all_to_all x9, waiting for transfers between devices: 21.1 us -> 26.9 us  [spread(): lax.all_to_all(x, AXES, 0, 0, axis_index_groups=same_core, tiled=True)]
  transfers between devices with their start and end apart: 18 -> 18, of which waited for: 10 -> 10; matrix products, arithmetic and copies ran while one was open for 46% -> 23% of each run, Pallas kernels for 0% -> 12%
where the time goes in v2:
time: 276 us; the launch traced here: 273 us
  starting transfers between devices  100 us (36%)
  waiting for transfers between devices  50 us (18%)
  local copies, waits for them, and re-layouts  43.5 us (16%)
  Pallas kernels  35.2 us (13%)
  matrix products  22.8 us (8%)
  other arithmetic  19.9 us (7%)
    all_to_all x9, starting transfers between devices, spread(): lax.all_to_all(x, AXES, 0, 0, axis_index_groups=same_core, tiled=True)  65 us
    pallas_call x6, Pallas kernels, call(): pl.pallas_call(body, grid=(tok_count // block,), in_specs=[spec(x.shape,...  35.2 us
    all_to_all x9, waiting for transfers between devices, spread(): lax.all_to_all(x, AXES, 0, 0, axis_index_groups=same_core, tiled=True)  26.9 us
    unnamed x50, local copies, waits for them, and re-layouts  23 us
    dot_general x5, matrix products, dot(): lax.dot_general(a, b, ((contract[:1], contract[1:]), ((), ())), preferred...  22.1 us
    all_to_all x1, starting transfers between devices, per_device(): lax.all_to_all(kgrad_part.reshape(n, -1, kgrad_part.shape[1]), AXES, 0, 0...  11.7 us
    all_to_all x1, starting transfers between devices, per_device(): lax.all_to_all(to_send.reshape((n,) + halves[0].shape), AXES, 0, 0, tiled...  10.2 us
    ppermute x1, waiting for transfers between devices, per_device(): lax.ppermute(w_out, AXES, [(c * chips + p, 2 * p + c) for p in range(chip...  9.87 us
  transfers between devices with their start and end apart: 18, of which 10 were waited for; matrix products, arithmetic and copies ran while one was open for 23% of the time, Pallas kernels for 12%

profile of v2, /device:TPU:1, one launch (start us, length us, event | category | flops | bytes accessed | tf_op | source)
XLA Modules:
  0.0 272.7 jit_solution(6580421535031002766)
XLA Ops:
  0.6 1.5 collective-permute-start
  4.6 1.2 broadcast_in_dim.18
  5.8 10.2 %all-to-all-start = ((bf16[128,8,640]{2,1,0:T(8,128)(2,1)}), bf16[128,8,640]{2,1,0:T(8,128)(2,1)S(1)}, u32[]{:S(2)}, u32[]{:S(2)}) async-start(bf16[128,8,640]{2,1,0:T(8,128)(2,1)} %bitcast.2), calls=%async_computation | async-start | bytes 2621440 | tf_op jit(solution)/shard_map/all_to_all | solution.py:353
  16.0 1.1 collective-permute-start.1
  17.1 2.6 collective-permute-start.2
  19.7 9.9 %collective-permute-done.2 = bf16[8,1024]{1,0:T(8,128)(2,1)S(1)} collective-permute-done((bf16[8,1024]{1,0:T(8,128)(2,1)S(1)}, bf16[8,1024]{1,0:T(8,128)(2,1)S(1)}, u32[]{:S(2)}, u32[]{:S(2)}) %collective-permute-start.2) | collective-permute-done | bytes 16416 | tf_op jit(solution)/shard_map/ppermute | solution.py:355
  29.6 8.3 %all-to-all-done = bf16[128,8,640]{2,1,0:T(8,128)(2,1)S(1)} async-done(((bf16[128,8,640]{2,1,0:T(8,128)(2,1)}), bf16[128,8,640]{2,1,0:T(8,128)(2,1)S(1)}, u32[]{:S(2)}, u32[]{:S(2)}) %all-to-all-start) | async-done | bytes 1310752 | tf_op jit(solution)/shard_map/all_to_all | solution.py:353
  37.9 1.2 broadcast_in_dim.19
  39.1 4.9 %all-to-all-start.1 = ((bf16[64,8,1024]{2,1,0:T(8,128)(2,1)}), bf16[64,8,1024]{2,1,0:T(8,128)(2,1)S(1)}, u32[]{:S(2)}, u32[]{:S(2)}) async-start(bf16[64,8,1024]{2,1,0:T(8,128)(2,1)} %broadcast_in_dim.19), calls=%async_computation.1 | async-start | bytes 2097152 | tf_op jit(solution)/shard_map/all_to_all | solution.py:330
  44.0 1.8 constant_dynamic-update-slice_fusion.1
  45.8 1.8 constant_dynamic-update-slice_fusion.tok_ref
  47.6 1.9 copy-done
  49.6 8.2 %shard_map.109 = (bf16[128,2048]{1,0:T(8,128)(2,1)S(1)}, bf16[2048,512]{1,0:T(8,128)(2,1)S(1)}, bf16[704,2048]{1,0:T(8,128)(2,1)}, bf16[1024,128]{1,0:T(8,128)(2,1)}, f32[8,256]{1,0:T(8,128)S(1)}) custom-call(bf16[2048,1024]{1,0:T(8,128)(2,1)} %copy-done, bf16[1024,640]{1,0:T(8,128)(2,1)S(1)} %bitcast.41), custom_call_target="tpu_custom_call" | custom-call | flops 3422552064 | bytes 11280384 | tf_op jit(solution)/shard_map/pallas_call | solution.py:79
  57.7 1.3 copy-done.2
  59.0 1.9 all-to-all-done.1
  60.9 0.9 broadcast_in_dim.20
  61.8 7.9 %all-to-all-start.2 = ((f32[64,8,256]{2,1,0:T(8,128)}), f32[64,8,256]{2,1,0:T(8,128)S(1)}, u32[]{:S(2)}, u32[]{:S(2)}) async-start(f32[64,8,256]{2,1,0:T(8,128)} %broadcast_in_dim.20), calls=%async_computation.2 | async-start | bytes 1048576 | tf_op jit(solution)/shard_map/all_to_all | solution.py:330
  69.7 3.1 %constant_dynamic-update-slice_fusion.3 = bf16[2048,1024]{1,0:T(8,128)(2,1)} fusion(bf16[1024,1024]{1,0:T(8,128)(2,1)} %param.11), kind=kLoop, calls=%fused_computation.35 | loop fusion | bytes 4194304
  72.8 3.1 %constant_dynamic-update-slice_fusion.2.cot_ref = bf16[2048,1024]{1,0:T(8,128)(2,1)} fusion(bf16[2048,1024]{1,0:T(8,128)(2,1)} %constant_dynamic-update-slice_fusion.3, bf16[1024,1024]{1,0:T(8,128)(2,1)} %collective-permute-done.1), kind=kLoop, calls=%fused_computation.34 | loop fusion | bytes 4194304 | tf_op jit(solution)/shard_map/concatenate | solution.py:359
  75.9 5.0 %all-to-all-done.2 = f32[64,8,256]{2,1,0:T(8,128)S(1)} async-done(((f32[64,8,256]{2,1,0:T(8,128)}), f32[64,8,256]{2,1,0:T(8,128)S(1)}, u32[]{:S(2)}, u32[]{:S(2)}) %all-to-all-start.2) | async-done | bytes 524320 | tf_op jit(solution)/shard_map/all_to_all | solution.py:330
  80.9 5.5 %all-to-all-start.3 = ((bf16[64,16,128]{2,1,0:T(8,128)(2,1)}), bf16[64,16,128]{2,1,0:T(8,128)(2,1)}, u32[]{:S(2)}, u32[]{:S(2)}) async-start(bf16[64,16,128]{2,1,0:T(8,128)(2,1)} %bitcast.5), calls=%async_computation.3 | async-start | bytes 524288 | tf_op jit(solution)/shard_map/all_to_all | solution.py:330
  86.4 1.2 copy-done.7
  87.6 6.9 %shard_map.110 = (f32[512,2048]{1,0:T(8,128)}, bf16[704,2048]{1,0:T(8,128)(2,1)S(1)}) custom-call(bf16[128,2048]{1,0:T(8,128)(2,1)S(1)} %get-tuple-element.22.qk_ref, bf16[2048,1024]{1,0:T(8,128)(2,1)} %constant_dynamic-update-slice_fusion.2.cot_ref, bf16[512,1024]{1,0:T(8,128)(2,1)S(1)} %bitcast.42), custom_call_target="tpu_custom_call" | custom-call | flops 2147483648 | bytes 12845056 | tf_op jit(solution)/shard_map/pallas_call | solution.py:79
  94.5 1.1 reduce_sum.69.norm_ref
  95.6 5.9 %shard_map.111 = (f32[8,2048]{1,0:T(8,128)S(1)}, bf16[1024,128]{1,0:T(8,128)(2,1)S(1)}) custom-call(bf16[704,2048]{1,0:T(8,128)(2,1)S(1)} %get-tuple-element.23.feat_ref, f32[512,2048]{1,0:T(8,128)} %get-tuple-element.24.up_ref, f32[8,256]{1,0:T(8,128)S(1)} %reduce_sum.69.norm_ref), custom_call_target="tpu_custom_call" | custom-call | flops 738197504 | bytes 7413760 | tf_op jit(solution)/shard_map/pallas_call | solution.py:79
  102.2 10.0 %all-to-all-start.5 = ((bf16[64,16,128]{2,1,0:T(8,128)(2,1)}), bf16[64,16,128]{2,1,0:T(8,128)(2,1)}, u32[]{:S(2)}, u32[]{:S(2)}) async-start(bf16[64,16,128]{2,1,0:T(8,128)(2,1)} %bitcast.44), calls=%async_computation.5 | async-start | bytes 524288 | tf_op jit(solution)/shard_map/all_to_all | solution.py:330
  112.2 1.0 reduce_sum.70
  113.2 8.2 %all-to-all-done.5 = bf16[64,16,128]{2,1,0:T(8,128)(2,1)} async-done(((bf16[64,16,128]{2,1,0:T(8,128)(2,1)}), bf16[64,16,128]{2,1,0:T(8,128)(2,1)}, u32[]{:S(2)}, u32[]{:S(2)}) %all-to-all-start.5) | async-done | bytes 262176 | tf_op jit(solution)/shard_map/all_to_all | solution.py:330
  122.1 5.5 %all-to-all-start.4 = ((bf16[64,16,128]{2,1,0:T(8,128)(2,1)}), bf16[64,16,128]{2,1,0:T(8,128)(2,1)}, u32[]{:S(2)}, u32[]{:S(2)}) async-start(bf16[64,16,128]{2,1,0:T(8,128)(2,1)} %broadcast_in_dim.21), calls=%async_computation.4 | async-start | bytes 524288 | tf_op jit(solution)/shard_map/all_to_all | solution.py:330
  127.6 1.0 reduce_sum.71
  128.6 8.1 %all-to-all-done.4 = bf16[64,16,128]{2,1,0:T(8,128)(2,1)} async-done(((bf16[64,16,128]{2,1,0:T(8,128)(2,1)}), bf16[64,16,128]{2,1,0:T(8,128)(2,1)}, u32[]{:S(2)}, u32[]{:S(2)}) %all-to-all-start.4) | async-done | bytes 262176 | tf_op jit(solution)/shard_map/all_to_all | solution.py:330
  137.5 5.7 %all-to-all-start.6 = ((bf16[64,16,128]{2,1,0:T(8,128)(2,1)}), bf16[64,16,128]{2,1,0:T(8,128)(2,1)}, u32[]{:S(2)}, u32[]{:S(2)}) async-start(bf16[64,16,128]{2,1,0:T(8,128)(2,1)} %broadcast_in_dim.22), calls=%async_computation.6 | async-start | bytes 524288 | tf_op jit(solution)/shard_map/all_to_all | solution.py:330
  143.1 7.1 %shard_map.112 = (bf16[512,2048]{1,0:T(8,128)(2,1)S(1)}, bf16[64,2048]{1,0:T(8,128)(2,1)S(1)}, f32[8,256]{1,0:T(8,128)S(1)}) custom-call(bf16[128,2048]{1,0:T(8,128)(2,1)S(1)} %get-tuple-element.22.qk_ref, bf16[704,2048]{1,0:T(8,128)(2,1)S(1)} %get-tuple-element.23.feat_ref, f32[8,2048]{1,0:T(8,128)S(1)} %get-tuple-element.26.scale_ref, ...), custom_call_target="tpu_custom_call" | custom-call | flops 1476395008 | bytes 10305536 | tf_op jit(solution)/shard_map/pallas_call | solution.py:79
  151.0 1.3 copy-done.12
  153.1 9.6 %all-to-all-start.7 = ((f32[64,8,256]{2,1,0:T(8,128)}), f32[64,8,256]{2,1,0:T(8,128)S(1)}, u32[]{:S(2)}, u32[]{:S(2)}) async-start(f32[64,8,256]{2,1,0:T(8,128)} %broadcast_in_dim.23), calls=%async_computation.7 | async-start | bytes 1048576 | tf_op jit(solution)/shard_map/all_to_all | solution.py:330
  162.7 1.6 copy-done.3
  164.3 4.2 %shard_map.113 = (f32[64,2048]{1,0:T(8,128)S(1)}, bf16[512,2048]{1,0:T(8,128)(2,1)S(1)}) custom-call(bf16[128,2048]{1,0:T(8,128)(2,1)S(1)} %get-tuple-element.22.qk_ref, bf16[2048,512]{1,0:T(8,128)(2,1)S(1)} %copy-done.3, bf16[704,2048]{1,0:T(8,128)(2,1)} %get-tuple-element.31.feat_ref, bf16[1024,128]{1,0:T(8,128)(2,1)} %bitcast.8.sgrad_ref), custom_call_target="tpu_custom_call" | custom-call | flops 1107296256 | bytes 8388608 | tf_op jit(solution)/shard_map/pallas_call | solution.py:79
  168.5 1.3 copy-done.14
  169.8 3.4 %all-to-all-done.7 = f32[64,8,256]{2,1,0:T(8,128)S(1)} async-done(((f32[64,8,256]{2,1,0:T(8,128)}), f32[64,8,256]{2,1,0:T(8,128)S(1)}, u32[]{:S(2)}, u32[]{:S(2)}) %all-to-all-start.7) | async-done | bytes 524320 | tf_op jit(solution)/shard_map/all_to_all | solution.py:330
  173.3 2.2 copy-done.1
  175.5 3.1 %shard_map.114 = (bf16[64,2048]{1,0:T(8,128)(2,1)S(1)}, bf16[1024,64]{1,0:T(8,128)(2,1)S(1)}) custom-call(bf16[128,2048]{1,0:T(8,128)(2,1)S(1)} %get-tuple-element.22.qk_ref, f32[64,2048]{1,0:T(8,128)S(1)} %get-tuple-element.33.partial_ref, f32[8,256]{1,0:T(8,128)S(1)} %reduce_sum.72.ngrad_ref, bf16[2048,1024]{1,0:T(8,128)(2,1)S(1)} %copy-done.1), custom_call_target="tpu_custom_call" | custom-call | flops 268435456 | bytes 5644288 | tf_op jit(solution)/shard_map/pallas_call | solution.py:79
  180.2 11.7 %all-to-all-start.9 = ((bf16[128,2,256]{2,1,0:T(2,128)(2,1)}), bf16[128,2,256]{2,1,0:T(2,128)(2,1)S(1)}, u32[]{:S(2)}, u32[]{:S(2)}) async-start(bf16[128,2,256]{2,1,0:T(2,128)(2,1)} %reshape.80), calls=%async_computation.9 | async-start | bytes 262144 | tf_op jit(solution)/shard_map/all_to_all | solution.py:384
  191.9 5.5 %fusion.5 = bf16[64,8,1024]{2,1,0:T(8,128)(2,1)} fusion(bf16[512,2048]{1,0:T(8,128)(2,1)S(1)} %copy-done.13, bf16[2048,1024]{1,0:T(8,128)(2,1)} %constant_dynamic-update-slice_fusion.2.cot_ref), kind=kOutput, calls=%fused_computation.14 | convolution fusion | flops 2148007936 | bytes 7340032 | tf_op jit(solution)/shard_map/dot_general | solution.py:22
  197.4 4.6 %all-to-all-done.9 = bf16[128,2,256]{2,1,0:T(2,128)(2,1)S(1)} async-done(((bf16[128,2,256]{2,1,0:T(2,128)(2,1)}), bf16[128,2,256]{2,1,0:T(2,128)(2,1)S(1)}, u32[]{:S(2)}, u32[]{:S(2)}) %all-to-all-start.9) | async-done | bytes 131104 | tf_op jit(solution)/shard_map/all_to_all | solution.py:384
  202.1 6.2 %all-to-all-start.10 = ((bf16[64,8,1024]{2,1,0:T(8,128)(2,1)}), bf16[64,8,1024]{2,1,0:T(8,128)(2,1)}, u32[]{:S(2)}, u32[]{:S(2)}) async-start(bf16[64,8,1024]{2,1,0:T(8,128)(2,1)} %fusion.5), calls=%async_computation.10 | async-start | bytes 2097152 | tf_op jit(solution)/shard_map/all_to_all | solution.py:330
  208.3 7.3 %convolution_convert_fusion.2 = bf16[1024,704]{0,1:T(8,128)(2,1)} fusion(bf16[704,2048]{1,0:T(8,128)(2,1)} %get-tuple-element.31.feat_ref, bf16[2048,1024]{1,0:T(8,128)(2,1)} %copy-done), kind=kOutput, calls=%fused_computation.11 | convolution fusion | flops 2953510912 | bytes 8519680 | tf_op jit(solution)/shard_map/dot_general | solution.py:22
  215.6 2.6 copy.14
  218.2 3.0 %convolution_convert_fusion.4 = bf16[1024,64]{0,1:T(8,128)(2,1)S(1)} fusion(bf16[64,2048]{1,0:T(8,128)(2,1)S(1)} %copy-done.10, bf16[2048,1024]{1,0:T(8,128)(2,1)} %copy-done), kind=kOutput, calls=%fused_computation.15 | convolution fusion | flops 268500992 | bytes 4587520 | tf_op jit(solution)/shard_map/dot_general | solution.py:22
  222.1 2.9 %pad_maximum_fusion = bf16[64,16,768]{2,1,0:T(8,128)(2,1)} fusion(bf16[64,16,64]{2,1,0:T(8,128)(2,1)} %bitcast.47, bf16[64,16,704]{2,1,0:T(8,128)(2,1)} %bitcast.45), kind=kLoop, calls=%fused_computation.12 | loop fusion | flops 3145728 | bytes 3145728 | tf_op jit(solution)/shard_map/concatenate | solution.py:376
  225.3 9.9 %all-to-all-start.8 = ((bf16[64,16,768]{2,1,0:T(8,128)(2,1)}), bf16[64,16,768]{2,1,0:T(8,128)(2,1)}, u32[]{:S(2)}, u32[]{:S(2)}) async-start(bf16[64,16,768]{2,1,0:T(8,128)(2,1)} %pad_maximum_fusion), calls=%async_computation.8 | async-start | bytes 3145728 | tf_op jit(solution)/shard_map/all_to_all | solution.py:330
  235.2 2.4 convolution_convert_fusion.1
  237.6 2.0 copy-done.18
  239.6 1.5 slice.117
  241.1 1.2 collective-permute-start.3
  242.3 3.8 %convolution_convert_fusion = bf16[2048,1024]{1,0:T(8,128)(2,1)S(1)} fusion(bf16[512,2048]{1,0:T(8,128)(2,1)S(1)} %copy-done.15, bf16[64,2048]{1,0:T(8,128)(2,1)S(1)} %copy-done.17, bf16[64,2048]{1,0:T(8,128)(2,1)S(1)} %copy-done.10, bf16[128,8,640]{2,1,0:T(8,128)(2,1)S(1)} %copy-done.5), kind=kOutput, calls=%fused_computation.2 | convolution fusion | flops 2694316032 | bytes 8126464 | tf_op jit(solution)/shard_map/dot_general | solution.py:22
  246.1 2.0 copy-done.19
  248.2 1.5 slice.119
  249.7 1.2 collective-permute-start.4
  252.8 1.4 convert_reduce_fusion.1
  254.2 4.4 %collective-permute-start.6 = (f32[8,1024]{1,0:T(8,128)S(1)}, f32[8,1024]{1,0:T(8,128)S(1)}, u32[]{:S(2)}, u32[]{:S(2)}) collective-permute-start(f32[8,1024]{1,0:T(8,128)S(1)} %convert_reduce_fusion.1), channel_id=1, source_target_pairs={{0,0},{1,64},{2,1},{3,65},{4,2},{5,66},{6,3},{7,67},{8,4},{9,68},{... | collective-permute-start | bytes 98312 | tf_op jit(solution)/shard_map/ppermute | solution.py:380
  258.6 1.7 convert_reduce_fusion
  261.2 1.4 collective-permute-start.5
  264.8 4.0 %add_convert_fusion.1 = bf16[1024,1024]{1,0:T(8,128)(2,1)} fusion(bf16[1024,1024]{1,0:T(8,128)(2,1)S(1)} %collective-permute-done.3, bf16[2048,1024]{1,0:T(8,128)(2,1)} %copy-done.18), kind=kLoop, calls=%fused_computation.1 | loop fusion | flops 4194304 | bytes 6291456 | tf_op jit(solution)/shard_map/convert_element_type | solution.py:374
  268.9 3.9 %add_convert_fusion = bf16[1024,1024]{1,0:T(8,128)(2,1)} fusion(bf16[1024,1024]{1,0:T(8,128)(2,1)} %collective-permute-done.4, bf16[2048,1024]{1,0:T(8,128)(2,1)S(1)} %copy-done.20), kind=kLoop, calls=%fused_computation | loop fusion | flops 4194304 | bytes 6291456 | tf_op jit(solution)/shard_map/convert_element_type | solution.py:389
  (79 shorter events, 14.1 us)
Async XLA Ops:
  0.6 16.5 %copy-start.22 = (bf16[8,1024]{1,0:T(8,128)(2,1)S(1)}, bf16[8,1024]{1,0:T(8,128)(2,1)}, u32[]{:S(2)}) copy-start(bf16[8,1024]{1,0:T(8,128)(2,1)} %param.10) | copy-start | bytes 49156
  0.6 45.2 %collective-permute-start = (bf16[1024,1024]{1,0:T(8,128)(2,1)}, bf16[1024,1024]{1,0:T(8,128)(2,1)}, u32[]{:S(2)}, u32[]{:S(2)}) collective-permute-start(bf16[1024,1024]{1,0:T(8,128)(2,1)} %param.6), channel_id=1, source_target_pairs={{0,1},{1,0},{2,3},{3,2},{4,5},{5,4},{6,7},{7,6},{8,9},{9,8},{10,11... | collective-permute-start | bytes 6291464 | tf_op jit(solution)/shard_map/ppermute | solution.py:327
  5.8 32.2 %all-to-all-start = ((bf16[128,8,640]{2,1,0:T(8,128)(2,1)}), bf16[128,8,640]{2,1,0:T(8,128)(2,1)S(1)}, u32[]{:S(2)}, u32[]{:S(2)}) async-start(bf16[128,8,640]{2,1,0:T(8,128)(2,1)} %bitcast.2), calls=%async_computation | async-start | bytes 2621440 | tf_op jit(solution)/shard_map/all_to_all | solution.py:353
  16.0 56.8 %collective-permute-start.1 = (bf16[1024,1024]{1,0:T(8,128)(2,1)}, bf16[1024,1024]{1,0:T(8,128)(2,1)}, u32[]{:S(2)}, u32[]{:S(2)}) collective-permute-start(bf16[1024,1024]{1,0:T(8,128)(2,1)} %param.11), channel_id=1, source_target_pairs={{0,1},{1,0},{2,3},{3,2},{4,5},{5,4},{6,7},{7,6},{8,9},{9,8},{10,11... | collective-permute-start | bytes 6291464 | tf_op jit(solution)/shard_map/ppermute | solution.py:327
  17.1 12.5 %collective-permute-start.2 = (bf16[8,1024]{1,0:T(8,128)(2,1)S(1)}, bf16[8,1024]{1,0:T(8,128)(2,1)S(1)}, u32[]{:S(2)}, u32[]{:S(2)}) collective-permute-start(bf16[8,1024]{1,0:T(8,128)(2,1)S(1)} %copy-done.22), channel_id=1, source_target_pairs={{0,0},{64,1},{1,2},{65,3},{2,4},{66,5},{3,6},{67,7},{4,8},{68,9},{... | collective-permute-start | bytes 49160 | tf_op jit(solution)/shard_map/ppermute | solution.py:355
  37.9 9.7 %copy-start.4 = (bf16[128,8,640]{2,1,0:T(8,128)(2,1)}, bf16[128,8,640]{2,1,0:T(8,128)(2,1)S(1)}, u32[]{:S(2)}) copy-start(bf16[128,8,640]{2,1,0:T(8,128)(2,1)S(1)} %all-to-all-done) | copy-start | bytes 3932164
  39.1 21.8 %all-to-all-start.1 = ((bf16[64,8,1024]{2,1,0:T(8,128)(2,1)}), bf16[64,8,1024]{2,1,0:T(8,128)(2,1)S(1)}, u32[]{:S(2)}, u32[]{:S(2)}) async-start(bf16[64,8,1024]{2,1,0:T(8,128)(2,1)} %broadcast_in_dim.19), calls=%async_computation.1 | async-start | bytes 2097152 | tf_op jit(solution)/shard_map/all_to_all | solution.py:330
  47.6 2.0 copy-start
  57.7 1.3 copy-start.2
  60.9 11.9 %copy-start.6 = (bf16[64,8,1024]{2,1,0:T(8,128)(2,1)}, bf16[64,8,1024]{2,1,0:T(8,128)(2,1)S(1)}, u32[]{:S(2)}) copy-start(bf16[64,8,1024]{2,1,0:T(8,128)(2,1)S(1)} %all-to-all-done.1) | copy-start | bytes 3145732
  61.8 19.1 %all-to-all-start.2 = ((f32[64,8,256]{2,1,0:T(8,128)}), f32[64,8,256]{2,1,0:T(8,128)S(1)}, u32[]{:S(2)}, u32[]{:S(2)}) async-start(f32[64,8,256]{2,1,0:T(8,128)} %broadcast_in_dim.20), calls=%async_computation.2 | async-start | bytes 1048576 | tf_op jit(solution)/shard_map/all_to_all | solution.py:330
  80.9 5.5 %copy-start.21 = (f32[64,8,256]{2,1,0:T(8,128)}, f32[64,8,256]{2,1,0:T(8,128)S(1)}, u32[]{:S(2)}) copy-start(f32[64,8,256]{2,1,0:T(8,128)S(1)} %all-to-all-done.2) | copy-start | bytes 1572868
  80.9 21.3 %all-to-all-start.3 = ((bf16[64,16,128]{2,1,0:T(8,128)(2,1)}), bf16[64,16,128]{2,1,0:T(8,128)(2,1)}, u32[]{:S(2)}, u32[]{:S(2)}) async-start(bf16[64,16,128]{2,1,0:T(8,128)(2,1)} %bitcast.5), calls=%async_computation.3 | async-start | bytes 524288 | tf_op jit(solution)/shard_map/all_to_all | solution.py:330
  86.4 1.2 copy-start.7
  101.5 0.7 copy-start.11
  102.2 19.2 %all-to-all-start.5 = ((bf16[64,16,128]{2,1,0:T(8,128)(2,1)}), bf16[64,16,128]{2,1,0:T(8,128)(2,1)}, u32[]{:S(2)}, u32[]{:S(2)}) async-start(bf16[64,16,128]{2,1,0:T(8,128)(2,1)} %bitcast.44), calls=%async_computation.5 | async-start | bytes 524288 | tf_op jit(solution)/shard_map/all_to_all | solution.py:330
  122.1 14.6 %all-to-all-start.4 = ((bf16[64,16,128]{2,1,0:T(8,128)(2,1)}), bf16[64,16,128]{2,1,0:T(8,128)(2,1)}, u32[]{:S(2)}, u32[]{:S(2)}) async-start(bf16[64,16,128]{2,1,0:T(8,128)(2,1)} %broadcast_in_dim.21), calls=%async_computation.4 | async-start | bytes 524288 | tf_op jit(solution)/shard_map/all_to_all | solution.py:330
  137.5 14.8 %all-to-all-start.6 = ((bf16[64,16,128]{2,1,0:T(8,128)(2,1)}), bf16[64,16,128]{2,1,0:T(8,128)(2,1)}, u32[]{:S(2)}, u32[]{:S(2)}) async-start(bf16[64,16,128]{2,1,0:T(8,128)(2,1)} %broadcast_in_dim.22), calls=%async_computation.6 | async-start | bytes 524288 | tf_op jit(solution)/shard_map/all_to_all | solution.py:330
  150.2 0.7 copy-start.9
  151.0 1.3 copy-start.12
  153.1 20.1 %all-to-all-start.7 = ((f32[64,8,256]{2,1,0:T(8,128)}), f32[64,8,256]{2,1,0:T(8,128)S(1)}, u32[]{:S(2)}, u32[]{:S(2)}) async-start(f32[64,8,256]{2,1,0:T(8,128)} %broadcast_in_dim.23), calls=%async_computation.7 | async-start | bytes 1048576 | tf_op jit(solution)/shard_map/all_to_all | solution.py:330
  162.7 1.6 copy-start.3
  168.5 1.3 copy-start.14
  173.3 2.2 copy-start.1
  175.5 16.4 %copy-start.13 = (bf16[512,2048]{1,0:T(8,128)(2,1)S(1)}, bf16[512,2048]{1,0:T(8,128)(2,1)}, u32[]{:S(2)}) copy-start(bf16[512,2048]{1,0:T(8,128)(2,1)} %copy-done.12) | copy-start | bytes 6291460
  178.6 0.7 copy-start.16
  180.2 21.9 %all-to-all-start.9 = ((bf16[128,2,256]{2,1,0:T(2,128)(2,1)}), bf16[128,2,256]{2,1,0:T(2,128)(2,1)S(1)}, u32[]{:S(2)}, u32[]{:S(2)}) async-start(bf16[128,2,256]{2,1,0:T(2,128)(2,1)} %reshape.80), calls=%async_computation.9 | async-start | bytes 262144 | tf_op jit(solution)/shard_map/all_to_all | solution.py:384
  202.1 23.2 %all-to-all-start.10 = ((bf16[64,8,1024]{2,1,0:T(8,128)(2,1)}), bf16[64,8,1024]{2,1,0:T(8,128)(2,1)}, u32[]{:S(2)}, u32[]{:S(2)}) async-start(bf16[64,8,1024]{2,1,0:T(8,128)(2,1)} %fusion.5), calls=%async_computation.10 | async-start | bytes 2097152 | tf_op jit(solution)/shard_map/all_to_all | solution.py:330
  215.6 2.6 copy-start.10
  222.1 13.1 %copy-start.8 = (bf16[64,8,1024]{2,1,0:T(8,128)(2,1)S(1)}, bf16[64,8,1024]{2,1,0:T(8,128)(2,1)}, u32[]{:S(2)}) copy-start(bf16[64,8,1024]{2,1,0:T(8,128)(2,1)} %copy-done.6) | copy-start | bytes 3145732
  225.3 33.3 %all-to-all-start.8 = ((bf16[64,16,768]{2,1,0:T(8,128)(2,1)}), bf16[64,16,768]{2,1,0:T(8,128)(2,1)}, u32[]{:S(2)}, u32[]{:S(2)}) async-start(bf16[64,16,768]{2,1,0:T(8,128)(2,1)} %pad_maximum_fusion), calls=%async_computation.8 | async-start | bytes 3145728 | tf_op jit(solution)/shard_map/all_to_all | solution.py:330
  237.6 2.0 copy-start.18
  239.6 2.7 copy-start.5
  239.6 2.7 %copy-start.15 = (bf16[512,2048]{1,0:T(8,128)(2,1)S(1)}, bf16[512,2048]{1,0:T(8,128)(2,1)}, u32[]{:S(2)}) copy-start(bf16[512,2048]{1,0:T(8,128)(2,1)} %copy-done.14) | copy-start | bytes 6291460
  239.6 2.8 %copy-start.17 = (bf16[64,2048]{1,0:T(8,128)(2,1)S(1)}, bf16[64,2048]{1,0:T(8,128)(2,1)}, u32[]{:S(2)}) copy-start(bf16[64,2048]{1,0:T(8,128)(2,1)} %copy-done.16) | copy-start | bytes 786436
  241.1 23.7 %collective-permute-start.3 = (bf16[1024,1024]{1,0:T(8,128)(2,1)}, bf16[1024,1024]{1,0:T(8,128)(2,1)S(1)}, u32[]{:S(2)}, u32[]{:S(2)}) collective-permute-start(bf16[1024,1024]{1,0:T(8,128)(2,1)} %slice.117), channel_id=1, source_target_pairs={{0,1},{1,0},{2,3},{3,2},{4,5},{5,4},{6,7},{7,6},{8,9},{9,8},{10,11... | collective-permute-start | bytes 6291464 | tf_op jit(solution)/shard_map/ppermute | solution.py:327
  246.1 2.0 copy-start.19
  249.7 19.2 %collective-permute-start.4 = (bf16[1024,1024]{1,0:T(8,128)(2,1)}, bf16[1024,1024]{1,0:T(8,128)(2,1)}, u32[]{:S(2)}, u32[]{:S(2)}) collective-permute-start(bf16[1024,1024]{1,0:T(8,128)(2,1)} %slice.119), channel_id=1, source_target_pairs={{0,1},{1,0},{2,3},{3,2},{4,5},{5,4},{6,7},{7,6},{8,9},{9,8},{10,11... | collective-permute-start | bytes 6291464 | tf_op jit(solution)/shard_map/ppermute | solution.py:327
  254.2 8.4 %collective-permute-start.6 = (f32[8,1024]{1,0:T(8,128)S(1)}, f32[8,1024]{1,0:T(8,128)S(1)}, u32[]{:S(2)}, u32[]{:S(2)}) collective-permute-start(f32[8,1024]{1,0:T(8,128)S(1)} %convert_reduce_fusion.1), channel_id=1, source_target_pairs={{0,0},{1,64},{2,1},{3,65},{4,2},{5,66},{6,3},{7,67},{8,4},{9,68},{... | collective-permute-start | bytes 98312 | tf_op jit(solution)/shard_map/ppermute | solution.py:380
  261.2 2.2 collective-permute-start.5
  264.8 4.0 %copy-start.20 = (bf16[2048,1024]{1,0:T(8,128)(2,1)S(1)}, bf16[2048,1024]{1,0:T(8,128)(2,1)}, u32[]{:S(2)}) copy-start(bf16[2048,1024]{1,0:T(8,128)(2,1)} %copy-done.19) | copy-start | bytes 12582916

commit v3 on v2

v3 whole, which is shorter than its diff:
```python
import jax
import jax.numpy as jnp
from jax import lax
from jax.experimental import pallas as pl
from jax.experimental.pallas import tpu as pltpu
from jax.sharding import PartitionSpec as P

H = 8
DK = 16
DV = 128
BANDS = DK // 2 + 1
FPAD = (BANDS + 2) * DK
SPAD = 256
AXES = ("ctx", "seq")
BF = jnp.bfloat16
F32 = jnp.float32
SQUARE = (2.0 * DK) ** (-0.5)
LINEAR = DK ** (-0.25)


def dot(a, b, contract):
    return lax.dot_general(a, b, ((contract[:1], contract[1:]), ((), ())), preferred_element_type=F32)


def band_weight(shape, dim):
    row = lax.broadcasted_iota(jnp.int32, shape, dim)
    twice = (row >= DK) & (row < (BANDS - 1) * DK)
    return jnp.where(twice, 2.0, 1.0).astype(F32)


def shifted(u, d):
    return pltpu.roll(u, DK - d, 0) if d else u


def features(u):
    bands = [u * shifted(u, d) * SQUARE for d in range(BANDS)]
    first = lax.broadcasted_iota(jnp.int32, u.shape, 0) == 0
    return jnp.concatenate(bands + [u * LINEAR, jnp.where(first, 1.0, 0.0)], axis=0).astype(BF)


def features_back(u, fgrad):
    def band(d):
        return fgrad[d * DK : (d + 1) * DK]

    total = band(0) * u + band(BANDS - 1) * shifted(u, BANDS - 1)
    for d in range(1, BANDS - 1):
        total = total + band(d) * shifted(u, d) + shifted(band(d) * u, DK - d)
    return total * (2.0 * SQUARE) + band(BANDS) * LINEAR


def in_parts(row):
    high = row.astype(BF).astype(F32)
    rest = row - high
    mid = rest.astype(BF).astype(F32)
    at = lax.broadcasted_iota(jnp.int32, (16, row.shape[1]), 0)
    low = jnp.where(at == 2, rest - mid, 0.0)
    return jnp.where(at == 0, high, jnp.where(at == 1, mid, low)).astype(BF)


def rows_of(array, head, size):
    return array[head * size : (head + 1) * size]


def head_row(rows, head):
    first, second = rows[4 * head : 4 * head + 2, :], rows[4 * head + 2 : 4 * head + 4, :]
    both = first + second
    return jnp.concatenate([both[:1], both[1:]], axis=1)


def split_rows(per_head):
    found = []
    for row in per_head:
        high = row.astype(BF).astype(F32)
        for part in (high, row - high):
            found += [part[:, :128], part[:, 128:]]
    found += [jnp.zeros((1, 128), F32)] * (16 - len(found))
    return jnp.concatenate(found, axis=0).astype(BF)


def column(row):
    return jnp.broadcast_to(row, (8, row.shape[1])).T[:FPAD, :1]


def weighted_turned(state_ref, head):
    whole = state_ref[head * SPAD : (head + 1) * SPAD, :].astype(F32)
    return (whole * band_weight((SPAD, DV), 0)).T.astype(BF)


def call(body, count, ins, kinds, outs, out_kinds, scratch, flops, skip=0):
    block = min(512, count, *[x[0].shape[0] for x, k in zip(ins, kinds) if k == "pair"])
    steps, first = count // block, skip // block
    in_specs, args = [], []
    for x, kind in zip(ins, kinds):
        if kind is None:
            in_specs.append(pl.BlockSpec(x.shape, lambda i: (0, 0)))
        elif kind == 0:
            in_specs.append(pl.BlockSpec((block, x.shape[1]), lambda i: (i + first, 0)))
        elif kind == 1:
            in_specs.append(pl.BlockSpec((x.shape[0], block), lambda i: (0, i + first)))
        elif kind == "here":
            in_specs.append(pl.BlockSpec((block, x.shape[1]), lambda i: (i, 0)))
        else:
            half = steps // 2
            in_specs.append(pl.BlockSpec((block, x[0].shape[1]), lambda i: (jnp.minimum(i, half - 1), 0)))
            in_specs.append(pl.BlockSpec((block, x[0].shape[1]), lambda i: (jnp.maximum(i - half, 0), 0)))
        args += list(x) if kind == "pair" else [x]
    out_specs = []
    for x, kind in zip(outs, out_kinds):
        if kind is None:
            out_specs.append(pl.BlockSpec(x.shape, lambda i: (0, 0)))
        elif kind == 0:
            out_specs.append(pl.BlockSpec((block, x.shape[1]), lambda i: (i, 0)))
        else:
            out_specs.append(pl.BlockSpec((x.shape[0], block), lambda i: (0, i)))
    nbytes = sum(x.size * x.dtype.itemsize for x in args + list(outs))
    return pl.pallas_call(
        body,
        grid=(steps,),
        in_specs=in_specs,
        out_specs=out_specs,
        out_shape=outs,
        scratch_shapes=scratch,
        compiler_params=pltpu.CompilerParams(dimension_semantics=("arbitrary",), vmem_limit_bytes=48 * 2**20),
        cost_estimate=pl.CostEstimate(flops=flops, bytes_accessed=nbytes, transcendentals=0),
    )(*args)


def either(first_ref, second_ref):
    return jnp.where(pl.program_id(0) < pl.num_programs(0) // 2, first_ref[...], second_ref[...])


def shape(dims, dtype):
    return jax.ShapeDtypeStruct(dims, dtype)


def clear_at_first(*refs):
    @pl.when(pl.program_id(0) == 0)
    def _():
        for ref in refs:
            ref[...] = jnp.zeros(ref.shape, ref.dtype)


def at_first(fn):
    pl.when(pl.program_id(0) == 0)(fn)


def at_last(fn):
    pl.when(pl.program_id(0) == pl.num_programs(0) - 1)(fn)


def keys_phase(tokens, w_qkv, heads):
    qk = heads * DK

    def body(own_ref, other_ref, w_ref, qk_ref, value_ref, feat_ref, state_ref, norm_ref, state_acc, norm_acc):
        clear_at_first(state_acc, norm_acc)
        joined = dot(either(own_ref, other_ref), w_ref[...], (1, 0))
        qk_t = joined[:, : 2 * qk].T.astype(BF)
        value = joined[:, 2 * qk :].astype(BF)
        qk_ref[...] = qk_t
        value_ref[...] = value
        keys = qk_t.astype(F32)[qk:]
        ones = jnp.ones((16, value.shape[0]), BF)
        for head in range(heads):
            feat = features(rows_of(keys, head, DK))
            feat_ref[head * FPAD : (head + 1) * FPAD, :] = feat
            state_acc[head, :FPAD, :] += dot(feat, value[:, head * DV : (head + 1) * DV], (1, 0))
            norm_acc[head, :, :FPAD] += dot(ones, feat, (1, 1))

        @at_last
        def _():
            for head in range(heads):
                state_ref[head * SPAD : (head + 1) * SPAD, :] = state_acc[head].astype(BF)
            norm_ref[...] = split_rows([norm_acc[head][:1] for head in range(heads)])

    count = 2 * tokens[0].shape[0]
    return call(
        body,
        count,
        (tokens, w_qkv),
        ("pair", None),
        (
            shape((2 * qk, count), BF),
            shape((count, heads * DV), BF),
            shape((heads * FPAD, count), BF),
            shape((heads * SPAD, DV), BF),
            shape((16, 128), BF),
        ),
        (1, 0, 1, None, None),
        [pltpu.VMEM((heads, SPAD, DV), F32), pltpu.VMEM((heads, 16, SPAD), F32)],
        2 * count * (w_qkv.size + heads * FPAD * DV * 2),
    )


def upstream_phase(qk_t, cot, w_out_half, heads):
    count = qk_t.shape[1]

    def body(qk_ref, own_ref, other_ref, w_ref, up_ref, feat_ref):
        up_ref[...] = dot(w_ref[...], either(own_ref, other_ref), (1, 1))
        query = qk_ref[...].astype(F32)
        for head in range(heads):
            feat_ref[head * FPAD : (head + 1) * FPAD, :] = features(rows_of(query, head, DK))

    return call(
        body,
        count,
        (qk_t, cot, w_out_half),
        (1, "pair", None),
        (shape((heads * DV, count), F32), shape((heads * FPAD, count), BF)),
        (1, 1),
        [],
        2 * count * w_out_half.size,
    )


def product_phase(rows_t, slabs):
    rows, count = rows_t.shape
    width = slabs[0].shape[1]

    def body(rows_ref, own_ref, other_ref, out_ref, acc):
        clear_at_first(acc)
        acc[...] += dot(rows_ref[...], either(own_ref, other_ref), (1, 0))

        @at_last
        def _():
            out_ref[...] = acc[...].T.astype(BF)

    return call(
        body,
        count,
        (rows_t, slabs),
        (1, "pair"),
        (shape((width, rows), BF),),
        (None,),
        [pltpu.VMEM((rows, width), F32)],
        2 * count * rows * width,
    )[0]


def query_phase(feats, up_t, norm, heads):
    count = up_t.shape[1]

    def body(feat_ref, up_ref, norm_ref, scale_ref, sgrad_ref, acc):
        clear_at_first(acc)
        at = lax.broadcasted_iota(jnp.int32, scale_ref.shape, 0)
        scales = jnp.zeros(scale_ref.shape, F32)
        for head in range(heads):
            feat = feat_ref[head * FPAD : (head + 1) * FPAD, :]
            parts = in_parts(head_row(norm_ref[...], head) * band_weight((1, SPAD), 1))[:, :FPAD]
            scale = 1.0 / jnp.sum(dot(parts, feat, (1, 0)), axis=0, keepdims=True)
            grad_num = (up_ref[head * DV : (head + 1) * DV, :] * scale).astype(BF)
            acc[head, :FPAD, :] += dot(feat, grad_num, (1, 1))
            scales = jnp.where(at == head, scale, scales)
        scale_ref[...] = scales

        @at_last
        def _():
            for head in range(heads):
                sgrad_ref[head * SPAD : (head + 1) * SPAD, :] = acc[head].astype(BF)

    return call(
        body,
        count,
        (feats, up_t, norm),
        (1, 1, None),
        (shape((8, count), F32), shape((heads * SPAD, DV), BF)),
        (1, None),
        [pltpu.VMEM((heads, SPAD, DV), F32)],
        2 * count * heads * FPAD * DV * 2,
    )


def attend_phase(qk_t, feats, scales, up_t, state, norm, cot, heads):
    count = up_t.shape[1]
    width = cot[0].shape[1]

    def body(
        qk_ref, feat_ref, scale_ref, up_ref, state_ref, norm_ref, own_ref, other_ref,
        att_ref, qgrad_ref, ngrad_ref, out_ref, turned, acc, out_acc,
    ):
        clear_at_first(acc, out_acc)

        @at_first
        def _():
            for head in range(heads):
                turned[head] = weighted_turned(state_ref, head)

        query = qk_ref[...].astype(F32)
        for head in range(heads):
            feat = feat_ref[head * FPAD : (head + 1) * FPAD, :]
            scale = scale_ref[head : head + 1, :]
            att = dot(turned[head, :, :FPAD], feat, (1, 0)) * scale
            grad_num = up_ref[head * DV : (head + 1) * DV, :] * scale
            grad_den = -jnp.sum(grad_num * att, axis=0, keepdims=True)
            acc[head, :, :FPAD] += dot(in_parts(grad_den), feat, (1, 1))
            fgrad = dot(state_ref[head * SPAD : head * SPAD + FPAD, :], grad_num.astype(BF), (1, 0))
            fgrad = fgrad + column(head_row(norm_ref[...], head)) * grad_den
            qgrad_ref[head * DK : (head + 1) * DK, :] = features_back(rows_of(query, head, DK), fgrad).astype(BF)
            att_ref[head * DV : (head + 1) * DV, :] = att.astype(BF)
        out_acc[...] += dot(att_ref[...], either(own_ref, other_ref), (1, 0))

        @at_last
        def _():
            ngrad_ref[...] = split_rows([jnp.sum(acc[head], axis=0, keepdims=True) for head in range(heads)])
            out_ref[...] = out_acc[...].astype(BF)

    return call(
        body,
        count,
        (qk_t, feats, scales, up_t, state, norm, cot),
        (1, 1, 1, 1, None, None, "pair"),
        (
            shape((heads * DV, count), BF),
            shape((heads * DK, count), BF),
            shape((16, 128), BF),
            shape((heads * DV, width), BF),
        ),
        (1, 1, None, None),
        [
            pltpu.VMEM((heads, DV, SPAD), BF),
            pltpu.VMEM((heads, 16, SPAD), F32),
            pltpu.VMEM((heads * DV, width), F32),
        ],
        2 * count * (heads * FPAD * DV * 4 + heads * DV * width),
    )


def mixed_phase(attended_t, w_out_half, skip, arrived, count):
    def body(att_ref, w_ref, *refs):
        part = dot(att_ref[...], w_ref[...], (0, 0))
        if len(refs) > 1:
            part = part + refs[0][...].astype(F32)
        refs[-1][...] = part.astype(BF)

    more = () if arrived is None else (arrived,)
    return call(
        body,
        count,
        (attended_t, w_out_half) + more,
        (1, None) + ("here",) * len(more),
        (shape((count, w_out_half.shape[1]), BF),),
        (0,),
        [],
        2 * count * w_out_half.size,
        skip,
    )[0]


def key_phase(qk_t, value, sgrad, ngrad, qgrad_t, tokens, heads):
    count, qk = value.shape[0], heads * DK
    width = tokens[0].shape[1]

    def body(qk_ref, value_ref, sgrad_ref, ngrad_ref, qgrad_ref, own_ref, other_ref, kgrad_ref, wgrad_ref, acc):
        clear_at_first(acc)
        keys = qk_ref[...].astype(F32)[qk:]
        found = []
        for head in range(heads):
            fgrad = dot(
                sgrad_ref[head * SPAD : head * SPAD + FPAD, :],
                value_ref[:, head * DV : (head + 1) * DV],
                (1, 1),
            )
            fgrad = fgrad + column(head_row(ngrad_ref[...], head))
            found.append(features_back(rows_of(keys, head, DK), fgrad))
        kgrad = jnp.concatenate(found, axis=0).astype(BF)
        kgrad_ref[...] = kgrad
        both = jnp.concatenate([qgrad_ref[...], kgrad], axis=0)
        acc[...] += dot(both, either(own_ref, other_ref), (1, 0))

        @at_last
        def _():
            wgrad_ref[...] = acc[...].T.astype(BF)

    return call(
        body,
        count,
        (qk_t, value, sgrad, ngrad, qgrad_t, tokens),
        (1, 0, None, None, 1, "pair"),
        (shape((qk, count), BF), shape((width, 2 * qk), BF)),
        (1, None),
        [pltpu.VMEM((2 * qk, width), F32)],
        2 * count * (heads * FPAD * DV + 2 * qk * width),
    )


def tokens_phase(qgrad_t, kgrad_t, feats, sgrad, w_qkv, heads, skip, arrived, count):
    def body(qgrad_ref, kgrad_ref, feat_ref, sgrad_ref, w_ref, *refs):
        turned = refs[-1]

        @at_first
        def _():
            for head in range(heads):
                turned[head] = weighted_turned(sgrad_ref, head)

        joined = [qgrad_ref[...], kgrad_ref[...]]
        for head in range(heads):
            feat = feat_ref[head * FPAD : (head + 1) * FPAD, :]
            joined.append(dot(turned[head, :, :FPAD], feat, (1, 0)).astype(BF))
        part = dot(jnp.concatenate(joined, axis=0), w_ref[...], (0, 1))
        if len(refs) > 2:
            part = part + refs[0][...].astype(F32)
        refs[-2][...] = part.astype(BF)

    more = () if arrived is None else (arrived,)
    return call(
        body,
        count,
        (qgrad_t, kgrad_t, feats, sgrad, w_qkv) + more,
        (1, 1, 1, None, None) + ("here",) * len(more),
        (shape((count, w_qkv.shape[0]), BF),),
        (0,),
        [pltpu.VMEM((heads, DV, SPAD), BF)],
        2 * count * (w_qkv.size + heads * FPAD * DV),
        skip,
    )[0]


def per_device(chips, tokens, w_query, w_key, w_value, w_out, cotangent):
    n = 2 * chips
    heads = H // 2
    own = tokens.shape[0]
    qk = heads * DK
    core = lax.axis_index("seq") % 2
    same_core = [[2 * p + c for p in range(chips)] for c in range(2)]
    swap = [(i, i ^ 1) for i in range(n)]
    scale_factor = (own * n) ** (-0.5)

    def exchange(x):
        return lax.ppermute(x, AXES, swap)

    def spread(x):
        return lax.all_to_all(x, AXES, 0, 0, axis_index_groups=same_core, tiled=True)

    def to_all(x):
        return jnp.broadcast_to(x[None], (chips,) + x.shape)

    def to_each(x):
        return x.reshape(chips, -1, x.shape[1])

    def add_up(x):
        return jnp.sum(x.astype(F32), axis=0)

    def fold(x):
        return jnp.concatenate([x[:, :8], x[:, 8:]], axis=2)

    def unfold(x):
        return jnp.concatenate([x[:, :, :128], x[:, :, 128:]], axis=1)

    halves = [
        jnp.concatenate(
            [
                w_query[:, c * qk : (c + 1) * qk],
                w_key[:, c * qk : (c + 1) * qk],
                w_value[:, c * heads * DV : (c + 1) * heads * DV],
            ],
            axis=1,
        )
        for c in range(2)
    ]
    to_send = jnp.broadcast_to(jnp.stack(halves)[None], (chips, 2) + halves[0].shape)
    w_qkv = lax.all_to_all(to_send.reshape((n,) + halves[0].shape), AXES, 0, 0, tiled=True)
    w_qkv = w_qkv.reshape(-1, halves[0].shape[1])
    out_rows = lax.ppermute(w_out, AXES, [(c * chips + p, 2 * p + c) for p in range(chips) for c in range(2)])
    w_out_half = spread(to_all(out_rows)).reshape(-1, out_rows.shape[1])

    tok = (tokens, exchange(tokens))
    cot = (cotangent, exchange(cotangent))

    qk_t, value, key_feat, state_part, norm_part = keys_phase(tok, w_qkv, heads)
    first = spread(jnp.concatenate([to_each(state_part), to_all(norm_part)], axis=1))
    state_own, norm = add_up(first[:, :16]).astype(BF), add_up(first[:, 16:])

    up_t, query_feat = upstream_phase(qk_t, cot, w_out_half, heads)
    moments = product_phase(key_feat, tok)
    scales, sgrad_part = query_phase(query_feat, up_t, norm, heads)
    second = spread(jnp.concatenate([to_each(sgrad_part), to_all(state_own), to_each(moments)], axis=2))
    sgrad_own = add_up(second[:, :, :128]).astype(BF)
    state = second[:, :, 128:256].reshape(-1, 128)
    moment_sum = add_up(second[:, :, 256:])

    attended_t, qgrad_t, ngrad_part, out_part = attend_phase(
        qk_t, query_feat, scales, up_t, state, norm, cot, heads
    )
    third = spread(jnp.concatenate([to_each(out_part), fold(to_all(sgrad_own)), fold(to_all(ngrad_part))], axis=2))
    width = out_part.shape[1]
    sgrad = unfold(third[:, :, width : width + 256]).reshape(-1, 128)
    ngrad = add_up(unfold(third[:, :, width + 256 :]))
    out_sum = add_up(third[:, :, :width])
    grad_out = lax.ppermute(out_sum, AXES, [(2 * p + c, c * chips + p) for p in range(chips) for c in range(2)])

    mixed_other = exchange(mixed_phase(attended_t, w_out_half, own, None, own))
    mixed = mixed_phase(attended_t, w_out_half, 0, mixed_other, own)

    kgrad_t, wgrad = key_phase(qk_t, value, sgrad, ngrad, qgrad_t, tok, heads)
    fourth = lax.all_to_all(wgrad.reshape(n, -1, wgrad.shape[1]), AXES, 0, 0, tiled=True)
    wgrad_sum = jnp.sum(fourth.reshape((chips, 2) + fourth.shape[1:]).astype(F32), axis=0) * scale_factor
    gtok_other = exchange(tokens_phase(qgrad_t, kgrad_t, key_feat, sgrad, w_qkv, heads, own, None, own))
    grad_tokens = tokens_phase(qgrad_t, kgrad_t, key_feat, sgrad, w_qkv, heads, 0, gtok_other, own)

    weight = band_weight((1, FPAD), 1)
    gvalue = jnp.concatenate(
        [
            jnp.dot(
                moment_sum[:, h * FPAD : (h + 1) * FPAD] * weight,
                sgrad[h * SPAD : h * SPAD + FPAD].astype(F32),
                precision=lax.Precision.HIGH,
            )
            for h in range(heads)
        ],
        axis=1,
    )
    rows = gvalue.shape[0] // 2
    got = exchange(lax.dynamic_slice_in_dim(gvalue, (1 - core) * rows, rows, 0))
    kept = lax.dynamic_slice_in_dim(gvalue, core * rows, rows, 0)
    low, high = jnp.where(core == 0, kept, got), jnp.where(core == 0, got, kept)
    grad_value = jnp.concatenate([low, high], axis=1) * scale_factor
    grad_query = jnp.concatenate([wgrad_sum[0, :, :qk], wgrad_sum[1, :, :qk]], axis=1)
    grad_key = jnp.concatenate([wgrad_sum[0, :, qk:], wgrad_sum[1, :, qk:]], axis=1)
    return (mixed, grad_tokens, grad_query, grad_key, grad_value, grad_out * scale_factor)


def solution(mesh):
    chips = mesh.size // 2
    placed = P(AXES, None)
    return jax.shard_map(
        lambda *args: per_device(chips, *args),
        mesh=mesh,
        in_specs=(placed,) * 6,
        out_specs=(placed,) * 6,
        check_vma=False,
    )
```

time: 276 us -> 228 us (0.83)
  starting transfers between devices: 100 us -> 51.1 us
  blocking collectives: 0 us -> 34.9 us
  Pallas kernels: 35.2 us -> 60.5 us
  matrix products: 22.8 us -> 0.69 us
  local copies, waits for them, and re-layouts: 43.5 us -> 22.7 us
  other arithmetic: 19.9 us -> 8.01 us
    all_to_all x9 -> x3, starting transfers between devices: 65 us -> 18.5 us  [spread(): lax.all_to_all(x, AXES, 0, 0, axis_index_groups=same_core, tiled=True)]
    all_to_all x0 -> x1, blocking collectives: none -> 34.9 us  [spread(): lax.all_to_all(x, AXES, 0, 0, axis_index_groups=same_core, tiled=True)]
    pallas_call x6 -> x10, Pallas kernels: 35.2 us -> 60.5 us  [call(): pl.pallas_call(body, grid=(steps,), in_specs=in_specs, out_specs=out_spec...]
    dot_general x9 -> x4, matrix products: 22.8 us -> 0.69 us  [per_device(): jnp.dot(moment_sum[:, h * FPAD:(h + 1) * FPAD] * weight, sgrad[h * SPAD:h...]
    convert_element_type x2 -> x0, other arithmetic: 7.91 us -> none  [the longest x1 4.04 us: per_device(): mixed = (mixed_part[:own].astype(F32) + mixed_other.astype(F32)).astype(BF)]
    all_to_all x9 -> x3, waiting for transfers between devices: 26.9 us -> 19.3 us  [spread(): lax.all_to_all(x, AXES, 0, 0, axis_index_groups=same_core, tiled=True)]
    unnamed x50 -> x34, local copies, waits for them, and re-layouts: 23 us -> 15.9 us
    all_to_all x1, waiting for transfers between devices: 4.64 us -> 10.1 us  [per_device(): lax.all_to_all(wgrad.reshape(n, -1, wgrad.shape[1]), AXES, 0, 0, tiled=True)]
  transfers between devices with their start and end apart: 18 -> 12, of which waited for: 10 -> 5; matrix products, arithmetic and copies ran while one was open for 23% -> 5% of each run, Pallas kernels for 12% -> 17%
where the time goes in v3:
time: 228 us; the launch traced here: 226 us
  Pallas kernels  60.5 us (27%)
  starting transfers between devices  51.1 us (22%)
  waiting for transfers between devices  47.6 us (21%)
  blocking collectives  34.9 us (15%)
  local copies, waits for them, and re-layouts  22.7 us (10%)
  other arithmetic  8.01 us (4%)
    pallas_call x10, Pallas kernels, call(): pl.pallas_call(body, grid=(steps,), in_specs=in_specs, out_specs=out_spec...  60.5 us
    all_to_all x1, blocking collectives, spread(): lax.all_to_all(x, AXES, 0, 0, axis_index_groups=same_core, tiled=True)  34.9 us
    all_to_all x3, waiting for transfers between devices, spread(): lax.all_to_all(x, AXES, 0, 0, axis_index_groups=same_core, tiled=True)  19.3 us
    all_to_all x3, starting transfers between devices, spread(): lax.all_to_all(x, AXES, 0, 0, axis_index_groups=same_core, tiled=True)  18.5 us
    unnamed x34, local copies, waits for them, and re-layouts  15.9 us
    all_to_all x1, starting transfers between devices, per_device(): lax.all_to_all(to_send.reshape((n,) + halves[0].shape), AXES, 0, 0, tiled...  10.2 us
    all_to_all x1, waiting for transfers between devices, per_device(): lax.all_to_all(wgrad.reshape(n, -1, wgrad.shape[1]), AXES, 0, 0, tiled=True)  10.1 us
    ppermute x5, starting transfers between devices, exchange(): return lax.ppermute(x, AXES, swap)  10 us
  transfers between devices with their start and end apart: 12, of which 5 were waited for; matrix products, arithmetic and copies ran while one was open for 5% of the time, Pallas kernels for 17%

profile of v3, /device:TPU:1, one launch (start us, length us, event | category | flops | bytes accessed | tf_op | source)
XLA Modules:
  0.0 226.3 jit_solution(3529166844287275818)
XLA Ops:
  0.6 1.5 collective-permute-start
  2.1 0.8 fusion.16
  3.0 0.8 fusion.17
  3.8 0.7 fusion.13
  4.6 1.2 broadcast_in_dim.22
  5.8 10.2 %all-to-all-start = ((bf16[128,8,640]{2,1,0:T(8,128)(2,1)}), bf16[128,8,640]{2,1,0:T(8,128)(2,1)S(1)}, u32[]{:S(2)}, u32[]{:S(2)}) async-start(bf16[128,8,640]{2,1,0:T(8,128)(2,1)} %bitcast.2), calls=%async_computation | async-start | bytes 2621440 | tf_op jit(solution)/shard_map/all_to_all | solution.py:460
  16.0 1.1 collective-permute-start.1
  17.1 2.6 %collective-permute-start.2 = (bf16[8,1024]{1,0:T(8,128)(2,1)S(1)}, bf16[8,1024]{1,0:T(8,128)(2,1)S(1)}, u32[]{:S(2)}, u32[]{:S(2)}) collective-permute-start(bf16[8,1024]{1,0:T(8,128)(2,1)S(1)} %copy-done.14), channel_id=1, source_target_pairs={{0,0},{64,1},{1,2},{65,3},{2,4},{66,5},{3,6},{67,7},{4,8},{68,9},{... | collective-permute-start | bytes 49160 | tf_op jit(solution)/shard_map/ppermute | solution.py:462
  19.7 9.9 %collective-permute-done.2 = bf16[8,1024]{1,0:T(8,128)(2,1)S(1)} collective-permute-done((bf16[8,1024]{1,0:T(8,128)(2,1)S(1)}, bf16[8,1024]{1,0:T(8,128)(2,1)S(1)}, u32[]{:S(2)}, u32[]{:S(2)}) %collective-permute-start.2) | collective-permute-done | bytes 16416 | tf_op jit(solution)/shard_map/ppermute | solution.py:462
  29.6 8.3 %all-to-all-done = bf16[128,8,640]{2,1,0:T(8,128)(2,1)S(1)} async-done(((bf16[128,8,640]{2,1,0:T(8,128)(2,1)}), bf16[128,8,640]{2,1,0:T(8,128)(2,1)S(1)}, u32[]{:S(2)}, u32[]{:S(2)}) %all-to-all-start) | async-done | bytes 1310752 | tf_op jit(solution)/shard_map/all_to_all | solution.py:460
  37.9 1.1 broadcast_in_dim.23
  39.0 4.9 %all-to-all-start.1 = ((bf16[64,8,1024]{2,1,0:T(8,128)(2,1)}), bf16[64,8,1024]{2,1,0:T(8,128)(2,1)S(1)}, u32[]{:S(2)}, u32[]{:S(2)}) async-start(bf16[64,8,1024]{2,1,0:T(8,128)(2,1)} %broadcast_in_dim.23), calls=%async_computation.1 | async-start | bytes 2097152 | tf_op jit(solution)/shard_map/all_to_all | solution.py:431
  44.0 8.5 %shard_map.109 = (bf16[128,2048]{1,0:T(8,128)(2,1)S(1)}, bf16[2048,512]{1,0:T(8,128)(2,1)S(1)}, bf16[704,2048]{1,0:T(8,128)(2,1)}, bf16[1024,128]{1,0:T(8,128)(2,1)S(1)}, bf16[16,128]{1,0:T(8,128)(2,1)S(1)}) custom-call(bf16[1024,1024]{1,0:T(8,128)(2,1)} %own_ref.9, bf16[1024,1024]{1,0:T(8,128)(2,1)} %collective-permute-done.other_ref, ...), custom_call_target="tpu_custom_call" | custom-call | flops 3422552064 | bytes 11276288 | tf_op jit(solution)/shard_map/pallas_call | solution.py:116
  52.4 1.4 copy-done.6
  53.8 0.9 pad_maximum_fusion.1
  54.7 6.1 %all-to-all-done.1 = bf16[64,8,1024]{2,1,0:T(8,128)(2,1)S(1)} async-done(((bf16[64,8,1024]{2,1,0:T(8,128)(2,1)}), bf16[64,8,1024]{2,1,0:T(8,128)(2,1)S(1)}, u32[]{:S(2)}, u32[]{:S(2)}) %all-to-all-start.1) | async-done | bytes 1048608 | tf_op jit(solution)/shard_map/all_to_all | solution.py:431
  60.8 5.5 %all-to-all-start.2 = ((bf16[64,32,128]{2,1,0:T(8,128)(2,1)}), bf16[64,32,128]{2,1,0:T(8,128)(2,1)}, u32[]{:S(2)}, u32[]{:S(2)}) async-start(bf16[64,32,128]{2,1,0:T(8,128)(2,1)} %pad_maximum_fusion.1), calls=%async_computation.2 | async-start | bytes 1048576 | tf_op jit(solution)/shard_map/all_to_all | solution.py:431
  66.4 7.3 %shard_map.110 = (f32[512,2048]{1,0:T(8,128)}, bf16[704,2048]{1,0:T(8,128)(2,1)}) custom-call(bf16[128,2048]{1,0:T(8,128)(2,1)S(1)} %get-tuple-element.21.qk_ref, bf16[1024,1024]{1,0:T(8,128)(2,1)} %own_ref.8, bf16[1024,1024]{1,0:T(8,128)(2,1)} %collective-permute-done.1.other_ref, bf16[512,1024]{1,0:T(8,128)(2,1)S(1)} %bitcast.36), custom_call_target="tpu_custom_call" | custom-call | flops 2147483648 | bytes 12845056 | tf_op jit(solution)/shard_map/pallas_call | solution.py:116
  73.6 6.4 %shard_map.112 = bf16[1024,704]{1,0:T(8,128)(2,1)S(1)} custom-call(bf16[704,2048]{1,0:T(8,128)(2,1)} %get-tuple-element.28.rows_ref.feat_ref, bf16[1024,1024]{1,0:T(8,128)(2,1)S(1)} %copy-done.4, bf16[1024,1024]{1,0:T(8,128)(2,1)} %collective-permute-done.other_ref), custom_call_target="tpu_custom_call" | custom-call | flops 2952790016 | bytes 8519680 | tf_op jit(solution)/shard_map/pallas_call | solution.py:116
  80.1 1.1 copy-done.8
  81.2 1.0 convert_reduce_fusion.4.norm_ref
  82.2 1.8 copy-done.3
  84.1 6.0 %shard_map.111 = (f32[8,2048]{1,0:T(8,128)S(1)}, bf16[1024,128]{1,0:T(8,128)(2,1)S(1)}) custom-call(bf16[704,2048]{1,0:T(8,128)(2,1)S(1)} %copy-done.3, f32[512,2048]{1,0:T(8,128)} %get-tuple-element.23.up_ref, f32[16,128]{1,0:T(8,128)S(1)} %convert_reduce_fusion.4.norm_ref), custom_call_target="tpu_custom_call" | custom-call | flops 738197504 | bytes 7413760 | tf_op jit(solution)/shard_map/pallas_call | solution.py:116
  90.0 1.0 slice_reduce_fusion.1
  91.1 0.3 pad_maximum_fusion
  91.5 34.9 %all_to_all.30 = bf16[64,16,960]{2,1,0:T(8,128)(2,1)S(1)} all-to-all(bf16[64,16,960]{2,1,0:T(8,128)(2,1)S(1)} %pad_maximum_fusion), channel_id=1, replica_groups={{0,2,4,6,8,10,12,14,16,18,20,22,24,26,28,30,32,34,36,38,40,42,44,46,48,..., dimensions={0} | all-to-all | bytes 3932160 | tf_op jit(solution)/shard_map/all_to_all | solution.py:431
  126.3 0.1 slice_reduce_fusion
  126.4 1.2 copy-done.12
  127.6 10.3 %shard_map.113 = (bf16[512,2048]{1,0:T(8,128)(2,1)S(1)}, bf16[64,2048]{1,0:T(8,128)(2,1)S(1)}, bf16[16,128]{1,0:T(8,128)(2,1)S(1)}, bf16[512,1024]{1,0:T(8,128)(2,1)S(1)}) custom-call(bf16[128,2048]{1,0:T(8,128)(2,1)S(1)} %get-tuple-element.21.qk_ref, bf16[704,2048]{1,0:T(8,128)(2,1)} %get-tuple-element.22.feat_ref, ...), custom_call_target="tpu_custom_call" | custom-call | flops 3623878656 | bytes 15544320 | tf_op jit(solution)/shard_map/pallas_call | solution.py:116
  138.0 1.3 copy-done
  139.3 1.1 bitcast_dynamic-update-slice_fusion
  140.4 0.7 broadcast_dynamic-update-slice_fusion.3
  141.1 0.7 broadcast_dynamic-update-slice_fusion.2
  141.7 0.7 broadcast_dynamic-update-slice_fusion.1
  142.5 0.7 broadcast_dynamic-update-slice_fusion
  143.1 8.2 %all-to-all-start.4 = ((bf16[64,8,1536]{2,1,0:T(8,128)(2,1)}), bf16[64,8,1536]{2,1,0:T(8,128)(2,1)}, u32[]{:S(2)}, u32[]{:S(2)}) async-start(bf16[64,8,1536]{2,1,0:T(8,128)(2,1)} %broadcast_dynamic-update-slice_fusion), calls=%async_computation.4 | async-start | bytes 3145728 | tf_op jit(solution)/shard_map/all_to_all | solution.py:431
  151.3 1.6 copy-done.1
  152.9 2.6 %shard_map.114 = bf16[1024,1024]{1,0:T(8,128)(2,1)} custom-call(bf16[512,2048]{1,0:T(8,128)(2,1)S(1)} %copy-done.1, bf16[512,1024]{1,0:T(8,128)(2,1)S(1)} %bitcast.37), custom_call_target="tpu_custom_call" | custom-call | flops 1073741824 | bytes 5242880 | tf_op jit(solution)/shard_map/pallas_call | solution.py:116
  155.5 2.7 %collective-permute-start.3 = (bf16[1024,1024]{1,0:T(8,128)(2,1)}, bf16[1024,1024]{1,0:T(8,128)(2,1)}, u32[]{:S(2)}, u32[]{:S(2)}) collective-permute-start(bf16[1024,1024]{1,0:T(8,128)(2,1)} %shard_map.114), channel_id=1, source_target_pairs={{0,1},{1,0},{2,3},{3,2},{4,5},{5,4},{6,7},{7,6},{8,9},{9,8},{10,11... | collective-permute-start | bytes 6291464 | tf_op jit(solution)/shard_map/ppermute | solution.py:428
  158.2 0.3 convert_reduce_fusion
  158.4 13.1 %all-to-all-done.4 = bf16[64,8,1536]{2,1,0:T(8,128)(2,1)} async-done(((bf16[64,8,1536]{2,1,0:T(8,128)(2,1)}), bf16[64,8,1536]{2,1,0:T(8,128)(2,1)}, u32[]{:S(2)}, u32[]{:S(2)}) %all-to-all-start.4) | async-done | bytes 1572896 | tf_op jit(solution)/shard_map/all_to_all | solution.py:431
  171.6 1.3 fusion.12
  173.0 0.1 fusion.7
  173.1 0.2 fusion.6
  173.3 0.1 convert_reduce_fusion.3.ngrad_ref
  173.4 1.6 copy-done.7
  175.0 1.0 copy-done.11
  176.1 6.1 %shard_map.116 = (bf16[64,2048]{1,0:T(8,128)(2,1)S(1)}, bf16[1024,128]{1,0:T(8,128)(2,1)}) custom-call(bf16[128,2048]{1,0:T(8,128)(2,1)S(1)} %copy-done.11, bf16[2048,512]{1,0:T(8,128)(2,1)S(1)} %copy-done.7, bf16[1024,128]{1,0:T(8,128)(2,1)S(1)} %bitcast.39, f32[16,128]{1,0:T(8,128)S(1)} %convert_reduce_fusion.3.ngrad_ref, ...), custom_call_target="tpu_custom_call" | custom-call | flops 905969664 | bytes 7872512 | tf_op jit(solution)/shard_map/pallas_call | solution.py:116
  182.1 4.6 %shard_map.117 = bf16[1024,1024]{1,0:T(8,128)(2,1)} custom-call(bf16[64,2048]{1,0:T(8,128)(2,1)S(1)} %get-tuple-element.30.qgrad_ref, bf16[64,2048]{1,0:T(8,128)(2,1)S(1)} %get-tuple-element.34.kgrad_ref, bf16[704,2048]{1,0:T(8,128)(2,1)} %get-tuple-element.28.rows_ref.feat_ref, bf16[1024,128]{1,0:T(8,128)(2,1)S(1)} %bitcast.40, bf16[1024,640]{1,0:T(8,128)(2,1)S(1)} %bitcast.34), custom_call_target="tpu_custom_call" | custom-call | flops 1526726656 | bytes 7077888 | tf_op jit(solution)/shard_map/pallas_call | solution.py:116
  186.8 4.6 %collective-permute-start.4 = (bf16[1024,1024]{1,0:T(8,128)(2,1)}, bf16[1024,1024]{1,0:T(8,128)(2,1)}, u32[]{:S(2)}, u32[]{:S(2)}) collective-permute-start(bf16[1024,1024]{1,0:T(8,128)(2,1)} %shard_map.117), channel_id=1, source_target_pairs={{0,1},{1,0},{2,3},{3,2},{4,5},{5,4},{6,7},{7,6},{8,9},{9,8},{10,11... | collective-permute-start | bytes 6291464 | tf_op jit(solution)/shard_map/ppermute | solution.py:428
  191.4 0.2 fusion.5
  191.6 0.2 fusion.4
  191.8 0.1 collective-permute-start.5
  191.9 1.4 convert_reduce_fusion.1
  193.3 2.6 %collective-permute-start.6 = (f32[8,1024]{1,0:T(8,128)S(1)}, f32[8,1024]{1,0:T(8,128)S(1)}, u32[]{:S(2)}, u32[]{:S(2)}) collective-permute-start(f32[8,1024]{1,0:T(8,128)S(1)} %convert_reduce_fusion.1), channel_id=1, source_target_pairs={{0,0},{1,64},{2,1},{3,65},{4,2},{5,66},{6,3},{7,67},{8,4},{9,68},{... | collective-permute-start | bytes 98312 | tf_op jit(solution)/shard_map/ppermute | solution.py:488
  195.9 7.1 %all-to-all-start.5 = ((bf16[128,8,128]{2,1,0:T(8,128)(2,1)}), bf16[128,8,128]{2,1,0:T(8,128)(2,1)S(1)}, u32[]{:S(2)}, u32[]{:S(2)}) async-start(bf16[128,8,128]{2,1,0:T(8,128)(2,1)} %bitcast.11), calls=%async_computation.5 | async-start | bytes 524288 | tf_op jit(solution)/shard_map/all_to_all | solution.py:494
  203.1 0.6 maximum_multiply_fusion
  203.7 0.6 broadcast_multiply_fusion
  204.3 10.1 %all-to-all-done.5 = bf16[128,8,128]{2,1,0:T(8,128)(2,1)S(1)} async-done(((bf16[128,8,128]{2,1,0:T(8,128)(2,1)}), bf16[128,8,128]{2,1,0:T(8,128)(2,1)S(1)}, u32[]{:S(2)}, u32[]{:S(2)}) %all-to-all-start.5) | async-done | bytes 262176 | tf_op jit(solution)/shard_map/all_to_all | solution.py:494
  214.6 0.7 pad_maximum_fusion.6
  215.3 0.7 pad_maximum_fusion.5
  215.9 1.6 copy-done.2
  217.5 3.7 %shard_map.115 = bf16[1024,1024]{1,0:T(8,128)(2,1)} custom-call(bf16[512,2048]{1,0:T(8,128)(2,1)S(1)} %copy-done.2, bf16[512,1024]{1,0:T(8,128)(2,1)S(1)} %bitcast.38, bf16[1024,1024]{1,0:T(8,128)(2,1)} %collective-permute-done.3.refs_0_), custom_call_target="tpu_custom_call" | custom-call | flops 1073741824 | bytes 7340032 | tf_op jit(solution)/shard_map/pallas_call | solution.py:116
  221.3 5.0 %shard_map.118 = bf16[1024,1024]{1,0:T(8,128)(2,1)} custom-call(bf16[64,2048]{1,0:T(8,128)(2,1)S(1)} %get-tuple-element.30.qgrad_ref, bf16[64,2048]{1,0:T(8,128)(2,1)S(1)} %get-tuple-element.34.kgrad_ref, bf16[704,2048]{1,0:T(8,128)(2,1)} %get-tuple-element.28.rows_ref.feat_ref, bf16[1024,128]{1,0:T(8,128)(2,1)S(1)} %bitcast.41, ...), custom_call_target="tpu_custom_call" | custom-call | flops 1526726656 | bytes 9175040 | tf_op jit(solution)/shard_map/pallas_call | solution.py:116
  (43 shorter events, 0.6 us)
Async XLA Ops:
  0.6 16.5 %copy-start.14 = (bf16[8,1024]{1,0:T(8,128)(2,1)S(1)}, bf16[8,1024]{1,0:T(8,128)(2,1)}, u32[]{:S(2)}) copy-start(bf16[8,1024]{1,0:T(8,128)(2,1)} %param.10) | copy-start | bytes 49156
  0.6 43.3 %collective-permute-start = (bf16[1024,1024]{1,0:T(8,128)(2,1)}, bf16[1024,1024]{1,0:T(8,128)(2,1)}, u32[]{:S(2)}, u32[]{:S(2)}) collective-permute-start(bf16[1024,1024]{1,0:T(8,128)(2,1)} %own_ref.9), channel_id=1, source_target_pairs={{0,1},{1,0},{2,3},{3,2},{4,5},{5,4},{6,7},{7,6},{8,9},{9,8},{10,11... | collective-permute-start | bytes 6291464 | tf_op jit(solution)/shard_map/ppermute | solution.py:428
  5.8 32.2 %all-to-all-start = ((bf16[128,8,640]{2,1,0:T(8,128)(2,1)}), bf16[128,8,640]{2,1,0:T(8,128)(2,1)S(1)}, u32[]{:S(2)}, u32[]{:S(2)}) async-start(bf16[128,8,640]{2,1,0:T(8,128)(2,1)} %bitcast.2), calls=%async_computation | async-start | bytes 2621440 | tf_op jit(solution)/shard_map/all_to_all | solution.py:460
  16.0 50.4 %collective-permute-start.1 = (bf16[1024,1024]{1,0:T(8,128)(2,1)}, bf16[1024,1024]{1,0:T(8,128)(2,1)}, u32[]{:S(2)}, u32[]{:S(2)}) collective-permute-start(bf16[1024,1024]{1,0:T(8,128)(2,1)} %own_ref.8), channel_id=1, source_target_pairs={{0,1},{1,0},{2,3},{3,2},{4,5},{5,4},{6,7},{7,6},{8,9},{9,8},{10,11... | collective-permute-start | bytes 6291464 | tf_op jit(solution)/shard_map/ppermute | solution.py:428
  17.1 12.5 %collective-permute-start.2 = (bf16[8,1024]{1,0:T(8,128)(2,1)S(1)}, bf16[8,1024]{1,0:T(8,128)(2,1)S(1)}, u32[]{:S(2)}, u32[]{:S(2)}) collective-permute-start(bf16[8,1024]{1,0:T(8,128)(2,1)S(1)} %copy-done.14), channel_id=1, source_target_pairs={{0,0},{64,1},{1,2},{65,3},{2,4},{66,5},{3,6},{67,7},{4,8},{68,9},{... | collective-permute-start | bytes 49160 | tf_op jit(solution)/shard_map/ppermute | solution.py:462
  39.0 21.8 %all-to-all-start.1 = ((bf16[64,8,1024]{2,1,0:T(8,128)(2,1)}), bf16[64,8,1024]{2,1,0:T(8,128)(2,1)S(1)}, u32[]{:S(2)}, u32[]{:S(2)}) async-start(bf16[64,8,1024]{2,1,0:T(8,128)(2,1)} %broadcast_in_dim.23), calls=%async_computation.1 | async-start | bytes 2097152 | tf_op jit(solution)/shard_map/all_to_all | solution.py:431
  52.4 1.4 copy-start.6
  53.8 73.9 %copy-start.10 = (bf16[128,2048]{1,0:T(8,128)(2,1)}, bf16[128,2048]{1,0:T(8,128)(2,1)S(1)}, u32[]{:S(2)}) copy-start(bf16[128,2048]{1,0:T(8,128)(2,1)S(1)} %get-tuple-element.21.qk_ref) | copy-start | bytes 1572868
  60.8 20.4 %all-to-all-start.2 = ((bf16[64,32,128]{2,1,0:T(8,128)(2,1)}), bf16[64,32,128]{2,1,0:T(8,128)(2,1)}, u32[]{:S(2)}, u32[]{:S(2)}) async-start(bf16[64,32,128]{2,1,0:T(8,128)(2,1)} %pad_maximum_fusion.1), calls=%async_computation.2 | async-start | bytes 1048576 | tf_op jit(solution)/shard_map/all_to_all | solution.py:431
  66.3 7.3 %copy-start.4 = (bf16[1024,1024]{1,0:T(8,128)(2,1)S(1)}, bf16[1024,1024]{1,0:T(8,128)(2,1)}, u32[]{:S(2)}) copy-start(bf16[1024,1024]{1,0:T(8,128)(2,1)} %own_ref.9) | copy-start | bytes 6291460
  80.1 1.1 copy-start.8
  82.2 1.8 copy-start.3
  84.0 7.0 %copy-start.9 = (bf16[1024,704]{1,0:T(8,128)(2,1)S(1)}, bf16[1024,704]{1,0:T(8,128)(2,1)}, u32[]{:S(2)}) copy-start(bf16[1024,704]{1,0:T(8,128)(2,1)} %copy-done.8) | copy-start | bytes 4325380
  126.3 1.3 copy-start.12
  138.0 1.3 copy-start
  143.1 28.4 %all-to-all-start.4 = ((bf16[64,8,1536]{2,1,0:T(8,128)(2,1)}), bf16[64,8,1536]{2,1,0:T(8,128)(2,1)}, u32[]{:S(2)}, u32[]{:S(2)}) async-start(bf16[64,8,1536]{2,1,0:T(8,128)(2,1)} %broadcast_dynamic-update-slice_fusion), calls=%async_computation.4 | async-start | bytes 3145728 | tf_op jit(solution)/shard_map/all_to_all | solution.py:431
  151.3 1.6 copy-start.1
  152.9 5.2 %copy-start.13 = (bf16[64,16,960]{2,1,0:T(8,128)(2,1)S(1)}, bf16[64,16,960]{2,1,0:T(8,128)(2,1)}, u32[]{:S(2)}) copy-start(bf16[64,16,960]{2,1,0:T(8,128)(2,1)} %copy-done.12) | copy-start | bytes 5898244
  155.5 60.5 %collective-permute-start.3 = (bf16[1024,1024]{1,0:T(8,128)(2,1)}, bf16[1024,1024]{1,0:T(8,128)(2,1)}, u32[]{:S(2)}, u32[]{:S(2)}) collective-permute-start(bf16[1024,1024]{1,0:T(8,128)(2,1)} %shard_map.114), channel_id=1, source_target_pairs={{0,1},{1,0},{2,3},{3,2},{4,5},{5,4},{6,7},{7,6},{8,9},{9,8},{10,11... | collective-permute-start | bytes 6291464 | tf_op jit(solution)/shard_map/ppermute | solution.py:428
  171.6 1.9 copy-start.5
  173.4 1.6 copy-start.7
  175.0 1.0 copy-start.11
  186.8 34.5 %collective-permute-start.4 = (bf16[1024,1024]{1,0:T(8,128)(2,1)}, bf16[1024,1024]{1,0:T(8,128)(2,1)}, u32[]{:S(2)}, u32[]{:S(2)}) collective-permute-start(bf16[1024,1024]{1,0:T(8,128)(2,1)} %shard_map.117), channel_id=1, source_target_pairs={{0,1},{1,0},{2,3},{3,2},{4,5},{5,4},{6,7},{7,6},{8,9},{9,8},{10,11... | collective-permute-start | bytes 6291464 | tf_op jit(solution)/shard_map/ppermute | solution.py:428
  191.8 11.3 %collective-permute-start.5 = (f32[8,512]{1,0:T(8,128)S(1)}, f32[8,512]{1,0:T(8,128)S(1)}, u32[]{:S(2)}, u32[]{:S(2)}) collective-permute-start(f32[8,512]{1,0:T(8,128)S(1)} %constant_dynamic-slice_fusion), channel_id=1, source_target_pairs={{0,1},{1,0},{2,3},{3,2},{4,5},{5,4},{6,7},{7,6},{8,9},{9,8},{10,11... | collective-permute-start | bytes 49160 | tf_op jit(solution)/shard_map/ppermute | solution.py:428
  193.3 10.4 %collective-permute-start.6 = (f32[8,1024]{1,0:T(8,128)S(1)}, f32[8,1024]{1,0:T(8,128)S(1)}, u32[]{:S(2)}, u32[]{:S(2)}) collective-permute-start(f32[8,1024]{1,0:T(8,128)S(1)} %convert_reduce_fusion.1), channel_id=1, source_target_pairs={{0,0},{1,64},{2,1},{3,65},{4,2},{5,66},{6,3},{7,67},{8,4},{9,68},{... | collective-permute-start | bytes 98312 | tf_op jit(solution)/shard_map/ppermute | solution.py:488
  195.9 18.5 %all-to-all-start.5 = ((bf16[128,8,128]{2,1,0:T(8,128)(2,1)}), bf16[128,8,128]{2,1,0:T(8,128)(2,1)S(1)}, u32[]{:S(2)}, u32[]{:S(2)}) async-start(bf16[128,8,128]{2,1,0:T(8,128)(2,1)} %bitcast.11), calls=%async_computation.5 | async-start | bytes 524288 | tf_op jit(solution)/shard_map/all_to_all | solution.py:494
  215.9 1.6 copy-start.2

commit v4 on v3

v4 whole, which is shorter than its diff:
```python
import jax
import jax.numpy as jnp
from jax import lax
from jax.experimental import pallas as pl
from jax.experimental.pallas import tpu as pltpu
from jax.sharding import PartitionSpec as P

H = 8
DK = 16
DV = 128
BANDS = DK // 2 + 1
FPAD = (BANDS + 2) * DK
SPAD = 256
AXES = ("ctx", "seq")
VMEM = 60 * 2**20
BF = jnp.bfloat16
F32 = jnp.float32
SQUARE = (2.0 * DK) ** (-0.5)
LINEAR = DK ** (-0.25)


def dot(a, b, contract):
    return lax.dot_general(a, b, ((contract[:1], contract[1:]), ((), ())), preferred_element_type=F32)


def band_weight(shape, dim):
    row = lax.broadcasted_iota(jnp.int32, shape, dim)
    twice = (row >= DK) & (row < (BANDS - 1) * DK)
    return jnp.where(twice, 2.0, 1.0).astype(F32)


def shifted(u, d):
    return pltpu.roll(u, DK - d, 0) if d else u


def features(u):
    bands = [u * shifted(u, d) * SQUARE for d in range(BANDS)]
    first = lax.broadcasted_iota(jnp.int32, u.shape, 0) == 0
    return jnp.concatenate(bands + [u * LINEAR, jnp.where(first, 1.0, 0.0)], axis=0).astype(BF)


def features_back(u, fgrad):
    def band(d):
        return fgrad[d * DK : (d + 1) * DK]

    total = band(0) * u + band(BANDS - 1) * shifted(u, BANDS - 1)
    for d in range(1, BANDS - 1):
        total = total + band(d) * shifted(u, d) + shifted(band(d) * u, DK - d)
    return total * (2.0 * SQUARE) + band(BANDS) * LINEAR


def in_parts(row):
    high = row.astype(BF).astype(F32)
    rest = row - high
    mid = rest.astype(BF).astype(F32)
    at = lax.broadcasted_iota(jnp.int32, (16, row.shape[1]), 0)
    low = jnp.where(at == 2, rest - mid, 0.0)
    return jnp.where(at == 0, high, jnp.where(at == 1, mid, low)).astype(BF)


def rows_of(array, head, size):
    return array[head * size : (head + 1) * size]


def head_row(rows, head):
    first, second = rows[4 * head : 4 * head + 2, :], rows[4 * head + 2 : 4 * head + 4, :]
    both = first + second
    return jnp.concatenate([both[:1], both[1:]], axis=1)


def split_rows(per_head):
    found = []
    for row in per_head:
        high = row.astype(BF).astype(F32)
        for part in (high, row - high):
            found += [part[:, :128], part[:, 128:]]
    found += [jnp.zeros((1, 128), F32)] * (16 - len(found))
    return jnp.concatenate(found, axis=0).astype(BF)


def column(row):
    return jnp.broadcast_to(row, (8, row.shape[1])).T[:FPAD, :1]


def add_chips(ref, rows):
    total = ref[:rows, :].astype(F32)
    for at in range(rows, ref.shape[0], rows):
        total = total + ref[at : at + rows, :].astype(F32)
    return total


def lane_sums(x):
    return sum(x[:, i : i + 128] for i in range(0, x.shape[1], 128))


def weighted_turned(state_ref, head):
    whole = state_ref[head * SPAD : (head + 1) * SPAD, :].astype(F32)
    return (whole * band_weight((SPAD, DV), 0)).T.astype(BF)


def call(body, count, ins, kinds, outs, out_kinds, scratch, flops):
    block = min(512, count, count // 2 if "pair" in kinds else count)
    steps = count // block
    in_specs, args = [], []
    for x, kind in zip(ins, kinds):
        if kind is None:
            in_specs.append(pl.BlockSpec(x.shape, lambda i: (0, 0)))
        elif kind == 0:
            in_specs.append(pl.BlockSpec((block, x.shape[1]), lambda i: (i, 0)))
        elif kind == 1:
            in_specs.append(pl.BlockSpec((x.shape[0], block), lambda i: (0, i)))
        elif kind == "scalar":
            in_specs.append(pl.BlockSpec(memory_space=pltpu.SMEM))
        elif kind == "any":
            in_specs.append(pl.BlockSpec(memory_space=pl.ANY))
        elif isinstance(kind, tuple):
            width, at = kind
            in_specs.append(pl.BlockSpec((x.shape[0], width), lambda i, at=at: (0, at)))
        elif kind == "pair1":
            half = steps // 2
            in_specs.append(pl.BlockSpec((x[0].shape[0], block), lambda i: (0, jnp.minimum(i, half - 1))))
            in_specs.append(pl.BlockSpec((x[0].shape[0], block), lambda i: (0, jnp.maximum(i - half, 0))))
        else:
            half = steps // 2
            in_specs.append(pl.BlockSpec((block, x[0].shape[1]), lambda i: (jnp.minimum(i, half - 1), 0)))
            in_specs.append(pl.BlockSpec((block, x[0].shape[1]), lambda i: (jnp.maximum(i - half, 0), 0)))
        args += list(x) if kind in ("pair", "pair1") else [x]
    out_specs = []
    for x, kind in zip(outs, out_kinds):
        half = steps // 2
        if kind == "first":
            out_specs.append(pl.BlockSpec((x.shape[0], block), lambda i: (0, jnp.minimum(i, half - 1))))
            continue
        if kind == "second":
            out_specs.append(pl.BlockSpec((x.shape[0], block), lambda i: (0, jnp.maximum(i - half, 0))))
            continue
        if kind is None:
            out_specs.append(pl.BlockSpec(x.shape, lambda i: (0, 0)))
        elif kind == 0:
            out_specs.append(pl.BlockSpec((block, x.shape[1]), lambda i: (i, 0)))
        else:
            out_specs.append(pl.BlockSpec((x.shape[0], block), lambda i: (0, i)))
    nbytes = sum(x.size * x.dtype.itemsize for x in args + list(outs))
    return pl.pallas_call(
        body,
        grid=(steps,),
        in_specs=in_specs,
        out_specs=out_specs,
        out_shape=outs,
        scratch_shapes=scratch,
        compiler_params=pltpu.CompilerParams(dimension_semantics=("arbitrary",), vmem_limit_bytes=VMEM),
        cost_estimate=pl.CostEstimate(flops=flops, bytes_accessed=nbytes, transcendentals=0),
    )(*args)


def either(first_ref, second_ref):
    return jnp.where(pl.program_id(0) < pl.num_programs(0) // 2, first_ref[...], second_ref[...])


def store_half(first_ref, second_ref, value):
    @pl.when(pl.program_id(0) < pl.num_programs(0) // 2)
    def _():
        first_ref[...] = value

    @pl.when(pl.program_id(0) >= pl.num_programs(0) // 2)
    def _():
        second_ref[...] = value


def shape(dims, dtype):
    return jax.ShapeDtypeStruct(dims, dtype)


def clear_at_first(*refs):
    @pl.when(pl.program_id(0) == 0)
    def _():
        for ref in refs:
            ref[...] = jnp.zeros(ref.shape, ref.dtype)


def at_first(fn):
    pl.when(pl.program_id(0) == 0)(fn)


def at_last(fn):
    pl.when(pl.program_id(0) == pl.num_programs(0) - 1)(fn)


def weights_phase(w_query, w_key, w_value, w_out, chips, heads):
    qk, cols, half = heads * DK, heads * DV, w_out.shape[1] // 2

    def body(q_ref, k_ref, v_ref, o_ref, out_ref):
        query, key, value, rest = (ref[...].astype(F32) for ref in (q_ref, k_ref, v_ref, o_ref))
        halves = [
            jnp.concatenate(
                [
                    query[:, c * qk : (c + 1) * qk],
                    key[:, c * qk : (c + 1) * qk],
                    value[:, c * cols : (c + 1) * cols],
                    rest[:, c * half : (c + 1) * half],
                ],
                axis=1,
            )
            for c in range(2)
        ]
        pair = jnp.concatenate(halves, axis=0).astype(BF)
        for p in range(chips):
            out_ref[p * pair.shape[0] : (p + 1) * pair.shape[0], :] = pair

    rows = w_query.shape[0]
    return pl.pallas_call(
        body,
        out_shape=shape((2 * chips * rows, 2 * qk + cols + half), BF),
        compiler_params=pltpu.CompilerParams(vmem_limit_bytes=VMEM),
        cost_estimate=pl.CostEstimate(flops=0, bytes_accessed=2 * 2 * chips * rows * (2 * qk + cols + half), transcendentals=0),
    )(w_query, w_key, w_value, w_out)


def keys_phase(tokens, w_qkv, chips, heads):
    qk = heads * DK

    def body(own_ref, other_ref, w_ref, qk_ref, value_ref, feat_ref, feat_other_ref, sent_ref, state_acc, norm_acc):
        clear_at_first(state_acc, norm_acc)
        joined = dot(either(own_ref, other_ref), w_ref[:, : 2 * qk + heads * DV], (1, 0))
        qk_t = joined[:, : 2 * qk].T.astype(BF)
        value = joined[:, 2 * qk :].astype(BF)
        qk_ref[...] = qk_t
        value_ref[...] = value
        keys = qk_t.astype(F32)[qk:]
        found = []
        for head in range(heads):
            feat = features(rows_of(keys, head, DK))
            found.append(feat)
            state_acc[head, :FPAD, :] += dot(feat, value[:, head * DV : (head + 1) * DV], (1, 0))
            norm_acc[head, :FPAD, :] += lane_sums(feat.astype(F32))
        store_half(feat_ref, feat_other_ref, jnp.concatenate(found, axis=0))

        @at_last
        def _():
            norm = split_rows([jnp.sum(norm_acc[head], axis=1)[None] for head in range(heads)])
            state = state_acc[...].reshape(heads * SPAD, DV).astype(BF)
            part = heads * SPAD // chips
            for p in range(chips):
                sent_ref[2 * part * p : 2 * part * p + part, :] = state[part * p : part * (p + 1)]
                sent_ref[2 * part * p + part : 2 * part * (p + 1), :] = norm

    count = 2 * tokens[0].shape[0]
    return call(
        body,
        count,
        (tokens, w_qkv),
        ("pair", None),
        (
            shape((2 * qk, count), BF),
            shape((count, heads * DV), BF),
            shape((heads * FPAD, count // 2), BF),
            shape((heads * FPAD, count // 2), BF),
            shape((2 * heads * SPAD, DV), BF),
        ),
        (1, 0, "first", "second", None),
        [pltpu.VMEM((heads, SPAD, DV), F32), pltpu.VMEM((heads, SPAD, 128), F32)],
        2 * count * heads * (w_qkv.shape[0] * (2 * DK + DV) + FPAD * DV * 2),
    )


def upstream_phase(core, qk_t, cot, weights, other_weights, heads):
    count, width = qk_t.shape[1], cot[0].shape[1]
    rows, half = heads * DV, width // 2
    joined = 2 * heads * DK + heads * DV

    def body(core_ref, qk_ref, own_ref, other_ref, mine_ref, theirs_ref, up_ref, feat_ref, w_ref):
        at = core_ref[0, 0]

        @at_first
        def _():
            mine, theirs = mine_ref[:, joined:], theirs_ref[:, joined:]
            w_ref[:, :half] = jnp.where(at == 0, mine, theirs)
            w_ref[:, half:] = jnp.where(at == 0, theirs, mine)

        here = w_ref[pl.ds(pl.multiple_of(at * rows, rows), rows), :]
        up_ref[...] = dot(here, either(own_ref, other_ref), (1, 1))
        query = qk_ref[...].astype(F32)
        for head in range(heads):
            feat_ref[head * FPAD : (head + 1) * FPAD, :] = features(rows_of(query, head, DK))

    return call(
        body,
        count,
        (core, qk_t, cot, weights, other_weights),
        ("scalar", 1, "pair", None, None),
        (shape((rows, count), F32), shape((heads * FPAD, count), BF), shape((2 * rows, width), BF)),
        (1, 1, None),
        [],
        2 * count * rows * width,
    )


def product_phase(rows_t, slabs, after, parts):
    rows, count = rows_t[0].shape[0], 2 * rows_t[0].shape[1]
    size = rows // parts
    width = slabs[0].shape[1]

    def body(rows_ref, rows_other_ref, own_ref, other_ref, after_ref, out_ref, acc):
        clear_at_first(acc)
        acc[...] += dot(either(rows_ref, rows_other_ref), either(own_ref, other_ref), (1, 0))

        @at_last
        def _():
            for part in range(parts):
                out_ref[part * width : (part + 1) * width, :] = acc[part * size : (part + 1) * size, :].T.astype(BF)

    return call(
        body,
        count,
        (rows_t, slabs, after),
        ("pair1", "pair", "any"),
        (shape((parts * width, size), BF),),
        (None,),
        [pltpu.VMEM((rows, width), F32)],
        2 * count * rows * width,
    )[0]


def query_phase(feats, up_t, first, chips, heads):
    count = up_t.shape[1]
    part = heads * SPAD // chips

    def body(feat_ref, up_ref, first_ref, scale_ref, norm_ref, sent_ref, acc, state_own):
        clear_at_first(acc)

        @at_first
        def _():
            total = add_chips(first_ref, 2 * part)
            state_own[...] = total[:part].astype(BF)
            norm_ref[...] = total[part:]

        at = lax.broadcasted_iota(jnp.int32, scale_ref.shape, 0)
        scales = jnp.zeros(scale_ref.shape, F32)
        for head in range(heads):
            feat = feat_ref[head * FPAD : (head + 1) * FPAD, :]
            parts = in_parts(head_row(norm_ref[...], head) * band_weight((1, SPAD), 1))[:, :FPAD]
            scale = 1.0 / jnp.sum(dot(parts, feat, (1, 0)), axis=0, keepdims=True)
            grad_num = (up_ref[head * DV : (head + 1) * DV, :] * scale).astype(BF)
            acc[head, :FPAD, :] += dot(feat, grad_num, (1, 1))
            scales = jnp.where(at == head, scale, scales)
        scale_ref[...] = scales

        @at_last
        def _():
            sent_ref[:, :DV] = acc[...].reshape(heads * SPAD, DV).astype(BF)
            for p in range(chips):
                sent_ref[p * part : (p + 1) * part, DV:] = state_own[...]

    return call(
        body,
        count,
        (feats, up_t, first),
        (1, 1, None),
        (shape((8, count), F32), shape((16, 128), F32), shape((heads * SPAD, 2 * DV), BF)),
        (1, None, None),
        [pltpu.VMEM((heads, SPAD, DV), F32), pltpu.VMEM((part, DV), BF)],
        2 * count * heads * FPAD * DV * 2,
    )


def attend_phase(feats, scales, up_t, second, cot, moments, chips, heads):
    count = up_t.shape[1]
    width = cot[0].shape[1]
    quarter = width // 4

    def body(
        feat_ref, scale_ref, up_ref, state_ref, sgrad_ref, own_ref, other_ref, moment_ref,
        att_ref, att_other_ref, den_ref, out_ref, sent_ref, turned, acc, out_acc,
    ):
        clear_at_first(acc, out_acc)

        @at_first
        def _():
            for head in range(heads):
                turned[head] = weighted_turned(state_ref, head)

        at = lax.broadcasted_iota(jnp.int32, den_ref.shape, 0)
        dens = jnp.zeros(den_ref.shape, F32)
        found = []
        for head in range(heads):
            feat = feat_ref[head * FPAD : (head + 1) * FPAD, :]
            scale = scale_ref[head : head + 1, :]
            att = dot(turned[head, :, :FPAD], feat, (1, 0)) * scale
            grad_num = up_ref[head * DV : (head + 1) * DV, :] * scale
            grad_den = -jnp.sum(grad_num * att, axis=0, keepdims=True)
            acc[head, :FPAD, :] += lane_sums(feat.astype(F32) * grad_den)
            found.append(att.astype(BF))
            dens = jnp.where(at == head, grad_den, dens)
        den_ref[...] = dens
        attended = jnp.concatenate(found, axis=0)
        store_half(att_ref, att_other_ref, attended)
        out_acc[...] += dot(attended, either(own_ref, other_ref), (1, 0))

        @at_last
        def _():
            ngrad = split_rows([jnp.sum(acc[head], axis=1)[None] for head in range(heads)])
            sgrad_own = add_chips(sgrad_ref, ngrad.shape[0]).astype(BF)
            both = jnp.concatenate([sgrad_own, ngrad], axis=1)
            for p in range(chips):
                sent_ref[p * both.shape[0] : (p + 1) * both.shape[0], :] = both
            for k in range(4):
                rows = slice(k * heads * DV, (k + 1) * heads * DV)
                out_ref[rows, :quarter] = out_acc[:, k * quarter : (k + 1) * quarter].astype(BF)
                for j in range(2):
                    part = moment_ref[(2 * k + j) * heads * DV : (2 * k + j + 1) * heads * DV, :]
                    out_ref[rows, quarter + j * FPAD : quarter + (j + 1) * FPAD] = part

    return call(
        body,
        count,
        (feats, scales, up_t, second, second, cot, moments),
        (1, 1, 1, (DV, 1), (DV, 0), "pair", None),
        (
            shape((heads * DV, count // 2), BF),
            shape((heads * DV, count // 2), BF),
            shape((8, count), F32),
            shape((4 * heads * DV, quarter + 2 * FPAD), BF),
            shape(second.shape, BF),
        ),
        ("first", "second", 1, None, None),
        [
            pltpu.VMEM((heads, DV, SPAD), BF),
            pltpu.VMEM((heads, SPAD, 128), F32),
            pltpu.VMEM((heads * DV, width), F32),
        ],
        2 * count * (heads * FPAD * DV * 2 + heads * DV * width),
    )


def query_back_phase(qk_t, scales, dens, up_t, second, norm, heads):
    count = up_t.shape[1]

    def body(qk_ref, scale_ref, den_ref, up_ref, state_ref, norm_ref, qgrad_ref, qgrad_other_ref):
        query = qk_ref[...].astype(F32)
        found = []
        for head in range(heads):
            grad_num = (up_ref[head * DV : (head + 1) * DV, :] * scale_ref[head : head + 1, :]).astype(BF)
            fgrad = dot(state_ref[head * SPAD : head * SPAD + FPAD, :], grad_num, (1, 0))
            fgrad = fgrad + column(head_row(norm_ref[...], head)) * den_ref[head : head + 1, :]
            found.append(features_back(rows_of(query, head, DK), fgrad).astype(BF))
        store_half(qgrad_ref, qgrad_other_ref, jnp.concatenate(found, axis=0))

    return call(
        body,
        count,
        (qk_t, scales, dens, up_t, second, norm),
        (1, 1, 1, 1, (DV, 1), None),
        (shape((heads * DK, count // 2), BF), shape((heads * DK, count // 2), BF)),
        ("first", "second"),
        [],
        2 * count * heads * FPAD * DV,
    )


def key_phase(qk_t, value, third, qgrads, tokens, after, heads):
    count, qk = value.shape[0], heads * DK
    width = tokens[0].shape[1]

    def body(
        qk_ref, value_ref, sgrad_ref, rows_ref, qgrad_ref, qgrad_other_ref, own_ref, other_ref, after_ref,
        kgrad_ref, kgrad_other_ref, copy_ref, sent_ref, acc, ngrad_ref,
    ):
        clear_at_first(acc)

        @at_first
        def _():
            ngrad_ref[...] = add_chips(rows_ref, 16)
            copy_ref[...] = sgrad_ref[...]

        keys = qk_ref[...].astype(F32)[qk:]
        found = []
        for head in range(heads):
            fgrad = dot(
                sgrad_ref[head * SPAD : head * SPAD + FPAD, :],
                value_ref[:, head * DV : (head + 1) * DV],
                (1, 1),
            )
            fgrad = fgrad + column(head_row(ngrad_ref[...], head))
            found.append(features_back(rows_of(keys, head, DK), fgrad))
        kgrad = jnp.concatenate(found, axis=0).astype(BF)
        store_half(kgrad_ref, kgrad_other_ref, kgrad)
        both = jnp.concatenate([either(qgrad_ref, qgrad_other_ref), kgrad], axis=0)
        acc[...] += dot(both, either(own_ref, other_ref), (1, 0))

        @at_last
        def _():
            sent_ref[...] = acc[...].T.astype(BF)

    return call(
        body,
        count,
        (qk_t, value, third, third, qgrads, tokens, after),
        (1, 0, (DV, 0), (DV, 1), "pair1", "pair", "any"),
        (
            shape((qk, count // 2), BF),
            shape((qk, count // 2), BF),
            shape((third.shape[0], DV), BF),
            shape((width, 2 * qk), BF),
        ),
        ("first", "second", None, None),
        [pltpu.VMEM((2 * qk, width), F32), pltpu.VMEM((16, DV), F32)],
        2 * count * (heads * FPAD * DV + 2 * qk * width),
    )


def last_payload(core, wgrad, along_x):
    rows, cols = wgrad.shape
    half = along_x.shape[0]
    quarter = along_x.shape[1] - 2 * FPAD

    def body(core_ref, wgrad_ref, terms_ref, sent_ref):
        first = core_ref[0, 0] == 0
        sent_ref[:, :cols] = wgrad_ref[...]
        for j in range(2):
            here = slice(j * half, (j + 1) * half)
            sent_ref[here, cols : cols + FPAD] = terms_ref[:, quarter + j * FPAD : quarter + (j + 1) * FPAD]
            out = terms_ref[:, :quarter]
            sent_ref[here, cols + FPAD :] = jnp.where(first == (j == 0), out, jnp.zeros_like(out))

    vmem = pl.BlockSpec(memory_space=pltpu.VMEM)
    return pl.pallas_call(
        body,
        in_specs=[pl.BlockSpec(memory_space=pltpu.SMEM)] + [vmem] * 2,
        out_specs=vmem,
        out_shape=shape((rows, cols + FPAD + quarter), BF),
        compiler_params=pltpu.CompilerParams(vmem_limit_bytes=VMEM),
        cost_estimate=pl.CostEstimate(flops=0, bytes_accessed=4 * rows * cols, transcendentals=0),
    )(core, wgrad, along_x)


def outputs_phase(core, attended, qgrads, kgrads, feats, sgrads, weights, w_out, heads):
    count, width = attended[0].shape[1], w_out.shape[1]
    rows, joined = heads * DV, 2 * heads * DK + heads * DV

    def body(core_ref, *refs):
        atts, qs, ks, fs, ss, ws = (refs[2 * i : 2 * i + 2] for i in range(6))
        out_ref, mixed_ref, gtok_ref, turned = refs[12:]
        at = core_ref[0, 0]

        @at_first
        def _():
            for c in range(2):
                for head in range(heads):
                    turned[c, head] = weighted_turned(ss[c], head)

        mixed, gtok = 0.0, 0.0
        for c in range(2):
            first = pl.multiple_of((at if c == 0 else 1 - at) * rows, rows)
            mixed = mixed + dot(atts[c][...], out_ref[pl.ds(first, rows), :], (0, 0))
            parts = [qs[c][...], ks[c][...]]
            for head in range(heads):
                feat = fs[c][head * FPAD : (head + 1) * FPAD, :]
                parts.append(dot(turned[c, head, :, :FPAD], feat, (1, 0)).astype(BF))
            gtok = gtok + dot(jnp.concatenate(parts, axis=0), ws[c][:, :joined], (0, 1))
        mixed_ref[...] = mixed.astype(BF)
        gtok_ref[...] = gtok.astype(BF)

    return call(
        body,
        count,
        (core, *attended, *qgrads, *kgrads, *feats, *sgrads, *weights, w_out),
        ("scalar",) + (1,) * 8 + (None,) * 5,
        (shape((count, width), BF), shape((count, width), BF)),
        (0, 0),
        [pltpu.VMEM((2, heads, DV, SPAD), BF)],
        2 * count * 2 * (joined * width + rows * width + heads * FPAD * DV),
    )


def finish_phase(core, fourth, sgrads, after, heads, scale_factor):
    rows, qk, n = 8, heads * DK, fourth.shape[0] // 8
    quarter = fourth.shape[1] - 2 * qk - FPAD

    def body(core_ref, recv_ref, mine_ref, other_ref, *refs):
        query_ref, key_ref, value_ref, out_ref = refs[-4:]
        first = core_ref[0, 0] == 0
        wgrad = jnp.zeros((2 * rows, 2 * qk), F32)
        moment = [jnp.zeros((2 * rows, FPAD), F32) for _ in range(heads)]
        out = [jnp.zeros((2 * rows, quarter), F32) for _ in range(4)]
        for p in range(n // 2):
            both = recv_ref[2 * rows * p : 2 * rows * (p + 1), :].astype(F32)
            x = 2 * ((p // 8) % 2) + p % 2
            wgrad = wgrad + both[:, : 2 * qk]
            moment[x] = moment[x] + both[:, 2 * qk : 2 * qk + FPAD]
            out[x] = out[x] + both[:, 2 * qk + FPAD :]
        for x in range(4):
            out_ref[:, x * quarter : (x + 1) * quarter] = (out[x][:rows] + out[x][rows:]) * scale_factor
        wgrad = wgrad * scale_factor
        query_ref[...] = jnp.concatenate([wgrad[:rows, :qk], wgrad[rows:, :qk]], axis=1)
        key_ref[...] = jnp.concatenate([wgrad[:rows, qk:], wgrad[rows:, qk:]], axis=1)
        weight = band_weight((1, FPAD), 1) * scale_factor
        found = [[], []]
        for head in range(heads):
            whole = moment[head] * weight
            high = whole.astype(BF)
            parts = jnp.concatenate([high, (whole - high.astype(F32)).astype(BF)], axis=0)
            for which, ref in enumerate((mine_ref, other_ref)):
                both = dot(parts, ref[head * SPAD : head * SPAD + FPAD, :], (1, 0))
                both = both[: 2 * rows] + both[2 * rows :]
                low, up = both[:rows], both[rows:]
                found[which].append(jnp.where(first, low, up) if which == 0 else jnp.where(first, up, low))
        mine, other = (jnp.concatenate(part, axis=1) for part in found)
        value_ref[:, : heads * DV] = jnp.where(first, mine, other)
        value_ref[:, heads * DV :] = jnp.where(first, other, mine)

    vmem = pl.BlockSpec(memory_space=pltpu.VMEM)
    return pl.pallas_call(
        body,
        in_specs=[pl.BlockSpec(memory_space=pltpu.SMEM)] + [vmem] * 3 + [pl.BlockSpec(memory_space=pl.ANY)] * len(after),
        out_specs=[vmem] * 4,
        out_shape=(
            shape((rows, 2 * qk), F32),
            shape((rows, 2 * qk), F32),
            shape((rows, 2 * heads * DV), F32),
            shape((rows, 4 * quarter), F32),
        ),
        compiler_params=pltpu.CompilerParams(vmem_limit_bytes=VMEM),
        cost_estimate=pl.CostEstimate(flops=0, bytes_accessed=fourth.size * 2, transcendentals=0),
    )(core, fourth, *sgrads, *after)


def per_device(chips, tokens, w_query, w_key, w_value, w_out, cotangent):
    n = 2 * chips
    heads = H // 2
    own, width = tokens.shape
    qk = heads * DK
    core = lax.axis_index("seq") % 2
    core_at = core.astype(jnp.int32).reshape(1, 1)
    same_core = [[2 * p + c for p in range(chips)] for c in range(2)]
    swap = [(i, i ^ 1) for i in range(n)]
    scale_factor = (own * n) ** (-0.5)

    def exchange(x):
        return lax.ppermute(x, AXES, swap)

    def spread(x):
        return lax.all_to_all(x, AXES, 0, 0, axis_index_groups=same_core, tiled=True)

    def add_along_x(x):
        quarters = x.reshape((4, -1) + x.shape[1:])
        total = lax.dynamic_index_in_dim(quarters, me_x, 0, keepdims=False).astype(F32)
        for step in (1, 2, 3):
            moves = []
            for i in range(n):
                y, at, z, c = place(i)
                moves.append((i, device(y, (at + step) % 4, z, c)))
            there = lax.dynamic_index_in_dim(quarters, (me_x + step) % 4, 0, keepdims=False)
            total = total + lax.ppermute(there, AXES, moves).astype(F32)
        return total.astype(BF)

    def place(i):
        return (i // 32, 2 * (i // 16 % 2) + i // 2 % 2, i // 4 % 4, i % 2)

    def device(y, x, z, c):
        return (((y * 2 + x // 2) * 4 + z) * 2 + x % 2) * 2 + c

    def to_each(x):
        return x.reshape(chips, -1, x.shape[1])

    ctx, seq = lax.axis_index("ctx"), lax.axis_index("seq")
    me_x = 2 * (ctx // 4 % 2) + seq // 2
    along_x = [[device(y, x, z, c) for x in range(4)] for y in range(4) for z in range(4) for c in range(2)]

    to_send = weights_phase(w_query, w_key, w_value, w_out, chips, heads)
    weights = lax.all_to_all(to_send.reshape(n, -1, to_send.shape[1]), AXES, 0, 0, tiled=True)
    weights = weights.reshape(-1, to_send.shape[1])
    tok = (tokens, exchange(tokens))
    cot = (cotangent, exchange(cotangent))
    other_weights = exchange(weights)

    qk_t, value, key_feat, key_feat_sent, sent = keys_phase(tok, weights, chips, heads)
    first = spread(to_each(sent)).reshape(sent.shape)
    key_feats = (key_feat, exchange(key_feat_sent))

    up_t, query_feat, w_out_whole = upstream_phase(core_at, qk_t, cot, weights, other_weights, heads)
    scales, norm, sent = query_phase(query_feat, up_t, first, chips, heads)
    second = spread(to_each(sent)).reshape(sent.shape)
    moments = product_phase((key_feat, key_feat_sent), tok, sent, heads)

    attended, attended_sent, dens, terms, sent = attend_phase(
        query_feat, scales, up_t, second, cot, moments, chips, heads
    )
    third = spread(to_each(sent)).reshape(sent.shape)
    terms = add_along_x(terms)
    attendeds = (attended, exchange(attended_sent))
    qgrad, qgrad_sent = query_back_phase(qk_t, scales, dens, up_t, second, norm, heads)
    qgrads = (qgrad, exchange(qgrad_sent))

    kgrad, kgrad_sent, sgrad, wgrad = key_phase(qk_t, value, third, (qgrad, qgrad_sent), tok, terms, heads)
    sent = last_payload(core_at, wgrad, terms)
    fourth = lax.all_to_all(sent.reshape(n, -1, sent.shape[1]), AXES, 0, 0, tiled=True).reshape(sent.shape)
    kgrads, sgrads = (kgrad, exchange(kgrad_sent)), (sgrad, exchange(sgrad))
    mixed, grad_tokens = outputs_phase(
        core_at, attendeds, qgrads, kgrads, key_feats, sgrads, (weights, other_weights), w_out_whole, heads
    )
    grad_query, grad_key, grad_value, grad_out = finish_phase(
        core_at, fourth, sgrads, (grad_tokens, mixed), heads, scale_factor
    )
    return (mixed, grad_tokens, grad_query, grad_key, grad_value, grad_out)


def solution(mesh):
    chips = mesh.size // 2
    placed = P(AXES, None)
    return jax.shard_map(
        lambda *args: per_device(chips, *args),
        mesh=mesh,
        in_specs=(placed,) * 6,
        out_specs=(placed,) * 6,
        check_vma=False,
    )
```

time: 228 us -> 200 us (0.88)
  blocking collectives: 34.9 us -> 0 us
  Pallas kernels: 60.5 us -> 79.8 us
  local copies, waits for them, and re-layouts: 22.7 us -> 9.91 us
  waiting for transfers between devices: 47.6 us -> 58 us
  other arithmetic: 8.01 us -> 2.25 us
  starting transfers between devices: 51.1 us -> 48.1 us
    all_to_all x1 -> x0, blocking collectives: 34.9 us -> none  [spread(): lax.all_to_all(x, AXES, 0, 0, axis_index_groups=same_core, tiled=True)]
    all_to_all x2, waiting for transfers between devices: 18.4 us -> 38.6 us  [the longest x1 31.9 us: per_device(): lax.all_to_all(to_send.reshape(n, -1, to_send.shape[1]), AXES, 0, 0, tile...]
    pallas_call x10 -> x8, Pallas kernels: 60.5 us -> 72.5 us  [call(): pl.pallas_call(body, grid=(steps,), in_specs=in_specs, out_specs=out_spec...]
    unnamed x34 -> x22, local copies, waits for them, and re-layouts: 15.9 us -> 4.5 us
    all_to_all x3, waiting for transfers between devices: 19.3 us -> 8.01 us  [spread(): lax.all_to_all(x, AXES, 0, 0, axis_index_groups=same_core, tiled=True)]
    pallas_call x0 -> x3, Pallas kernels: none -> 7.28 us  [the longest x1 2.57 us: last_payload(): pl.pallas_call(body, in_specs=[pl.BlockSpec(memory_space=pltpu.SMEM)] + [...]
    reduce_sum x7 -> x0, other arithmetic: 3.99 us -> none  [the longest x6 3.92 us: add_up(): return jnp.sum(x.astype(F32), axis=0)]
    slice x6 -> x0, local copies, waits for them, and re-layouts: 3.67 us -> none  [the longest x1 1.29 us: unfold(): return jnp.concatenate([x[:, :, :128], x[:, :, 128:]], axis=1)]
  transfers between devices with their start and end apart: 12 -> 16, of which waited for: 5 -> 9; matrix products, arithmetic and copies ran while one was open for 5% -> 3% of each run, Pallas kernels for 17% -> 28%
where the time goes in v4:
time: 200 us; the launch traced here: 199 us
  Pallas kernels  79.8 us (40%)
  waiting for transfers between devices  58 us (29%)
  starting transfers between devices  48.1 us (24%)
  local copies, waits for them, and re-layouts  9.91 us (5%)
  other arithmetic  2.25 us (1%)
    pallas_call x8, Pallas kernels, call(): pl.pallas_call(body, grid=(steps,), in_specs=in_specs, out_specs=out_spec...  72.5 us
    all_to_all x1, waiting for transfers between devices, per_device(): lax.all_to_all(to_send.reshape(n, -1, to_send.shape[1]), AXES, 0, 0, tile...  31.9 us
    all_to_all x3, starting transfers between devices, spread(): lax.all_to_all(x, AXES, 0, 0, axis_index_groups=same_core, tiled=True)  20 us
    all_to_all x1, starting transfers between devices, per_device(): lax.all_to_all(to_send.reshape(n, -1, to_send.shape[1]), AXES, 0, 0, tile...  11.5 us
    ppermute x3, waiting for transfers between devices, add_along_x(): total = total + lax.ppermute(there, AXES, moves).astype(F32)  10.3 us
    all_to_all x3, waiting for transfers between devices, spread(): lax.all_to_all(x, AXES, 0, 0, axis_index_groups=same_core, tiled=True)  8.01 us
    ppermute x8, starting transfers between devices, exchange(): return lax.ppermute(x, AXES, swap)  7.75 us
    all_to_all x1, waiting for transfers between devices, per_device(): lax.all_to_all(sent.reshape(n, -1, sent.shape[1]), AXES, 0, 0, tiled=True)  6.62 us
  transfers between devices with their start and end apart: 16, of which 9 were waited for; matrix products, arithmetic and copies ran while one was open for 3% of the time, Pallas kernels for 28%

profile of v4, /device:TPU:1, one launch (start us, length us, event | category | flops | bytes accessed | tf_op | source)
XLA Modules:
  0.0 199.0 jit_solution(848851219305978644)
XLA Ops:
  0.6 2.4 %shard_map.109 = bf16[1024,1152]{1,0:T(8,128)(2,1)} custom-call(bf16[8,128]{1,0:T(8,128)(2,1)} %q_ref.1, bf16[8,128]{1,0:T(8,128)(2,1)} %k_ref.1, bf16[8,1024]{1,0:T(8,128)(2,1)} %v_ref.1, bf16[8,1024]{1,0:T(8,128)(2,1)} %o_ref.1), custom_call_target="tpu_custom_call" | custom-call | bytes 2359296 | tf_op jit(solution)/shard_map/pallas_call | solution.py:211
  3.0 11.5 %all-to-all-start = ((bf16[128,8,1152]{2,1,0:T(8,128)(2,1)}), bf16[128,8,1152]{2,1,0:T(8,128)(2,1)S(1)}, u32[]{:S(2)}, u32[]{:S(2)}) async-start(bf16[128,8,1152]{2,1,0:T(8,128)(2,1)} %bitcast.18), calls=%async_computation | async-start | bytes 4718592 | tf_op jit(solution)/shard_map/all_to_all | solution.py:670
  14.5 1.1 collective-permute-start
  15.7 31.9 %all-to-all-done = bf16[128,8,1152]{2,1,0:T(8,128)(2,1)S(1)} async-done(((bf16[128,8,1152]{2,1,0:T(8,128)(2,1)}), bf16[128,8,1152]{2,1,0:T(8,128)(2,1)S(1)}, u32[]{:S(2)}, u32[]{:S(2)}) %all-to-all-start) | async-done | bytes 2359328 | tf_op jit(solution)/shard_map/all_to_all | solution.py:670
  47.6 1.2 collective-permute-start.2
  48.8 0.0 collective-permute-start.1
  48.8 0.0 collective-permute-done.other_ref
  48.8 0.2 copy-done
  49.0 10.1 %shard_map.110 = (bf16[128,2048]{1,0:T(8,128)(2,1)}, bf16[2048,512]{1,0:T(8,128)(2,1)}, bf16[704,1024]{1,0:T(8,128)(2,1)}, bf16[704,1024]{1,0:T(8,128)(2,1)}, bf16[2048,128]{1,0:T(8,128)(2,1)}) custom-call(bf16[1024,1024]{1,0:T(8,128)(2,1)} %own_ref.9, bf16[1024,1024]{1,0:T(8,128)(2,1)} %collective-permute-done.other_ref, bf16[1024,1152]{1,0:T(8,128)(2,1)} %bitcast.20), custom_call_target="tpu_custom_call" | custom-call | flops 3422552064 | bytes 12582912 | tf_op jit(solution)/shard_map/pallas_call | solution.py:144
  59.1 5.0 %all-to-all-start.1 = ((bf16[64,32,128]{2,1,0:T(8,128)(2,1)}), bf16[64,32,128]{2,1,0:T(8,128)(2,1)S(1)}, u32[]{:S(2)}, u32[]{:S(2)}) async-start(bf16[64,32,128]{2,1,0:T(8,128)(2,1)} %bitcast.38), calls=%async_computation.1 | async-start | bytes 1048576 | tf_op jit(solution)/shard_map/all_to_all | solution.py:642
  64.1 0.0 collective-permute-done.1.other_ref
  64.1 0.0 collective-permute-done.2.theirs_ref.refs_11_
  64.1 9.9 %shard_map.111 = (f32[512,2048]{1,0:T(8,128)}, bf16[704,2048]{1,0:T(8,128)(2,1)}, bf16[1024,1024]{1,0:T(8,128)(2,1)}) custom-call(s32[1,1]{1,0:T(1,128)} %bitcast.core_ref, bf16[128,2048]{1,0:T(8,128)(2,1)} %get-tuple-element.34.qk_ref, bf16[1024,1024]{1,0:T(8,128)(2,1)} %own_ref.8, bf16[1024,1024]{1,0:T(8,128)(2,1)} %collective-permute-done.1.other_ref, ...), custom_call_target="tpu_custom_call" | custom-call | flops 2147483648 | bytes 18612228 | tf_op jit(solution)/shard_map/pallas_call | solution.py:144
  74.0 1.9 all-to-all-done.1
  75.9 0.8 copy-done.4
  76.7 7.3 %shard_map.112 = (f32[8,2048]{1,0:T(8,128)}, f32[16,128]{1,0:T(8,128)}, bf16[1024,256]{1,0:T(8,128)(2,1)}) custom-call(bf16[704,2048]{1,0:T(8,128)(2,1)} %get-tuple-element.35.feat_ref, f32[512,2048]{1,0:T(8,128)} %get-tuple-element.36.up_ref, bf16[2048,128]{1,0:T(8,128)(2,1)} %bitcast.32), custom_call_target="tpu_custom_call" | custom-call | flops 738197504 | bytes 8200192 | tf_op jit(solution)/shard_map/pallas_call | solution.py:144
  84.0 7.9 %all-to-all-start.2 = ((bf16[64,16,256]{2,1,0:T(8,128)(2,1)}), bf16[64,16,256]{2,1,0:T(8,128)(2,1)S(1)}, u32[]{:S(2)}, u32[]{:S(2)}) async-start(bf16[64,16,256]{2,1,0:T(8,128)(2,1)} %bitcast.36), calls=%async_computation.2 | async-start | bytes 1048576 | tf_op jit(solution)/shard_map/all_to_all | solution.py:642
  92.0 8.4 %shard_map.113.moment_ref = bf16[4096,176]{1,0:T(8,128)(2,1)} custom-call(bf16[704,1024]{1,0:T(8,128)(2,1)} %get-tuple-element.40.rows_ref.refs_6_, bf16[704,1024]{1,0:T(8,128)(2,1)} %get-tuple-element.41.rows_other_ref, bf16[1024,1024]{1,0:T(8,128)(2,1)} %own_ref.9, bf16[1024,1024]{1,0:T(8,128)(2,1)} %collective-permute-done.other_ref, ...), custom_call_target="tpu_custom_call" | custom-call | flops 2952790016 | bytes 9043968 | tf_op jit(solution)/shard_map/pallas_call | solution.py:144
  100.4 2.7 %all-to-all-done.2 = bf16[64,16,256]{2,1,0:T(8,128)(2,1)S(1)} async-done(((bf16[64,16,256]{2,1,0:T(8,128)(2,1)}), bf16[64,16,256]{2,1,0:T(8,128)(2,1)S(1)}, u32[]{:S(2)}, u32[]{:S(2)}) %all-to-all-start.2) | async-done | bytes 524320 | tf_op jit(solution)/shard_map/all_to_all | solution.py:642
  103.2 0.8 copy-done.1
  104.0 12.1 %shard_map.114 = (bf16[512,1024]{1,0:T(8,128)(2,1)}, bf16[512,1024]{1,0:T(8,128)(2,1)}, f32[8,2048]{1,0:T(8,128)}, bf16[2048,608]{1,0:T(8,128)(2,1)}, bf16[1024,256]{1,0:T(8,128)(2,1)}) custom-call(bf16[704,2048]{1,0:T(8,128)(2,1)} %get-tuple-element.35.feat_ref, f32[8,2048]{1,0:T(8,128)} %get-tuple-element.38.scale_ref, ...), custom_call_target="tpu_custom_call" | custom-call | flops 2885681152 | bytes 19005440 | tf_op jit(solution)/shard_map/pallas_call | solution.py:144
  116.1 1.7 constant_dynamic-slice_fusion.2
  117.8 0.2 copy.15
  118.0 0.2 copy.19
  118.3 0.2 copy.17
  118.5 1.2 collective-permute-start.6
  119.7 1.7 collective-permute-start.7
  121.3 0.0 collective-permute-start.5
  121.3 3.4 %collective-permute-start.9 = (bf16[704,1024]{1,0:T(8,128)(2,1)}, bf16[704,1024]{1,0:T(8,128)(2,1)}, u32[]{:S(2)}, u32[]{:S(2)}) collective-permute-start(bf16[704,1024]{1,0:T(8,128)(2,1)} %get-tuple-element.41.rows_other_ref), channel_id=1, source_target_pairs={{0,1},{1,0},{2,3},{3,2},{4,5},{5,4},{6,7},{7,6},{8,9},{9,8},{10,11... | collective-permute-start | bytes 4325384 | tf_op jit(solution)/shard_map/ppermute | solution.py:639
  124.8 7.1 %all-to-all-start.3 = ((bf16[64,16,256]{2,1,0:T(8,128)(2,1)}), bf16[64,16,256]{2,1,0:T(8,128)(2,1)S(1)}, u32[]{:S(2)}, u32[]{:S(2)}) async-start(bf16[64,16,256]{2,1,0:T(8,128)(2,1)} %bitcast.37), calls=%async_computation.3 | async-start | bytes 1048576 | tf_op jit(solution)/shard_map/all_to_all | solution.py:642
  131.9 0.4 collective-permute-start.3
  132.2 5.3 %shard_map.115 = (bf16[64,1024]{1,0:T(8,128)(2,1)}, bf16[64,1024]{1,0:T(8,128)(2,1)}) custom-call(bf16[128,2048]{1,0:T(8,128)(2,1)} %get-tuple-element.34.qk_ref, f32[8,2048]{1,0:T(8,128)} %get-tuple-element.38.scale_ref, f32[8,2048]{1,0:T(8,128)} %get-tuple-element.44.den_ref, f32[512,2048]{1,0:T(8,128)} %get-tuple-element.36.up_ref, ...), custom_call_target="tpu_custom_call" | custom-call | flops 369098752 | bytes 5644288 | tf_op jit(solution)/shard_map/pallas_call | solution.py:144
  137.6 0.0 collective-permute-done.6
  137.6 1.4 copy.18
  139.0 8.7 %collective-permute-done.7 = bf16[512,608]{0,1:T(8,128)(2,1)} collective-permute-done((bf16[512,608]{0,1:T(8,128)(2,1)S(1)}, bf16[512,608]{0,1:T(8,128)(2,1)}, u32[]{:S(2)}, u32[]{:S(2)}) %collective-permute-start.7) | collective-permute-done | bytes 622624 | tf_op jit(solution)/shard_map/ppermute | solution.py:653
  147.7 1.4 copy.20
  149.1 1.6 collective-permute-done.5
  150.7 0.3 copy.16
  151.0 2.3 %fusion.2.after_ref.terms_ref = bf16[512,608]{1,0:T(8,128)(2,1)} fusion(bf16[512,608]{1,0:T(8,128)(2,1)S(1)} %copy.20, bf16[512,608]{1,0:T(8,128)(2,1)S(1)} %copy.18, bf16[512,608]{1,0:T(8,128)(2,1)S(1)} %copy.16, bf16[4,512,608]{2,1,0:T(8,128)(2,1)} %bitcast.31, s32[]{:T(128)S(6)} %select_n.47), kind=kLoop, calls=%fused_computation.3 | loop fusion | flops 2490368 | bytes 3112964 | tf_op jit(solution)/shard_map/convert_element_type | solution.py:654
  153.2 3.4 %all-to-all-done.3 = bf16[64,16,256]{2,1,0:T(8,128)(2,1)S(1)} async-done(((bf16[64,16,256]{2,1,0:T(8,128)(2,1)}), bf16[64,16,256]{2,1,0:T(8,128)(2,1)S(1)}, u32[]{:S(2)}, u32[]{:S(2)}) %all-to-all-start.3) | async-done | bytes 524320 | tf_op jit(solution)/shard_map/all_to_all | solution.py:642
  156.6 0.8 copy-done.3
  157.5 7.5 %shard_map.116 = (bf16[64,1024]{1,0:T(8,128)(2,1)}, bf16[64,1024]{1,0:T(8,128)(2,1)}, bf16[1024,128]{1,0:T(8,128)(2,1)}, bf16[1024,128]{1,0:T(8,128)(2,1)}) custom-call(bf16[128,2048]{1,0:T(8,128)(2,1)} %get-tuple-element.34.qk_ref, bf16[2048,512]{1,0:T(8,128)(2,1)} %get-tuple-element.48.value_ref, bf16[1024,256]{1,0:T(8,128)(2,1)} %bitcast.28, ...), custom_call_target="tpu_custom_call" | custom-call | flops 905969664 | bytes 9535488 | tf_op jit(solution)/shard_map/pallas_call | solution.py:144
  164.9 0.0 copy-start.5
  165.0 0.0 copy-start.7
  165.0 0.0 copy-start.9
  165.0 2.6 %shard_map.118 = bf16[1024,560]{1,0:T(8,128)(2,1)} custom-call(s32[1,1]{1,0:T(1,128)} %bitcast.core_ref, bf16[1024,128]{1,0:T(8,128)(2,1)} %get-tuple-element.57.wgrad_ref, bf16[512,608]{1,0:T(8,128)(2,1)} %fusion.2.after_ref.terms_ref), custom_call_target="tpu_custom_call" | custom-call | bytes 524288 | tf_op jit(solution)/shard_map/pallas_call | solution.py:526
  167.5 6.0 %all-to-all-start.4 = ((bf16[128,8,560]{2,1,0:T(8,128)(2,1)}), bf16[128,8,560]{2,1,0:T(8,128)(2,1)S(1)}, u32[]{:S(2)}, u32[]{:S(2)}) async-start(bf16[128,8,560]{2,1,0:T(8,128)(2,1)} %bitcast.26), calls=%async_computation.4 | async-start | bytes 2621440 | tf_op jit(solution)/shard_map/all_to_all | solution.py:696
  173.5 0.0 copy-done.5
  173.6 1.1 collective-permute-start.10
  174.7 0.0 copy-done.7
  174.7 0.1 collective-permute-start.4
  174.8 0.4 collective-permute-start.8
  175.2 0.0 collective-permute-done.9.refs_7_
  175.2 0.8 collective-permute-done.4.refs_3_
  176.1 0.2 collective-permute-done.8.refs_5_
  176.2 0.0 collective-permute-done.10.refs_9_.other_ref
  176.2 0.0 collective-permute-done.3.refs_1_
  176.3 0.4 copy-done.8
  176.7 0.2 copy-done.10
  176.9 0.1 copy-done.6
  177.0 11.9 %shard_map.117 = (bf16[1024,1024]{1,0:T(8,128)(2,1)}, bf16[1024,1024]{1,0:T(8,128)(2,1)}) custom-call(s32[1,1]{1,0:T(1,128)} %bitcast.core_ref, bf16[512,1024]{1,0:T(8,128)(2,1)} %get-tuple-element.42.refs_0_, bf16[512,1024]{1,0:T(8,128)(2,1)} %collective-permute-done.3.refs_1_, bf16[64,1024]{1,0:T(8,128)(2,1)} %get-tuple-element.46.qgrad_ref.refs_2_, ...), custom_call_target="tpu_custom_call" | custom-call | flops 5200936960 | bytes 17039364 | tf_op jit(solution)/shard_map/pallas_call | solution.py:144
  188.9 6.6 %all-to-all-done.4 = bf16[128,8,560]{2,1,0:T(8,128)(2,1)S(1)} async-done(((bf16[128,8,560]{2,1,0:T(8,128)(2,1)}), bf16[128,8,560]{2,1,0:T(8,128)(2,1)S(1)}, u32[]{:S(2)}, u32[]{:S(2)}) %all-to-all-start.4) | async-done | bytes 1146912 | tf_op jit(solution)/shard_map/all_to_all | solution.py:696
  195.5 1.1 copy-done.2
  196.6 2.3 %shard_map.119 = (f32[8,128]{1,0:T(8,128)}, f32[8,128]{1,0:T(8,128)}, f32[8,1024]{1,0:T(8,128)}, f32[8,1024]{1,0:T(8,128)}) custom-call(s32[1,1]{1,0:T(1,128)} %bitcast.core_ref, bf16[1024,560]{1,0:T(8,128)(2,1)} %bitcast.27, bf16[1024,128]{1,0:T(8,128)(2,1)} %get-tuple-element.53.refs_8_.mine_ref, bf16[1024,128]{1,0:T(8,128)(2,1)} %copy-done.6, ...), custom_call_target="tpu_custom_call" | custom-call | bytes 1146880 | tf_op jit(solution)/shard_map/pallas_call | solution.py:612
  (9 shorter events, 0.0 us)
Async XLA Ops:
  3.0 44.6 %all-to-all-start = ((bf16[128,8,1152]{2,1,0:T(8,128)(2,1)}), bf16[128,8,1152]{2,1,0:T(8,128)(2,1)S(1)}, u32[]{:S(2)}, u32[]{:S(2)}) async-start(bf16[128,8,1152]{2,1,0:T(8,128)(2,1)} %bitcast.18), calls=%async_computation | async-start | bytes 4718592 | tf_op jit(solution)/shard_map/all_to_all | solution.py:670
  14.5 34.3 %collective-permute-start = (bf16[1024,1024]{1,0:T(8,128)(2,1)}, bf16[1024,1024]{1,0:T(8,128)(2,1)}, u32[]{:S(2)}, u32[]{:S(2)}) collective-permute-start(bf16[1024,1024]{1,0:T(8,128)(2,1)} %own_ref.9), channel_id=1, source_target_pairs={{0,1},{1,0},{2,3},{3,2},{4,5},{5,4},{6,7},{7,6},{8,9},{9,8},{10,11... | collective-permute-start | bytes 6291464 | tf_op jit(solution)/shard_map/ppermute | solution.py:639
  47.6 1.4 copy-start
  47.6 16.5 %collective-permute-start.2 = (bf16[1024,1152]{1,0:T(8,128)(2,1)S(1)}, bf16[1024,1152]{1,0:T(8,128)(2,1)}, u32[]{:S(2)}, u32[]{:S(2)}) collective-permute-start(bf16[1024,1152]{1,0:T(8,128)(2,1)S(1)} %bitcast.19), channel_id=1, source_target_pairs={{0,1},{1,0},{2,3},{3,2},{4,5},{5,4},{6,7},{7,6},{8,9},{9,8},{10,11... | collective-permute-start | bytes 7077896 | tf_op jit(solution)/shard_map/ppermute | solution.py:639
  48.8 15.4 %collective-permute-start.1 = (bf16[1024,1024]{1,0:T(8,128)(2,1)}, bf16[1024,1024]{1,0:T(8,128)(2,1)}, u32[]{:S(2)}, u32[]{:S(2)}) collective-permute-start(bf16[1024,1024]{1,0:T(8,128)(2,1)} %own_ref.8), channel_id=1, source_target_pairs={{0,1},{1,0},{2,3},{3,2},{4,5},{5,4},{6,7},{7,6},{8,9},{9,8},{10,11... | collective-permute-start | bytes 6291464 | tf_op jit(solution)/shard_map/ppermute | solution.py:639
  59.1 16.8 %all-to-all-start.1 = ((bf16[64,32,128]{2,1,0:T(8,128)(2,1)}), bf16[64,32,128]{2,1,0:T(8,128)(2,1)S(1)}, u32[]{:S(2)}, u32[]{:S(2)}) async-start(bf16[64,32,128]{2,1,0:T(8,128)(2,1)} %bitcast.38), calls=%async_computation.1 | async-start | bytes 1048576 | tf_op jit(solution)/shard_map/all_to_all | solution.py:642
  75.9 0.8 copy-start.4
  84.0 19.2 %all-to-all-start.2 = ((bf16[64,16,256]{2,1,0:T(8,128)(2,1)}), bf16[64,16,256]{2,1,0:T(8,128)(2,1)S(1)}, u32[]{:S(2)}, u32[]{:S(2)}) async-start(bf16[64,16,256]{2,1,0:T(8,128)(2,1)} %bitcast.36), calls=%async_computation.2 | async-start | bytes 1048576 | tf_op jit(solution)/shard_map/all_to_all | solution.py:642
  103.2 0.8 copy-start.1
  118.5 19.1 %collective-permute-start.6 = (bf16[512,608]{0,1:T(8,128)(2,1)S(1)}, bf16[512,608]{0,1:T(8,128)(2,1)}, u32[]{:S(2)}, u32[]{:S(2)}) collective-permute-start(bf16[512,608]{0,1:T(8,128)(2,1)S(1)} %bitcast.35), channel_id=1, source_target_pairs={{0,16},{1,17},{2,18},{3,19},{4,20},{5,21},{6,22},{7,23},{8,24},{9,... | collective-permute-start | bytes 1867784 | tf_op jit(solution)/shard_map/ppermute | solution.py:653
  119.7 28.0 %collective-permute-start.7 = (bf16[512,608]{0,1:T(8,128)(2,1)S(1)}, bf16[512,608]{0,1:T(8,128)(2,1)}, u32[]{:S(2)}, u32[]{:S(2)}) collective-permute-start(bf16[512,608]{0,1:T(8,128)(2,1)S(1)} %bitcast.34), channel_id=1, source_target_pairs={{0,18},{1,19},{2,0},{3,1},{4,22},{5,23},{6,4},{7,5},{8,26},{9,27},... | collective-permute-start | bytes 1867784 | tf_op jit(solution)/shard_map/ppermute | solution.py:653
  121.3 29.3 %collective-permute-start.5 = (bf16[512,608]{0,1:T(8,128)(2,1)S(1)}, bf16[512,608]{0,1:T(8,128)(2,1)S(1)}, u32[]{:S(2)}, u32[]{:S(2)}) collective-permute-start(bf16[512,608]{0,1:T(8,128)(2,1)S(1)} %bitcast.33), channel_id=1, source_target_pairs={{0,2},{1,3},{2,16},{3,17},{4,6},{5,7},{6,20},{7,21},{8,10},{9,11},... | collective-permute-start | bytes 1867784 | tf_op jit(solution)/shard_map/ppermute | solution.py:653
  121.3 53.9 %collective-permute-start.9 = (bf16[704,1024]{1,0:T(8,128)(2,1)}, bf16[704,1024]{1,0:T(8,128)(2,1)}, u32[]{:S(2)}, u32[]{:S(2)}) collective-permute-start(bf16[704,1024]{1,0:T(8,128)(2,1)} %get-tuple-element.41.rows_other_ref), channel_id=1, source_target_pairs={{0,1},{1,0},{2,3},{3,2},{4,5},{5,4},{6,7},{7,6},{8,9},{9,8},{10,11... | collective-permute-start | bytes 4325384 | tf_op jit(solution)/shard_map/ppermute | solution.py:639
  124.8 31.9 %all-to-all-start.3 = ((bf16[64,16,256]{2,1,0:T(8,128)(2,1)}), bf16[64,16,256]{2,1,0:T(8,128)(2,1)S(1)}, u32[]{:S(2)}, u32[]{:S(2)}) async-start(bf16[64,16,256]{2,1,0:T(8,128)(2,1)} %bitcast.37), calls=%async_computation.3 | async-start | bytes 1048576 | tf_op jit(solution)/shard_map/all_to_all | solution.py:642
  131.9 44.4 %collective-permute-start.3 = (bf16[512,1024]{1,0:T(8,128)(2,1)}, bf16[512,1024]{1,0:T(8,128)(2,1)}, u32[]{:S(2)}, u32[]{:S(2)}) collective-permute-start(bf16[512,1024]{1,0:T(8,128)(2,1)} %get-tuple-element.43), channel_id=1, source_target_pairs={{0,1},{1,0},{2,3},{3,2},{4,5},{5,4},{6,7},{7,6},{8,9},{9,8},{10,11... | collective-permute-start | bytes 3145736 | tf_op jit(solution)/shard_map/ppermute | solution.py:639
  156.6 0.8 copy-start.3
  164.9 8.6 %copy-start.5 = (bf16[1024,128]{1,0:T(8,128)(2,1)S(1)}, bf16[1024,128]{1,0:T(8,128)(2,1)}, u32[]{:S(2)}) copy-start(bf16[1024,128]{1,0:T(8,128)(2,1)} %get-tuple-element.53.refs_8_.mine_ref) | copy-start | bytes 786436
  165.0 9.8 %copy-start.7 = (bf16[64,1024]{1,0:T(8,128)(2,1)S(1)}, bf16[64,1024]{1,0:T(8,128)(2,1)}, u32[]{:S(2)}) copy-start(bf16[64,1024]{1,0:T(8,128)(2,1)} %get-tuple-element.47.qgrad_other_ref) | copy-start | bytes 393220
  165.0 9.8 %copy-start.9 = (bf16[64,1024]{1,0:T(8,128)(2,1)S(1)}, bf16[64,1024]{1,0:T(8,128)(2,1)}, u32[]{:S(2)}) copy-start(bf16[64,1024]{1,0:T(8,128)(2,1)} %get-tuple-element.52) | copy-start | bytes 393220
  167.5 28.0 %all-to-all-start.4 = ((bf16[128,8,560]{2,1,0:T(8,128)(2,1)}), bf16[128,8,560]{2,1,0:T(8,128)(2,1)S(1)}, u32[]{:S(2)}, u32[]{:S(2)}) async-start(bf16[128,8,560]{2,1,0:T(8,128)(2,1)} %bitcast.26), calls=%async_computation.4 | async-start | bytes 2621440 | tf_op jit(solution)/shard_map/all_to_all | solution.py:696
  173.6 2.7 %collective-permute-start.10 = (bf16[1024,128]{1,0:T(8,128)(2,1)S(1)}, bf16[1024,128]{1,0:T(8,128)(2,1)S(1)}, u32[]{:S(2)}, u32[]{:S(2)}) collective-permute-start(bf16[1024,128]{1,0:T(8,128)(2,1)S(1)} %copy-done.5), channel_id=1, source_target_pairs={{0,1},{1,0},{2,3},{3,2},{4,5},{5,4},{6,7},{7,6},{8,9},{9,8},{10,11... | collective-permute-start | bytes 786440 | tf_op jit(solution)/shard_map/ppermute | solution.py:639
  174.7 1.3 collective-permute-start.4
  174.8 1.4 collective-permute-start.8
  176.1 0.6 copy-start.8
  176.2 0.6 copy-start.10
  176.2 0.8 copy-start.6
  195.5 1.1 copy-start.2

commit v5 on v4

--- a/solution.py
+++ b/solution.py
@@ -12,6 +12,7 @@
 FPAD = (BANDS + 2) * DK
 SPAD = 256
 AXES = ("ctx", "seq")
+BLOCK = 512
 VMEM = 60 * 2**20
 BF = jnp.bfloat16
 F32 = jnp.float32
@@ -99,91 +100,111 @@
 
 
 def call(body, count, ins, kinds, outs, out_kinds, scratch, flops):
-    block = min(512, count, count // 2 if "pair" in kinds else count)
+    block = min(BLOCK, count // 2 if "pair" in kinds or "pair1" in out_kinds else count)
     steps = count // block
-    in_specs, args = [], []
-    for x, kind in zip(ins, kinds):
-        if kind is None:
-            in_specs.append(pl.BlockSpec(x.shape, lambda i: (0, 0)))
-        elif kind == 0:
-            in_specs.append(pl.BlockSpec((block, x.shape[1]), lambda i: (i, 0)))
-        elif kind == 1:
-            in_specs.append(pl.BlockSpec((x.shape[0], block), lambda i: (0, i)))
-        elif kind == "scalar":
-            in_specs.append(pl.BlockSpec(memory_space=pltpu.SMEM))
-        elif kind == "any":
-            in_specs.append(pl.BlockSpec(memory_space=pl.ANY))
-        elif isinstance(kind, tuple):
-            width, at = kind
-            in_specs.append(pl.BlockSpec((x.shape[0], width), lambda i, at=at: (0, at)))
-        elif kind == "pair1":
+
+    def pieces(x, kind):
+        if kind in ("pair", "pair1"):
             half = steps // 2
-            in_specs.append(pl.BlockSpec((x[0].shape[0], block), lambda i: (0, jnp.minimum(i, half - 1))))
-            in_specs.append(pl.BlockSpec((x[0].shape[0], block), lambda i: (0, jnp.maximum(i - half, 0))))
-        else:
-            half = steps // 2
-            in_specs.append(pl.BlockSpec((block, x[0].shape[1]), lambda i: (jnp.minimum(i, half - 1), 0)))
-            in_specs.append(pl.BlockSpec((block, x[0].shape[1]), lambda i: (jnp.maximum(i - half, 0), 0)))
-        args += list(x) if kind in ("pair", "pair1") else [x]
-    out_specs = []
-    for x, kind in zip(outs, out_kinds):
-        half = steps // 2
-        if kind == "first":
-            out_specs.append(pl.BlockSpec((x.shape[0], block), lambda i: (0, jnp.minimum(i, half - 1))))
-            continue
-        if kind == "second":
-            out_specs.append(pl.BlockSpec((x.shape[0], block), lambda i: (0, jnp.maximum(i - half, 0))))
-            continue
-        if kind is None:
-            out_specs.append(pl.BlockSpec(x.shape, lambda i: (0, 0)))
-        elif kind == 0:
-            out_specs.append(pl.BlockSpec((block, x.shape[1]), lambda i: (i, 0)))
-        else:
-            out_specs.append(pl.BlockSpec((x.shape[0], block), lambda i: (0, i)))
-    nbytes = sum(x.size * x.dtype.itemsize for x in args + list(outs))
+            return pieces_of(0, half, x[0].shape, kind) + pieces_of(1, half, x[1].shape, kind)
+        if kind in (0, 1):
+            return pieces_of(0, steps, x.shape, kind)
+        if kind is not None and kind[0] == "from":
+            return [(0, pl.ds(0, x.shape[0]), pl.ds(kind[1], x.shape[1] - kind[1]))]
+        if kind is not None:
+            return [(0, pl.ds(0, x.shape[0]), pl.ds(kind[0] * kind[1], kind[0]))]
+        return [(0, pl.ds(0, x.shape[0]), pl.ds(0, x.shape[1]))]
+
+    def pieces_of(which, number, dims, kind):
+        if kind in (0, "pair"):
+            return [(which, pl.ds(i * block, block), pl.ds(0, dims[1])) for i in range(number)]
+        return [(which, pl.ds(0, dims[0]), pl.ds(i * block, block)) for i in range(number)]
+
+    def members(x, kind):
+        return list(x) if kind in ("pair", "pair1") else [x]
+
+    plans = [[] if kind in ("scalar", "any") else pieces(x, kind) for x, kind in zip(ins, kinds)]
+    out_plans = [pieces(x, kind) for x, kind in zip(outs, out_kinds)]
+    buffers = [
+        pltpu.VMEM((rows.size, cols.size), members(x, kind)[0].dtype)
+        for x, kind, plan in zip(tuple(ins) + tuple(outs), tuple(kinds) + tuple(out_kinds), plans + out_plans)
+        for _, rows, cols in plan
+    ]
+
+    def kernel(*refs):
+        refs = list(refs)
+
+        def take(number):
+            found = refs[:number]
+            del refs[:number]
+            return found
+
+        given = [take(len(members(x, kind))) for x, kind in zip(ins, kinds)]
+        made = [take(len(members(x, kind))) for x, kind in zip(outs, out_kinds)]
+        held, sent = [take(len(plan)) for plan in plans], [take(len(plan)) for plan in out_plans]
+        arrived, left = take(2)
+        own = refs
+
+        reads, at = [[] for _ in range(steps)], 0
+        for source, buffer, plan in zip(given, held, plans):
+            for i, (which, rows, cols) in enumerate(plan):
+                reads[i].append(pltpu.make_async_copy(source[which].at[rows, cols], buffer[i], arrived.at[at]))
+                at += 1
+        writes, at = [], 0
+        for target, buffer, plan in zip(made, sent, out_plans):
+            writes.append([])
+            for i, (which, rows, cols) in enumerate(plan):
+                writes[-1].append(pltpu.make_async_copy(buffer[i], target[which].at[rows, cols], left.at[at]))
+                at += 1
+        for step in reads:
+            for copy in step:
+                copy.start()
+        for i in range(steps):
+            for copy in reads[i]:
+                copy.wait()
+            body(
+                lambda fn: fn() if i == 0 else None,
+                lambda fn: fn() if i == steps - 1 else None,
+                *[buffer[min(i, len(buffer) - 1)] if buffer else source[0] for buffer, source in zip(held, given)],
+                *[buffer[min(i, len(buffer) - 1)] for buffer in sent],
+                *own,
+            )
+            for copies in writes:
+                if len(copies) == steps:
+                    copies[i].start()
+                elif i == steps - 1:
+                    copies[0].start()
+        for copies in writes:
+            for copy in copies:
+                copy.wait()
+
+    args = [y for x, kind in zip(ins, kinds) for y in members(x, kind)]
+    results = [y for x, kind in zip(outs, out_kinds) for y in members(x, kind)]
+    spaces = [pltpu.SMEM if kind == "scalar" else pl.ANY for x, kind in zip(ins, kinds) for _ in members(x, kind)]
+    nbytes = sum(x.size * x.dtype.itemsize for x in args + results)
     return pl.pallas_call(
-        body,
-        grid=(steps,),
-        in_specs=in_specs,
-        out_specs=out_specs,
-        out_shape=outs,
-        scratch_shapes=scratch,
-        compiler_params=pltpu.CompilerParams(dimension_semantics=("arbitrary",), vmem_limit_bytes=VMEM),
+        kernel,
+        in_specs=[pl.BlockSpec(memory_space=space) for space in spaces],
+        out_specs=[pl.BlockSpec(memory_space=pl.ANY)] * len(results),
+        out_shape=results,
+        scratch_shapes=buffers
+        + [
+            pltpu.SemaphoreType.DMA((sum(len(plan) for plan in plans),)),
+            pltpu.SemaphoreType.DMA((sum(len(plan) for plan in out_plans),)),
+        ]
+        + list(scratch),
+        compiler_params=pltpu.CompilerParams(vmem_limit_bytes=VMEM),
         cost_estimate=pl.CostEstimate(flops=flops, bytes_accessed=nbytes, transcendentals=0),
     )(*args)
 
 
-def either(first_ref, second_ref):
-    return jnp.where(pl.program_id(0) < pl.num_programs(0) // 2, first_ref[...], second_ref[...])
-
-
-def store_half(first_ref, second_ref, value):
-    @pl.when(pl.program_id(0) < pl.num_programs(0) // 2)
-    def _():
-        first_ref[...] = value
-
-    @pl.when(pl.program_id(0) >= pl.num_programs(0) // 2)
-    def _():
-        second_ref[...] = value
-
-
 def shape(dims, dtype):
     return jax.ShapeDtypeStruct(dims, dtype)
 
 
-def clear_at_first(*refs):
-    @pl.when(pl.program_id(0) == 0)
-    def _():
-        for ref in refs:
-            ref[...] = jnp.zeros(ref.shape, ref.dtype)
-
-
-def at_first(fn):
-    pl.when(pl.program_id(0) == 0)(fn)
-
-
-def at_last(fn):
-    pl.when(pl.program_id(0) == pl.num_programs(0) - 1)(fn)
+def clear(*refs):
+    for ref in refs:
+        ref[...] = jnp.zeros(ref.shape, ref.dtype)
 
 
 def weights_phase(w_query, w_key, w_value, w_out, chips, heads):
@@ -219,9 +240,9 @@
 def keys_phase(tokens, w_qkv, chips, heads):
     qk = heads * DK
 
-    def body(own_ref, other_ref, w_ref, qk_ref, value_ref, feat_ref, feat_other_ref, sent_ref, state_acc, norm_acc):
-        clear_at_first(state_acc, norm_acc)
-        joined = dot(either(own_ref, other_ref), w_ref[:, : 2 * qk + heads * DV], (1, 0))
+    def body(at_first, at_last, slab_ref, w_ref, qk_ref, value_ref, feat_ref, sent_ref, state_acc, norm_acc):
+        at_first(lambda: clear(state_acc, norm_acc))
+        joined = dot(slab_ref[...], w_ref[...], (1, 0))
         qk_t = joined[:, : 2 * qk].T.astype(BF)
         value = joined[:, 2 * qk :].astype(BF)
         qk_ref[...] = qk_t
@@ -233,7 +254,7 @@
             found.append(feat)
             state_acc[head, :FPAD, :] += dot(feat, value[:, head * DV : (head + 1) * DV], (1, 0))
             norm_acc[head, :FPAD, :] += lane_sums(feat.astype(F32))
-        store_half(feat_ref, feat_other_ref, jnp.concatenate(found, axis=0))
+        feat_ref[...] = jnp.concatenate(found, axis=0)
 
         @at_last
         def _():
@@ -249,15 +270,14 @@
         body,
         count,
         (tokens, w_qkv),
-        ("pair", None),
+        ("pair", (2 * qk + heads * DV, 0)),
         (
             shape((2 * qk, count), BF),
             shape((count, heads * DV), BF),
-            shape((heads * FPAD, count // 2), BF),
-            shape((heads * FPAD, count // 2), BF),
+            (shape((heads * FPAD, count // 2), BF),) * 2,
             shape((2 * heads * SPAD, DV), BF),
         ),
-        (1, 0, "first", "second", None),
+        (1, 0, "pair1", None),
         [pltpu.VMEM((heads, SPAD, DV), F32), pltpu.VMEM((heads, SPAD, 128), F32)],
         2 * count * heads * (w_qkv.shape[0] * (2 * DK + DV) + FPAD * DV * 2),
     )
@@ -268,17 +288,17 @@
     rows, half = heads * DV, width // 2
     joined = 2 * heads * DK + heads * DV
 
-    def body(core_ref, qk_ref, own_ref, other_ref, mine_ref, theirs_ref, up_ref, feat_ref, w_ref):
+    def body(at_first, at_last, core_ref, qk_ref, slab_ref, mine_ref, theirs_ref, up_ref, feat_ref, w_ref):
         at = core_ref[0, 0]
 
         @at_first
         def _():
-            mine, theirs = mine_ref[:, joined:], theirs_ref[:, joined:]
+            mine, theirs = mine_ref[...], theirs_ref[...]
             w_ref[:, :half] = jnp.where(at == 0, mine, theirs)
             w_ref[:, half:] = jnp.where(at == 0, theirs, mine)
 
         here = w_ref[pl.ds(pl.multiple_of(at * rows, rows), rows), :]
-        up_ref[...] = dot(here, either(own_ref, other_ref), (1, 1))
+        up_ref[...] = dot(here, slab_ref[...], (1, 1))
         query = qk_ref[...].astype(F32)
         for head in range(heads):
             feat_ref[head * FPAD : (head + 1) * FPAD, :] = features(rows_of(query, head, DK))
@@ -287,7 +307,7 @@
         body,
         count,
         (core, qk_t, cot, weights, other_weights),
-        ("scalar", 1, "pair", None, None),
+        ("scalar", 1, "pair", ("from", joined), ("from", joined)),
         (shape((rows, count), F32), shape((heads * FPAD, count), BF), shape((2 * rows, width), BF)),
         (1, 1, None),
         [],
@@ -300,9 +320,9 @@
     size = rows // parts
     width = slabs[0].shape[1]
 
-    def body(rows_ref, rows_other_ref, own_ref, other_ref, after_ref, out_ref, acc):
-        clear_at_first(acc)
-        acc[...] += dot(either(rows_ref, rows_other_ref), either(own_ref, other_ref), (1, 0))
+    def body(at_first, at_last, rows_ref, slab_ref, after_ref, out_ref, acc):
+        at_first(lambda: clear(acc))
+        acc[...] += dot(rows_ref[...], slab_ref[...], (1, 0))
 
         @at_last
         def _():
@@ -325,8 +345,8 @@
     count = up_t.shape[1]
     part = heads * SPAD // chips
 
-    def body(feat_ref, up_ref, first_ref, scale_ref, norm_ref, sent_ref, acc, state_own):
-        clear_at_first(acc)
+    def body(at_first, at_last, feat_ref, up_ref, first_ref, scale_ref, norm_ref, sent_ref, acc, state_own):
+        at_first(lambda: clear(acc))
 
         @at_first
         def _():
@@ -369,10 +389,10 @@
     quarter = width // 4
 
     def body(
-        feat_ref, scale_ref, up_ref, state_ref, sgrad_ref, own_ref, other_ref, moment_ref,
-        att_ref, att_other_ref, den_ref, out_ref, sent_ref, turned, acc, out_acc,
+        at_first, at_last, feat_ref, scale_ref, up_ref, state_ref, sgrad_ref, slab_ref, moment_ref,
+        att_ref, den_ref, out_ref, sent_ref, turned, acc, out_acc,
     ):
-        clear_at_first(acc, out_acc)
+        at_first(lambda: clear(acc, out_acc))
 
         @at_first
         def _():
@@ -393,8 +413,8 @@
             dens = jnp.where(at == head, grad_den, dens)
         den_ref[...] = dens
         attended = jnp.concatenate(found, axis=0)
-        store_half(att_ref, att_other_ref, attended)
-        out_acc[...] += dot(attended, either(own_ref, other_ref), (1, 0))
+        att_ref[...] = attended
+        out_acc[...] += dot(attended, slab_ref[...], (1, 0))
 
         @at_last
         def _():
@@ -416,13 +436,12 @@
         (feats, scales, up_t, second, second, cot, moments),
         (1, 1, 1, (DV, 1), (DV, 0), "pair", None),
         (
-            shape((heads * DV, count // 2), BF),
-            shape((heads * DV, count // 2), BF),
+            (shape((heads * DV, count // 2), BF),) * 2,
             shape((8, count), F32),
             shape((4 * heads * DV, quarter + 2 * FPAD), BF),
             shape(second.shape, BF),
         ),
-        ("first", "second", 1, None, None),
+        ("pair1", 1, None, None),
         [
             pltpu.VMEM((heads, DV, SPAD), BF),
             pltpu.VMEM((heads, SPAD, 128), F32),
@@ -435,7 +454,7 @@
 def query_back_phase(qk_t, scales, dens, up_t, second, norm, heads):
     count = up_t.shape[1]
 
-    def body(qk_ref, scale_ref, den_ref, up_ref, state_ref, norm_ref, qgrad_ref, qgrad_other_ref):
+    def body(at_first, at_last, qk_ref, scale_ref, den_ref, up_ref, state_ref, norm_ref, qgrad_ref):
         query = qk_ref[...].astype(F32)
         found = []
         for head in range(heads):
@@ -443,15 +462,15 @@
             fgrad = dot(state_ref[head * SPAD : head * SPAD + FPAD, :], grad_num, (1, 0))
             fgrad = fgrad + column(head_row(norm_ref[...], head)) * den_ref[head : head + 1, :]
             found.append(features_back(rows_of(query, head, DK), fgrad).astype(BF))
-        store_half(qgrad_ref, qgrad_other_ref, jnp.concatenate(found, axis=0))
+        qgrad_ref[...] = jnp.concatenate(found, axis=0)
 
     return call(
         body,
         count,
         (qk_t, scales, dens, up_t, second, norm),
         (1, 1, 1, 1, (DV, 1), None),
-        (shape((heads * DK, count // 2), BF), shape((heads * DK, count // 2), BF)),
-        ("first", "second"),
+        ((shape((heads * DK, count // 2), BF),) * 2,),
+        ("pair1",),
         [],
         2 * count * heads * FPAD * DV,
     )
@@ -462,10 +481,10 @@
     width = tokens[0].shape[1]
 
     def body(
-        qk_ref, value_ref, sgrad_ref, rows_ref, qgrad_ref, qgrad_other_ref, own_ref, other_ref, after_ref,
-        kgrad_ref, kgrad_other_ref, copy_ref, sent_ref, acc, ngrad_ref,
+        at_first, at_last, qk_ref, value_ref, sgrad_ref, rows_ref, qgrad_ref, slab_ref, after_ref,
+        kgrad_ref, copy_ref, sent_ref, acc, ngrad_ref,
     ):
-        clear_at_first(acc)
+        at_first(lambda: clear(acc))
 
         @at_first
         def _():
@@ -483,9 +502,9 @@
             fgrad = fgrad + column(head_row(ngrad_ref[...], head))
             found.append(features_back(rows_of(keys, head, DK), fgrad))
         kgrad = jnp.concatenate(found, axis=0).astype(BF)
-        store_half(kgrad_ref, kgrad_other_ref, kgrad)
-        both = jnp.concatenate([either(qgrad_ref, qgrad_other_ref), kgrad], axis=0)
-        acc[...] += dot(both, either(own_ref, other_ref), (1, 0))
+        kgrad_ref[...] = kgrad
+        both = jnp.concatenate([qgrad_ref[...], kgrad], axis=0)
+        acc[...] += dot(both, slab_ref[...], (1, 0))
 
         @at_last
         def _():
@@ -497,12 +516,11 @@
         (qk_t, value, third, third, qgrads, tokens, after),
         (1, 0, (DV, 0), (DV, 1), "pair1", "pair", "any"),
         (
-            shape((qk, count // 2), BF),
-            shape((qk, count // 2), BF),
+            (shape((qk, count // 2), BF),) * 2,
             shape((third.shape[0], DV), BF),
             shape((width, 2 * qk), BF),
         ),
-        ("first", "second", None, None),
+        ("pair1", None, None),
         [pltpu.VMEM((2 * qk, width), F32), pltpu.VMEM((16, DV), F32)],
         2 * count * (heads * FPAD * DV + 2 * qk * width),
     )
@@ -537,7 +555,7 @@
     count, width = attended[0].shape[1], w_out.shape[1]
     rows, joined = heads * DV, 2 * heads * DK + heads * DV
 
-    def body(core_ref, *refs):
+    def body(at_first, at_last, core_ref, *refs):
         atts, qs, ks, fs, ss, ws = (refs[2 * i : 2 * i + 2] for i in range(6))
         out_ref, mixed_ref, gtok_ref, turned = refs[12:]
         at = core_ref[0, 0]
@@ -556,7 +574,7 @@
             for head in range(heads):
                 feat = fs[c][head * FPAD : (head + 1) * FPAD, :]
                 parts.append(dot(turned[c, head, :, :FPAD], feat, (1, 0)).astype(BF))
-            gtok = gtok + dot(jnp.concatenate(parts, axis=0), ws[c][:, :joined], (0, 1))
+            gtok = gtok + dot(jnp.concatenate(parts, axis=0), ws[c][...], (0, 1))
         mixed_ref[...] = mixed.astype(BF)
         gtok_ref[...] = gtok.astype(BF)
 
@@ -564,7 +582,7 @@
         body,
         count,
         (core, *attended, *qgrads, *kgrads, *feats, *sgrads, *weights, w_out),
-        ("scalar",) + (1,) * 8 + (None,) * 5,
+        ("scalar",) + (1,) * 8 + (None,) * 2 + ((joined, 0),) * 2 + (None,),
         (shape((count, width), BF), shape((count, width), BF)),
         (0, 0),
         [pltpu.VMEM((2, heads, DV, SPAD), BF)],

time: 200 us -> 189 us (0.945)
  Pallas kernels: 79.8 us -> 65.8 us
  waiting for transfers between devices: 58 us -> 62.3 us
    pallas_call x8, Pallas kernels: 72.5 us -> 58.5 us  [call(): pl.pallas_call(kernel, in_specs=[pl.BlockSpec(memory_space=space) for spa...]
    all_to_all x3, waiting for transfers between devices: 8.01 us -> 11.1 us  [spread(): lax.all_to_all(x, AXES, 0, 0, axis_index_groups=same_core, tiled=True)]
    all_to_all x3, starting transfers between devices: 20 us -> 17.9 us  [spread(): lax.all_to_all(x, AXES, 0, 0, axis_index_groups=same_core, tiled=True)]
  transfers between devices with their start and end apart: 16 -> 16, of which waited for: 9 -> 9; matrix products, arithmetic and copies ran while one was open for 3% -> 3% of each run, Pallas kernels for 28% -> 25%
where the time goes in v5:
time: 189 us; the launch traced here: 188 us
  Pallas kernels  65.8 us (35%)
  waiting for transfers between devices  62.3 us (33%)
  starting transfers between devices  46.6 us (25%)
  local copies, waits for them, and re-layouts  9.91 us (5%)
  other arithmetic  2.25 us (1%)
    pallas_call x8, Pallas kernels, call(): pl.pallas_call(kernel, in_specs=[pl.BlockSpec(memory_space=space) for spa...  58.5 us
    all_to_all x1, waiting for transfers between devices, per_device(): lax.all_to_all(to_send.reshape(n, -1, to_send.shape[1]), AXES, 0, 0, tile...  31.9 us
    all_to_all x3, starting transfers between devices, spread(): lax.all_to_all(x, AXES, 0, 0, axis_index_groups=same_core, tiled=True)  17.9 us
    all_to_all x1, starting transfers between devices, per_device(): lax.all_to_all(to_send.reshape(n, -1, to_send.shape[1]), AXES, 0, 0, tile...  11.5 us
    all_to_all x3, waiting for transfers between devices, spread(): lax.all_to_all(x, AXES, 0, 0, axis_index_groups=same_core, tiled=True)  11.1 us
    ppermute x3, waiting for transfers between devices, add_along_x(): total = total + lax.ppermute(there, AXES, moves).astype(F32)  10.9 us
    ppermute x8, starting transfers between devices, exchange(): return lax.ppermute(x, AXES, swap)  8.02 us
    all_to_all x1, waiting for transfers between devices, per_device(): lax.all_to_all(sent.reshape(n, -1, sent.shape[1]), AXES, 0, 0, tiled=True)  7.25 us
  transfers between devices with their start and end apart: 16, of which 9 were waited for; matrix products, arithmetic and copies ran while one was open for 3% of the time, Pallas kernels for 25%

profile of v5, /device:TPU:1, one launch (start us, length us, event | category | flops | bytes accessed | tf_op | source)
XLA Modules:
  0.0 187.9 jit_solution(17678263649494483004)
XLA Ops:
  0.6 2.4 %shard_map.109 = bf16[1024,1152]{1,0:T(8,128)(2,1)} custom-call(bf16[8,128]{1,0:T(8,128)(2,1)} %q_ref.1, bf16[8,128]{1,0:T(8,128)(2,1)} %k_ref.1, bf16[8,1024]{1,0:T(8,128)(2,1)} %v_ref.1, bf16[8,1024]{1,0:T(8,128)(2,1)} %o_ref.1), custom_call_target="tpu_custom_call" | custom-call | bytes 2359296 | tf_op jit(solution)/shard_map/pallas_call | solution.py:232
  3.0 11.5 %all-to-all-start = ((bf16[128,8,1152]{2,1,0:T(8,128)(2,1)}), bf16[128,8,1152]{2,1,0:T(8,128)(2,1)S(1)}, u32[]{:S(2)}, u32[]{:S(2)}) async-start(bf16[128,8,1152]{2,1,0:T(8,128)(2,1)} %bitcast.18), calls=%async_computation | async-start | bytes 4718592 | tf_op jit(solution)/shard_map/all_to_all | solution.py:688
  14.5 1.1 collective-permute-start
  15.7 31.9 %all-to-all-done = bf16[128,8,1152]{2,1,0:T(8,128)(2,1)S(1)} async-done(((bf16[128,8,1152]{2,1,0:T(8,128)(2,1)}), bf16[128,8,1152]{2,1,0:T(8,128)(2,1)S(1)}, u32[]{:S(2)}, u32[]{:S(2)}) %all-to-all-start) | async-done | bytes 2359328 | tf_op jit(solution)/shard_map/all_to_all | solution.py:688
  47.6 1.2 collective-permute-start.2
  48.8 0.0 collective-permute-start.1
  48.8 0.0 collective-permute-done.refs_1_.refs_3_.refs_7_
  48.8 0.2 copy-done
  49.0 8.6 %shard_map.110 = (bf16[128,2048]{1,0:T(8,128)(2,1)}, bf16[2048,512]{1,0:T(8,128)(2,1)}, bf16[704,1024]{1,0:T(8,128)(2,1)}, bf16[704,1024]{1,0:T(8,128)(2,1)}, bf16[2048,128]{1,0:T(8,128)(2,1)}) custom-call(bf16[1024,1024]{1,0:T(8,128)(2,1)} %refs_6_.1, bf16[1024,1024]{1,0:T(8,128)(2,1)} %collective-permute-done.refs_1_.refs_3_.refs_7_, ...), custom_call_target="tpu_custom_call" | custom-call | flops 3422552064 | bytes 12582912 | tf_op jit(solution)/shard_map/pallas_call | solution.py:185
  57.7 5.0 %all-to-all-start.1 = ((bf16[64,32,128]{2,1,0:T(8,128)(2,1)}), bf16[64,32,128]{2,1,0:T(8,128)(2,1)S(1)}, u32[]{:S(2)}, u32[]{:S(2)}) async-start(bf16[64,32,128]{2,1,0:T(8,128)(2,1)} %bitcast.38), calls=%async_computation.1 | async-start | bytes 1048576 | tf_op jit(solution)/shard_map/all_to_all | solution.py:660
  62.7 0.0 collective-permute-done.1.refs_3_.refs_6_
  62.7 0.0 collective-permute-done.2.refs_5_.refs_12_
  62.7 7.5 %shard_map.111 = (f32[512,2048]{1,0:T(8,128)}, bf16[704,2048]{1,0:T(8,128)(2,1)}, bf16[1024,1024]{1,0:T(8,128)(2,1)}) custom-call(s32[1,1]{1,0:T(1,128)} %bitcast.refs_0_.core_ref, bf16[128,2048]{1,0:T(8,128)(2,1)} %get-tuple-element.34.refs_1_.refs_0_, bf16[1024,1024]{1,0:T(8,128)(2,1)} %refs_5_.1, ...), custom_call_target="tpu_custom_call" | custom-call | flops 2147483648 | bytes 18612228 | tf_op jit(solution)/shard_map/pallas_call | solution.py:185
  70.2 4.2 %all-to-all-done.1 = bf16[64,32,128]{2,1,0:T(8,128)(2,1)S(1)} async-done(((bf16[64,32,128]{2,1,0:T(8,128)(2,1)}), bf16[64,32,128]{2,1,0:T(8,128)(2,1)S(1)}, u32[]{:S(2)}, u32[]{:S(2)}) %all-to-all-start.1) | async-done | bytes 524320 | tf_op jit(solution)/shard_map/all_to_all | solution.py:660
  74.4 0.8 copy-done.4
  75.2 5.0 %shard_map.112 = (f32[8,2048]{1,0:T(8,128)}, f32[16,128]{1,0:T(8,128)}, bf16[1024,256]{1,0:T(8,128)(2,1)}) custom-call(bf16[704,2048]{1,0:T(8,128)(2,1)} %get-tuple-element.35.refs_0_, f32[512,2048]{1,0:T(8,128)} %get-tuple-element.36.refs_1_.refs_2_.refs_3_, bf16[2048,128]{1,0:T(8,128)(2,1)} %bitcast.32), custom_call_target="tpu_custom_call" | custom-call | flops 738197504 | bytes 8200192 | tf_op jit(solution)/shard_map/pallas_call | solution.py:185
  80.3 5.8 %all-to-all-start.2 = ((bf16[64,16,256]{2,1,0:T(8,128)(2,1)}), bf16[64,16,256]{2,1,0:T(8,128)(2,1)S(1)}, u32[]{:S(2)}, u32[]{:S(2)}) async-start(bf16[64,16,256]{2,1,0:T(8,128)(2,1)} %bitcast.36), calls=%async_computation.2 | async-start | bytes 1048576 | tf_op jit(solution)/shard_map/all_to_all | solution.py:660
  86.2 6.7 %shard_map.113.refs_7_ = bf16[4096,176]{1,0:T(8,128)(2,1)} custom-call(bf16[704,1024]{1,0:T(8,128)(2,1)} %get-tuple-element.40.refs_0_.refs_7_, bf16[704,1024]{1,0:T(8,128)(2,1)} %get-tuple-element.41.refs_1_, bf16[1024,1024]{1,0:T(8,128)(2,1)} %refs_6_.1, bf16[1024,1024]{1,0:T(8,128)(2,1)} %collective-permute-done.refs_1_.refs_3_.refs_7_, ...), custom_call_target="tpu_custom_call" | custom-call | flops 2952790016 | bytes 9043968 | tf_op jit(solution)/shard_map/pallas_call | solution.py:185
  92.9 4.4 %all-to-all-done.2 = bf16[64,16,256]{2,1,0:T(8,128)(2,1)S(1)} async-done(((bf16[64,16,256]{2,1,0:T(8,128)(2,1)}), bf16[64,16,256]{2,1,0:T(8,128)(2,1)S(1)}, u32[]{:S(2)}, u32[]{:S(2)}) %all-to-all-start.2) | async-done | bytes 524320 | tf_op jit(solution)/shard_map/all_to_all | solution.py:660
  97.3 0.8 copy-done.1
  98.1 9.2 %shard_map.114 = (bf16[512,1024]{1,0:T(8,128)(2,1)}, bf16[512,1024]{1,0:T(8,128)(2,1)}, f32[8,2048]{1,0:T(8,128)}, bf16[2048,608]{1,0:T(8,128)(2,1)}, bf16[1024,256]{1,0:T(8,128)(2,1)}) custom-call(bf16[704,2048]{1,0:T(8,128)(2,1)} %get-tuple-element.35.refs_0_, f32[8,2048]{1,0:T(8,128)} %get-tuple-element.38.refs_1_, ...), custom_call_target="tpu_custom_call" | custom-call | flops 2885681152 | bytes 19005440 | tf_op jit(solution)/shard_map/pallas_call | solution.py:185
  107.3 1.7 constant_dynamic-slice_fusion.2
  109.0 0.2 copy.15
  109.3 0.2 copy.19
  109.5 0.2 copy.17
  109.8 0.7 collective-permute-start.6
  110.5 1.9 %collective-permute-start.7 = (bf16[512,608]{0,1:T(8,128)(2,1)S(1)}, bf16[512,608]{0,1:T(8,128)(2,1)}, u32[]{:S(2)}, u32[]{:S(2)}) collective-permute-start(bf16[512,608]{0,1:T(8,128)(2,1)S(1)} %bitcast.34), channel_id=1, source_target_pairs={{0,18},{1,19},{2,0},{3,1},{4,22},{5,23},{6,4},{7,5},{8,26},{9,27},... | collective-permute-start | bytes 1867784 | tf_op jit(solution)/shard_map/ppermute | solution.py:671
  112.4 0.0 collective-permute-start.5
  112.4 3.5 %collective-permute-start.9 = (bf16[704,1024]{1,0:T(8,128)(2,1)}, bf16[704,1024]{1,0:T(8,128)(2,1)}, u32[]{:S(2)}, u32[]{:S(2)}) collective-permute-start(bf16[704,1024]{1,0:T(8,128)(2,1)} %get-tuple-element.41.refs_1_), channel_id=1, source_target_pairs={{0,1},{1,0},{2,3},{3,2},{4,5},{5,4},{6,7},{7,6},{8,9},{9,8},{10,11... | collective-permute-start | bytes 4325384 | tf_op jit(solution)/shard_map/ppermute | solution.py:657
  115.8 7.1 %all-to-all-start.3 = ((bf16[64,16,256]{2,1,0:T(8,128)(2,1)}), bf16[64,16,256]{2,1,0:T(8,128)(2,1)S(1)}, u32[]{:S(2)}, u32[]{:S(2)}) async-start(bf16[64,16,256]{2,1,0:T(8,128)(2,1)} %bitcast.37), calls=%async_computation.3 | async-start | bytes 1048576 | tf_op jit(solution)/shard_map/all_to_all | solution.py:660
  122.9 0.6 collective-permute-start.3
  123.5 4.6 %shard_map.115 = (bf16[64,1024]{1,0:T(8,128)(2,1)}, bf16[64,1024]{1,0:T(8,128)(2,1)}) custom-call(bf16[128,2048]{1,0:T(8,128)(2,1)} %get-tuple-element.34.refs_1_.refs_0_, f32[8,2048]{1,0:T(8,128)} %get-tuple-element.38.refs_1_, f32[8,2048]{1,0:T(8,128)} %get-tuple-element.44.refs_2_, f32[512,2048]{1,0:T(8,128)} %get-tuple-element.36.refs_1_.refs_2_.refs_3_, ...), custom_call_target="tpu_custom_call" | custom-call | flops 369098752 | bytes 5644288 | tf_op jit(solution)/shard_map/pallas_call | solution.py:185
  128.1 0.0 collective-permute-done.6
  128.1 1.4 copy.18
  129.5 9.1 %collective-permute-done.7 = bf16[512,608]{0,1:T(8,128)(2,1)} collective-permute-done((bf16[512,608]{0,1:T(8,128)(2,1)S(1)}, bf16[512,608]{0,1:T(8,128)(2,1)}, u32[]{:S(2)}, u32[]{:S(2)}) %collective-permute-start.7) | collective-permute-done | bytes 622624 | tf_op jit(solution)/shard_map/ppermute | solution.py:671
  138.6 1.4 copy.20
  139.9 1.8 collective-permute-done.5
  141.7 0.3 copy.16
  142.0 2.3 %fusion.2.refs_8_.terms_ref = bf16[512,608]{1,0:T(8,128)(2,1)} fusion(bf16[512,608]{1,0:T(8,128)(2,1)S(1)} %copy.20, bf16[512,608]{1,0:T(8,128)(2,1)S(1)} %copy.18, bf16[512,608]{1,0:T(8,128)(2,1)S(1)} %copy.16, bf16[4,512,608]{2,1,0:T(8,128)(2,1)} %bitcast.31, s32[]{:T(128)S(6)} %select_n.47), kind=kLoop, calls=%fused_computation.3 | loop fusion | flops 2490368 | bytes 3112964 | tf_op jit(solution)/shard_map/convert_element_type | solution.py:672
  144.3 2.5 %all-to-all-done.3 = bf16[64,16,256]{2,1,0:T(8,128)(2,1)S(1)} async-done(((bf16[64,16,256]{2,1,0:T(8,128)(2,1)}), bf16[64,16,256]{2,1,0:T(8,128)(2,1)S(1)}, u32[]{:S(2)}, u32[]{:S(2)}) %all-to-all-start.3) | async-done | bytes 524320 | tf_op jit(solution)/shard_map/all_to_all | solution.py:660
  146.8 0.8 copy-done.3
  147.6 5.7 %shard_map.116 = (bf16[64,1024]{1,0:T(8,128)(2,1)}, bf16[64,1024]{1,0:T(8,128)(2,1)}, bf16[1024,128]{1,0:T(8,128)(2,1)}, bf16[1024,128]{1,0:T(8,128)(2,1)}) custom-call(bf16[128,2048]{1,0:T(8,128)(2,1)} %get-tuple-element.34.refs_1_.refs_0_, bf16[2048,512]{1,0:T(8,128)(2,1)} %get-tuple-element.48.refs_1_, bf16[1024,256]{1,0:T(8,128)(2,1)} %bitcast.28, ...), custom_call_target="tpu_custom_call" | custom-call | flops 905969664 | bytes 9535488 | tf_op jit(solution)/shard_map/pallas_call | solution.py:185
  153.3 0.0 copy-start.5
  153.3 0.0 copy-start.7
  153.3 0.0 copy-start.9
  153.3 2.6 %shard_map.118 = bf16[1024,560]{1,0:T(8,128)(2,1)} custom-call(s32[1,1]{1,0:T(1,128)} %bitcast.refs_0_.core_ref, bf16[1024,128]{1,0:T(8,128)(2,1)} %get-tuple-element.57.wgrad_ref, bf16[512,608]{1,0:T(8,128)(2,1)} %fusion.2.refs_8_.terms_ref), custom_call_target="tpu_custom_call" | custom-call | bytes 524288 | tf_op jit(solution)/shard_map/pallas_call | solution.py:544
  155.9 6.6 %all-to-all-start.4 = ((bf16[128,8,560]{2,1,0:T(8,128)(2,1)}), bf16[128,8,560]{2,1,0:T(8,128)(2,1)S(1)}, u32[]{:S(2)}, u32[]{:S(2)}) async-start(bf16[128,8,560]{2,1,0:T(8,128)(2,1)} %bitcast.26), calls=%async_computation.4 | async-start | bytes 2621440 | tf_op jit(solution)/shard_map/all_to_all | solution.py:714
  162.5 0.0 copy-done.5
  162.5 1.1 collective-permute-start.10
  163.7 0.0 copy-done.7
  163.7 0.1 collective-permute-start.4
  163.8 0.4 collective-permute-start.8
  164.2 0.0 collective-permute-done.9.refs_8_
  164.2 0.8 collective-permute-done.4.refs_4_
  165.0 0.3 collective-permute-done.8.refs_6_
  165.4 0.0 collective-permute-done.10.refs_10_.other_ref
  165.4 0.0 collective-permute-done.3.refs_2_
  165.4 0.3 copy-done.8
  165.7 0.3 copy-done.10
  166.0 0.1 copy-done.6
  166.1 11.1 %shard_map.117 = (bf16[1024,1024]{1,0:T(8,128)(2,1)}, bf16[1024,1024]{1,0:T(8,128)(2,1)}) custom-call(s32[1,1]{1,0:T(1,128)} %bitcast.refs_0_.core_ref, bf16[512,1024]{1,0:T(8,128)(2,1)} %get-tuple-element.42.refs_1_, bf16[512,1024]{1,0:T(8,128)(2,1)} %collective-permute-done.3.refs_2_, bf16[64,1024]{1,0:T(8,128)(2,1)} %get-tuple-element.46.refs_4_.refs_3_, ...), custom_call_target="tpu_custom_call" | custom-call | flops 5200936960 | bytes 17039364 | tf_op jit(solution)/shard_map/pallas_call | solution.py:185
  177.2 7.3 %all-to-all-done.4 = bf16[128,8,560]{2,1,0:T(8,128)(2,1)S(1)} async-done(((bf16[128,8,560]{2,1,0:T(8,128)(2,1)}), bf16[128,8,560]{2,1,0:T(8,128)(2,1)S(1)}, u32[]{:S(2)}, u32[]{:S(2)}) %all-to-all-start.4) | async-done | bytes 1146912 | tf_op jit(solution)/shard_map/all_to_all | solution.py:714
  184.5 1.1 copy-done.2
  185.6 2.4 %shard_map.119 = (f32[8,128]{1,0:T(8,128)}, f32[8,128]{1,0:T(8,128)}, f32[8,1024]{1,0:T(8,128)}, f32[8,1024]{1,0:T(8,128)}) custom-call(s32[1,1]{1,0:T(1,128)} %bitcast.refs_0_.core_ref, bf16[1024,560]{1,0:T(8,128)(2,1)} %bitcast.27, bf16[1024,128]{1,0:T(8,128)(2,1)} %get-tuple-element.53.refs_9_.mine_ref, bf16[1024,128]{1,0:T(8,128)(2,1)} %copy-done.6, ...), custom_call_target="tpu_custom_call" | custom-call | bytes 1146880 | tf_op jit(solution)/shard_map/pallas_call | solution.py:630
  (9 shorter events, 0.0 us)
Async XLA Ops:
  3.0 44.6 %all-to-all-start = ((bf16[128,8,1152]{2,1,0:T(8,128)(2,1)}), bf16[128,8,1152]{2,1,0:T(8,128)(2,1)S(1)}, u32[]{:S(2)}, u32[]{:S(2)}) async-start(bf16[128,8,1152]{2,1,0:T(8,128)(2,1)} %bitcast.18), calls=%async_computation | async-start | bytes 4718592 | tf_op jit(solution)/shard_map/all_to_all | solution.py:688
  14.5 34.3 %collective-permute-start = (bf16[1024,1024]{1,0:T(8,128)(2,1)}, bf16[1024,1024]{1,0:T(8,128)(2,1)}, u32[]{:S(2)}, u32[]{:S(2)}) collective-permute-start(bf16[1024,1024]{1,0:T(8,128)(2,1)} %refs_6_.1), channel_id=1, source_target_pairs={{0,1},{1,0},{2,3},{3,2},{4,5},{5,4},{6,7},{7,6},{8,9},{9,8},{10,11... | collective-permute-start | bytes 6291464 | tf_op jit(solution)/shard_map/ppermute | solution.py:657
  47.6 1.4 copy-start
  47.6 15.1 %collective-permute-start.2 = (bf16[1024,1152]{1,0:T(8,128)(2,1)S(1)}, bf16[1024,1152]{1,0:T(8,128)(2,1)}, u32[]{:S(2)}, u32[]{:S(2)}) collective-permute-start(bf16[1024,1152]{1,0:T(8,128)(2,1)S(1)} %bitcast.19), channel_id=1, source_target_pairs={{0,1},{1,0},{2,3},{3,2},{4,5},{5,4},{6,7},{7,6},{8,9},{9,8},{10,11... | collective-permute-start | bytes 7077896 | tf_op jit(solution)/shard_map/ppermute | solution.py:657
  48.8 13.9 %collective-permute-start.1 = (bf16[1024,1024]{1,0:T(8,128)(2,1)}, bf16[1024,1024]{1,0:T(8,128)(2,1)}, u32[]{:S(2)}, u32[]{:S(2)}) collective-permute-start(bf16[1024,1024]{1,0:T(8,128)(2,1)} %refs_5_.1), channel_id=1, source_target_pairs={{0,1},{1,0},{2,3},{3,2},{4,5},{5,4},{6,7},{7,6},{8,9},{9,8},{10,11... | collective-permute-start | bytes 6291464 | tf_op jit(solution)/shard_map/ppermute | solution.py:657
  57.7 16.8 %all-to-all-start.1 = ((bf16[64,32,128]{2,1,0:T(8,128)(2,1)}), bf16[64,32,128]{2,1,0:T(8,128)(2,1)S(1)}, u32[]{:S(2)}, u32[]{:S(2)}) async-start(bf16[64,32,128]{2,1,0:T(8,128)(2,1)} %bitcast.38), calls=%async_computation.1 | async-start | bytes 1048576 | tf_op jit(solution)/shard_map/all_to_all | solution.py:660
  74.4 0.8 copy-start.4
  80.3 17.1 %all-to-all-start.2 = ((bf16[64,16,256]{2,1,0:T(8,128)(2,1)}), bf16[64,16,256]{2,1,0:T(8,128)(2,1)S(1)}, u32[]{:S(2)}, u32[]{:S(2)}) async-start(bf16[64,16,256]{2,1,0:T(8,128)(2,1)} %bitcast.36), calls=%async_computation.2 | async-start | bytes 1048576 | tf_op jit(solution)/shard_map/all_to_all | solution.py:660
  97.3 0.8 copy-start.1
  109.8 18.4 %collective-permute-start.6 = (bf16[512,608]{0,1:T(8,128)(2,1)S(1)}, bf16[512,608]{0,1:T(8,128)(2,1)}, u32[]{:S(2)}, u32[]{:S(2)}) collective-permute-start(bf16[512,608]{0,1:T(8,128)(2,1)S(1)} %bitcast.35), channel_id=1, source_target_pairs={{0,16},{1,17},{2,18},{3,19},{4,20},{5,21},{6,22},{7,23},{8,24},{9,... | collective-permute-start | bytes 1867784 | tf_op jit(solution)/shard_map/ppermute | solution.py:671
  110.5 28.1 %collective-permute-start.7 = (bf16[512,608]{0,1:T(8,128)(2,1)S(1)}, bf16[512,608]{0,1:T(8,128)(2,1)}, u32[]{:S(2)}, u32[]{:S(2)}) collective-permute-start(bf16[512,608]{0,1:T(8,128)(2,1)S(1)} %bitcast.34), channel_id=1, source_target_pairs={{0,18},{1,19},{2,0},{3,1},{4,22},{5,23},{6,4},{7,5},{8,26},{9,27},... | collective-permute-start | bytes 1867784 | tf_op jit(solution)/shard_map/ppermute | solution.py:671
  112.4 29.4 %collective-permute-start.5 = (bf16[512,608]{0,1:T(8,128)(2,1)S(1)}, bf16[512,608]{0,1:T(8,128)(2,1)S(1)}, u32[]{:S(2)}, u32[]{:S(2)}) collective-permute-start(bf16[512,608]{0,1:T(8,128)(2,1)S(1)} %bitcast.33), channel_id=1, source_target_pairs={{0,2},{1,3},{2,16},{3,17},{4,6},{5,7},{6,20},{7,21},{8,10},{9,11},... | collective-permute-start | bytes 1867784 | tf_op jit(solution)/shard_map/ppermute | solution.py:671
  112.4 51.8 %collective-permute-start.9 = (bf16[704,1024]{1,0:T(8,128)(2,1)}, bf16[704,1024]{1,0:T(8,128)(2,1)}, u32[]{:S(2)}, u32[]{:S(2)}) collective-permute-start(bf16[704,1024]{1,0:T(8,128)(2,1)} %get-tuple-element.41.refs_1_), channel_id=1, source_target_pairs={{0,1},{1,0},{2,3},{3,2},{4,5},{5,4},{6,7},{7,6},{8,9},{9,8},{10,11... | collective-permute-start | bytes 4325384 | tf_op jit(solution)/shard_map/ppermute | solution.py:657
  115.8 31.0 %all-to-all-start.3 = ((bf16[64,16,256]{2,1,0:T(8,128)(2,1)}), bf16[64,16,256]{2,1,0:T(8,128)(2,1)S(1)}, u32[]{:S(2)}, u32[]{:S(2)}) async-start(bf16[64,16,256]{2,1,0:T(8,128)(2,1)} %bitcast.37), calls=%async_computation.3 | async-start | bytes 1048576 | tf_op jit(solution)/shard_map/all_to_all | solution.py:660
  122.9 42.4 %collective-permute-start.3 = (bf16[512,1024]{1,0:T(8,128)(2,1)}, bf16[512,1024]{1,0:T(8,128)(2,1)}, u32[]{:S(2)}, u32[]{:S(2)}) collective-permute-start(bf16[512,1024]{1,0:T(8,128)(2,1)} %get-tuple-element.43), channel_id=1, source_target_pairs={{0,1},{1,0},{2,3},{3,2},{4,5},{5,4},{6,7},{7,6},{8,9},{9,8},{10,11... | collective-permute-start | bytes 3145736 | tf_op jit(solution)/shard_map/ppermute | solution.py:657
  146.8 0.8 copy-start.3
  153.3 9.2 %copy-start.5 = (bf16[1024,128]{1,0:T(8,128)(2,1)S(1)}, bf16[1024,128]{1,0:T(8,128)(2,1)}, u32[]{:S(2)}) copy-start(bf16[1024,128]{1,0:T(8,128)(2,1)} %get-tuple-element.53.refs_9_.mine_ref) | copy-start | bytes 786436
  153.3 10.3 %copy-start.7 = (bf16[64,1024]{1,0:T(8,128)(2,1)S(1)}, bf16[64,1024]{1,0:T(8,128)(2,1)}, u32[]{:S(2)}) copy-start(bf16[64,1024]{1,0:T(8,128)(2,1)} %get-tuple-element.47.refs_5_) | copy-start | bytes 393220
  153.3 10.4 %copy-start.9 = (bf16[64,1024]{1,0:T(8,128)(2,1)S(1)}, bf16[64,1024]{1,0:T(8,128)(2,1)}, u32[]{:S(2)}) copy-start(bf16[64,1024]{1,0:T(8,128)(2,1)} %get-tuple-element.52) | copy-start | bytes 393220
  155.9 28.6 %all-to-all-start.4 = ((bf16[128,8,560]{2,1,0:T(8,128)(2,1)}), bf16[128,8,560]{2,1,0:T(8,128)(2,1)S(1)}, u32[]{:S(2)}, u32[]{:S(2)}) async-start(bf16[128,8,560]{2,1,0:T(8,128)(2,1)} %bitcast.26), calls=%async_computation.4 | async-start | bytes 2621440 | tf_op jit(solution)/shard_map/all_to_all | solution.py:714
  162.5 2.9 %collective-permute-start.10 = (bf16[1024,128]{1,0:T(8,128)(2,1)S(1)}, bf16[1024,128]{1,0:T(8,128)(2,1)S(1)}, u32[]{:S(2)}, u32[]{:S(2)}) collective-permute-start(bf16[1024,128]{1,0:T(8,128)(2,1)S(1)} %copy-done.5), channel_id=1, source_target_pairs={{0,1},{1,0},{2,3},{3,2},{4,5},{5,4},{6,7},{7,6},{8,9},{9,8},{10,11... | collective-permute-start | bytes 786440 | tf_op jit(solution)/shard_map/ppermute | solution.py:657
  163.7 1.3 collective-permute-start.4
  163.8 1.6 collective-permute-start.8
  165.0 0.6 copy-start.8
  165.4 0.6 copy-start.10
  165.4 0.8 copy-start.6
  184.5 1.1 copy-start.2

commit v6 on v5

--- a/solution.py
+++ b/solution.py
@@ -99,8 +99,8 @@
     return (whole * band_weight((SPAD, DV), 0)).T.astype(BF)
 
 
-def call(body, count, ins, kinds, outs, out_kinds, scratch, flops):
-    block = min(BLOCK, count // 2 if "pair" in kinds or "pair1" in out_kinds else count)
+def call(body, count, ins, kinds, outs, out_kinds, scratch, flops, size=BLOCK):
+    block = min(size, count // 2 if "pair" in kinds or "pair1" in out_kinds else count)
     steps = count // block
 
     def pieces(x, kind):
@@ -210,7 +210,7 @@
 def weights_phase(w_query, w_key, w_value, w_out, chips, heads):
     qk, cols, half = heads * DK, heads * DV, w_out.shape[1] // 2
 
-    def body(q_ref, k_ref, v_ref, o_ref, out_ref):
+    def body(q_ref, k_ref, v_ref, o_ref, out_ref, pair_ref, sems):
         query, key, value, rest = (ref[...].astype(F32) for ref in (q_ref, k_ref, v_ref, o_ref))
         halves = [
             jnp.concatenate(
@@ -224,14 +224,21 @@
             )
             for c in range(2)
         ]
-        pair = jnp.concatenate(halves, axis=0).astype(BF)
-        for p in range(chips):
-            out_ref[p * pair.shape[0] : (p + 1) * pair.shape[0], :] = pair
+        pair_ref[...] = jnp.concatenate(halves, axis=0).astype(BF)
+        copies = [
+            pltpu.make_async_copy(pair_ref, out_ref.at[pl.ds(2 * rows * p, 2 * rows), :], sems.at[p]) for p in range(chips)
+        ]
+        for copy in copies:
+            copy.start()
+        for copy in copies:
+            copy.wait()
 
     rows = w_query.shape[0]
     return pl.pallas_call(
         body,
+        out_specs=pl.BlockSpec(memory_space=pl.ANY),
         out_shape=shape((2 * chips * rows, 2 * qk + cols + half), BF),
+        scratch_shapes=[pltpu.VMEM((2 * rows, 2 * qk + cols + half), BF), pltpu.SemaphoreType.DMA((chips,))],
         compiler_params=pltpu.CompilerParams(vmem_limit_bytes=VMEM),
         cost_estimate=pl.CostEstimate(flops=0, bytes_accessed=2 * 2 * chips * rows * (2 * qk + cols + half), transcendentals=0),
     )(w_query, w_key, w_value, w_out)
@@ -315,30 +322,32 @@
     )
 
 
-def product_phase(rows_t, slabs, after, parts):
+def product_phase(turn, rows_t, slabs, after, parts):
     rows, count = rows_t[0].shape[0], 2 * rows_t[0].shape[1]
     size = rows // parts
     width = slabs[0].shape[1]
 
-    def body(at_first, at_last, rows_ref, slab_ref, after_ref, out_ref, acc):
+    def body(at_first, at_last, turn_ref, rows_ref, slab_ref, after_ref, *refs):
+        out_refs, acc = refs[:parts], refs[parts]
         at_first(lambda: clear(acc))
         acc[...] += dot(rows_ref[...], slab_ref[...], (1, 0))
 
         @at_last
         def _():
-            for part in range(parts):
-                out_ref[part * width : (part + 1) * width, :] = acc[part * size : (part + 1) * size, :].T.astype(BF)
+            for k in range(parts):
+                part = turn_ref[0, 0] ^ k
+                out_refs[k][...] = acc[pl.ds(pl.multiple_of(part * size, 16), size), :].T.astype(BF)
 
     return call(
         body,
         count,
-        (rows_t, slabs, after),
-        ("pair1", "pair", "any"),
-        (shape((parts * width, size), BF),),
-        (None,),
+        (turn, rows_t, slabs, after),
+        ("scalar", "pair1", "pair", "any"),
+        (shape((width, size), BF),) * parts,
+        (None,) * parts,
         [pltpu.VMEM((rows, width), F32)],
         2 * count * rows * width,
-    )[0]
+    )
 
 
 def query_phase(feats, up_t, first, chips, heads):
@@ -383,14 +392,14 @@
     )
 
 
-def attend_phase(feats, scales, up_t, second, cot, moments, chips, heads):
+def attend_phase(turn, feats, scales, up_t, second, cot, chips, heads):
     count = up_t.shape[1]
     width = cot[0].shape[1]
     quarter = width // 4
 
     def body(
-        at_first, at_last, feat_ref, scale_ref, up_ref, state_ref, sgrad_ref, slab_ref, moment_ref,
-        att_ref, den_ref, out_ref, sent_ref, turned, acc, out_acc,
+        at_first, at_last, turn_ref, feat_ref, scale_ref, up_ref, state_ref, sgrad_ref, slab_ref,
+        att_ref, den_ref, sent_ref, out0, out1, out2, out3, turned, acc, out_acc,
     ):
         at_first(lambda: clear(acc, out_acc))
 
@@ -423,25 +432,22 @@
             both = jnp.concatenate([sgrad_own, ngrad], axis=1)
             for p in range(chips):
                 sent_ref[p * both.shape[0] : (p + 1) * both.shape[0], :] = both
-            for k in range(4):
-                rows = slice(k * heads * DV, (k + 1) * heads * DV)
-                out_ref[rows, :quarter] = out_acc[:, k * quarter : (k + 1) * quarter].astype(BF)
-                for j in range(2):
-                    part = moment_ref[(2 * k + j) * heads * DV : (2 * k + j + 1) * heads * DV, :]
-                    out_ref[rows, quarter + j * FPAD : quarter + (j + 1) * FPAD] = part
+            for k, out_ref in enumerate((out0, out1, out2, out3)):
+                part = turn_ref[0, 0] ^ k
+                out_ref[...] = out_acc[:, pl.ds(pl.multiple_of(part * quarter, 128), quarter)].astype(BF)
 
     return call(
         body,
         count,
-        (feats, scales, up_t, second, second, cot, moments),
-        (1, 1, 1, (DV, 1), (DV, 0), "pair", None),
+        (turn, feats, scales, up_t, second, second, cot),
+        ("scalar", 1, 1, 1, (DV, 1), (DV, 0), "pair"),
         (
             (shape((heads * DV, count // 2), BF),) * 2,
             shape((8, count), F32),
-            shape((4 * heads * DV, quarter + 2 * FPAD), BF),
             shape(second.shape, BF),
-        ),
-        ("pair1", 1, None, None),
+        )
+        + (shape((heads * DV, quarter), BF),) * 4,
+        ("pair1", 1) + (None,) * 5,
         [
             pltpu.VMEM((heads, DV, SPAD), BF),
             pltpu.VMEM((heads, SPAD, 128), F32),
@@ -476,12 +482,12 @@
     )
 
 
-def key_phase(qk_t, value, third, qgrads, tokens, after, heads):
+def key_phase(qk_t, value, third, qgrads, tokens, terms, heads):
     count, qk = value.shape[0], heads * DK
     width = tokens[0].shape[1]
 
     def body(
-        at_first, at_last, qk_ref, value_ref, sgrad_ref, rows_ref, qgrad_ref, slab_ref, after_ref,
+        at_first, at_last, qk_ref, value_ref, sgrad_ref, rows_ref, qgrad_ref, slab_ref, terms_ref,
         kgrad_ref, copy_ref, sent_ref, acc, ngrad_ref,
     ):
         at_first(lambda: clear(acc))
@@ -508,17 +514,18 @@
 
         @at_last
         def _():
-            sent_ref[...] = acc[...].T.astype(BF)
+            sent_ref[:, : 2 * qk] = acc[...].T.astype(BF)
+            sent_ref[:, 2 * qk :] = terms_ref[...]
 
     return call(
         body,
         count,
-        (qk_t, value, third, third, qgrads, tokens, after),
-        (1, 0, (DV, 0), (DV, 1), "pair1", "pair", "any"),
+        (qk_t, value, third, third, qgrads, tokens, terms),
+        (1, 0, (DV, 0), (DV, 1), "pair1", "pair", None),
         (
             (shape((qk, count // 2), BF),) * 2,
             shape((third.shape[0], DV), BF),
-            shape((width, 2 * qk), BF),
+            shape((width, 2 * qk + terms.shape[1]), BF),
         ),
         ("pair1", None, None),
         [pltpu.VMEM((2 * qk, width), F32), pltpu.VMEM((16, DV), F32)],
@@ -526,29 +533,32 @@
     )
 
 
-def last_payload(core, wgrad, along_x):
-    rows, cols = wgrad.shape
-    half = along_x.shape[0]
-    quarter = along_x.shape[1] - 2 * FPAD
-
-    def body(core_ref, wgrad_ref, terms_ref, sent_ref):
+def terms_phase(core, moments, outs):
+    rows = moments[0].shape[0]
+    half, quarter = outs[0].shape
+
+    def body(at_first, at_last, core_ref, m0, m1, m2, m3, o0, o1, o2, o3, sent_ref):
         first = core_ref[0, 0] == 0
-        sent_ref[:, :cols] = wgrad_ref[...]
-        for j in range(2):
-            here = slice(j * half, (j + 1) * half)
-            sent_ref[here, cols : cols + FPAD] = terms_ref[:, quarter + j * FPAD : quarter + (j + 1) * FPAD]
-            out = terms_ref[:, :quarter]
-            sent_ref[here, cols + FPAD :] = jnp.where(first == (j == 0), out, jnp.zeros_like(out))
-
-    vmem = pl.BlockSpec(memory_space=pltpu.VMEM)
-    return pl.pallas_call(
-        body,
-        in_specs=[pl.BlockSpec(memory_space=pltpu.SMEM)] + [vmem] * 2,
-        out_specs=vmem,
-        out_shape=shape((rows, cols + FPAD + quarter), BF),
-        compiler_params=pltpu.CompilerParams(vmem_limit_bytes=VMEM),
-        cost_estimate=pl.CostEstimate(flops=0, bytes_accessed=4 * rows * cols, transcendentals=0),
-    )(core, wgrad, along_x)
+        sent_ref[:, :FPAD] = sum(ref[...].astype(F32) for ref in (m0, m1, m2, m3)).astype(BF)
+
+        def put(here):
+            out = sum(ref[...].astype(F32) for ref in (o0, o1, o2, o3))
+            sent_ref[:, FPAD:] = jnp.where(here, out, 0.0).astype(BF)
+
+        at_first(lambda: put(first))
+        at_last(lambda: put(jnp.logical_not(first)))
+
+    return call(
+        body,
+        rows,
+        (core, *moments, *outs),
+        ("scalar",) + (0,) * 4 + (None,) * 4,
+        (shape((rows, FPAD + quarter), BF),),
+        (0,),
+        [],
+        0,
+        half,
+    )[0]
 
 
 def outputs_phase(core, attended, qgrads, kgrads, feats, sgrads, weights, w_out, heads):
@@ -602,10 +612,11 @@
         out = [jnp.zeros((2 * rows, quarter), F32) for _ in range(4)]
         for p in range(n // 2):
             both = recv_ref[2 * rows * p : 2 * rows * (p + 1), :].astype(F32)
-            x = 2 * ((p // 8) % 2) + p % 2
+            y = p // 16
+            in_yz, in_xy = 2 * (y % 2) + p // 2 % 2, 2 * (p % 2) + 1 - y % 2
             wgrad = wgrad + both[:, : 2 * qk]
-            moment[x] = moment[x] + both[:, 2 * qk : 2 * qk + FPAD]
-            out[x] = out[x] + both[:, 2 * qk + FPAD :]
+            moment[in_yz] = moment[in_yz] + both[:, 2 * qk : 2 * qk + FPAD]
+            out[in_xy] = out[in_xy] + both[:, 2 * qk + FPAD :]
         for x in range(4):
             out_ref[:, x * quarter : (x + 1) * quarter] = (out[x][:rows] + out[x][rows:]) * scale_factor
         wgrad = wgrad * scale_factor
@@ -659,17 +670,20 @@
     def spread(x):
         return lax.all_to_all(x, AXES, 0, 0, axis_index_groups=same_core, tiled=True)
 
-    def add_along_x(x):
-        quarters = x.reshape((4, -1) + x.shape[1:])
-        total = lax.dynamic_index_in_dim(quarters, me_x, 0, keepdims=False).astype(F32)
+    def among_four(flips, parts):
+        found = [parts[0]]
         for step in (1, 2, 3):
             moves = []
             for i in range(n):
-                y, at, z, c = place(i)
-                moves.append((i, device(y, (at + step) % 4, z, c)))
-            there = lax.dynamic_index_in_dim(quarters, (me_x + step) % 4, 0, keepdims=False)
-            total = total + lax.ppermute(there, AXES, moves).astype(F32)
-        return total.astype(BF)
+                at = place(i)
+                for bit in (0, 1):
+                    at = flips[bit](*at) if step >> bit & 1 else at
+                moves.append((i, device(*at)))
+            found.append(lax.ppermute(parts[step], AXES, moves))
+        return found
+
+    yz = (lambda y, x, z, c: (y, x, z ^ 1, c), lambda y, x, z, c: (y ^ 1, x, z, c))
+    xy = (lambda y, x, z, c: ((y + 2 * (y % 2) - 1) % 4, x, z, c), lambda y, x, z, c: (y, x ^ 1, z, c))
 
     def place(i):
         return (i // 32, 2 * (i // 16 % 2) + i // 2 % 2, i // 4 % 4, i % 2)
@@ -681,8 +695,10 @@
         return x.reshape(chips, -1, x.shape[1])
 
     ctx, seq = lax.axis_index("ctx"), lax.axis_index("seq")
-    me_x = 2 * (ctx // 4 % 2) + seq // 2
-    along_x = [[device(y, x, z, c) for x in range(4)] for y in range(4) for z in range(4) for c in range(2)]
+    in_yz, in_xy = (
+        v.astype(jnp.int32).reshape(1, 1)
+        for v in (2 * (ctx // 8 % 2) + ctx % 2, 2 * (seq // 2) + 1 - ctx // 8 % 2)
+    )
 
     to_send = weights_phase(w_query, w_key, w_value, w_out, chips, heads)
     weights = lax.all_to_all(to_send.reshape(n, -1, to_send.shape[1]), AXES, 0, 0, tiled=True)
@@ -696,21 +712,20 @@
     key_feats = (key_feat, exchange(key_feat_sent))
 
     up_t, query_feat, w_out_whole = upstream_phase(core_at, qk_t, cot, weights, other_weights, heads)
+    moments = among_four(yz, product_phase(in_yz, (key_feat, key_feat_sent), tok, up_t, heads))
     scales, norm, sent = query_phase(query_feat, up_t, first, chips, heads)
     second = spread(to_each(sent)).reshape(sent.shape)
-    moments = product_phase((key_feat, key_feat_sent), tok, sent, heads)
-
-    attended, attended_sent, dens, terms, sent = attend_phase(
-        query_feat, scales, up_t, second, cot, moments, chips, heads
+
+    attended, attended_sent, dens, sent, *outs = attend_phase(
+        in_xy, query_feat, scales, up_t, second, cot, chips, heads
     )
     third = spread(to_each(sent)).reshape(sent.shape)
-    terms = add_along_x(terms)
+    terms = terms_phase(core_at, moments, among_four(xy, outs))
     attendeds = (attended, exchange(attended_sent))
     qgrad, qgrad_sent = query_back_phase(qk_t, scales, dens, up_t, second, norm, heads)
     qgrads = (qgrad, exchange(qgrad_sent))
 
-    kgrad, kgrad_sent, sgrad, wgrad = key_phase(qk_t, value, third, (qgrad, qgrad_sent), tok, terms, heads)
-    sent = last_payload(core_at, wgrad, terms)
+    kgrad, kgrad_sent, sgrad, sent = key_phase(qk_t, value, third, (qgrad, qgrad_sent), tok, terms, heads)
     fourth = lax.all_to_all(sent.reshape(n, -1, sent.shape[1]), AXES, 0, 0, tiled=True).reshape(sent.shape)
     kgrads, sgrads = (kgrad, exchange(kgrad_sent)), (sgrad, exchange(sgrad))
     mixed, grad_tokens = outputs_phase(

time: 189 us -> 183 us (0.968)
  starting transfers between devices: 46.6 us -> 59.7 us
  waiting for transfers between devices: 62.3 us -> 49.3 us
  local copies, waits for them, and re-layouts: 9.91 us -> 5.72 us
  other arithmetic: 2.25 us -> 0 us
    ppermute x3 -> x6, starting transfers between devices: 2.61 us -> 11.4 us  [among_four(): found.append(lax.ppermute(parts[step], AXES, moves))]
    all_to_all x3, waiting for transfers between devices: 11.1 us -> 4.19 us  [spread(): lax.all_to_all(x, AXES, 0, 0, axis_index_groups=same_core, tiled=True)]
    ppermute x3 -> x6, waiting for transfers between devices: 10.9 us -> 5.06 us  [among_four(): found.append(lax.ppermute(parts[step], AXES, moves))]
    ppermute x3 -> x0, local copies, waits for them, and re-layouts: 3.03 us -> none  [add_along_x(): total = total + lax.ppermute(there, AXES, moves).astype(F32)]
    all_to_all x3, starting transfers between devices: 17.9 us -> 20.9 us  [spread(): lax.all_to_all(x, AXES, 0, 0, axis_index_groups=same_core, tiled=True)]
    pallas_call x8 -> x9, Pallas kernels: 58.5 us -> 61.2 us  [call(): pl.pallas_call(kernel, in_specs=[pl.BlockSpec(memory_space=space) for spa...]
    all_to_all x1, starting transfers between devices: 6.58 us -> 9.03 us  [per_device(): lax.all_to_all(sent.reshape(n, -1, sent.shape[1]), AXES, 0, 0, tiled=True)]
    dynamic_slice x4 -> x0, local copies, waits for them, and re-layouts: 2.39 us -> none  [add_along_x(): lax.dynamic_index_in_dim(quarters, (me_x + step) % 4, 0, keepdims=False)]
  transfers between devices with their start and end apart: 16 -> 19, of which waited for: 9 -> 8; matrix products, arithmetic and copies ran while one was open for 3% -> 0% of each run, Pallas kernels for 25% -> 31%
where the time goes in v6:
time: 183 us; the launch traced here: 182 us
  Pallas kernels  66.4 us (36%)
  starting transfers between devices  59.7 us (33%)
  waiting for transfers between devices  49.3 us (27%)
  local copies, waits for them, and re-layouts  5.72 us (3%)
    pallas_call x9, Pallas kernels, call(): pl.pallas_call(kernel, in_specs=[pl.BlockSpec(memory_space=space) for spa...  61.2 us
    all_to_all x1, waiting for transfers between devices, per_device(): lax.all_to_all(to_send.reshape(n, -1, to_send.shape[1]), AXES, 0, 0, tile...  31.9 us
    all_to_all x3, starting transfers between devices, spread(): lax.all_to_all(x, AXES, 0, 0, axis_index_groups=same_core, tiled=True)  20.9 us
    all_to_all x1, starting transfers between devices, per_device(): lax.all_to_all(to_send.reshape(n, -1, to_send.shape[1]), AXES, 0, 0, tile...  11.5 us
    ppermute x6, starting transfers between devices, among_four(): found.append(lax.ppermute(parts[step], AXES, moves))  11.4 us
    all_to_all x1, starting transfers between devices, per_device(): lax.all_to_all(sent.reshape(n, -1, sent.shape[1]), AXES, 0, 0, tiled=True)  9.03 us
    all_to_all x1, waiting for transfers between devices, per_device(): lax.all_to_all(sent.reshape(n, -1, sent.shape[1]), AXES, 0, 0, tiled=True)  6.91 us
    ppermute x8, starting transfers between devices, exchange(): return lax.ppermute(x, AXES, swap)  6.89 us
  transfers between devices with their start and end apart: 19, of which 8 were waited for; matrix products, arithmetic and copies ran while one was open for 0% of the time, Pallas kernels for 31%

profile of v6, /device:TPU:1, one launch (start us, length us, event | category | flops | bytes accessed | tf_op | source)
XLA Modules:
  0.0 182.1 jit_solution(2787819457810661276)
XLA Ops:
  0.6 2.8 %shard_map.109 = bf16[1024,1152]{1,0:T(8,128)(2,1)} custom-call(bf16[8,128]{1,0:T(8,128)(2,1)} %q_ref.1, bf16[8,128]{1,0:T(8,128)(2,1)} %k_ref.1, bf16[8,1024]{1,0:T(8,128)(2,1)} %v_ref.1, bf16[8,1024]{1,0:T(8,128)(2,1)} %o_ref.1), custom_call_target="tpu_custom_call" | custom-call | bytes 2359296 | tf_op jit(solution)/shard_map/pallas_call | solution.py:237
  3.5 11.5 %all-to-all-start = ((bf16[128,8,1152]{2,1,0:T(8,128)(2,1)}), bf16[128,8,1152]{2,1,0:T(8,128)(2,1)S(1)}, u32[]{:S(2)}, u32[]{:S(2)}) async-start(bf16[128,8,1152]{2,1,0:T(8,128)(2,1)} %bitcast.13), calls=%async_computation | async-start | bytes 4718592 | tf_op jit(solution)/shard_map/all_to_all | solution.py:704
  15.0 1.1 collective-permute-start
  16.1 31.9 %all-to-all-done = bf16[128,8,1152]{2,1,0:T(8,128)(2,1)S(1)} async-done(((bf16[128,8,1152]{2,1,0:T(8,128)(2,1)}), bf16[128,8,1152]{2,1,0:T(8,128)(2,1)S(1)}, u32[]{:S(2)}, u32[]{:S(2)}) %all-to-all-start) | async-done | bytes 2359328 | tf_op jit(solution)/shard_map/all_to_all | solution.py:704
  48.1 1.2 collective-permute-start.2
  49.2 0.0 collective-permute-start.1
  49.3 0.0 collective-permute-done.refs_1_.refs_4_.refs_7_
  49.3 0.3 copy-done
  49.6 8.7 %shard_map.110 = (bf16[128,2048]{1,0:T(8,128)(2,1)}, bf16[2048,512]{1,0:T(8,128)(2,1)}, bf16[704,1024]{1,0:T(8,128)(2,1)}, bf16[704,1024]{1,0:T(8,128)(2,1)}, bf16[2048,128]{1,0:T(8,128)(2,1)}) custom-call(bf16[1024,1024]{1,0:T(8,128)(2,1)} %refs_6_.3, bf16[1024,1024]{1,0:T(8,128)(2,1)} %collective-permute-done.refs_1_.refs_4_.refs_7_, ...), custom_call_target="tpu_custom_call" | custom-call | flops 3422552064 | bytes 12582912 | tf_op jit(solution)/shard_map/pallas_call | solution.py:185
  58.2 5.0 %all-to-all-start.1 = ((bf16[64,32,128]{2,1,0:T(8,128)(2,1)}), bf16[64,32,128]{2,1,0:T(8,128)(2,1)S(1)}, u32[]{:S(2)}, u32[]{:S(2)}) async-start(bf16[64,32,128]{2,1,0:T(8,128)(2,1)} %bitcast.28), calls=%async_computation.1 | async-start | bytes 1048576 | tf_op jit(solution)/shard_map/all_to_all | solution.py:671
  63.2 0.0 collective-permute-done.1.refs_3_.refs_7_
  63.2 0.0 collective-permute-done.2.refs_5_.refs_12_
  63.2 7.6 %shard_map.111 = (f32[512,2048]{1,0:T(8,128)}, bf16[704,2048]{1,0:T(8,128)(2,1)}, bf16[1024,1024]{1,0:T(8,128)(2,1)}) custom-call(s32[1,1]{1,0:T(1,128)} %bitcast.refs_0_.core_ref, bf16[128,2048]{1,0:T(8,128)(2,1)} %get-tuple-element.41.refs_1_.refs_0_, bf16[1024,1024]{1,0:T(8,128)(2,1)} %refs_6_.2, ...), custom_call_target="tpu_custom_call" | custom-call | flops 2147483648 | bytes 18612228 | tf_op jit(solution)/shard_map/pallas_call | solution.py:185
  70.8 4.2 %all-to-all-done.1 = bf16[64,32,128]{2,1,0:T(8,128)(2,1)S(1)} async-done(((bf16[64,32,128]{2,1,0:T(8,128)(2,1)}), bf16[64,32,128]{2,1,0:T(8,128)(2,1)S(1)}, u32[]{:S(2)}, u32[]{:S(2)}) %all-to-all-start.1) | async-done | bytes 524320 | tf_op jit(solution)/shard_map/all_to_all | solution.py:671
  75.0 0.8 copy-done.4
  75.8 5.1 %shard_map.112 = (f32[8,2048]{1,0:T(8,128)}, f32[16,128]{1,0:T(8,128)}, bf16[1024,256]{1,0:T(8,128)(2,1)}) custom-call(bf16[704,2048]{1,0:T(8,128)(2,1)} %get-tuple-element.42.refs_0_.refs_1_, f32[512,2048]{1,0:T(8,128)} %get-tuple-element.43.refs_1_.refs_3_.refs_5_, bf16[2048,128]{1,0:T(8,128)(2,1)} %bitcast.24), custom_call_target="tpu_custom_call" | custom-call | flops 738197504 | bytes 8200192 | tf_op jit(solution)/shard_map/pallas_call | solution.py:185
  80.9 5.8 %all-to-all-start.2 = ((bf16[64,16,256]{2,1,0:T(8,128)(2,1)}), bf16[64,16,256]{2,1,0:T(8,128)(2,1)S(1)}, u32[]{:S(2)}, u32[]{:S(2)}) async-start(bf16[64,16,256]{2,1,0:T(8,128)(2,1)} %bitcast.26), calls=%async_computation.2 | async-start | bytes 1048576 | tf_op jit(solution)/shard_map/all_to_all | solution.py:671
  86.7 1.7 collective-permute-start.12
  88.4 7.0 %shard_map.115 = (bf16[1024,176]{1,0:T(8,128)(2,1)}, bf16[1024,176]{1,0:T(8,128)(2,1)}, bf16[1024,176]{1,0:T(8,128)(2,1)}, bf16[1024,176]{1,0:T(8,128)(2,1)}) custom-call(s32[1,1]{1,0:T(1,128)} %bitcast.10.refs_0_, bf16[704,1024]{1,0:T(8,128)(2,1)} %get-tuple-element.55.refs_1_.refs_7_, bf16[704,1024]{1,0:T(8,128)(2,1)} %get-tuple-element.56.refs_2_, ...), custom_call_target="tpu_custom_call" | custom-call | flops 2952790016 | bytes 12713988 | tf_op jit(solution)/shard_map/pallas_call | solution.py:185
  95.4 1.4 collective-permute-start.5
  96.8 1.2 collective-permute-start.6
  98.0 0.2 collective-permute-start.7
  98.2 0.0 all-to-all-done.2
  98.2 0.8 copy-done.1
  99.0 7.8 %shard_map.113 = (bf16[512,1024]{1,0:T(8,128)(2,1)}, bf16[512,1024]{1,0:T(8,128)(2,1)}, f32[8,2048]{1,0:T(8,128)}, bf16[1024,256]{1,0:T(8,128)(2,1)}, bf16[512,2...) custom-call(s32[1,1]{1,0:T(1,128)} %bitcast.1.refs_0_, ...), custom_call_target="tpu_custom_call" | custom-call | flops 2885681152 | bytes 16121860 | tf_op jit(solution)/shard_map/pallas_call | solution.py:185
  106.8 10.1 %all-to-all-start.3 = ((bf16[64,16,256]{2,1,0:T(8,128)(2,1)}), bf16[64,16,256]{2,1,0:T(8,128)(2,1)S(1)}, u32[]{:S(2)}, u32[]{:S(2)}) async-start(bf16[64,16,256]{2,1,0:T(8,128)(2,1)} %bitcast.27), calls=%async_computation.3 | async-start | bytes 1048576 | tf_op jit(solution)/shard_map/all_to_all | solution.py:671
  116.9 1.2 collective-permute-start.3
  118.2 0.0 collective-permute-done.5.refs_2_
  118.2 2.7 %collective-permute-start.8 = (bf16[512,256]{1,0:T(8,128)(2,1)}, bf16[512,256]{1,0:T(8,128)(2,1)S(1)}, u32[]{:S(2)}, u32[]{:S(2)}) collective-permute-start(bf16[512,256]{1,0:T(8,128)(2,1)} %get-tuple-element.62), channel_id=1, source_target_pairs={{0,96},{1,97},{2,98},{3,99},{4,100},{5,101},{6,102},{7,103},{8,104... | collective-permute-start | bytes 786440 | tf_op jit(solution)/shard_map/ppermute | solution.py:682
  120.9 0.0 collective-permute-done.6.refs_3_
  120.9 1.2 collective-permute-start.9
  122.1 1.9 %collective-permute-done.7.refs_4_ = bf16[1024,176]{1,0:T(8,128)(2,1)S(1)} collective-permute-done((bf16[1024,176]{1,0:T(8,128)(2,1)}, bf16[1024,176]{1,0:T(8,128)(2,1)S(1)}, u32[]{:S(2)}, u32[]{:S(2)}) %collective-permute-start.7) | collective-permute-done | bytes 360480 | tf_op jit(solution)/shard_map/ppermute | solution.py:682
  124.0 4.8 %collective-permute-start.10 = (bf16[512,256]{1,0:T(8,128)(2,1)}, bf16[512,256]{1,0:T(8,128)(2,1)S(1)}, u32[]{:S(2)}, u32[]{:S(2)}) collective-permute-start(bf16[512,256]{1,0:T(8,128)(2,1)} %get-tuple-element.64), channel_id=1, source_target_pairs={{0,98},{1,99},{2,96},{3,97},{4,102},{5,103},{6,100},{7,101},{8,106... | collective-permute-start | bytes 786440 | tf_op jit(solution)/shard_map/ppermute | solution.py:682
  128.8 4.6 %shard_map.114 = (bf16[64,1024]{1,0:T(8,128)(2,1)}, bf16[64,1024]{1,0:T(8,128)(2,1)}) custom-call(bf16[128,2048]{1,0:T(8,128)(2,1)} %get-tuple-element.41.refs_1_.refs_0_, f32[8,2048]{1,0:T(8,128)} %get-tuple-element.45.refs_2_.refs_1_, f32[8,2048]{1,0:T(8,128)} %get-tuple-element.49.refs_2_, f32[512,2048]{1,0:T(8,128)} %get-tuple-element.43.refs_1_.refs_3_.refs_5_, ...), custom_call_target="tpu_custom_call" | custom-call | flops 369098752 | bytes 5644288 | tf_op jit(solution)/shard_map/pallas_call | solution.py:185
  133.4 2.5 %collective-permute-done.8.refs_6_ = bf16[512,256]{1,0:T(8,128)(2,1)S(1)} collective-permute-done((bf16[512,256]{1,0:T(8,128)(2,1)}, bf16[512,256]{1,0:T(8,128)(2,1)S(1)}, u32[]{:S(2)}, u32[]{:S(2)}) %collective-permute-start.8) | collective-permute-done | bytes 262176 | tf_op jit(solution)/shard_map/ppermute | solution.py:682
  135.9 0.0 collective-permute-done.9.refs_7_
  135.9 0.6 collective-permute-done.10.refs_8_
  136.5 0.1 copy-done.10
  136.6 0.1 copy-done.11
  136.7 0.5 copy-done.12
  137.2 3.0 %shard_map.116.refs_8_ = bf16[1024,432]{1,0:T(8,128)(2,1)} custom-call(s32[1,1]{1,0:T(1,128)} %bitcast.refs_0_.core_ref, bf16[1024,176]{1,0:T(8,128)(2,1)} %get-tuple-element.57.refs_1_, bf16[1024,176]{1,0:T(8,128)(2,1)} %copy-done.5, bf16[1024,176]{1,0:T(8,128)(2,1)} %copy-done.6, bf16[1024,176]{1,0:T(8,128)(2,1)} %copy-done.7, ...), custom_call_target="tpu_custom_call" | custom-call | bytes 3375108 | tf_op jit(solution)/shard_map/pallas_call | solution.py:185
  140.3 0.0 all-to-all-done.3
  140.3 0.0 copy-start.3
  140.3 0.8 copy-done.3
  141.1 6.4 %shard_map.117 = (bf16[64,1024]{1,0:T(8,128)(2,1)}, bf16[64,1024]{1,0:T(8,128)(2,1)}, bf16[1024,128]{1,0:T(8,128)(2,1)}, bf16[1024,560]{1,0:T(8,128)(2,1)}) custom-call(bf16[128,2048]{1,0:T(8,128)(2,1)} %get-tuple-element.41.refs_1_.refs_0_, bf16[2048,512]{1,0:T(8,128)(2,1)} %get-tuple-element.53.refs_1_, bf16[1024,256]{1,0:T(8,128)(2,1)} %bitcast.22, ...), custom_call_target="tpu_custom_call" | custom-call | flops 905969664 | bytes 10682368 | tf_op jit(solution)/shard_map/pallas_call | solution.py:185
  147.6 9.0 %all-to-all-start.4 = ((bf16[128,8,560]{2,1,0:T(8,128)(2,1)}), bf16[128,8,560]{2,1,0:T(8,128)(2,1)S(1)}, u32[]{:S(2)}, u32[]{:S(2)}) async-start(bf16[128,8,560]{2,1,0:T(8,128)(2,1)} %bitcast.25), calls=%async_computation.4 | async-start | bytes 2621440 | tf_op jit(solution)/shard_map/all_to_all | solution.py:729
  156.6 1.1 collective-permute-start.13
  157.8 0.0 copy-done.13
  157.8 0.1 collective-permute-start.4
  157.9 0.0 copy-done.17
  157.9 0.4 collective-permute-start.11
  158.3 0.0 collective-permute-done.12.refs_8_
  158.3 0.8 collective-permute-done.4.refs_4_
  159.1 0.3 collective-permute-done.11.refs_6_
  159.5 0.0 collective-permute-done.13.refs_10_.other_ref
  159.5 0.0 collective-permute-done.3.refs_2_
  159.5 0.3 copy-done.15
  159.8 0.3 copy-done.16
  160.1 0.1 copy-done.9
  160.2 0.4 copy-done.14
  160.6 11.1 %shard_map.118 = (bf16[1024,1024]{1,0:T(8,128)(2,1)}, bf16[1024,1024]{1,0:T(8,128)(2,1)}) custom-call(s32[1,1]{1,0:T(1,128)} %bitcast.refs_0_.core_ref, bf16[512,1024]{1,0:T(8,128)(2,1)} %get-tuple-element.47.refs_1_, bf16[512,1024]{1,0:T(8,128)(2,1)} %copy-done.14, bf16[64,1024]{1,0:T(8,128)(2,1)} %get-tuple-element.51.refs_4_.refs_3_, ...), custom_call_target="tpu_custom_call" | custom-call | flops 5200936960 | bytes 17039364 | tf_op jit(solution)/shard_map/pallas_call | solution.py:185
  171.7 6.9 %all-to-all-done.4 = bf16[128,8,560]{2,1,0:T(8,128)(2,1)S(1)} async-done(((bf16[128,8,560]{2,1,0:T(8,128)(2,1)}), bf16[128,8,560]{2,1,0:T(8,128)(2,1)S(1)}, u32[]{:S(2)}, u32[]{:S(2)}) %all-to-all-start.4) | async-done | bytes 1146912 | tf_op jit(solution)/shard_map/all_to_all | solution.py:729
  178.6 1.1 copy-done.2
  179.7 2.4 %shard_map.119 = (f32[8,128]{1,0:T(8,128)}, f32[8,128]{1,0:T(8,128)}, f32[8,1024]{1,0:T(8,128)}, f32[8,1024]{1,0:T(8,128)}) custom-call(s32[1,1]{1,0:T(1,128)} %bitcast.refs_0_.core_ref, bf16[1024,560]{1,0:T(8,128)(2,1)} %bitcast.21, bf16[1024,128]{1,0:T(8,128)(2,1)} %get-tuple-element.67.refs_9_.mine_ref, bf16[1024,128]{1,0:T(8,128)(2,1)} %copy-done.9, ...), custom_call_target="tpu_custom_call" | custom-call | bytes 1146880 | tf_op jit(solution)/shard_map/pallas_call | solution.py:641
  (21 shorter events, 0.0 us)
Async XLA Ops:
  3.5 44.6 %all-to-all-start = ((bf16[128,8,1152]{2,1,0:T(8,128)(2,1)}), bf16[128,8,1152]{2,1,0:T(8,128)(2,1)S(1)}, u32[]{:S(2)}, u32[]{:S(2)}) async-start(bf16[128,8,1152]{2,1,0:T(8,128)(2,1)} %bitcast.13), calls=%async_computation | async-start | bytes 4718592 | tf_op jit(solution)/shard_map/all_to_all | solution.py:704
  15.0 34.3 %collective-permute-start = (bf16[1024,1024]{1,0:T(8,128)(2,1)}, bf16[1024,1024]{1,0:T(8,128)(2,1)}, u32[]{:S(2)}, u32[]{:S(2)}) collective-permute-start(bf16[1024,1024]{1,0:T(8,128)(2,1)} %refs_6_.3), channel_id=1, source_target_pairs={{0,1},{1,0},{2,3},{3,2},{4,5},{5,4},{6,7},{7,6},{8,9},{9,8},{10,11... | collective-permute-start | bytes 6291464 | tf_op jit(solution)/shard_map/ppermute | solution.py:668
  48.1 1.5 copy-start
  48.1 15.2 %collective-permute-start.2 = (bf16[1024,1152]{1,0:T(8,128)(2,1)S(1)}, bf16[1024,1152]{1,0:T(8,128)(2,1)}, u32[]{:S(2)}, u32[]{:S(2)}) collective-permute-start(bf16[1024,1152]{1,0:T(8,128)(2,1)S(1)} %bitcast.14), channel_id=1, source_target_pairs={{0,1},{1,0},{2,3},{3,2},{4,5},{5,4},{6,7},{7,6},{8,9},{9,8},{10,11... | collective-permute-start | bytes 7077896 | tf_op jit(solution)/shard_map/ppermute | solution.py:668
  49.2 14.0 %collective-permute-start.1 = (bf16[1024,1024]{1,0:T(8,128)(2,1)}, bf16[1024,1024]{1,0:T(8,128)(2,1)}, u32[]{:S(2)}, u32[]{:S(2)}) collective-permute-start(bf16[1024,1024]{1,0:T(8,128)(2,1)} %refs_6_.2), channel_id=1, source_target_pairs={{0,1},{1,0},{2,3},{3,2},{4,5},{5,4},{6,7},{7,6},{8,9},{9,8},{10,11... | collective-permute-start | bytes 6291464 | tf_op jit(solution)/shard_map/ppermute | solution.py:668
  58.2 16.8 %all-to-all-start.1 = ((bf16[64,32,128]{2,1,0:T(8,128)(2,1)}), bf16[64,32,128]{2,1,0:T(8,128)(2,1)S(1)}, u32[]{:S(2)}, u32[]{:S(2)}) async-start(bf16[64,32,128]{2,1,0:T(8,128)(2,1)} %bitcast.28), calls=%async_computation.1 | async-start | bytes 1048576 | tf_op jit(solution)/shard_map/all_to_all | solution.py:671
  75.0 0.8 copy-start.4
  80.9 17.3 %all-to-all-start.2 = ((bf16[64,16,256]{2,1,0:T(8,128)(2,1)}), bf16[64,16,256]{2,1,0:T(8,128)(2,1)S(1)}, u32[]{:S(2)}, u32[]{:S(2)}) async-start(bf16[64,16,256]{2,1,0:T(8,128)(2,1)} %bitcast.26), calls=%async_computation.2 | async-start | bytes 1048576 | tf_op jit(solution)/shard_map/all_to_all | solution.py:671
  86.7 71.6 %collective-permute-start.12 = (bf16[704,1024]{1,0:T(8,128)(2,1)}, bf16[704,1024]{1,0:T(8,128)(2,1)}, u32[]{:S(2)}, u32[]{:S(2)}) collective-permute-start(bf16[704,1024]{1,0:T(8,128)(2,1)} %get-tuple-element.56.refs_2_), channel_id=1, source_target_pairs={{0,1},{1,0},{2,3},{3,2},{4,5},{5,4},{6,7},{7,6},{8,9},{9,8},{10,11... | collective-permute-start | bytes 4325384 | tf_op jit(solution)/shard_map/ppermute | solution.py:668
  95.4 22.7 %collective-permute-start.5 = (bf16[1024,176]{1,0:T(8,128)(2,1)}, bf16[1024,176]{1,0:T(8,128)(2,1)S(1)}, u32[]{:S(2)}, u32[]{:S(2)}) collective-permute-start(bf16[1024,176]{1,0:T(8,128)(2,1)} %get-tuple-element.58), channel_id=1, source_target_pairs={{0,4},{1,5},{2,6},{3,7},{4,0},{5,1},{6,2},{7,3},{8,12},{9,13},{10,... | collective-permute-start | bytes 1081352 | tf_op jit(solution)/shard_map/ppermute | solution.py:682
  96.8 24.1 %collective-permute-start.6 = (bf16[1024,176]{1,0:T(8,128)(2,1)}, bf16[1024,176]{1,0:T(8,128)(2,1)S(1)}, u32[]{:S(2)}, u32[]{:S(2)}) collective-permute-start(bf16[1024,176]{1,0:T(8,128)(2,1)} %get-tuple-element.59), channel_id=1, source_target_pairs={{0,32},{1,33},{2,34},{3,35},{4,36},{5,37},{6,38},{7,39},{8,40},{9,... | collective-permute-start | bytes 1081352 | tf_op jit(solution)/shard_map/ppermute | solution.py:682
  98.0 26.0 %collective-permute-start.7 = (bf16[1024,176]{1,0:T(8,128)(2,1)}, bf16[1024,176]{1,0:T(8,128)(2,1)S(1)}, u32[]{:S(2)}, u32[]{:S(2)}) collective-permute-start(bf16[1024,176]{1,0:T(8,128)(2,1)} %get-tuple-element.60), channel_id=1, source_target_pairs={{0,36},{1,37},{2,38},{3,39},{4,32},{5,33},{6,34},{7,35},{8,44},{9,... | collective-permute-start | bytes 1081352 | tf_op jit(solution)/shard_map/ppermute | solution.py:682
  98.2 0.8 copy-start.1
  106.8 33.5 %all-to-all-start.3 = ((bf16[64,16,256]{2,1,0:T(8,128)(2,1)}), bf16[64,16,256]{2,1,0:T(8,128)(2,1)S(1)}, u32[]{:S(2)}, u32[]{:S(2)}) async-start(bf16[64,16,256]{2,1,0:T(8,128)(2,1)} %bitcast.27), calls=%async_computation.3 | async-start | bytes 1048576 | tf_op jit(solution)/shard_map/all_to_all | solution.py:671
  116.9 42.6 %collective-permute-start.3 = (bf16[512,1024]{1,0:T(8,128)(2,1)}, bf16[512,1024]{1,0:T(8,128)(2,1)S(1)}, u32[]{:S(2)}, u32[]{:S(2)}) collective-permute-start(bf16[512,1024]{1,0:T(8,128)(2,1)} %get-tuple-element.48), channel_id=1, source_target_pairs={{0,1},{1,0},{2,3},{3,2},{4,5},{5,4},{6,7},{7,6},{8,9},{9,8},{10,11... | collective-permute-start | bytes 3145736 | tf_op jit(solution)/shard_map/ppermute | solution.py:668
  118.2 15.2 %copy-start.5 = (bf16[1024,176]{1,0:T(8,128)(2,1)}, bf16[1024,176]{1,0:T(8,128)(2,1)S(1)}, u32[]{:S(2)}) copy-start(bf16[1024,176]{1,0:T(8,128)(2,1)S(1)} %collective-permute-done.5.refs_2_) | copy-start | bytes 1081348
  118.2 17.8 %collective-permute-start.8 = (bf16[512,256]{1,0:T(8,128)(2,1)}, bf16[512,256]{1,0:T(8,128)(2,1)S(1)}, u32[]{:S(2)}, u32[]{:S(2)}) collective-permute-start(bf16[512,256]{1,0:T(8,128)(2,1)} %get-tuple-element.62), channel_id=1, source_target_pairs={{0,96},{1,97},{2,98},{3,99},{4,100},{5,101},{6,102},{7,103},{8,104... | collective-permute-start | bytes 786440 | tf_op jit(solution)/shard_map/ppermute | solution.py:682
  120.9 12.5 %copy-start.6 = (bf16[1024,176]{1,0:T(8,128)(2,1)}, bf16[1024,176]{1,0:T(8,128)(2,1)S(1)}, u32[]{:S(2)}) copy-start(bf16[1024,176]{1,0:T(8,128)(2,1)S(1)} %collective-permute-done.6.refs_3_) | copy-start | bytes 1081348
  120.9 15.0 %collective-permute-start.9 = (bf16[512,256]{1,0:T(8,128)(2,1)}, bf16[512,256]{1,0:T(8,128)(2,1)S(1)}, u32[]{:S(2)}, u32[]{:S(2)}) collective-permute-start(bf16[512,256]{1,0:T(8,128)(2,1)} %get-tuple-element.63), channel_id=1, source_target_pairs={{0,2},{1,3},{2,0},{3,1},{4,6},{5,7},{6,4},{7,5},{8,10},{9,11},{10,... | collective-permute-start | bytes 786440 | tf_op jit(solution)/shard_map/ppermute | solution.py:682
  124.0 9.4 %copy-start.7 = (bf16[1024,176]{1,0:T(8,128)(2,1)}, bf16[1024,176]{1,0:T(8,128)(2,1)S(1)}, u32[]{:S(2)}) copy-start(bf16[1024,176]{1,0:T(8,128)(2,1)S(1)} %collective-permute-done.7.refs_4_) | copy-start | bytes 1081348
  124.0 12.5 %collective-permute-start.10 = (bf16[512,256]{1,0:T(8,128)(2,1)}, bf16[512,256]{1,0:T(8,128)(2,1)S(1)}, u32[]{:S(2)}, u32[]{:S(2)}) collective-permute-start(bf16[512,256]{1,0:T(8,128)(2,1)} %get-tuple-element.64), channel_id=1, source_target_pairs={{0,98},{1,99},{2,96},{3,97},{4,102},{5,103},{6,100},{7,101},{8,106... | collective-permute-start | bytes 786440 | tf_op jit(solution)/shard_map/ppermute | solution.py:682
  135.9 0.7 copy-start.10
  135.9 0.8 copy-start.11
  136.5 0.7 copy-start.12
  140.3 0.8 copy-start.3
  147.5 9.1 %copy-start.8 = (bf16[1024,128]{1,0:T(8,128)(2,1)S(1)}, bf16[1024,128]{1,0:T(8,128)(2,1)}, u32[]{:S(2)}) copy-start(bf16[1024,128]{1,0:T(8,128)(2,1)} %get-tuple-element.67.refs_9_.mine_ref) | copy-start | bytes 786436
  147.6 10.2 %copy-start.13 = (bf16[64,1024]{1,0:T(8,128)(2,1)S(1)}, bf16[64,1024]{1,0:T(8,128)(2,1)}, u32[]{:S(2)}) copy-start(bf16[64,1024]{1,0:T(8,128)(2,1)} %get-tuple-element.52.refs_5_) | copy-start | bytes 393220
  147.6 10.3 %copy-start.17 = (bf16[64,1024]{1,0:T(8,128)(2,1)S(1)}, bf16[64,1024]{1,0:T(8,128)(2,1)}, u32[]{:S(2)}) copy-start(bf16[64,1024]{1,0:T(8,128)(2,1)} %get-tuple-element.66) | copy-start | bytes 393220
  147.6 31.0 %all-to-all-start.4 = ((bf16[128,8,560]{2,1,0:T(8,128)(2,1)}), bf16[128,8,560]{2,1,0:T(8,128)(2,1)S(1)}, u32[]{:S(2)}, u32[]{:S(2)}) async-start(bf16[128,8,560]{2,1,0:T(8,128)(2,1)} %bitcast.25), calls=%async_computation.4 | async-start | bytes 2621440 | tf_op jit(solution)/shard_map/all_to_all | solution.py:729
  156.6 2.9 %collective-permute-start.13 = (bf16[1024,128]{1,0:T(8,128)(2,1)S(1)}, bf16[1024,128]{1,0:T(8,128)(2,1)S(1)}, u32[]{:S(2)}, u32[]{:S(2)}) collective-permute-start(bf16[1024,128]{1,0:T(8,128)(2,1)S(1)} %copy-done.8), channel_id=1, source_target_pairs={{0,1},{1,0},{2,3},{3,2},{4,5},{5,4},{6,7},{7,6},{8,9},{9,8},{10,11... | collective-permute-start | bytes 786440 | tf_op jit(solution)/shard_map/ppermute | solution.py:668
  157.8 1.3 collective-permute-start.4
  157.9 1.6 collective-permute-start.11
  159.1 0.7 copy-start.15
  159.5 0.6 copy-start.16
  159.5 0.8 copy-start.9
  159.5 1.1 copy-start.14
  178.6 1.1 copy-start.2

commit v7 on v6

--- a/solution.py
+++ b/solution.py
@@ -109,6 +109,8 @@
             return pieces_of(0, half, x[0].shape, kind) + pieces_of(1, half, x[1].shape, kind)
         if kind in (0, 1):
             return pieces_of(0, steps, x.shape, kind)
+        if kind == "late":
+            return [(0, pl.ds(0, x.shape[0]), pl.ds(0, x.shape[1]))]
         if kind is not None and kind[0] == "from":
             return [(0, pl.ds(0, x.shape[0]), pl.ds(kind[1], x.shape[1] - kind[1]))]
         if kind is not None:
@@ -146,9 +148,9 @@
         own = refs
 
         reads, at = [[] for _ in range(steps)], 0
-        for source, buffer, plan in zip(given, held, plans):
+        for source, buffer, plan, kind in zip(given, held, plans, kinds):
             for i, (which, rows, cols) in enumerate(plan):
-                reads[i].append(pltpu.make_async_copy(source[which].at[rows, cols], buffer[i], arrived.at[at]))
+                reads[steps - 1 if kind == "late" else i].append(pltpu.make_async_copy(source[which].at[rows, cols], buffer[i], arrived.at[at]))
                 at += 1
         writes, at = [], 0
         for target, buffer, plan in zip(made, sent, out_plans):
@@ -162,9 +164,11 @@
         for i in range(steps):
             for copy in reads[i]:
                 copy.wait()
+            at_first = lambda fn, i=i: fn() if i == 0 else None
+            at_first.block = i
             body(
-                lambda fn: fn() if i == 0 else None,
-                lambda fn: fn() if i == steps - 1 else None,
+                at_first,
+                lambda fn, i=i: fn() if i == steps - 1 else None,
                 *[buffer[min(i, len(buffer) - 1)] if buffer else source[0] for buffer, source in zip(held, given)],
                 *[buffer[min(i, len(buffer) - 1)] for buffer in sent],
                 *own,
@@ -224,10 +228,11 @@
             )
             for c in range(2)
         ]
-        pair_ref[...] = jnp.concatenate(halves, axis=0).astype(BF)
-        copies = [
-            pltpu.make_async_copy(pair_ref, out_ref.at[pl.ds(2 * rows * p, 2 * rows), :], sems.at[p]) for p in range(chips)
-        ]
+        pair = jnp.concatenate(halves, axis=0).astype(BF)
+        for p in range(chips // 8):
+            pair_ref[2 * rows * p : 2 * rows * (p + 1), :] = pair
+        part = pair_ref.shape[0]
+        copies = [pltpu.make_async_copy(pair_ref, out_ref.at[pl.ds(part * k, part), :], sems.at[k]) for k in range(8)]
         for copy in copies:
             copy.start()
         for copy in copies:
@@ -238,7 +243,7 @@
         body,
         out_specs=pl.BlockSpec(memory_space=pl.ANY),
         out_shape=shape((2 * chips * rows, 2 * qk + cols + half), BF),
-        scratch_shapes=[pltpu.VMEM((2 * rows, 2 * qk + cols + half), BF), pltpu.SemaphoreType.DMA((chips,))],
+        scratch_shapes=[pltpu.VMEM((2 * rows * (chips // 8), 2 * qk + cols + half), BF), pltpu.SemaphoreType.DMA((8,))],
         compiler_params=pltpu.CompilerParams(vmem_limit_bytes=VMEM),
         cost_estimate=pl.CostEstimate(flops=0, bytes_accessed=2 * 2 * chips * rows * (2 * qk + cols + half), transcendentals=0),
     )(w_query, w_key, w_value, w_out)
@@ -482,12 +487,12 @@
     )
 
 
-def key_phase(qk_t, value, third, qgrads, tokens, terms, heads):
+def key_phase(qk_t, value, third, qgrads, tokens, core, moments, outs, heads):
     count, qk = value.shape[0], heads * DK
     width = tokens[0].shape[1]
 
     def body(
-        at_first, at_last, qk_ref, value_ref, sgrad_ref, rows_ref, qgrad_ref, slab_ref, terms_ref,
+        at_first, at_last, qk_ref, value_ref, sgrad_ref, rows_ref, qgrad_ref, slab_ref, core_ref, m0, m1, m2, m3, o0, o1, o2, o3,
         kgrad_ref, copy_ref, sent_ref, acc, ngrad_ref,
     ):
         at_first(lambda: clear(acc))
@@ -515,50 +520,27 @@
         @at_last
         def _():
             sent_ref[:, : 2 * qk] = acc[...].T.astype(BF)
-            sent_ref[:, 2 * qk :] = terms_ref[...]
+            sent_ref[:, 2 * qk : 2 * qk + FPAD] = sum(ref[...].astype(F32) for ref in (m0, m1, m2, m3)).astype(BF)
+            first = core_ref[0, 0] == 0
+            out = sum(ref[...].astype(F32) for ref in (o0, o1, o2, o3))
+            half = out.shape[0]
+            for j in range(2):
+                sent_ref[j * half : (j + 1) * half, 2 * qk + FPAD :] = jnp.where(first == (j == 0), out, 0.0).astype(BF)
 
     return call(
         body,
         count,
-        (qk_t, value, third, third, qgrads, tokens, terms),
-        (1, 0, (DV, 0), (DV, 1), "pair1", "pair", None),
+        (qk_t, value, third, third, qgrads, tokens, core, *moments, *outs),
+        (1, 0, (DV, 0), (DV, 1), "pair1", "pair", "scalar") + ("late",) * 8,
         (
             (shape((qk, count // 2), BF),) * 2,
             shape((third.shape[0], DV), BF),
-            shape((width, 2 * qk + terms.shape[1]), BF),
+            shape((width, 2 * qk + FPAD + outs[0].shape[1]), BF),
         ),
         ("pair1", None, None),
         [pltpu.VMEM((2 * qk, width), F32), pltpu.VMEM((16, DV), F32)],
         2 * count * (heads * FPAD * DV + 2 * qk * width),
     )
-
-
-def terms_phase(core, moments, outs):
-    rows = moments[0].shape[0]
-    half, quarter = outs[0].shape
-
-    def body(at_first, at_last, core_ref, m0, m1, m2, m3, o0, o1, o2, o3, sent_ref):
-        first = core_ref[0, 0] == 0
-        sent_ref[:, :FPAD] = sum(ref[...].astype(F32) for ref in (m0, m1, m2, m3)).astype(BF)
-
-        def put(here):
-            out = sum(ref[...].astype(F32) for ref in (o0, o1, o2, o3))
-            sent_ref[:, FPAD:] = jnp.where(here, out, 0.0).astype(BF)
-
-        at_first(lambda: put(first))
-        at_last(lambda: put(jnp.logical_not(first)))
-
-    return call(
-        body,
-        rows,
-        (core, *moments, *outs),
-        ("scalar",) + (0,) * 4 + (None,) * 4,
-        (shape((rows, FPAD + quarter), BF),),
-        (0,),
-        [],
-        0,
-        half,
-    )[0]
 
 
 def outputs_phase(core, attended, qgrads, kgrads, feats, sgrads, weights, w_out, heads):
@@ -601,56 +583,68 @@
 
 
 def finish_phase(core, fourth, sgrads, after, heads, scale_factor):
-    rows, qk, n = 8, heads * DK, fourth.shape[0] // 8
+    rows, qk = 8, heads * DK
     quarter = fourth.shape[1] - 2 * qk - FPAD
 
-    def body(core_ref, recv_ref, mine_ref, other_ref, *refs):
-        query_ref, key_ref, value_ref, out_ref = refs[-4:]
-        first = core_ref[0, 0] == 0
-        wgrad = jnp.zeros((2 * rows, 2 * qk), F32)
-        moment = [jnp.zeros((2 * rows, FPAD), F32) for _ in range(heads)]
-        out = [jnp.zeros((2 * rows, quarter), F32) for _ in range(4)]
-        for p in range(n // 2):
-            both = recv_ref[2 * rows * p : 2 * rows * (p + 1), :].astype(F32)
-            y = p // 16
-            in_yz, in_xy = 2 * (y % 2) + p // 2 % 2, 2 * (p % 2) + 1 - y % 2
-            wgrad = wgrad + both[:, : 2 * qk]
-            moment[in_yz] = moment[in_yz] + both[:, 2 * qk : 2 * qk + FPAD]
-            out[in_xy] = out[in_xy] + both[:, 2 * qk + FPAD :]
-        for x in range(4):
-            out_ref[:, x * quarter : (x + 1) * quarter] = (out[x][:rows] + out[x][rows:]) * scale_factor
-        wgrad = wgrad * scale_factor
-        query_ref[...] = jnp.concatenate([wgrad[:rows, :qk], wgrad[rows:, :qk]], axis=1)
-        key_ref[...] = jnp.concatenate([wgrad[:rows, qk:], wgrad[rows:, qk:]], axis=1)
-        weight = band_weight((1, FPAD), 1) * scale_factor
-        found = [[], []]
-        for head in range(heads):
-            whole = moment[head] * weight
-            high = whole.astype(BF)
-            parts = jnp.concatenate([high, (whole - high.astype(F32)).astype(BF)], axis=0)
-            for which, ref in enumerate((mine_ref, other_ref)):
-                both = dot(parts, ref[head * SPAD : head * SPAD + FPAD, :], (1, 0))
-                both = both[: 2 * rows] + both[2 * rows :]
-                low, up = both[:rows], both[rows:]
-                found[which].append(jnp.where(first, low, up) if which == 0 else jnp.where(first, up, low))
-        mine, other = (jnp.concatenate(part, axis=1) for part in found)
-        value_ref[:, : heads * DV] = jnp.where(first, mine, other)
-        value_ref[:, heads * DV :] = jnp.where(first, other, mine)
-
-    vmem = pl.BlockSpec(memory_space=pltpu.VMEM)
-    return pl.pallas_call(
-        body,
-        in_specs=[pl.BlockSpec(memory_space=pltpu.SMEM)] + [vmem] * 3 + [pl.BlockSpec(memory_space=pl.ANY)] * len(after),
-        out_specs=[vmem] * 4,
-        out_shape=(
+    def body(at_first, at_last, core_ref, recv_ref, mine_ref, other_ref, *refs):
+        query_ref, key_ref, value_ref, out_ref, wgrad, moment, out = refs[-7:]
+
+        at_first(lambda: clear(wgrad, moment, out))
+        odd = at_first.block % 2
+        wgrad[...] += add_chips(recv_ref.at[:, pl.ds(0, 2 * qk)], 2 * rows)
+        parts = recv_ref.shape[0] // (2 * rows)
+        for which in range(2):
+            some = [p for p in range(parts) if p // 2 % 2 == which]
+            moment[2 * odd + which] += sum(
+                recv_ref[2 * rows * p : 2 * rows * (p + 1), 2 * qk : 2 * qk + FPAD].astype(F32) for p in some
+            )
+            some = [p for p in range(parts) if p % 2 == which]
+            out[2 * which + 1 - odd] += sum(
+                recv_ref[2 * rows * p : 2 * rows * (p + 1), 2 * qk + FPAD :].astype(F32) for p in some
+            )
+        @at_last
+        def _():
+            for x in range(4):
+                out_ref[:, x * quarter : (x + 1) * quarter] = (out[x, :rows] + out[x, rows:]) * scale_factor
+            first = core_ref[0, 0] == 0
+            both = wgrad[...] * scale_factor
+            query_ref[...] = jnp.concatenate([both[:rows, :qk], both[rows:, :qk]], axis=1)
+            key_ref[...] = jnp.concatenate([both[:rows, qk:], both[rows:, qk:]], axis=1)
+            weight = band_weight((1, FPAD), 1) * scale_factor
+            found = [[], []]
+            for head in range(heads):
+                whole = moment[head] * weight
+                high = whole.astype(BF)
+                split = jnp.concatenate([high, (whole - high.astype(F32)).astype(BF)], axis=0)
+                for which, ref in enumerate((mine_ref, other_ref)):
+                    both = dot(split, ref[head * SPAD : head * SPAD + FPAD, :], (1, 0))
+                    both = both[: 2 * rows] + both[2 * rows :]
+                    low, up = both[:rows], both[rows:]
+                    found[which].append(jnp.where(first, low, up) if which == 0 else jnp.where(first, up, low))
+            mine, other = (jnp.concatenate(part, axis=1) for part in found)
+            value_ref[:, : heads * DV] = jnp.where(first, mine, other)
+            value_ref[:, heads * DV :] = jnp.where(first, other, mine)
+
+    return call(
+        body,
+        fourth.shape[0],
+        (core, fourth, *sgrads, *after),
+        ("scalar", 0, "late", "late") + ("any",) * len(after),
+        (
             shape((rows, 2 * qk), F32),
             shape((rows, 2 * qk), F32),
             shape((rows, 2 * heads * DV), F32),
             shape((rows, 4 * quarter), F32),
         ),
-        compiler_params=pltpu.CompilerParams(vmem_limit_bytes=VMEM),
-        cost_estimate=pl.CostEstimate(flops=0, bytes_accessed=fourth.size * 2, transcendentals=0),
-    )(core, fourth, *sgrads, *after)
+        (None,) * 4,
+        [
+            pltpu.VMEM((2 * rows, 2 * qk), F32),
+            pltpu.VMEM((heads, 2 * rows, FPAD), F32),
+            pltpu.VMEM((4, 2 * rows, quarter), F32),
+        ],
+        0,
+        fourth.shape[0] // 4,
+    )
 
 
 def per_device(chips, tokens, w_query, w_key, w_value, w_out, cotangent):
@@ -720,12 +714,12 @@
         in_xy, query_feat, scales, up_t, second, cot, chips, heads
     )
     third = spread(to_each(sent)).reshape(sent.shape)
-    terms = terms_phase(core_at, moments, among_four(xy, outs))
+    outs = among_four(xy, outs)
     attendeds = (attended, exchange(attended_sent))
     qgrad, qgrad_sent = query_back_phase(qk_t, scales, dens, up_t, second, norm, heads)
     qgrads = (qgrad, exchange(qgrad_sent))
 
-    kgrad, kgrad_sent, sgrad, sent = key_phase(qk_t, value, third, (qgrad, qgrad_sent), tok, terms, heads)
+    kgrad, kgrad_sent, sgrad, sent = key_phase(qk_t, value, third, (qgrad, qgrad_sent), tok, core_at, moments, outs, heads)
     fourth = lax.all_to_all(sent.reshape(n, -1, sent.shape[1]), AXES, 0, 0, tiled=True).reshape(sent.shape)
     kgrads, sgrads = (kgrad, exchange(kgrad_sent)), (sgrad, exchange(sgrad))
     mixed, grad_tokens = outputs_phase(

time: 183 us -> 179 us (0.978)
  Pallas kernels: 66.4 us -> 63.1 us
    pallas_call x1 -> x0, Pallas kernels: 2.39 us -> none  [finish_phase(): pl.pallas_call(body, in_specs=[pl.BlockSpec(memory_space=pltpu.SMEM)] + [...]
    unnamed x36 -> x34, local copies, waits for them, and re-layouts: 5.72 us -> 4.71 us
  transfers between devices with their start and end apart: 19 -> 19, of which waited for: 8 -> 8; matrix products, arithmetic and copies ran while one was open for 0% -> 0% of each run, Pallas kernels for 31% -> 30%
where the time goes in v7:
time: 179 us; the launch traced here: 178 us
  Pallas kernels  63.1 us (35%)
  starting transfers between devices  59.9 us (33%)
  waiting for transfers between devices  49.5 us (28%)
  local copies, waits for them, and re-layouts  4.71 us (3%)
    pallas_call x9, Pallas kernels, call(): pl.pallas_call(kernel, in_specs=[pl.BlockSpec(memory_space=space) for spa...  60.8 us
    all_to_all x1, waiting for transfers between devices, per_device(): lax.all_to_all(to_send.reshape(n, -1, to_send.shape[1]), AXES, 0, 0, tile...  31.9 us
    all_to_all x3, starting transfers between devices, spread(): lax.all_to_all(x, AXES, 0, 0, axis_index_groups=same_core, tiled=True)  20.8 us
    ppermute x6, starting transfers between devices, among_four(): found.append(lax.ppermute(parts[step], AXES, moves))  11.6 us
    all_to_all x1, starting transfers between devices, per_device(): lax.all_to_all(to_send.reshape(n, -1, to_send.shape[1]), AXES, 0, 0, tile...  11.5 us
    all_to_all x1, starting transfers between devices, per_device(): lax.all_to_all(sent.reshape(n, -1, sent.shape[1]), AXES, 0, 0, tiled=True)  9.01 us
    all_to_all x1, waiting for transfers between devices, per_device(): lax.all_to_all(sent.reshape(n, -1, sent.shape[1]), AXES, 0, 0, tiled=True)  7.25 us
    ppermute x8, starting transfers between devices, exchange(): return lax.ppermute(x, AXES, swap)  6.93 us
  transfers between devices with their start and end apart: 19, of which 8 were waited for; matrix products, arithmetic and copies ran while one was open for 0% of the time, Pallas kernels for 30%

profile of v7, /device:TPU:1, one launch (start us, length us, event | category | flops | bytes accessed | tf_op | source)
XLA Modules:
  0.0 178.3 jit_solution(4629447164652972380)
XLA Ops:
  0.6 2.3 %shard_map.109 = bf16[1024,1152]{1,0:T(8,128)(2,1)} custom-call(bf16[8,128]{1,0:T(8,128)(2,1)} %q_ref.1, bf16[8,128]{1,0:T(8,128)(2,1)} %k_ref.1, bf16[8,1024]{1,0:T(8,128)(2,1)} %v_ref.1, bf16[8,1024]{1,0:T(8,128)(2,1)} %o_ref.1), custom_call_target="tpu_custom_call" | custom-call | bytes 2359296 | tf_op jit(solution)/shard_map/pallas_call | solution.py:242
  3.0 11.5 %all-to-all-start = ((bf16[128,8,1152]{2,1,0:T(8,128)(2,1)}), bf16[128,8,1152]{2,1,0:T(8,128)(2,1)S(1)}, u32[]{:S(2)}, u32[]{:S(2)}) async-start(bf16[128,8,1152]{2,1,0:T(8,128)(2,1)} %bitcast.13), calls=%async_computation | async-start | bytes 4718592 | tf_op jit(solution)/shard_map/all_to_all | solution.py:698
  14.5 1.1 collective-permute-start
  15.6 31.9 %all-to-all-done = bf16[128,8,1152]{2,1,0:T(8,128)(2,1)S(1)} async-done(((bf16[128,8,1152]{2,1,0:T(8,128)(2,1)}), bf16[128,8,1152]{2,1,0:T(8,128)(2,1)S(1)}, u32[]{:S(2)}, u32[]{:S(2)}) %all-to-all-start) | async-done | bytes 2359328 | tf_op jit(solution)/shard_map/all_to_all | solution.py:698
  47.6 1.2 collective-permute-start.2
  48.8 0.0 collective-permute-start.1
  48.8 0.0 collective-permute-done.refs_1_.refs_4_.refs_7_
  48.8 0.3 copy-done
  49.1 8.6 %shard_map.110 = (bf16[128,2048]{1,0:T(8,128)(2,1)}, bf16[2048,512]{1,0:T(8,128)(2,1)}, bf16[704,1024]{1,0:T(8,128)(2,1)}, bf16[704,1024]{1,0:T(8,128)(2,1)}, bf16[2048,128]{1,0:T(8,128)(2,1)}) custom-call(bf16[1024,1024]{1,0:T(8,128)(2,1)} %refs_6_.3, bf16[1024,1024]{1,0:T(8,128)(2,1)} %collective-permute-done.refs_1_.refs_4_.refs_7_, ...), custom_call_target="tpu_custom_call" | custom-call | flops 3422552064 | bytes 12582912 | tf_op jit(solution)/shard_map/pallas_call | solution.py:189
  57.7 5.0 %all-to-all-start.1 = ((bf16[64,32,128]{2,1,0:T(8,128)(2,1)}), bf16[64,32,128]{2,1,0:T(8,128)(2,1)S(1)}, u32[]{:S(2)}, u32[]{:S(2)}) async-start(bf16[64,32,128]{2,1,0:T(8,128)(2,1)} %bitcast.28), calls=%async_computation.1 | async-start | bytes 1048576 | tf_op jit(solution)/shard_map/all_to_all | solution.py:665
  62.7 0.0 collective-permute-done.1.refs_3_.refs_7_
  62.7 0.0 collective-permute-done.2.refs_5_.refs_12_
  62.7 7.5 %shard_map.111 = (f32[512,2048]{1,0:T(8,128)}, bf16[704,2048]{1,0:T(8,128)(2,1)}, bf16[1024,1024]{1,0:T(8,128)(2,1)}) custom-call(s32[1,1]{1,0:T(1,128)} %bitcast.refs_0_.refs_8_, bf16[128,2048]{1,0:T(8,128)(2,1)} %get-tuple-element.41.refs_1_.refs_0_, bf16[1024,1024]{1,0:T(8,128)(2,1)} %refs_6_.2, ...), custom_call_target="tpu_custom_call" | custom-call | flops 2147483648 | bytes 18612228 | tf_op jit(solution)/shard_map/pallas_call | solution.py:189
  70.3 4.2 %all-to-all-done.1 = bf16[64,32,128]{2,1,0:T(8,128)(2,1)S(1)} async-done(((bf16[64,32,128]{2,1,0:T(8,128)(2,1)}), bf16[64,32,128]{2,1,0:T(8,128)(2,1)S(1)}, u32[]{:S(2)}, u32[]{:S(2)}) %all-to-all-start.1) | async-done | bytes 524320 | tf_op jit(solution)/shard_map/all_to_all | solution.py:665
  74.5 0.8 copy-done.4
  75.3 5.1 %shard_map.112 = (f32[8,2048]{1,0:T(8,128)}, f32[16,128]{1,0:T(8,128)}, bf16[1024,256]{1,0:T(8,128)(2,1)}) custom-call(bf16[704,2048]{1,0:T(8,128)(2,1)} %get-tuple-element.42.refs_0_.refs_1_, f32[512,2048]{1,0:T(8,128)} %get-tuple-element.43.refs_1_.refs_3_.refs_5_, bf16[2048,128]{1,0:T(8,128)(2,1)} %bitcast.24), custom_call_target="tpu_custom_call" | custom-call | flops 738197504 | bytes 8200192 | tf_op jit(solution)/shard_map/pallas_call | solution.py:189
  80.4 5.8 %all-to-all-start.2 = ((bf16[64,16,256]{2,1,0:T(8,128)(2,1)}), bf16[64,16,256]{2,1,0:T(8,128)(2,1)S(1)}, u32[]{:S(2)}, u32[]{:S(2)}) async-start(bf16[64,16,256]{2,1,0:T(8,128)(2,1)} %bitcast.26), calls=%async_computation.2 | async-start | bytes 1048576 | tf_op jit(solution)/shard_map/all_to_all | solution.py:665
  86.2 1.7 collective-permute-start.12
  87.9 7.0 %shard_map.115 = (bf16[1024,176]{1,0:T(8,128)(2,1)}, bf16[1024,176]{1,0:T(8,128)(2,1)}, bf16[1024,176]{1,0:T(8,128)(2,1)}, bf16[1024,176]{1,0:T(8,128)(2,1)}) custom-call(s32[1,1]{1,0:T(1,128)} %bitcast.10.refs_0_, bf16[704,1024]{1,0:T(8,128)(2,1)} %get-tuple-element.55.refs_1_.refs_7_, bf16[704,1024]{1,0:T(8,128)(2,1)} %get-tuple-element.56.refs_2_, ...), custom_call_target="tpu_custom_call" | custom-call | flops 2952790016 | bytes 12713988 | tf_op jit(solution)/shard_map/pallas_call | solution.py:189
  94.9 1.4 collective-permute-start.5
  96.3 1.2 collective-permute-start.6
  97.5 0.2 collective-permute-start.7
  97.6 0.0 all-to-all-done.2
  97.7 0.8 copy-done.1
  98.5 7.8 %shard_map.113 = (bf16[512,1024]{1,0:T(8,128)(2,1)}, bf16[512,1024]{1,0:T(8,128)(2,1)}, f32[8,2048]{1,0:T(8,128)}, bf16[1024,256]{1,0:T(8,128)(2,1)}, bf16[512,2...) custom-call(s32[1,1]{1,0:T(1,128)} %bitcast.1.refs_0_, ...), custom_call_target="tpu_custom_call" | custom-call | flops 2885681152 | bytes 16121860 | tf_op jit(solution)/shard_map/pallas_call | solution.py:189
  106.3 10.1 %all-to-all-start.3 = ((bf16[64,16,256]{2,1,0:T(8,128)(2,1)}), bf16[64,16,256]{2,1,0:T(8,128)(2,1)S(1)}, u32[]{:S(2)}, u32[]{:S(2)}) async-start(bf16[64,16,256]{2,1,0:T(8,128)(2,1)} %bitcast.27), calls=%async_computation.3 | async-start | bytes 1048576 | tf_op jit(solution)/shard_map/all_to_all | solution.py:665
  116.4 1.2 collective-permute-start.3
  117.7 0.0 collective-permute-done.5.refs_10_
  117.7 2.7 %collective-permute-start.8 = (bf16[512,256]{1,0:T(8,128)(2,1)}, bf16[512,256]{1,0:T(8,128)(2,1)S(1)}, u32[]{:S(2)}, u32[]{:S(2)}) collective-permute-start(bf16[512,256]{1,0:T(8,128)(2,1)} %get-tuple-element.62), channel_id=1, source_target_pairs={{0,96},{1,97},{2,98},{3,99},{4,100},{5,101},{6,102},{7,103},{8,104... | collective-permute-start | bytes 786440 | tf_op jit(solution)/shard_map/ppermute | solution.py:676
  120.4 0.0 collective-permute-done.6.refs_11_
  120.4 1.2 collective-permute-start.9
  121.6 1.7 collective-permute-done.7.refs_12_
  123.3 4.9 %collective-permute-start.10 = (bf16[512,256]{1,0:T(8,128)(2,1)}, bf16[512,256]{1,0:T(8,128)(2,1)S(1)}, u32[]{:S(2)}, u32[]{:S(2)}) collective-permute-start(bf16[512,256]{1,0:T(8,128)(2,1)} %get-tuple-element.64), channel_id=1, source_target_pairs={{0,98},{1,99},{2,96},{3,97},{4,102},{5,103},{6,100},{7,101},{8,106... | collective-permute-start | bytes 786440 | tf_op jit(solution)/shard_map/ppermute | solution.py:676
  128.3 4.6 %shard_map.114 = (bf16[64,1024]{1,0:T(8,128)(2,1)}, bf16[64,1024]{1,0:T(8,128)(2,1)}) custom-call(bf16[128,2048]{1,0:T(8,128)(2,1)} %get-tuple-element.41.refs_1_.refs_0_, f32[8,2048]{1,0:T(8,128)} %get-tuple-element.45.refs_2_.refs_1_, f32[8,2048]{1,0:T(8,128)} %get-tuple-element.49.refs_2_, f32[512,2048]{1,0:T(8,128)} %get-tuple-element.43.refs_1_.refs_3_.refs_5_, ...), custom_call_target="tpu_custom_call" | custom-call | flops 369098752 | bytes 5644288 | tf_op jit(solution)/shard_map/pallas_call | solution.py:189
  132.8 0.0 copy-done.5
  132.9 0.0 copy-done.6
  132.9 2.6 %collective-permute-done.8.refs_14_ = bf16[512,256]{1,0:T(8,128)(2,1)S(1)} collective-permute-done((bf16[512,256]{1,0:T(8,128)(2,1)}, bf16[512,256]{1,0:T(8,128)(2,1)S(1)}, u32[]{:S(2)}, u32[]{:S(2)}) %collective-permute-start.8) | collective-permute-done | bytes 262176 | tf_op jit(solution)/shard_map/ppermute | solution.py:676
  135.4 0.0 collective-permute-done.9.refs_15_
  135.5 0.6 collective-permute-done.10.refs_16_
  136.0 0.0 all-to-all-done.3
  136.0 0.1 copy-done.9
  136.2 0.1 copy-done.11
  136.3 0.5 copy-done.12
  136.8 0.2 copy-done.3
  136.9 6.7 %shard_map.116 = (bf16[64,1024]{1,0:T(8,128)(2,1)}, bf16[64,1024]{1,0:T(8,128)(2,1)}, bf16[1024,128]{1,0:T(8,128)(2,1)}, bf16[1024,560]{1,0:T(8,128)(2,1)}) custom-call(bf16[128,2048]{1,0:T(8,128)(2,1)} %get-tuple-element.41.refs_1_.refs_0_, bf16[2048,512]{1,0:T(8,128)(2,1)} %get-tuple-element.53.refs_1_, bf16[1024,256]{1,0:T(8,128)(2,1)} %bitcast.22, ...), custom_call_target="tpu_custom_call" | custom-call | flops 905969664 | bytes 12288004 | tf_op jit(solution)/shard_map/pallas_call | solution.py:189
  143.6 0.0 copy-start.8
  143.6 0.0 copy-start.13
  143.6 0.0 copy-start.14
  143.6 9.0 %all-to-all-start.4 = ((bf16[128,8,560]{2,1,0:T(8,128)(2,1)}), bf16[128,8,560]{2,1,0:T(8,128)(2,1)S(1)}, u32[]{:S(2)}, u32[]{:S(2)}) async-start(bf16[128,8,560]{2,1,0:T(8,128)(2,1)} %bitcast.25), calls=%async_computation.4 | async-start | bytes 2621440 | tf_op jit(solution)/shard_map/all_to_all | solution.py:723
  152.7 1.1 collective-permute-start.13
  153.8 0.1 collective-permute-start.4
  153.9 0.4 collective-permute-start.11
  154.3 0.0 collective-permute-done.12.refs_8_
  154.3 0.8 collective-permute-done.4.refs_4_
  155.2 0.3 collective-permute-done.11.refs_6_
  155.5 0.0 collective-permute-done.13.refs_10_.refs_3_
  155.5 0.0 collective-permute-done.3.refs_2_
  155.5 0.3 copy-done.15
  155.8 0.3 copy-done.16
  156.2 0.1 copy-done.10
  156.3 11.1 %shard_map.117 = (bf16[1024,1024]{1,0:T(8,128)(2,1)}, bf16[1024,1024]{1,0:T(8,128)(2,1)}) custom-call(s32[1,1]{1,0:T(1,128)} %bitcast.refs_0_.refs_8_, bf16[512,1024]{1,0:T(8,128)(2,1)} %get-tuple-element.47.refs_1_, bf16[512,1024]{1,0:T(8,128)(2,1)} %collective-permute-done.3.refs_2_, bf16[64,1024]{1,0:T(8,128)(2,1)} %get-tuple-element.51.refs_4_.refs_3_, ...), custom_call_target="tpu_custom_call" | custom-call | flops 5200936960 | bytes 17039364 | tf_op jit(solution)/shard_map/pallas_call | solution.py:189
  167.4 7.3 %all-to-all-done.4 = bf16[128,8,560]{2,1,0:T(8,128)(2,1)S(1)} async-done(((bf16[128,8,560]{2,1,0:T(8,128)(2,1)}), bf16[128,8,560]{2,1,0:T(8,128)(2,1)S(1)}, u32[]{:S(2)}, u32[]{:S(2)}) %all-to-all-start.4) | async-done | bytes 1146912 | tf_op jit(solution)/shard_map/all_to_all | solution.py:723
  174.6 1.1 copy-done.2
  175.7 2.4 %shard_map.118 = (f32[8,128]{1,0:T(8,128)}, f32[8,128]{1,0:T(8,128)}, f32[8,1024]{1,0:T(8,128)}, f32[8,1024]{1,0:T(8,128)}) custom-call(s32[1,1]{1,0:T(1,128)} %bitcast.refs_0_.refs_8_, bf16[1024,560]{1,0:T(8,128)(2,1)} %bitcast.21, bf16[1024,128]{1,0:T(8,128)(2,1)} %get-tuple-element.67.refs_9_.refs_2_, bf16[1024,128]{1,0:T(8,128)(2,1)} %copy-done.10, ...), custom_call_target="tpu_custom_call" | custom-call | bytes 5939204 | tf_op jit(solution)/shard_map/pallas_call | solution.py:189
  (18 shorter events, 0.0 us)
Async XLA Ops:
  3.0 44.6 %all-to-all-start = ((bf16[128,8,1152]{2,1,0:T(8,128)(2,1)}), bf16[128,8,1152]{2,1,0:T(8,128)(2,1)S(1)}, u32[]{:S(2)}, u32[]{:S(2)}) async-start(bf16[128,8,1152]{2,1,0:T(8,128)(2,1)} %bitcast.13), calls=%async_computation | async-start | bytes 4718592 | tf_op jit(solution)/shard_map/all_to_all | solution.py:698
  14.5 34.3 %collective-permute-start = (bf16[1024,1024]{1,0:T(8,128)(2,1)}, bf16[1024,1024]{1,0:T(8,128)(2,1)}, u32[]{:S(2)}, u32[]{:S(2)}) collective-permute-start(bf16[1024,1024]{1,0:T(8,128)(2,1)} %refs_6_.3), channel_id=1, source_target_pairs={{0,1},{1,0},{2,3},{3,2},{4,5},{5,4},{6,7},{7,6},{8,9},{9,8},{10,11... | collective-permute-start | bytes 6291464 | tf_op jit(solution)/shard_map/ppermute | solution.py:662
  47.6 1.5 copy-start
  47.6 15.1 %collective-permute-start.2 = (bf16[1024,1152]{1,0:T(8,128)(2,1)S(1)}, bf16[1024,1152]{1,0:T(8,128)(2,1)}, u32[]{:S(2)}, u32[]{:S(2)}) collective-permute-start(bf16[1024,1152]{1,0:T(8,128)(2,1)S(1)} %bitcast.14), channel_id=1, source_target_pairs={{0,1},{1,0},{2,3},{3,2},{4,5},{5,4},{6,7},{7,6},{8,9},{9,8},{10,11... | collective-permute-start | bytes 7077896 | tf_op jit(solution)/shard_map/ppermute | solution.py:662
  48.8 14.0 %collective-permute-start.1 = (bf16[1024,1024]{1,0:T(8,128)(2,1)}, bf16[1024,1024]{1,0:T(8,128)(2,1)}, u32[]{:S(2)}, u32[]{:S(2)}) collective-permute-start(bf16[1024,1024]{1,0:T(8,128)(2,1)} %refs_6_.2), channel_id=1, source_target_pairs={{0,1},{1,0},{2,3},{3,2},{4,5},{5,4},{6,7},{7,6},{8,9},{9,8},{10,11... | collective-permute-start | bytes 6291464 | tf_op jit(solution)/shard_map/ppermute | solution.py:662
  57.7 16.8 %all-to-all-start.1 = ((bf16[64,32,128]{2,1,0:T(8,128)(2,1)}), bf16[64,32,128]{2,1,0:T(8,128)(2,1)S(1)}, u32[]{:S(2)}, u32[]{:S(2)}) async-start(bf16[64,32,128]{2,1,0:T(8,128)(2,1)} %bitcast.28), calls=%async_computation.1 | async-start | bytes 1048576 | tf_op jit(solution)/shard_map/all_to_all | solution.py:665
  74.5 0.8 copy-start.4
  80.4 17.3 %all-to-all-start.2 = ((bf16[64,16,256]{2,1,0:T(8,128)(2,1)}), bf16[64,16,256]{2,1,0:T(8,128)(2,1)S(1)}, u32[]{:S(2)}, u32[]{:S(2)}) async-start(bf16[64,16,256]{2,1,0:T(8,128)(2,1)} %bitcast.26), calls=%async_computation.2 | async-start | bytes 1048576 | tf_op jit(solution)/shard_map/all_to_all | solution.py:665
  86.2 68.1 %collective-permute-start.12 = (bf16[704,1024]{1,0:T(8,128)(2,1)}, bf16[704,1024]{1,0:T(8,128)(2,1)}, u32[]{:S(2)}, u32[]{:S(2)}) collective-permute-start(bf16[704,1024]{1,0:T(8,128)(2,1)} %get-tuple-element.56.refs_2_), channel_id=1, source_target_pairs={{0,1},{1,0},{2,3},{3,2},{4,5},{5,4},{6,7},{7,6},{8,9},{9,8},{10,11... | collective-permute-start | bytes 4325384 | tf_op jit(solution)/shard_map/ppermute | solution.py:662
  94.9 22.7 %collective-permute-start.5 = (bf16[1024,176]{1,0:T(8,128)(2,1)}, bf16[1024,176]{1,0:T(8,128)(2,1)S(1)}, u32[]{:S(2)}, u32[]{:S(2)}) collective-permute-start(bf16[1024,176]{1,0:T(8,128)(2,1)} %get-tuple-element.58), channel_id=1, source_target_pairs={{0,4},{1,5},{2,6},{3,7},{4,0},{5,1},{6,2},{7,3},{8,12},{9,13},{10,... | collective-permute-start | bytes 1081352 | tf_op jit(solution)/shard_map/ppermute | solution.py:676
  96.3 24.1 %collective-permute-start.6 = (bf16[1024,176]{1,0:T(8,128)(2,1)}, bf16[1024,176]{1,0:T(8,128)(2,1)S(1)}, u32[]{:S(2)}, u32[]{:S(2)}) collective-permute-start(bf16[1024,176]{1,0:T(8,128)(2,1)} %get-tuple-element.59), channel_id=1, source_target_pairs={{0,32},{1,33},{2,34},{3,35},{4,36},{5,37},{6,38},{7,39},{8,40},{9,... | collective-permute-start | bytes 1081352 | tf_op jit(solution)/shard_map/ppermute | solution.py:676
  97.5 25.9 %collective-permute-start.7 = (bf16[1024,176]{1,0:T(8,128)(2,1)}, bf16[1024,176]{1,0:T(8,128)(2,1)S(1)}, u32[]{:S(2)}, u32[]{:S(2)}) collective-permute-start(bf16[1024,176]{1,0:T(8,128)(2,1)} %get-tuple-element.60), channel_id=1, source_target_pairs={{0,36},{1,37},{2,38},{3,39},{4,32},{5,33},{6,34},{7,35},{8,44},{9,... | collective-permute-start | bytes 1081352 | tf_op jit(solution)/shard_map/ppermute | solution.py:676
  97.6 0.8 copy-start.1
  106.3 29.7 %all-to-all-start.3 = ((bf16[64,16,256]{2,1,0:T(8,128)(2,1)}), bf16[64,16,256]{2,1,0:T(8,128)(2,1)S(1)}, u32[]{:S(2)}, u32[]{:S(2)}) async-start(bf16[64,16,256]{2,1,0:T(8,128)(2,1)} %bitcast.27), calls=%async_computation.3 | async-start | bytes 1048576 | tf_op jit(solution)/shard_map/all_to_all | solution.py:665
  116.4 39.1 %collective-permute-start.3 = (bf16[512,1024]{1,0:T(8,128)(2,1)}, bf16[512,1024]{1,0:T(8,128)(2,1)}, u32[]{:S(2)}, u32[]{:S(2)}) collective-permute-start(bf16[512,1024]{1,0:T(8,128)(2,1)} %get-tuple-element.48), channel_id=1, source_target_pairs={{0,1},{1,0},{2,3},{3,2},{4,5},{5,4},{6,7},{7,6},{8,9},{9,8},{10,11... | collective-permute-start | bytes 3145736 | tf_op jit(solution)/shard_map/ppermute | solution.py:662
  117.7 15.2 %copy-start.5 = (bf16[1024,176]{1,0:T(8,128)(2,1)}, bf16[1024,176]{1,0:T(8,128)(2,1)S(1)}, u32[]{:S(2)}) copy-start(bf16[1024,176]{1,0:T(8,128)(2,1)S(1)} %collective-permute-done.5.refs_10_) | copy-start | bytes 1081348
  117.7 17.8 %collective-permute-start.8 = (bf16[512,256]{1,0:T(8,128)(2,1)}, bf16[512,256]{1,0:T(8,128)(2,1)S(1)}, u32[]{:S(2)}, u32[]{:S(2)}) collective-permute-start(bf16[512,256]{1,0:T(8,128)(2,1)} %get-tuple-element.62), channel_id=1, source_target_pairs={{0,96},{1,97},{2,98},{3,99},{4,100},{5,101},{6,102},{7,103},{8,104... | collective-permute-start | bytes 786440 | tf_op jit(solution)/shard_map/ppermute | solution.py:676
  120.4 12.5 %copy-start.6 = (bf16[1024,176]{1,0:T(8,128)(2,1)}, bf16[1024,176]{1,0:T(8,128)(2,1)S(1)}, u32[]{:S(2)}) copy-start(bf16[1024,176]{1,0:T(8,128)(2,1)S(1)} %collective-permute-done.6.refs_11_) | copy-start | bytes 1081348
  120.4 15.1 %collective-permute-start.9 = (bf16[512,256]{1,0:T(8,128)(2,1)}, bf16[512,256]{1,0:T(8,128)(2,1)S(1)}, u32[]{:S(2)}, u32[]{:S(2)}) collective-permute-start(bf16[512,256]{1,0:T(8,128)(2,1)} %get-tuple-element.63), channel_id=1, source_target_pairs={{0,2},{1,3},{2,0},{3,1},{4,6},{5,7},{6,4},{7,5},{8,10},{9,11},{10,... | collective-permute-start | bytes 786440 | tf_op jit(solution)/shard_map/ppermute | solution.py:676
  123.3 9.5 %copy-start.7 = (bf16[1024,176]{1,0:T(8,128)(2,1)}, bf16[1024,176]{1,0:T(8,128)(2,1)S(1)}, u32[]{:S(2)}) copy-start(bf16[1024,176]{1,0:T(8,128)(2,1)S(1)} %collective-permute-done.7.refs_12_) | copy-start | bytes 1081348
  123.3 12.7 %collective-permute-start.10 = (bf16[512,256]{1,0:T(8,128)(2,1)}, bf16[512,256]{1,0:T(8,128)(2,1)S(1)}, u32[]{:S(2)}, u32[]{:S(2)}) collective-permute-start(bf16[512,256]{1,0:T(8,128)(2,1)} %get-tuple-element.64), channel_id=1, source_target_pairs={{0,98},{1,99},{2,96},{3,97},{4,102},{5,103},{6,100},{7,101},{8,106... | collective-permute-start | bytes 786440 | tf_op jit(solution)/shard_map/ppermute | solution.py:676
  135.4 0.7 copy-start.9
  135.5 0.8 copy-start.11
  136.0 0.7 copy-start.12
  136.0 0.9 copy-start.3
  143.6 9.0 %copy-start.8 = (bf16[1024,128]{1,0:T(8,128)(2,1)S(1)}, bf16[1024,128]{1,0:T(8,128)(2,1)}, u32[]{:S(2)}) copy-start(bf16[1024,128]{1,0:T(8,128)(2,1)} %get-tuple-element.67.refs_9_.refs_2_) | copy-start | bytes 786436
  143.6 10.2 %copy-start.13 = (bf16[64,1024]{1,0:T(8,128)(2,1)S(1)}, bf16[64,1024]{1,0:T(8,128)(2,1)}, u32[]{:S(2)}) copy-start(bf16[64,1024]{1,0:T(8,128)(2,1)} %get-tuple-element.52.refs_5_) | copy-start | bytes 393220
  143.6 10.3 %copy-start.14 = (bf16[64,1024]{1,0:T(8,128)(2,1)S(1)}, bf16[64,1024]{1,0:T(8,128)(2,1)}, u32[]{:S(2)}) copy-start(bf16[64,1024]{1,0:T(8,128)(2,1)} %get-tuple-element.66) | copy-start | bytes 393220
  143.6 31.0 %all-to-all-start.4 = ((bf16[128,8,560]{2,1,0:T(8,128)(2,1)}), bf16[128,8,560]{2,1,0:T(8,128)(2,1)S(1)}, u32[]{:S(2)}, u32[]{:S(2)}) async-start(bf16[128,8,560]{2,1,0:T(8,128)(2,1)} %bitcast.25), calls=%async_computation.4 | async-start | bytes 2621440 | tf_op jit(solution)/shard_map/all_to_all | solution.py:723
  152.7 2.9 %collective-permute-start.13 = (bf16[1024,128]{1,0:T(8,128)(2,1)S(1)}, bf16[1024,128]{1,0:T(8,128)(2,1)S(1)}, u32[]{:S(2)}, u32[]{:S(2)}) collective-permute-start(bf16[1024,128]{1,0:T(8,128)(2,1)S(1)} %copy-done.8), channel_id=1, source_target_pairs={{0,1},{1,0},{2,3},{3,2},{4,5},{5,4},{6,7},{7,6},{8,9},{9,8},{10,11... | collective-permute-start | bytes 786440 | tf_op jit(solution)/shard_map/ppermute | solution.py:662
  153.8 1.3 collective-permute-start.4
  153.9 1.6 collective-permute-start.11
  155.2 0.6 copy-start.15
  155.5 0.7 copy-start.16
  155.5 0.8 copy-start.10
  174.6 1.1 copy-start.2

commit v8 on v7

--- a/solution.py
+++ b/solution.py
@@ -341,14 +341,14 @@
         def _():
             for k in range(parts):
                 part = turn_ref[0, 0] ^ k
-                out_refs[k][...] = acc[pl.ds(pl.multiple_of(part * size, 16), size), :].T.astype(BF)
+                out_refs[k][...] = acc[pl.ds(pl.multiple_of(part * size, 16), size), :].astype(BF)
 
     return call(
         body,
         count,
         (turn, rows_t, slabs, after),
         ("scalar", "pair1", "pair", "any"),
-        (shape((width, size), BF),) * parts,
+        (shape((size, width), BF),) * parts,
         (None,) * parts,
         [pltpu.VMEM((rows, width), F32)],
         2 * count * rows * width,
@@ -520,7 +520,7 @@
         @at_last
         def _():
             sent_ref[:, : 2 * qk] = acc[...].T.astype(BF)
-            sent_ref[:, 2 * qk : 2 * qk + FPAD] = sum(ref[...].astype(F32) for ref in (m0, m1, m2, m3)).astype(BF)
+            sent_ref[:, 2 * qk : 2 * qk + FPAD] = sum(ref[...].astype(F32) for ref in (m0, m1, m2, m3)).T.astype(BF)
             first = core_ref[0, 0] == 0
             out = sum(ref[...].astype(F32) for ref in (o0, o1, o2, o3))
             half = out.shape[0]

time: 179 us -> 177 us (0.989)
  starting transfers between devices: 59.9 us -> 53.9 us
  waiting for transfers between devices: 49.5 us -> 54.2 us
    ppermute x6, starting transfers between devices: 11.6 us -> 6.77 us  [among_four(): found.append(lax.ppermute(parts[step], AXES, moves))]
    ppermute x6, waiting for transfers between devices: 4.91 us -> 9.68 us  [among_four(): found.append(lax.ppermute(parts[step], AXES, moves))]
    unnamed x34 -> x36, local copies, waits for them, and re-layouts: 4.71 us -> 5.12 us
where the time goes in v8:
time: 177 us
  Pallas kernels  62.5 us (35%)
  waiting for transfers between devices  54.2 us (31%)
  starting transfers between devices  53.9 us (30%)
  local copies, waits for them, and re-layouts  5.12 us (3%)
    pallas_call x9, Pallas kernels, call(): pl.pallas_call(kernel, in_specs=[pl.BlockSpec(memory_space=space) for spa...  60.2 us
    all_to_all x1, waiting for transfers between devices, per_device(): lax.all_to_all(to_send.reshape(n, -1, to_send.shape[1]), AXES, 0, 0, tile...  31.9 us
    all_to_all x3, starting transfers between devices, spread(): lax.all_to_all(x, AXES, 0, 0, axis_index_groups=same_core, tiled=True)  20.6 us
    all_to_all x1, starting transfers between devices, per_device(): lax.all_to_all(to_send.reshape(n, -1, to_send.shape[1]), AXES, 0, 0, tile...  11.5 us
    ppermute x6, waiting for transfers between devices, among_four(): found.append(lax.ppermute(parts[step], AXES, moves))  9.68 us
    all_to_all x1, starting transfers between devices, per_device(): lax.all_to_all(sent.reshape(n, -1, sent.shape[1]), AXES, 0, 0, tiled=True)  8.17 us
    all_to_all x1, waiting for transfers between devices, per_device(): lax.all_to_all(sent.reshape(n, -1, sent.shape[1]), AXES, 0, 0, tiled=True)  6.9 us
    ppermute x8, starting transfers between devices, exchange(): return lax.ppermute(x, AXES, swap)  6.89 us
  transfers between devices with their start and end apart: 19, of which 8 were waited for; matrix products, arithmetic and copies ran while one was open for 0% of the time, Pallas kernels for 30%

profile of v8, /device:TPU:1, one launch (start us, length us, event | category | flops | bytes accessed | tf_op | source)
XLA Modules:
  0.0 176.9 jit_solution(10953542233131553928)
XLA Ops:
  0.6 2.3 %shard_map.109 = bf16[1024,1152]{1,0:T(8,128)(2,1)} custom-call(bf16[8,128]{1,0:T(8,128)(2,1)} %q_ref.1, bf16[8,128]{1,0:T(8,128)(2,1)} %k_ref.1, bf16[8,1024]{1,0:T(8,128)(2,1)} %v_ref.1, bf16[8,1024]{1,0:T(8,128)(2,1)} %o_ref.1), custom_call_target="tpu_custom_call" | custom-call | bytes 2359296 | tf_op jit(solution)/shard_map/pallas_call | solution.py:242
  3.0 11.5 %all-to-all-start = ((bf16[128,8,1152]{2,1,0:T(8,128)(2,1)}), bf16[128,8,1152]{2,1,0:T(8,128)(2,1)S(1)}, u32[]{:S(2)}, u32[]{:S(2)}) async-start(bf16[128,8,1152]{2,1,0:T(8,128)(2,1)} %bitcast.13), calls=%async_computation | async-start | bytes 4718592 | tf_op jit(solution)/shard_map/all_to_all | solution.py:698
  14.5 1.1 collective-permute-start
  15.6 31.9 %all-to-all-done = bf16[128,8,1152]{2,1,0:T(8,128)(2,1)S(1)} async-done(((bf16[128,8,1152]{2,1,0:T(8,128)(2,1)}), bf16[128,8,1152]{2,1,0:T(8,128)(2,1)S(1)}, u32[]{:S(2)}, u32[]{:S(2)}) %all-to-all-start) | async-done | bytes 2359328 | tf_op jit(solution)/shard_map/all_to_all | solution.py:698
  47.6 1.2 collective-permute-start.2
  48.7 0.0 collective-permute-start.1
  48.8 0.0 collective-permute-done.refs_1_.refs_4_.refs_7_
  48.8 0.3 copy-done
  49.1 8.7 %shard_map.110 = (bf16[128,2048]{1,0:T(8,128)(2,1)}, bf16[2048,512]{1,0:T(8,128)(2,1)}, bf16[704,1024]{1,0:T(8,128)(2,1)}, bf16[704,1024]{1,0:T(8,128)(2,1)}, bf16[2048,128]{1,0:T(8,128)(2,1)}) custom-call(bf16[1024,1024]{1,0:T(8,128)(2,1)} %refs_6_.3, bf16[1024,1024]{1,0:T(8,128)(2,1)} %collective-permute-done.refs_1_.refs_4_.refs_7_, ...), custom_call_target="tpu_custom_call" | custom-call | flops 3422552064 | bytes 12582912 | tf_op jit(solution)/shard_map/pallas_call | solution.py:189
  57.7 5.0 %all-to-all-start.1 = ((bf16[64,32,128]{2,1,0:T(8,128)(2,1)}), bf16[64,32,128]{2,1,0:T(8,128)(2,1)S(1)}, u32[]{:S(2)}, u32[]{:S(2)}) async-start(bf16[64,32,128]{2,1,0:T(8,128)(2,1)} %bitcast.28), calls=%async_computation.1 | async-start | bytes 1048576 | tf_op jit(solution)/shard_map/all_to_all | solution.py:665
  62.7 0.0 collective-permute-done.1.refs_3_.refs_7_
  62.7 0.0 collective-permute-done.2.refs_5_.refs_12_
  62.7 7.5 %shard_map.111 = (f32[512,2048]{1,0:T(8,128)}, bf16[704,2048]{1,0:T(8,128)(2,1)}, bf16[1024,1024]{1,0:T(8,128)(2,1)}) custom-call(s32[1,1]{1,0:T(1,128)} %bitcast.refs_0_.refs_8_, bf16[128,2048]{1,0:T(8,128)(2,1)} %get-tuple-element.41.refs_1_.refs_0_, bf16[1024,1024]{1,0:T(8,128)(2,1)} %refs_6_.2, ...), custom_call_target="tpu_custom_call" | custom-call | flops 2147483648 | bytes 18612228 | tf_op jit(solution)/shard_map/pallas_call | solution.py:189
  70.3 4.2 %all-to-all-done.1 = bf16[64,32,128]{2,1,0:T(8,128)(2,1)S(1)} async-done(((bf16[64,32,128]{2,1,0:T(8,128)(2,1)}), bf16[64,32,128]{2,1,0:T(8,128)(2,1)S(1)}, u32[]{:S(2)}, u32[]{:S(2)}) %all-to-all-start.1) | async-done | bytes 524320 | tf_op jit(solution)/shard_map/all_to_all | solution.py:665
  74.5 0.8 copy-done.4
  75.3 5.1 %shard_map.112 = (f32[8,2048]{1,0:T(8,128)}, f32[16,128]{1,0:T(8,128)}, bf16[1024,256]{1,0:T(8,128)(2,1)}) custom-call(bf16[704,2048]{1,0:T(8,128)(2,1)} %get-tuple-element.42.refs_0_.refs_1_, f32[512,2048]{1,0:T(8,128)} %get-tuple-element.43.refs_1_.refs_3_.refs_5_, bf16[2048,128]{1,0:T(8,128)(2,1)} %bitcast.24), custom_call_target="tpu_custom_call" | custom-call | flops 738197504 | bytes 8200192 | tf_op jit(solution)/shard_map/pallas_call | solution.py:189
  80.4 5.8 %all-to-all-start.2 = ((bf16[64,16,256]{2,1,0:T(8,128)(2,1)}), bf16[64,16,256]{2,1,0:T(8,128)(2,1)S(1)}, u32[]{:S(2)}, u32[]{:S(2)}) async-start(bf16[64,16,256]{2,1,0:T(8,128)(2,1)} %bitcast.26), calls=%async_computation.2 | async-start | bytes 1048576 | tf_op jit(solution)/shard_map/all_to_all | solution.py:665
  86.2 1.7 collective-permute-start.12
  87.9 6.4 %shard_map.115 = (bf16[176,1024]{1,0:T(8,128)(2,1)}, bf16[176,1024]{1,0:T(8,128)(2,1)}, bf16[176,1024]{1,0:T(8,128)(2,1)}, bf16[176,1024]{1,0:T(8,128)(2,1)}) custom-call(s32[1,1]{1,0:T(1,128)} %bitcast.10.refs_0_, bf16[704,1024]{1,0:T(8,128)(2,1)} %get-tuple-element.55.refs_1_.refs_7_, bf16[704,1024]{1,0:T(8,128)(2,1)} %get-tuple-element.56.refs_2_, ...), custom_call_target="tpu_custom_call" | custom-call | flops 2952790016 | bytes 12713988 | tf_op jit(solution)/shard_map/pallas_call | solution.py:189
  94.4 1.4 collective-permute-start.5
  95.7 1.2 collective-permute-start.6
  96.9 0.2 collective-permute-start.7
  97.1 0.3 all-to-all-done.2
  97.4 0.8 copy-done.1
  98.2 7.8 %shard_map.113 = (bf16[512,1024]{1,0:T(8,128)(2,1)}, bf16[512,1024]{1,0:T(8,128)(2,1)}, f32[8,2048]{1,0:T(8,128)}, bf16[1024,256]{1,0:T(8,128)(2,1)}, bf16[512,2...) custom-call(s32[1,1]{1,0:T(1,128)} %bitcast.1.refs_0_, ...), custom_call_target="tpu_custom_call" | custom-call | flops 2885681152 | bytes 16121860 | tf_op jit(solution)/shard_map/pallas_call | solution.py:189
  106.1 9.8 %all-to-all-start.3 = ((bf16[64,16,256]{2,1,0:T(8,128)(2,1)}), bf16[64,16,256]{2,1,0:T(8,128)(2,1)S(1)}, u32[]{:S(2)}, u32[]{:S(2)}) async-start(bf16[64,16,256]{2,1,0:T(8,128)(2,1)} %bitcast.27), calls=%async_computation.3 | async-start | bytes 1048576 | tf_op jit(solution)/shard_map/all_to_all | solution.py:665
  115.9 1.2 collective-permute-start.3
  117.1 0.0 collective-permute-done.5.refs_10_
  117.1 2.7 %collective-permute-start.8 = (bf16[512,256]{1,0:T(8,128)(2,1)}, bf16[512,256]{1,0:T(8,128)(2,1)S(1)}, u32[]{:S(2)}, u32[]{:S(2)}) collective-permute-start(bf16[512,256]{1,0:T(8,128)(2,1)} %get-tuple-element.62), channel_id=1, source_target_pairs={{0,96},{1,97},{2,98},{3,99},{4,100},{5,101},{6,102},{7,103},{8,104... | collective-permute-start | bytes 786440 | tf_op jit(solution)/shard_map/ppermute | solution.py:676
  119.9 0.0 collective-permute-done.6.refs_11_
  119.9 1.2 collective-permute-start.9
  121.0 0.0 collective-permute-done.7.refs_12_
  121.1 0.1 collective-permute-start.10
  121.2 4.6 %shard_map.114 = (bf16[64,1024]{1,0:T(8,128)(2,1)}, bf16[64,1024]{1,0:T(8,128)(2,1)}) custom-call(bf16[128,2048]{1,0:T(8,128)(2,1)} %get-tuple-element.41.refs_1_.refs_0_, f32[8,2048]{1,0:T(8,128)} %get-tuple-element.45.refs_2_.refs_1_, f32[8,2048]{1,0:T(8,128)} %get-tuple-element.49.refs_2_, f32[512,2048]{1,0:T(8,128)} %get-tuple-element.43.refs_1_.refs_3_.refs_5_, ...), custom_call_target="tpu_custom_call" | custom-call | flops 369098752 | bytes 5644288 | tf_op jit(solution)/shard_map/pallas_call | solution.py:189
  125.8 0.0 copy-done.5
  125.8 0.0 copy-done.6
  125.8 0.0 copy-done.7
  125.8 6.7 %collective-permute-done.8.refs_14_ = bf16[512,256]{1,0:T(8,128)(2,1)S(1)} collective-permute-done((bf16[512,256]{1,0:T(8,128)(2,1)}, bf16[512,256]{1,0:T(8,128)(2,1)S(1)}, u32[]{:S(2)}, u32[]{:S(2)}) %collective-permute-start.8) | collective-permute-done | bytes 262176 | tf_op jit(solution)/shard_map/ppermute | solution.py:676
  132.5 0.0 collective-permute-done.9.refs_15_
  132.5 3.0 %collective-permute-done.10.refs_16_ = bf16[512,256]{1,0:T(8,128)(2,1)S(1)} collective-permute-done((bf16[512,256]{1,0:T(8,128)(2,1)}, bf16[512,256]{1,0:T(8,128)(2,1)S(1)}, u32[]{:S(2)}, u32[]{:S(2)}) %collective-permute-start.10) | collective-permute-done | bytes 262176 | tf_op jit(solution)/shard_map/ppermute | solution.py:676
  135.5 0.0 all-to-all-done.3
  135.5 0.0 copy-done.9
  135.5 0.0 copy-done.11
  135.5 0.7 copy-done.12
  136.2 0.2 copy-done.3
  136.5 6.5 %shard_map.116 = (bf16[64,1024]{1,0:T(8,128)(2,1)}, bf16[64,1024]{1,0:T(8,128)(2,1)}, bf16[1024,128]{1,0:T(8,128)(2,1)}, bf16[1024,560]{1,0:T(8,128)(2,1)}) custom-call(bf16[128,2048]{1,0:T(8,128)(2,1)} %get-tuple-element.41.refs_1_.refs_0_, bf16[2048,512]{1,0:T(8,128)(2,1)} %get-tuple-element.53.refs_1_, bf16[1024,256]{1,0:T(8,128)(2,1)} %bitcast.22, ...), custom_call_target="tpu_custom_call" | custom-call | flops 905969664 | bytes 12288004 | tf_op jit(solution)/shard_map/pallas_call | solution.py:189
  143.0 8.2 %all-to-all-start.4 = ((bf16[128,8,560]{2,1,0:T(8,128)(2,1)}), bf16[128,8,560]{2,1,0:T(8,128)(2,1)S(1)}, u32[]{:S(2)}, u32[]{:S(2)}) async-start(bf16[128,8,560]{2,1,0:T(8,128)(2,1)} %bitcast.25), calls=%async_computation.4 | async-start | bytes 2621440 | tf_op jit(solution)/shard_map/all_to_all | solution.py:723
  151.2 0.0 copy-done.8
  151.2 1.1 collective-permute-start.13
  152.4 0.1 collective-permute-start.4
  152.5 0.4 collective-permute-start.11
  152.9 0.0 collective-permute-done.12.refs_8_
  152.9 0.8 collective-permute-done.4.refs_4_
  153.7 0.3 collective-permute-done.11.refs_6_
  154.1 0.0 collective-permute-done.13.refs_10_.refs_3_
  154.1 0.0 collective-permute-done.3.refs_2_
  154.1 0.3 copy-done.16
  154.4 0.3 copy-done.17
  154.7 0.1 copy-done.10
  154.8 0.4 copy-done.14
  155.2 11.1 %shard_map.117 = (bf16[1024,1024]{1,0:T(8,128)(2,1)}, bf16[1024,1024]{1,0:T(8,128)(2,1)}) custom-call(s32[1,1]{1,0:T(1,128)} %bitcast.refs_0_.refs_8_, bf16[512,1024]{1,0:T(8,128)(2,1)} %get-tuple-element.47.refs_1_, bf16[512,1024]{1,0:T(8,128)(2,1)} %copy-done.14, bf16[64,1024]{1,0:T(8,128)(2,1)} %get-tuple-element.51.refs_4_.refs_3_, ...), custom_call_target="tpu_custom_call" | custom-call | flops 5200936960 | bytes 17039364 | tf_op jit(solution)/shard_map/pallas_call | solution.py:189
  166.3 6.9 %all-to-all-done.4 = bf16[128,8,560]{2,1,0:T(8,128)(2,1)S(1)} async-done(((bf16[128,8,560]{2,1,0:T(8,128)(2,1)}), bf16[128,8,560]{2,1,0:T(8,128)(2,1)S(1)}, u32[]{:S(2)}, u32[]{:S(2)}) %all-to-all-start.4) | async-done | bytes 1146912 | tf_op jit(solution)/shard_map/all_to_all | solution.py:723
  173.2 1.1 copy-done.2
  174.3 2.4 %shard_map.118 = (f32[8,128]{1,0:T(8,128)}, f32[8,128]{1,0:T(8,128)}, f32[8,1024]{1,0:T(8,128)}, f32[8,1024]{1,0:T(8,128)}) custom-call(s32[1,1]{1,0:T(1,128)} %bitcast.refs_0_.refs_8_, bf16[1024,560]{1,0:T(8,128)(2,1)} %bitcast.21, bf16[1024,128]{1,0:T(8,128)(2,1)} %get-tuple-element.67.refs_9_.refs_2_, bf16[1024,128]{1,0:T(8,128)(2,1)} %copy-done.10, ...), custom_call_target="tpu_custom_call" | custom-call | bytes 5939204 | tf_op jit(solution)/shard_map/pallas_call | solution.py:189
  (20 shorter events, 0.0 us)
Async XLA Ops:
  3.0 44.6 %all-to-all-start = ((bf16[128,8,1152]{2,1,0:T(8,128)(2,1)}), bf16[128,8,1152]{2,1,0:T(8,128)(2,1)S(1)}, u32[]{:S(2)}, u32[]{:S(2)}) async-start(bf16[128,8,1152]{2,1,0:T(8,128)(2,1)} %bitcast.13), calls=%async_computation | async-start | bytes 4718592 | tf_op jit(solution)/shard_map/all_to_all | solution.py:698
  14.5 34.3 %collective-permute-start = (bf16[1024,1024]{1,0:T(8,128)(2,1)}, bf16[1024,1024]{1,0:T(8,128)(2,1)}, u32[]{:S(2)}, u32[]{:S(2)}) collective-permute-start(bf16[1024,1024]{1,0:T(8,128)(2,1)} %refs_6_.3), channel_id=1, source_target_pairs={{0,1},{1,0},{2,3},{3,2},{4,5},{5,4},{6,7},{7,6},{8,9},{9,8},{10,11... | collective-permute-start | bytes 6291464 | tf_op jit(solution)/shard_map/ppermute | solution.py:662
  47.6 1.5 copy-start
  47.6 15.2 %collective-permute-start.2 = (bf16[1024,1152]{1,0:T(8,128)(2,1)S(1)}, bf16[1024,1152]{1,0:T(8,128)(2,1)}, u32[]{:S(2)}, u32[]{:S(2)}) collective-permute-start(bf16[1024,1152]{1,0:T(8,128)(2,1)S(1)} %bitcast.14), channel_id=1, source_target_pairs={{0,1},{1,0},{2,3},{3,2},{4,5},{5,4},{6,7},{7,6},{8,9},{9,8},{10,11... | collective-permute-start | bytes 7077896 | tf_op jit(solution)/shard_map/ppermute | solution.py:662
  48.7 14.0 %collective-permute-start.1 = (bf16[1024,1024]{1,0:T(8,128)(2,1)}, bf16[1024,1024]{1,0:T(8,128)(2,1)}, u32[]{:S(2)}, u32[]{:S(2)}) collective-permute-start(bf16[1024,1024]{1,0:T(8,128)(2,1)} %refs_6_.2), channel_id=1, source_target_pairs={{0,1},{1,0},{2,3},{3,2},{4,5},{5,4},{6,7},{7,6},{8,9},{9,8},{10,11... | collective-permute-start | bytes 6291464 | tf_op jit(solution)/shard_map/ppermute | solution.py:662
  57.7 16.8 %all-to-all-start.1 = ((bf16[64,32,128]{2,1,0:T(8,128)(2,1)}), bf16[64,32,128]{2,1,0:T(8,128)(2,1)S(1)}, u32[]{:S(2)}, u32[]{:S(2)}) async-start(bf16[64,32,128]{2,1,0:T(8,128)(2,1)} %bitcast.28), calls=%async_computation.1 | async-start | bytes 1048576 | tf_op jit(solution)/shard_map/all_to_all | solution.py:665
  74.5 0.8 copy-start.4
  80.4 17.0 %all-to-all-start.2 = ((bf16[64,16,256]{2,1,0:T(8,128)(2,1)}), bf16[64,16,256]{2,1,0:T(8,128)(2,1)S(1)}, u32[]{:S(2)}, u32[]{:S(2)}) async-start(bf16[64,16,256]{2,1,0:T(8,128)(2,1)} %bitcast.26), calls=%async_computation.2 | async-start | bytes 1048576 | tf_op jit(solution)/shard_map/all_to_all | solution.py:665
  86.2 66.7 %collective-permute-start.12 = (bf16[704,1024]{1,0:T(8,128)(2,1)}, bf16[704,1024]{1,0:T(8,128)(2,1)}, u32[]{:S(2)}, u32[]{:S(2)}) collective-permute-start(bf16[704,1024]{1,0:T(8,128)(2,1)} %get-tuple-element.56.refs_2_), channel_id=1, source_target_pairs={{0,1},{1,0},{2,3},{3,2},{4,5},{5,4},{6,7},{7,6},{8,9},{9,8},{10,11... | collective-permute-start | bytes 4325384 | tf_op jit(solution)/shard_map/ppermute | solution.py:662
  94.4 22.7 %collective-permute-start.5 = (bf16[176,1024]{1,0:T(8,128)(2,1)}, bf16[176,1024]{1,0:T(8,128)(2,1)S(1)}, u32[]{:S(2)}, u32[]{:S(2)}) collective-permute-start(bf16[176,1024]{1,0:T(8,128)(2,1)} %get-tuple-element.58), channel_id=1, source_target_pairs={{0,4},{1,5},{2,6},{3,7},{4,0},{5,1},{6,2},{7,3},{8,12},{9,13},{10,... | collective-permute-start | bytes 1081352 | tf_op jit(solution)/shard_map/ppermute | solution.py:676
  95.7 24.1 %collective-permute-start.6 = (bf16[176,1024]{1,0:T(8,128)(2,1)}, bf16[176,1024]{1,0:T(8,128)(2,1)S(1)}, u32[]{:S(2)}, u32[]{:S(2)}) collective-permute-start(bf16[176,1024]{1,0:T(8,128)(2,1)} %get-tuple-element.59), channel_id=1, source_target_pairs={{0,32},{1,33},{2,34},{3,35},{4,36},{5,37},{6,38},{7,39},{8,40},{9,... | collective-permute-start | bytes 1081352 | tf_op jit(solution)/shard_map/ppermute | solution.py:676
  96.9 24.1 %collective-permute-start.7 = (bf16[176,1024]{1,0:T(8,128)(2,1)}, bf16[176,1024]{1,0:T(8,128)(2,1)S(1)}, u32[]{:S(2)}, u32[]{:S(2)}) collective-permute-start(bf16[176,1024]{1,0:T(8,128)(2,1)} %get-tuple-element.60), channel_id=1, source_target_pairs={{0,36},{1,37},{2,38},{3,39},{4,32},{5,33},{6,34},{7,35},{8,44},{9,... | collective-permute-start | bytes 1081352 | tf_op jit(solution)/shard_map/ppermute | solution.py:676
  97.4 0.8 copy-start.1
  106.1 29.4 %all-to-all-start.3 = ((bf16[64,16,256]{2,1,0:T(8,128)(2,1)}), bf16[64,16,256]{2,1,0:T(8,128)(2,1)S(1)}, u32[]{:S(2)}, u32[]{:S(2)}) async-start(bf16[64,16,256]{2,1,0:T(8,128)(2,1)} %bitcast.27), calls=%async_computation.3 | async-start | bytes 1048576 | tf_op jit(solution)/shard_map/all_to_all | solution.py:665
  115.9 38.2 %collective-permute-start.3 = (bf16[512,1024]{1,0:T(8,128)(2,1)}, bf16[512,1024]{1,0:T(8,128)(2,1)S(1)}, u32[]{:S(2)}, u32[]{:S(2)}) collective-permute-start(bf16[512,1024]{1,0:T(8,128)(2,1)} %get-tuple-element.48), channel_id=1, source_target_pairs={{0,1},{1,0},{2,3},{3,2},{4,5},{5,4},{6,7},{7,6},{8,9},{9,8},{10,11... | collective-permute-start | bytes 3145736 | tf_op jit(solution)/shard_map/ppermute | solution.py:662
  117.1 8.7 %copy-start.5 = (bf16[176,1024]{1,0:T(8,128)(2,1)}, bf16[176,1024]{1,0:T(8,128)(2,1)S(1)}, u32[]{:S(2)}) copy-start(bf16[176,1024]{1,0:T(8,128)(2,1)S(1)} %collective-permute-done.5.refs_10_) | copy-start | bytes 1081348
  117.1 15.4 %collective-permute-start.8 = (bf16[512,256]{1,0:T(8,128)(2,1)}, bf16[512,256]{1,0:T(8,128)(2,1)S(1)}, u32[]{:S(2)}, u32[]{:S(2)}) collective-permute-start(bf16[512,256]{1,0:T(8,128)(2,1)} %get-tuple-element.62), channel_id=1, source_target_pairs={{0,96},{1,97},{2,98},{3,99},{4,100},{5,101},{6,102},{7,103},{8,104... | collective-permute-start | bytes 786440 | tf_op jit(solution)/shard_map/ppermute | solution.py:676
  119.9 6.0 %copy-start.6 = (bf16[176,1024]{1,0:T(8,128)(2,1)}, bf16[176,1024]{1,0:T(8,128)(2,1)S(1)}, u32[]{:S(2)}) copy-start(bf16[176,1024]{1,0:T(8,128)(2,1)S(1)} %collective-permute-done.6.refs_11_) | copy-start | bytes 1081348
  119.9 12.7 %collective-permute-start.9 = (bf16[512,256]{1,0:T(8,128)(2,1)}, bf16[512,256]{1,0:T(8,128)(2,1)S(1)}, u32[]{:S(2)}, u32[]{:S(2)}) collective-permute-start(bf16[512,256]{1,0:T(8,128)(2,1)} %get-tuple-element.63), channel_id=1, source_target_pairs={{0,2},{1,3},{2,0},{3,1},{4,6},{5,7},{6,4},{7,5},{8,10},{9,11},{10,... | collective-permute-start | bytes 786440 | tf_op jit(solution)/shard_map/ppermute | solution.py:676
  121.1 4.8 %copy-start.7 = (bf16[176,1024]{1,0:T(8,128)(2,1)}, bf16[176,1024]{1,0:T(8,128)(2,1)S(1)}, u32[]{:S(2)}) copy-start(bf16[176,1024]{1,0:T(8,128)(2,1)S(1)} %collective-permute-done.7.refs_12_) | copy-start | bytes 1081348
  121.1 14.4 %collective-permute-start.10 = (bf16[512,256]{1,0:T(8,128)(2,1)}, bf16[512,256]{1,0:T(8,128)(2,1)S(1)}, u32[]{:S(2)}, u32[]{:S(2)}) collective-permute-start(bf16[512,256]{1,0:T(8,128)(2,1)} %get-tuple-element.64), channel_id=1, source_target_pairs={{0,98},{1,99},{2,96},{3,97},{4,102},{5,103},{6,100},{7,101},{8,106... | collective-permute-start | bytes 786440 | tf_op jit(solution)/shard_map/ppermute | solution.py:676
  132.5 3.0 %copy-start.9 = (bf16[512,256]{1,0:T(8,128)(2,1)}, bf16[512,256]{1,0:T(8,128)(2,1)S(1)}, u32[]{:S(2)}) copy-start(bf16[512,256]{1,0:T(8,128)(2,1)S(1)} %collective-permute-done.8.refs_14_) | copy-start | bytes 786436
  132.5 3.0 %copy-start.11 = (bf16[512,256]{1,0:T(8,128)(2,1)}, bf16[512,256]{1,0:T(8,128)(2,1)S(1)}, u32[]{:S(2)}) copy-start(bf16[512,256]{1,0:T(8,128)(2,1)S(1)} %collective-permute-done.9.refs_15_) | copy-start | bytes 786436
  135.5 0.7 copy-start.12
  135.5 0.9 copy-start.3
  143.0 8.2 %copy-start.8 = (bf16[1024,128]{1,0:T(8,128)(2,1)S(1)}, bf16[1024,128]{1,0:T(8,128)(2,1)}, u32[]{:S(2)}) copy-start(bf16[1024,128]{1,0:T(8,128)(2,1)} %get-tuple-element.67.refs_9_.refs_2_) | copy-start | bytes 786436
  143.0 9.4 %copy-start.13 = (bf16[64,1024]{1,0:T(8,128)(2,1)S(1)}, bf16[64,1024]{1,0:T(8,128)(2,1)}, u32[]{:S(2)}) copy-start(bf16[64,1024]{1,0:T(8,128)(2,1)} %get-tuple-element.52.refs_5_) | copy-start | bytes 393220
  143.0 9.4 %copy-start.15 = (bf16[64,1024]{1,0:T(8,128)(2,1)S(1)}, bf16[64,1024]{1,0:T(8,128)(2,1)}, u32[]{:S(2)}) copy-start(bf16[64,1024]{1,0:T(8,128)(2,1)} %get-tuple-element.66) | copy-start | bytes 393220
  143.0 30.2 %all-to-all-start.4 = ((bf16[128,8,560]{2,1,0:T(8,128)(2,1)}), bf16[128,8,560]{2,1,0:T(8,128)(2,1)S(1)}, u32[]{:S(2)}, u32[]{:S(2)}) async-start(bf16[128,8,560]{2,1,0:T(8,128)(2,1)} %bitcast.25), calls=%async_computation.4 | async-start | bytes 2621440 | tf_op jit(solution)/shard_map/all_to_all | solution.py:723
  151.2 2.9 %collective-permute-start.13 = (bf16[1024,128]{1,0:T(8,128)(2,1)S(1)}, bf16[1024,128]{1,0:T(8,128)(2,1)S(1)}, u32[]{:S(2)}, u32[]{:S(2)}) collective-permute-start(bf16[1024,128]{1,0:T(8,128)(2,1)S(1)} %copy-done.8), channel_id=1, source_target_pairs={{0,1},{1,0},{2,3},{3,2},{4,5},{5,4},{6,7},{7,6},{8,9},{9,8},{10,11... | collective-permute-start | bytes 786440 | tf_op jit(solution)/shard_map/ppermute | solution.py:662
  152.4 1.3 collective-permute-start.4
  152.5 1.6 collective-permute-start.11
  153.7 0.7 copy-start.16
  154.1 0.6 copy-start.17
  154.1 0.8 copy-start.10
  154.1 1.1 copy-start.14
  173.2 1.1 copy-start.2

commit v9 on v8

--- a/solution.py
+++ b/solution.py
@@ -310,7 +310,7 @@
             w_ref[:, half:] = jnp.where(at == 0, theirs, mine)
 
         here = w_ref[pl.ds(pl.multiple_of(at * rows, rows), rows), :]
-        up_ref[...] = dot(here, slab_ref[...], (1, 1))
+        up_ref[...] = dot(here, slab_ref[...], (1, 1)).astype(BF)
         query = qk_ref[...].astype(F32)
         for head in range(heads):
             feat_ref[head * FPAD : (head + 1) * FPAD, :] = features(rows_of(query, head, DK))
@@ -320,7 +320,7 @@
         count,
         (core, qk_t, cot, weights, other_weights),
         ("scalar", 1, "pair", ("from", joined), ("from", joined)),
-        (shape((rows, count), F32), shape((heads * FPAD, count), BF), shape((2 * rows, width), BF)),
+        (shape((rows, count), BF), shape((heads * FPAD, count), BF), shape((2 * rows, width), BF)),
         (1, 1, None),
         [],
         2 * count * rows * width,
@@ -374,7 +374,7 @@
             feat = feat_ref[head * FPAD : (head + 1) * FPAD, :]
             parts = in_parts(head_row(norm_ref[...], head) * band_weight((1, SPAD), 1))[:, :FPAD]
             scale = 1.0 / jnp.sum(dot(parts, feat, (1, 0)), axis=0, keepdims=True)
-            grad_num = (up_ref[head * DV : (head + 1) * DV, :] * scale).astype(BF)
+            grad_num = (up_ref[head * DV : (head + 1) * DV, :].astype(F32) * scale).astype(BF)
             acc[head, :FPAD, :] += dot(feat, grad_num, (1, 1))
             scales = jnp.where(at == head, scale, scales)
         scale_ref[...] = scales
@@ -420,7 +420,7 @@
             feat = feat_ref[head * FPAD : (head + 1) * FPAD, :]
             scale = scale_ref[head : head + 1, :]
             att = dot(turned[head, :, :FPAD], feat, (1, 0)) * scale
-            grad_num = up_ref[head * DV : (head + 1) * DV, :] * scale
+            grad_num = up_ref[head * DV : (head + 1) * DV, :].astype(F32) * scale
             grad_den = -jnp.sum(grad_num * att, axis=0, keepdims=True)
             acc[head, :FPAD, :] += lane_sums(feat.astype(F32) * grad_den)
             found.append(att.astype(BF))
@@ -469,7 +469,7 @@
         query = qk_ref[...].astype(F32)
         found = []
         for head in range(heads):
-            grad_num = (up_ref[head * DV : (head + 1) * DV, :] * scale_ref[head : head + 1, :]).astype(BF)
+            grad_num = (up_ref[head * DV : (head + 1) * DV, :].astype(F32) * scale_ref[head : head + 1, :]).astype(BF)
             fgrad = dot(state_ref[head * SPAD : head * SPAD + FPAD, :], grad_num, (1, 0))
             fgrad = fgrad + column(head_row(norm_ref[...], head)) * den_ref[head : head + 1, :]
             found.append(features_back(rows_of(query, head, DK), fgrad).astype(BF))

time: 177 us -> 177 us (level)
  transfers between devices with their start and end apart: 19 -> 19, of which waited for: 8 -> 7; matrix products, arithmetic and copies ran while one was open for 0% -> 0% of each run, Pallas kernels for 30% -> 30%
where the time goes in v9:
time: 177 us; the launch traced here: 176 us
  Pallas kernels  61.9 us (35%)
  waiting for transfers between devices  54.3 us (31%)
  starting transfers between devices  54.2 us (31%)
  local copies, waits for them, and re-layouts  4.92 us (3%)
    pallas_call x9, Pallas kernels, call(): pl.pallas_call(kernel, in_specs=[pl.BlockSpec(memory_space=space) for spa...  59.5 us
    all_to_all x1, waiting for transfers between devices, per_device(): lax.all_to_all(to_send.reshape(n, -1, to_send.shape[1]), AXES, 0, 0, tile...  31.9 us
    all_to_all x3, starting transfers between devices, spread(): lax.all_to_all(x, AXES, 0, 0, axis_index_groups=same_core, tiled=True)  20.7 us
    all_to_all x1, starting transfers between devices, per_device(): lax.all_to_all(to_send.reshape(n, -1, to_send.shape[1]), AXES, 0, 0, tile...  11.5 us
    ppermute x6, waiting for transfers between devices, among_four(): found.append(lax.ppermute(parts[step], AXES, moves))  9.85 us
    all_to_all x1, starting transfers between devices, per_device(): lax.all_to_all(sent.reshape(n, -1, sent.shape[1]), AXES, 0, 0, tiled=True)  8.19 us
    ppermute x8, starting transfers between devices, exchange(): return lax.ppermute(x, AXES, swap)  7.07 us
    all_to_all x1, waiting for transfers between devices, per_device(): lax.all_to_all(sent.reshape(n, -1, sent.shape[1]), AXES, 0, 0, tiled=True)  6.94 us
  transfers between devices with their start and end apart: 19, of which 7 were waited for; matrix products, arithmetic and copies ran while one was open for 0% of the time, Pallas kernels for 30%

profile of v9, /device:TPU:1, one launch (start us, length us, event | category | flops | bytes accessed | tf_op | source)
XLA Modules:
  0.0 176.4 jit_solution(6831617794505446717)
XLA Ops:
  0.6 2.3 %shard_map.109 = bf16[1024,1152]{1,0:T(8,128)(2,1)} custom-call(bf16[8,128]{1,0:T(8,128)(2,1)} %q_ref.1, bf16[8,128]{1,0:T(8,128)(2,1)} %k_ref.1, bf16[8,1024]{1,0:T(8,128)(2,1)} %v_ref.1, bf16[8,1024]{1,0:T(8,128)(2,1)} %o_ref.1), custom_call_target="tpu_custom_call" | custom-call | bytes 2359296 | tf_op jit(solution)/shard_map/pallas_call | solution.py:242
  3.0 11.5 %all-to-all-start = ((bf16[128,8,1152]{2,1,0:T(8,128)(2,1)}), bf16[128,8,1152]{2,1,0:T(8,128)(2,1)S(1)}, u32[]{:S(2)}, u32[]{:S(2)}) async-start(bf16[128,8,1152]{2,1,0:T(8,128)(2,1)} %bitcast.13), calls=%async_computation | async-start | bytes 4718592 | tf_op jit(solution)/shard_map/all_to_all | solution.py:698
  14.5 1.1 collective-permute-start
  15.6 31.9 %all-to-all-done = bf16[128,8,1152]{2,1,0:T(8,128)(2,1)S(1)} async-done(((bf16[128,8,1152]{2,1,0:T(8,128)(2,1)}), bf16[128,8,1152]{2,1,0:T(8,128)(2,1)S(1)}, u32[]{:S(2)}, u32[]{:S(2)}) %all-to-all-start) | async-done | bytes 2359328 | tf_op jit(solution)/shard_map/all_to_all | solution.py:698
  47.6 1.2 collective-permute-start.2
  48.7 0.0 collective-permute-start.1
  48.8 0.0 collective-permute-done.refs_1_.refs_4_.refs_7_
  48.8 0.2 copy-done
  49.0 8.7 %shard_map.110 = (bf16[128,2048]{1,0:T(8,128)(2,1)}, bf16[2048,512]{1,0:T(8,128)(2,1)}, bf16[704,1024]{1,0:T(8,128)(2,1)}, bf16[704,1024]{1,0:T(8,128)(2,1)}, bf16[2048,128]{1,0:T(8,128)(2,1)}) custom-call(bf16[1024,1024]{1,0:T(8,128)(2,1)} %refs_6_.3, bf16[1024,1024]{1,0:T(8,128)(2,1)} %collective-permute-done.refs_1_.refs_4_.refs_7_, ...), custom_call_target="tpu_custom_call" | custom-call | flops 3422552064 | bytes 12582912 | tf_op jit(solution)/shard_map/pallas_call | solution.py:189
  57.7 5.0 %all-to-all-start.1 = ((bf16[64,32,128]{2,1,0:T(8,128)(2,1)}), bf16[64,32,128]{2,1,0:T(8,128)(2,1)S(1)}, u32[]{:S(2)}, u32[]{:S(2)}) async-start(bf16[64,32,128]{2,1,0:T(8,128)(2,1)} %bitcast.28), calls=%async_computation.1 | async-start | bytes 1048576 | tf_op jit(solution)/shard_map/all_to_all | solution.py:665
  62.7 0.0 collective-permute-done.1.refs_3_.refs_7_
  62.7 0.0 collective-permute-done.2.refs_5_.refs_12_
  62.7 7.4 %shard_map.111 = (bf16[512,2048]{1,0:T(8,128)(2,1)}, bf16[704,2048]{1,0:T(8,128)(2,1)}, bf16[1024,1024]{1,0:T(8,128)(2,1)}) custom-call(s32[1,1]{1,0:T(1,128)} %bitcast.refs_0_.refs_8_, bf16[128,2048]{1,0:T(8,128)(2,1)} %get-tuple-element.41.refs_1_.refs_0_, bf16[1024,1024]{1,0:T(8,128)(2,1)} %refs_6_.2, ...), custom_call_target="tpu_custom_call" | custom-call | flops 2147483648 | bytes 16515076 | tf_op jit(solution)/shard_map/pallas_call | solution.py:189
  70.1 4.4 %all-to-all-done.1 = bf16[64,32,128]{2,1,0:T(8,128)(2,1)S(1)} async-done(((bf16[64,32,128]{2,1,0:T(8,128)(2,1)}), bf16[64,32,128]{2,1,0:T(8,128)(2,1)S(1)}, u32[]{:S(2)}, u32[]{:S(2)}) %all-to-all-start.1) | async-done | bytes 524320 | tf_op jit(solution)/shard_map/all_to_all | solution.py:665
  74.4 0.8 copy-done.4
  75.2 4.9 %shard_map.112 = (f32[8,2048]{1,0:T(8,128)}, f32[16,128]{1,0:T(8,128)}, bf16[1024,256]{1,0:T(8,128)(2,1)}) custom-call(bf16[704,2048]{1,0:T(8,128)(2,1)} %get-tuple-element.42.refs_0_.refs_1_, bf16[512,2048]{1,0:T(8,128)(2,1)} %get-tuple-element.43.refs_1_.refs_3_.refs_5_, bf16[2048,128]{1,0:T(8,128)(2,1)} %bitcast.24), custom_call_target="tpu_custom_call" | custom-call | flops 738197504 | bytes 6103040 | tf_op jit(solution)/shard_map/pallas_call | solution.py:189
  80.1 5.6 %all-to-all-start.2 = ((bf16[64,16,256]{2,1,0:T(8,128)(2,1)}), bf16[64,16,256]{2,1,0:T(8,128)(2,1)S(1)}, u32[]{:S(2)}, u32[]{:S(2)}) async-start(bf16[64,16,256]{2,1,0:T(8,128)(2,1)} %bitcast.26), calls=%async_computation.2 | async-start | bytes 1048576 | tf_op jit(solution)/shard_map/all_to_all | solution.py:665
  85.8 1.9 %collective-permute-start.12 = (bf16[704,1024]{1,0:T(8,128)(2,1)}, bf16[704,1024]{1,0:T(8,128)(2,1)}, u32[]{:S(2)}, u32[]{:S(2)}) collective-permute-start(bf16[704,1024]{1,0:T(8,128)(2,1)} %get-tuple-element.56.refs_2_), channel_id=1, source_target_pairs={{0,1},{1,0},{2,3},{3,2},{4,5},{5,4},{6,7},{7,6},{8,9},{9,8},{10,11... | collective-permute-start | bytes 4325384 | tf_op jit(solution)/shard_map/ppermute | solution.py:662
  87.7 6.4 %shard_map.115 = (bf16[176,1024]{1,0:T(8,128)(2,1)}, bf16[176,1024]{1,0:T(8,128)(2,1)}, bf16[176,1024]{1,0:T(8,128)(2,1)}, bf16[176,1024]{1,0:T(8,128)(2,1)}) custom-call(s32[1,1]{1,0:T(1,128)} %bitcast.10.refs_0_, bf16[704,1024]{1,0:T(8,128)(2,1)} %get-tuple-element.55.refs_1_.refs_7_, bf16[704,1024]{1,0:T(8,128)(2,1)} %get-tuple-element.56.refs_2_, ...), custom_call_target="tpu_custom_call" | custom-call | flops 2952790016 | bytes 10616836 | tf_op jit(solution)/shard_map/pallas_call | solution.py:189
  94.1 1.4 collective-permute-start.5
  95.5 1.2 collective-permute-start.6
  96.7 0.2 collective-permute-start.7
  96.9 0.0 all-to-all-done.2
  96.9 0.8 copy-done.3
  97.7 7.7 %shard_map.113 = (bf16[512,1024]{1,0:T(8,128)(2,1)}, bf16[512,1024]{1,0:T(8,128)(2,1)}, f32[8,2048]{1,0:T(8,128)}, bf16[1024,256]{1,0:T(8,128)(2,1)}, bf16[512,2...) custom-call(s32[1,1]{1,0:T(1,128)} %bitcast.1.refs_0_, ...), custom_call_target="tpu_custom_call" | custom-call | flops 2885681152 | bytes 14024708 | tf_op jit(solution)/shard_map/pallas_call | solution.py:189
  105.4 10.0 %all-to-all-start.3 = ((bf16[64,16,256]{2,1,0:T(8,128)(2,1)}), bf16[64,16,256]{2,1,0:T(8,128)(2,1)S(1)}, u32[]{:S(2)}, u32[]{:S(2)}) async-start(bf16[64,16,256]{2,1,0:T(8,128)(2,1)} %bitcast.27), calls=%async_computation.3 | async-start | bytes 1048576 | tf_op jit(solution)/shard_map/all_to_all | solution.py:665
  115.5 1.2 collective-permute-start.3
  116.7 0.0 collective-permute-done.5.refs_10_
  116.7 2.7 %collective-permute-start.8 = (bf16[512,256]{1,0:T(8,128)(2,1)}, bf16[512,256]{1,0:T(8,128)(2,1)S(1)}, u32[]{:S(2)}, u32[]{:S(2)}) collective-permute-start(bf16[512,256]{1,0:T(8,128)(2,1)} %get-tuple-element.62), channel_id=1, source_target_pairs={{0,96},{1,97},{2,98},{3,99},{4,100},{5,101},{6,102},{7,103},{8,104... | collective-permute-start | bytes 786440 | tf_op jit(solution)/shard_map/ppermute | solution.py:676
  119.4 0.0 collective-permute-done.6.refs_11_
  119.4 1.2 collective-permute-start.9
  120.6 0.0 collective-permute-done.7.refs_12_
  120.6 0.1 collective-permute-start.10
  120.8 4.4 %shard_map.114 = (bf16[64,1024]{1,0:T(8,128)(2,1)}, bf16[64,1024]{1,0:T(8,128)(2,1)}) custom-call(bf16[128,2048]{1,0:T(8,128)(2,1)} %get-tuple-element.41.refs_1_.refs_0_, f32[8,2048]{1,0:T(8,128)} %get-tuple-element.45.refs_2_.refs_1_, f32[8,2048]{1,0:T(8,128)} %get-tuple-element.49.refs_2_, bf16[512,2048]{1,0:T(8,128)(2,1)} %get-tuple-element.43.refs_1_.refs_3_.refs_5_, ...), custom_call_target="tpu_custom_call" | custom-call | flops 369098752 | bytes 3547136 | tf_op jit(solution)/shard_map/pallas_call | solution.py:189
  125.2 6.9 %collective-permute-done.8.refs_14_ = bf16[512,256]{1,0:T(8,128)(2,1)S(1)} collective-permute-done((bf16[512,256]{1,0:T(8,128)(2,1)}, bf16[512,256]{1,0:T(8,128)(2,1)S(1)}, u32[]{:S(2)}, u32[]{:S(2)}) %collective-permute-start.8) | collective-permute-done | bytes 262176 | tf_op jit(solution)/shard_map/ppermute | solution.py:676
  132.1 0.0 collective-permute-done.9.refs_15_
  132.1 2.9 %collective-permute-done.10.refs_16_ = bf16[512,256]{1,0:T(8,128)(2,1)S(1)} collective-permute-done((bf16[512,256]{1,0:T(8,128)(2,1)}, bf16[512,256]{1,0:T(8,128)(2,1)S(1)}, u32[]{:S(2)}, u32[]{:S(2)}) %collective-permute-start.10) | collective-permute-done | bytes 262176 | tf_op jit(solution)/shard_map/ppermute | solution.py:676
  135.1 0.0 all-to-all-done.3
  135.1 0.0 copy-done.6
  135.1 0.0 copy-done.7
  135.1 0.0 copy-done.9
  135.1 0.0 copy-done.11
  135.1 0.7 copy-done.12
  135.8 0.2 copy-done.2
  135.9 6.6 %shard_map.116 = (bf16[64,1024]{1,0:T(8,128)(2,1)}, bf16[64,1024]{1,0:T(8,128)(2,1)}, bf16[1024,128]{1,0:T(8,128)(2,1)}, bf16[1024,560]{1,0:T(8,128)(2,1)}) custom-call(bf16[128,2048]{1,0:T(8,128)(2,1)} %get-tuple-element.41.refs_1_.refs_0_, bf16[2048,512]{1,0:T(8,128)(2,1)} %get-tuple-element.53.refs_1_, bf16[1024,256]{1,0:T(8,128)(2,1)} %bitcast.19, ...), custom_call_target="tpu_custom_call" | custom-call | flops 905969664 | bytes 12288004 | tf_op jit(solution)/shard_map/pallas_call | solution.py:189
  142.6 0.0 copy-start.8
  142.6 0.0 copy-start.13
  142.6 8.2 %all-to-all-start.4 = ((bf16[128,8,560]{2,1,0:T(8,128)(2,1)}), bf16[128,8,560]{2,1,0:T(8,128)(2,1)S(1)}, u32[]{:S(2)}, u32[]{:S(2)}) async-start(bf16[128,8,560]{2,1,0:T(8,128)(2,1)} %bitcast.25), calls=%async_computation.4 | async-start | bytes 2621440 | tf_op jit(solution)/shard_map/all_to_all | solution.py:723
  150.8 1.1 collective-permute-start.13
  151.9 0.1 collective-permute-start.4
  152.0 0.4 collective-permute-start.11
  152.5 0.0 collective-permute-done.12.refs_8_
  152.5 0.8 collective-permute-done.4.refs_4_
  153.3 0.3 collective-permute-done.11.refs_6_
  153.6 0.0 collective-permute-done.13.refs_10_.refs_3_
  153.6 0.0 collective-permute-done.3.refs_2_
  153.7 0.3 copy-done.16
  153.9 0.3 copy-done.17
  154.3 0.1 copy-done.10
  154.4 0.3 copy-done.14
  154.7 11.1 %shard_map.117 = (bf16[1024,1024]{1,0:T(8,128)(2,1)}, bf16[1024,1024]{1,0:T(8,128)(2,1)}) custom-call(s32[1,1]{1,0:T(1,128)} %bitcast.refs_0_.refs_8_, bf16[512,1024]{1,0:T(8,128)(2,1)} %get-tuple-element.47.refs_1_, bf16[512,1024]{1,0:T(8,128)(2,1)} %copy-done.14, bf16[64,1024]{1,0:T(8,128)(2,1)} %get-tuple-element.51.refs_4_.refs_3_, ...), custom_call_target="tpu_custom_call" | custom-call | flops 5200936960 | bytes 17039364 | tf_op jit(solution)/shard_map/pallas_call | solution.py:189
  165.8 6.9 %all-to-all-done.4 = bf16[128,8,560]{2,1,0:T(8,128)(2,1)S(1)} async-done(((bf16[128,8,560]{2,1,0:T(8,128)(2,1)}), bf16[128,8,560]{2,1,0:T(8,128)(2,1)S(1)}, u32[]{:S(2)}, u32[]{:S(2)}) %all-to-all-start.4) | async-done | bytes 1146912 | tf_op jit(solution)/shard_map/all_to_all | solution.py:723
  172.8 1.1 copy-done.1
  173.9 2.4 %shard_map.118 = (f32[8,128]{1,0:T(8,128)}, f32[8,128]{1,0:T(8,128)}, f32[8,1024]{1,0:T(8,128)}, f32[8,1024]{1,0:T(8,128)}) custom-call(s32[1,1]{1,0:T(1,128)} %bitcast.refs_0_.refs_8_, bf16[1024,560]{1,0:T(8,128)(2,1)} %bitcast.18, bf16[1024,128]{1,0:T(8,128)(2,1)} %get-tuple-element.67.refs_9_.refs_2_, bf16[1024,128]{1,0:T(8,128)(2,1)} %copy-done.10, ...), custom_call_target="tpu_custom_call" | custom-call | bytes 5939204 | tf_op jit(solution)/shard_map/pallas_call | solution.py:189
  (20 shorter events, 0.0 us)
Async XLA Ops:
  3.0 44.6 %all-to-all-start = ((bf16[128,8,1152]{2,1,0:T(8,128)(2,1)}), bf16[128,8,1152]{2,1,0:T(8,128)(2,1)S(1)}, u32[]{:S(2)}, u32[]{:S(2)}) async-start(bf16[128,8,1152]{2,1,0:T(8,128)(2,1)} %bitcast.13), calls=%async_computation | async-start | bytes 4718592 | tf_op jit(solution)/shard_map/all_to_all | solution.py:698
  14.5 34.3 %collective-permute-start = (bf16[1024,1024]{1,0:T(8,128)(2,1)}, bf16[1024,1024]{1,0:T(8,128)(2,1)}, u32[]{:S(2)}, u32[]{:S(2)}) collective-permute-start(bf16[1024,1024]{1,0:T(8,128)(2,1)} %refs_6_.3), channel_id=1, source_target_pairs={{0,1},{1,0},{2,3},{3,2},{4,5},{5,4},{6,7},{7,6},{8,9},{9,8},{10,11... | collective-permute-start | bytes 6291464 | tf_op jit(solution)/shard_map/ppermute | solution.py:662
  47.6 1.4 copy-start
  47.6 15.1 %collective-permute-start.2 = (bf16[1024,1152]{1,0:T(8,128)(2,1)S(1)}, bf16[1024,1152]{1,0:T(8,128)(2,1)}, u32[]{:S(2)}, u32[]{:S(2)}) collective-permute-start(bf16[1024,1152]{1,0:T(8,128)(2,1)S(1)} %bitcast.14), channel_id=1, source_target_pairs={{0,1},{1,0},{2,3},{3,2},{4,5},{5,4},{6,7},{7,6},{8,9},{9,8},{10,11... | collective-permute-start | bytes 7077896 | tf_op jit(solution)/shard_map/ppermute | solution.py:662
  48.7 13.9 %collective-permute-start.1 = (bf16[1024,1024]{1,0:T(8,128)(2,1)}, bf16[1024,1024]{1,0:T(8,128)(2,1)}, u32[]{:S(2)}, u32[]{:S(2)}) collective-permute-start(bf16[1024,1024]{1,0:T(8,128)(2,1)} %refs_6_.2), channel_id=1, source_target_pairs={{0,1},{1,0},{2,3},{3,2},{4,5},{5,4},{6,7},{7,6},{8,9},{9,8},{10,11... | collective-permute-start | bytes 6291464 | tf_op jit(solution)/shard_map/ppermute | solution.py:662
  57.7 16.8 %all-to-all-start.1 = ((bf16[64,32,128]{2,1,0:T(8,128)(2,1)}), bf16[64,32,128]{2,1,0:T(8,128)(2,1)S(1)}, u32[]{:S(2)}, u32[]{:S(2)}) async-start(bf16[64,32,128]{2,1,0:T(8,128)(2,1)} %bitcast.28), calls=%async_computation.1 | async-start | bytes 1048576 | tf_op jit(solution)/shard_map/all_to_all | solution.py:665
  74.4 0.8 copy-start.4
  80.1 16.8 %all-to-all-start.2 = ((bf16[64,16,256]{2,1,0:T(8,128)(2,1)}), bf16[64,16,256]{2,1,0:T(8,128)(2,1)S(1)}, u32[]{:S(2)}, u32[]{:S(2)}) async-start(bf16[64,16,256]{2,1,0:T(8,128)(2,1)} %bitcast.26), calls=%async_computation.2 | async-start | bytes 1048576 | tf_op jit(solution)/shard_map/all_to_all | solution.py:665
  85.8 66.6 %collective-permute-start.12 = (bf16[704,1024]{1,0:T(8,128)(2,1)}, bf16[704,1024]{1,0:T(8,128)(2,1)}, u32[]{:S(2)}, u32[]{:S(2)}) collective-permute-start(bf16[704,1024]{1,0:T(8,128)(2,1)} %get-tuple-element.56.refs_2_), channel_id=1, source_target_pairs={{0,1},{1,0},{2,3},{3,2},{4,5},{5,4},{6,7},{7,6},{8,9},{9,8},{10,11... | collective-permute-start | bytes 4325384 | tf_op jit(solution)/shard_map/ppermute | solution.py:662
  94.1 22.6 %collective-permute-start.5 = (bf16[176,1024]{1,0:T(8,128)(2,1)}, bf16[176,1024]{1,0:T(8,128)(2,1)S(1)}, u32[]{:S(2)}, u32[]{:S(2)}) collective-permute-start(bf16[176,1024]{1,0:T(8,128)(2,1)} %get-tuple-element.58), channel_id=1, source_target_pairs={{0,4},{1,5},{2,6},{3,7},{4,0},{5,1},{6,2},{7,3},{8,12},{9,13},{10,... | collective-permute-start | bytes 1081352 | tf_op jit(solution)/shard_map/ppermute | solution.py:676
  95.5 23.9 %collective-permute-start.6 = (bf16[176,1024]{1,0:T(8,128)(2,1)}, bf16[176,1024]{1,0:T(8,128)(2,1)S(1)}, u32[]{:S(2)}, u32[]{:S(2)}) collective-permute-start(bf16[176,1024]{1,0:T(8,128)(2,1)} %get-tuple-element.59), channel_id=1, source_target_pairs={{0,32},{1,33},{2,34},{3,35},{4,36},{5,37},{6,38},{7,39},{8,40},{9,... | collective-permute-start | bytes 1081352 | tf_op jit(solution)/shard_map/ppermute | solution.py:676
  96.7 23.9 %collective-permute-start.7 = (bf16[176,1024]{1,0:T(8,128)(2,1)}, bf16[176,1024]{1,0:T(8,128)(2,1)S(1)}, u32[]{:S(2)}, u32[]{:S(2)}) collective-permute-start(bf16[176,1024]{1,0:T(8,128)(2,1)} %get-tuple-element.60), channel_id=1, source_target_pairs={{0,36},{1,37},{2,38},{3,39},{4,32},{5,33},{6,34},{7,35},{8,44},{9,... | collective-permute-start | bytes 1081352 | tf_op jit(solution)/shard_map/ppermute | solution.py:676
  96.9 0.8 copy-start.3
  105.4 29.7 %all-to-all-start.3 = ((bf16[64,16,256]{2,1,0:T(8,128)(2,1)}), bf16[64,16,256]{2,1,0:T(8,128)(2,1)S(1)}, u32[]{:S(2)}, u32[]{:S(2)}) async-start(bf16[64,16,256]{2,1,0:T(8,128)(2,1)} %bitcast.27), calls=%async_computation.3 | async-start | bytes 1048576 | tf_op jit(solution)/shard_map/all_to_all | solution.py:665
  115.5 38.2 %collective-permute-start.3 = (bf16[512,1024]{1,0:T(8,128)(2,1)}, bf16[512,1024]{1,0:T(8,128)(2,1)S(1)}, u32[]{:S(2)}, u32[]{:S(2)}) collective-permute-start(bf16[512,1024]{1,0:T(8,128)(2,1)} %get-tuple-element.48), channel_id=1, source_target_pairs={{0,1},{1,0},{2,3},{3,2},{4,5},{5,4},{6,7},{7,6},{8,9},{9,8},{10,11... | collective-permute-start | bytes 3145736 | tf_op jit(solution)/shard_map/ppermute | solution.py:662
  116.7 18.4 %copy-start.5 = (bf16[176,1024]{1,0:T(8,128)(2,1)}, bf16[176,1024]{1,0:T(8,128)(2,1)S(1)}, u32[]{:S(2)}) copy-start(bf16[176,1024]{1,0:T(8,128)(2,1)S(1)} %collective-permute-done.5.refs_10_) | copy-start | bytes 1081348
  116.7 15.4 %collective-permute-start.8 = (bf16[512,256]{1,0:T(8,128)(2,1)}, bf16[512,256]{1,0:T(8,128)(2,1)S(1)}, u32[]{:S(2)}, u32[]{:S(2)}) collective-permute-start(bf16[512,256]{1,0:T(8,128)(2,1)} %get-tuple-element.62), channel_id=1, source_target_pairs={{0,96},{1,97},{2,98},{3,99},{4,100},{5,101},{6,102},{7,103},{8,104... | collective-permute-start | bytes 786440 | tf_op jit(solution)/shard_map/ppermute | solution.py:676
  119.4 15.6 %copy-start.6 = (bf16[176,1024]{1,0:T(8,128)(2,1)}, bf16[176,1024]{1,0:T(8,128)(2,1)S(1)}, u32[]{:S(2)}) copy-start(bf16[176,1024]{1,0:T(8,128)(2,1)S(1)} %collective-permute-done.6.refs_11_) | copy-start | bytes 1081348
  119.4 12.7 %collective-permute-start.9 = (bf16[512,256]{1,0:T(8,128)(2,1)}, bf16[512,256]{1,0:T(8,128)(2,1)S(1)}, u32[]{:S(2)}, u32[]{:S(2)}) collective-permute-start(bf16[512,256]{1,0:T(8,128)(2,1)} %get-tuple-element.63), channel_id=1, source_target_pairs={{0,2},{1,3},{2,0},{3,1},{4,6},{5,7},{6,4},{7,5},{8,10},{9,11},{10,... | collective-permute-start | bytes 786440 | tf_op jit(solution)/shard_map/ppermute | solution.py:676
  120.6 14.5 %copy-start.7 = (bf16[176,1024]{1,0:T(8,128)(2,1)}, bf16[176,1024]{1,0:T(8,128)(2,1)S(1)}, u32[]{:S(2)}) copy-start(bf16[176,1024]{1,0:T(8,128)(2,1)S(1)} %collective-permute-done.7.refs_12_) | copy-start | bytes 1081348
  120.6 14.4 %collective-permute-start.10 = (bf16[512,256]{1,0:T(8,128)(2,1)}, bf16[512,256]{1,0:T(8,128)(2,1)S(1)}, u32[]{:S(2)}, u32[]{:S(2)}) collective-permute-start(bf16[512,256]{1,0:T(8,128)(2,1)} %get-tuple-element.64), channel_id=1, source_target_pairs={{0,98},{1,99},{2,96},{3,97},{4,102},{5,103},{6,100},{7,101},{8,106... | collective-permute-start | bytes 786440 | tf_op jit(solution)/shard_map/ppermute | solution.py:676
  132.1 3.0 %copy-start.9 = (bf16[512,256]{1,0:T(8,128)(2,1)}, bf16[512,256]{1,0:T(8,128)(2,1)S(1)}, u32[]{:S(2)}) copy-start(bf16[512,256]{1,0:T(8,128)(2,1)S(1)} %collective-permute-done.8.refs_14_) | copy-start | bytes 786436
  132.1 3.0 %copy-start.11 = (bf16[512,256]{1,0:T(8,128)(2,1)}, bf16[512,256]{1,0:T(8,128)(2,1)S(1)}, u32[]{:S(2)}) copy-start(bf16[512,256]{1,0:T(8,128)(2,1)S(1)} %collective-permute-done.9.refs_15_) | copy-start | bytes 786436
  135.1 0.7 copy-start.12
  135.1 0.9 copy-start.2
  142.6 8.2 %copy-start.8 = (bf16[1024,128]{1,0:T(8,128)(2,1)S(1)}, bf16[1024,128]{1,0:T(8,128)(2,1)}, u32[]{:S(2)}) copy-start(bf16[1024,128]{1,0:T(8,128)(2,1)} %get-tuple-element.67.refs_9_.refs_2_) | copy-start | bytes 786436
  142.6 9.4 %copy-start.13 = (bf16[64,1024]{1,0:T(8,128)(2,1)S(1)}, bf16[64,1024]{1,0:T(8,128)(2,1)}, u32[]{:S(2)}) copy-start(bf16[64,1024]{1,0:T(8,128)(2,1)} %get-tuple-element.52.refs_5_) | copy-start | bytes 393220
  142.6 9.5 %copy-start.15 = (bf16[64,1024]{1,0:T(8,128)(2,1)S(1)}, bf16[64,1024]{1,0:T(8,128)(2,1)}, u32[]{:S(2)}) copy-start(bf16[64,1024]{1,0:T(8,128)(2,1)} %get-tuple-element.66) | copy-start | bytes 393220
  142.6 30.2 %all-to-all-start.4 = ((bf16[128,8,560]{2,1,0:T(8,128)(2,1)}), bf16[128,8,560]{2,1,0:T(8,128)(2,1)S(1)}, u32[]{:S(2)}, u32[]{:S(2)}) async-start(bf16[128,8,560]{2,1,0:T(8,128)(2,1)} %bitcast.25), calls=%async_computation.4 | async-start | bytes 2621440 | tf_op jit(solution)/shard_map/all_to_all | solution.py:723
  150.8 2.9 %collective-permute-start.13 = (bf16[1024,128]{1,0:T(8,128)(2,1)S(1)}, bf16[1024,128]{1,0:T(8,128)(2,1)S(1)}, u32[]{:S(2)}, u32[]{:S(2)}) collective-permute-start(bf16[1024,128]{1,0:T(8,128)(2,1)S(1)} %copy-done.8), channel_id=1, source_target_pairs={{0,1},{1,0},{2,3},{3,2},{4,5},{5,4},{6,7},{7,6},{8,9},{9,8},{10,11... | collective-permute-start | bytes 786440 | tf_op jit(solution)/shard_map/ppermute | solution.py:662
  151.9 1.3 collective-permute-start.4
  152.0 1.6 collective-permute-start.11
  153.3 0.6 copy-start.16
  153.6 0.6 copy-start.17
  153.6 0.7 copy-start.10
  153.6 1.1 copy-start.14
  172.8 1.1 copy-start.1

commit v10 on v9

--- a/solution.py
+++ b/solution.py
@@ -158,12 +158,14 @@
             for i, (which, rows, cols) in enumerate(plan):
                 writes[-1].append(pltpu.make_async_copy(buffer[i], target[which].at[rows, cols], left.at[at]))
                 at += 1
-        for step in reads:
+        for step in reads[:2]:
             for copy in step:
                 copy.start()
         for i in range(steps):
             for copy in reads[i]:
                 copy.wait()
+            for copy in reads[i + 2] if i + 2 < steps else []:
+                copy.start()
             at_first = lambda fn, i=i: fn() if i == 0 else None
             at_first.block = i
             body(

time: 177 us -> 179 us (1.011)
  Pallas kernels: 61.9 us -> 63.7 us
    pallas_call x9, Pallas kernels: 59.5 us -> 61.4 us  [call(): pl.pallas_call(kernel, in_specs=[pl.BlockSpec(memory_space=space) for spa...]
where the time goes in v10:
time: 179 us; the launch traced here: 178 us
  Pallas kernels  63.7 us (36%)
  waiting for transfers between devices  54.3 us (30%)
  starting transfers between devices  54.2 us (30%)
  local copies, waits for them, and re-layouts  4.92 us (3%)
    pallas_call x9, Pallas kernels, call(): pl.pallas_call(kernel, in_specs=[pl.BlockSpec(memory_space=space) for spa...  61.4 us
    all_to_all x1, waiting for transfers between devices, per_device(): lax.all_to_all(to_send.reshape(n, -1, to_send.shape[1]), AXES, 0, 0, tile...  31.9 us
    all_to_all x3, starting transfers between devices, spread(): lax.all_to_all(x, AXES, 0, 0, axis_index_groups=same_core, tiled=True)  20.7 us
    all_to_all x1, starting transfers between devices, per_device(): lax.all_to_all(to_send.reshape(n, -1, to_send.shape[1]), AXES, 0, 0, tile...  11.5 us
    ppermute x6, waiting for transfers between devices, among_four(): found.append(lax.ppermute(parts[step], AXES, moves))  9.87 us
    all_to_all x1, starting transfers between devices, per_device(): lax.all_to_all(sent.reshape(n, -1, sent.shape[1]), AXES, 0, 0, tiled=True)  8.17 us
    ppermute x8, starting transfers between devices, exchange(): return lax.ppermute(x, AXES, swap)  7.06 us
    all_to_all x1, waiting for transfers between devices, per_device(): lax.all_to_all(sent.reshape(n, -1, sent.shape[1]), AXES, 0, 0, tiled=True)  6.95 us
  transfers between devices with their start and end apart: 19, of which 7 were waited for; matrix products, arithmetic and copies ran while one was open for 0% of the time, Pallas kernels for 30%

profile of v10, /device:TPU:1, one launch (start us, length us, event | category | flops | bytes accessed | tf_op | source)
XLA Modules:
  0.0 178.3 jit_solution(3008699911809057473)
XLA Ops:
  0.6 2.3 %shard_map.109 = bf16[1024,1152]{1,0:T(8,128)(2,1)} custom-call(bf16[8,128]{1,0:T(8,128)(2,1)} %q_ref.1, bf16[8,128]{1,0:T(8,128)(2,1)} %k_ref.1, bf16[8,1024]{1,0:T(8,128)(2,1)} %v_ref.1, bf16[8,1024]{1,0:T(8,128)(2,1)} %o_ref.1), custom_call_target="tpu_custom_call" | custom-call | bytes 2359296 | tf_op jit(solution)/shard_map/pallas_call | solution.py:244
  3.0 11.5 %all-to-all-start = ((bf16[128,8,1152]{2,1,0:T(8,128)(2,1)}), bf16[128,8,1152]{2,1,0:T(8,128)(2,1)S(1)}, u32[]{:S(2)}, u32[]{:S(2)}) async-start(bf16[128,8,1152]{2,1,0:T(8,128)(2,1)} %bitcast.13), calls=%async_computation | async-start | bytes 4718592 | tf_op jit(solution)/shard_map/all_to_all | solution.py:700
  14.5 1.1 collective-permute-start
  15.6 31.9 %all-to-all-done = bf16[128,8,1152]{2,1,0:T(8,128)(2,1)S(1)} async-done(((bf16[128,8,1152]{2,1,0:T(8,128)(2,1)}), bf16[128,8,1152]{2,1,0:T(8,128)(2,1)S(1)}, u32[]{:S(2)}, u32[]{:S(2)}) %all-to-all-start) | async-done | bytes 2359328 | tf_op jit(solution)/shard_map/all_to_all | solution.py:700
  47.6 1.2 collective-permute-start.2
  48.7 0.0 collective-permute-start.1
  48.8 0.0 collective-permute-done.refs_1_.refs_4_.refs_7_
  48.8 0.2 copy-done
  49.0 8.7 %shard_map.110 = (bf16[128,2048]{1,0:T(8,128)(2,1)}, bf16[2048,512]{1,0:T(8,128)(2,1)}, bf16[704,1024]{1,0:T(8,128)(2,1)}, bf16[704,1024]{1,0:T(8,128)(2,1)}, bf16[2048,128]{1,0:T(8,128)(2,1)}) custom-call(bf16[1024,1024]{1,0:T(8,128)(2,1)} %refs_6_.3, bf16[1024,1024]{1,0:T(8,128)(2,1)} %collective-permute-done.refs_1_.refs_4_.refs_7_, ...), custom_call_target="tpu_custom_call" | custom-call | flops 3422552064 | bytes 12582912 | tf_op jit(solution)/shard_map/pallas_call | solution.py:191
  57.7 5.0 %all-to-all-start.1 = ((bf16[64,32,128]{2,1,0:T(8,128)(2,1)}), bf16[64,32,128]{2,1,0:T(8,128)(2,1)S(1)}, u32[]{:S(2)}, u32[]{:S(2)}) async-start(bf16[64,32,128]{2,1,0:T(8,128)(2,1)} %bitcast.28), calls=%async_computation.1 | async-start | bytes 1048576 | tf_op jit(solution)/shard_map/all_to_all | solution.py:667
  62.7 0.0 collective-permute-done.1.refs_3_.refs_7_
  62.7 0.0 collective-permute-done.2.refs_5_.refs_12_
  62.7 7.4 %shard_map.111 = (bf16[512,2048]{1,0:T(8,128)(2,1)}, bf16[704,2048]{1,0:T(8,128)(2,1)}, bf16[1024,1024]{1,0:T(8,128)(2,1)}) custom-call(s32[1,1]{1,0:T(1,128)} %bitcast.refs_0_.refs_8_, bf16[128,2048]{1,0:T(8,128)(2,1)} %get-tuple-element.41.refs_1_.refs_0_, bf16[1024,1024]{1,0:T(8,128)(2,1)} %refs_6_.2, ...), custom_call_target="tpu_custom_call" | custom-call | flops 2147483648 | bytes 16515076 | tf_op jit(solution)/shard_map/pallas_call | solution.py:191
  70.1 4.4 %all-to-all-done.1 = bf16[64,32,128]{2,1,0:T(8,128)(2,1)S(1)} async-done(((bf16[64,32,128]{2,1,0:T(8,128)(2,1)}), bf16[64,32,128]{2,1,0:T(8,128)(2,1)S(1)}, u32[]{:S(2)}, u32[]{:S(2)}) %all-to-all-start.1) | async-done | bytes 524320 | tf_op jit(solution)/shard_map/all_to_all | solution.py:667
  74.4 0.8 copy-done.4
  75.2 5.1 %shard_map.112 = (f32[8,2048]{1,0:T(8,128)}, f32[16,128]{1,0:T(8,128)}, bf16[1024,256]{1,0:T(8,128)(2,1)}) custom-call(bf16[704,2048]{1,0:T(8,128)(2,1)} %get-tuple-element.42.refs_0_.refs_1_, bf16[512,2048]{1,0:T(8,128)(2,1)} %get-tuple-element.43.refs_1_.refs_3_.refs_5_, bf16[2048,128]{1,0:T(8,128)(2,1)} %bitcast.24), custom_call_target="tpu_custom_call" | custom-call | flops 738197504 | bytes 6103040 | tf_op jit(solution)/shard_map/pallas_call | solution.py:191
  80.3 5.6 %all-to-all-start.2 = ((bf16[64,16,256]{2,1,0:T(8,128)(2,1)}), bf16[64,16,256]{2,1,0:T(8,128)(2,1)S(1)}, u32[]{:S(2)}, u32[]{:S(2)}) async-start(bf16[64,16,256]{2,1,0:T(8,128)(2,1)} %bitcast.26), calls=%async_computation.2 | async-start | bytes 1048576 | tf_op jit(solution)/shard_map/all_to_all | solution.py:667
  86.0 1.9 %collective-permute-start.12 = (bf16[704,1024]{1,0:T(8,128)(2,1)}, bf16[704,1024]{1,0:T(8,128)(2,1)}, u32[]{:S(2)}, u32[]{:S(2)}) collective-permute-start(bf16[704,1024]{1,0:T(8,128)(2,1)} %get-tuple-element.56.refs_2_), channel_id=1, source_target_pairs={{0,1},{1,0},{2,3},{3,2},{4,5},{5,4},{6,7},{7,6},{8,9},{9,8},{10,11... | collective-permute-start | bytes 4325384 | tf_op jit(solution)/shard_map/ppermute | solution.py:664
  87.9 6.4 %shard_map.115 = (bf16[176,1024]{1,0:T(8,128)(2,1)}, bf16[176,1024]{1,0:T(8,128)(2,1)}, bf16[176,1024]{1,0:T(8,128)(2,1)}, bf16[176,1024]{1,0:T(8,128)(2,1)}) custom-call(s32[1,1]{1,0:T(1,128)} %bitcast.10.refs_0_, bf16[704,1024]{1,0:T(8,128)(2,1)} %get-tuple-element.55.refs_1_.refs_7_, bf16[704,1024]{1,0:T(8,128)(2,1)} %get-tuple-element.56.refs_2_, ...), custom_call_target="tpu_custom_call" | custom-call | flops 2952790016 | bytes 10616836 | tf_op jit(solution)/shard_map/pallas_call | solution.py:191
  94.3 1.4 collective-permute-start.5
  95.7 1.2 collective-permute-start.6
  96.9 0.2 collective-permute-start.7
  97.0 0.0 all-to-all-done.2
  97.1 0.8 copy-done.3
  97.9 7.7 %shard_map.113 = (bf16[512,1024]{1,0:T(8,128)(2,1)}, bf16[512,1024]{1,0:T(8,128)(2,1)}, f32[8,2048]{1,0:T(8,128)}, bf16[1024,256]{1,0:T(8,128)(2,1)}, bf16[512,2...) custom-call(s32[1,1]{1,0:T(1,128)} %bitcast.1.refs_0_, ...), custom_call_target="tpu_custom_call" | custom-call | flops 2885681152 | bytes 14024708 | tf_op jit(solution)/shard_map/pallas_call | solution.py:191
  105.6 10.1 %all-to-all-start.3 = ((bf16[64,16,256]{2,1,0:T(8,128)(2,1)}), bf16[64,16,256]{2,1,0:T(8,128)(2,1)S(1)}, u32[]{:S(2)}, u32[]{:S(2)}) async-start(bf16[64,16,256]{2,1,0:T(8,128)(2,1)} %bitcast.27), calls=%async_computation.3 | async-start | bytes 1048576 | tf_op jit(solution)/shard_map/all_to_all | solution.py:667
  115.6 1.2 collective-permute-start.3
  116.9 0.0 collective-permute-done.5.refs_10_
  116.9 2.7 %collective-permute-start.8 = (bf16[512,256]{1,0:T(8,128)(2,1)}, bf16[512,256]{1,0:T(8,128)(2,1)S(1)}, u32[]{:S(2)}, u32[]{:S(2)}) collective-permute-start(bf16[512,256]{1,0:T(8,128)(2,1)} %get-tuple-element.62), channel_id=1, source_target_pairs={{0,96},{1,97},{2,98},{3,99},{4,100},{5,101},{6,102},{7,103},{8,104... | collective-permute-start | bytes 786440 | tf_op jit(solution)/shard_map/ppermute | solution.py:678
  119.6 0.0 collective-permute-done.6.refs_11_
  119.6 1.2 collective-permute-start.9
  120.8 0.0 collective-permute-done.7.refs_12_
  120.8 0.1 collective-permute-start.10
  120.9 4.4 %shard_map.114 = (bf16[64,1024]{1,0:T(8,128)(2,1)}, bf16[64,1024]{1,0:T(8,128)(2,1)}) custom-call(bf16[128,2048]{1,0:T(8,128)(2,1)} %get-tuple-element.41.refs_1_.refs_0_, f32[8,2048]{1,0:T(8,128)} %get-tuple-element.45.refs_2_.refs_1_, f32[8,2048]{1,0:T(8,128)} %get-tuple-element.49.refs_2_, bf16[512,2048]{1,0:T(8,128)(2,1)} %get-tuple-element.43.refs_1_.refs_3_.refs_5_, ...), custom_call_target="tpu_custom_call" | custom-call | flops 369098752 | bytes 3547136 | tf_op jit(solution)/shard_map/pallas_call | solution.py:191
  125.4 6.9 %collective-permute-done.8.refs_14_ = bf16[512,256]{1,0:T(8,128)(2,1)S(1)} collective-permute-done((bf16[512,256]{1,0:T(8,128)(2,1)}, bf16[512,256]{1,0:T(8,128)(2,1)S(1)}, u32[]{:S(2)}, u32[]{:S(2)}) %collective-permute-start.8) | collective-permute-done | bytes 262176 | tf_op jit(solution)/shard_map/ppermute | solution.py:678
  132.3 0.0 collective-permute-done.9.refs_15_
  132.3 3.0 %collective-permute-done.10.refs_16_ = bf16[512,256]{1,0:T(8,128)(2,1)S(1)} collective-permute-done((bf16[512,256]{1,0:T(8,128)(2,1)}, bf16[512,256]{1,0:T(8,128)(2,1)S(1)}, u32[]{:S(2)}, u32[]{:S(2)}) %collective-permute-start.10) | collective-permute-done | bytes 262176 | tf_op jit(solution)/shard_map/ppermute | solution.py:678
  135.2 0.0 all-to-all-done.3
  135.3 0.0 copy-done.5
  135.3 0.0 copy-done.6
  135.3 0.0 copy-done.7
  135.3 0.0 copy-done.9
  135.3 0.0 copy-done.11
  135.3 0.7 copy-done.12
  136.0 0.2 copy-done.2
  136.1 7.5 %shard_map.116 = (bf16[64,1024]{1,0:T(8,128)(2,1)}, bf16[64,1024]{1,0:T(8,128)(2,1)}, bf16[1024,128]{1,0:T(8,128)(2,1)}, bf16[1024,560]{1,0:T(8,128)(2,1)}) custom-call(bf16[128,2048]{1,0:T(8,128)(2,1)} %get-tuple-element.41.refs_1_.refs_0_, bf16[2048,512]{1,0:T(8,128)(2,1)} %get-tuple-element.53.refs_1_, bf16[1024,256]{1,0:T(8,128)(2,1)} %bitcast.19, ...), custom_call_target="tpu_custom_call" | custom-call | flops 905969664 | bytes 12288004 | tf_op jit(solution)/shard_map/pallas_call | solution.py:191
  143.7 8.2 %all-to-all-start.4 = ((bf16[128,8,560]{2,1,0:T(8,128)(2,1)}), bf16[128,8,560]{2,1,0:T(8,128)(2,1)S(1)}, u32[]{:S(2)}, u32[]{:S(2)}) async-start(bf16[128,8,560]{2,1,0:T(8,128)(2,1)} %bitcast.25), calls=%async_computation.4 | async-start | bytes 2621440 | tf_op jit(solution)/shard_map/all_to_all | solution.py:725
  151.8 0.0 copy-done.8
  151.8 1.1 collective-permute-start.13
  153.0 0.1 collective-permute-start.4
  153.1 0.4 collective-permute-start.11
  153.5 0.0 collective-permute-done.12.refs_8_
  153.5 0.8 collective-permute-done.4.refs_4_
  154.3 0.3 collective-permute-done.11.refs_6_
  154.7 0.0 collective-permute-done.13.refs_10_.refs_3_
  154.7 0.0 collective-permute-done.3.refs_2_
  154.7 0.3 copy-done.16
  155.0 0.3 copy-done.17
  155.3 0.1 copy-done.10
  155.4 0.3 copy-done.14
  155.8 11.1 %shard_map.117 = (bf16[1024,1024]{1,0:T(8,128)(2,1)}, bf16[1024,1024]{1,0:T(8,128)(2,1)}) custom-call(s32[1,1]{1,0:T(1,128)} %bitcast.refs_0_.refs_8_, bf16[512,1024]{1,0:T(8,128)(2,1)} %get-tuple-element.47.refs_1_, bf16[512,1024]{1,0:T(8,128)(2,1)} %copy-done.14, bf16[64,1024]{1,0:T(8,128)(2,1)} %get-tuple-element.51.refs_4_.refs_3_, ...), custom_call_target="tpu_custom_call" | custom-call | flops 5200936960 | bytes 17039364 | tf_op jit(solution)/shard_map/pallas_call | solution.py:191
  166.9 6.9 %all-to-all-done.4 = bf16[128,8,560]{2,1,0:T(8,128)(2,1)S(1)} async-done(((bf16[128,8,560]{2,1,0:T(8,128)(2,1)}), bf16[128,8,560]{2,1,0:T(8,128)(2,1)S(1)}, u32[]{:S(2)}, u32[]{:S(2)}) %all-to-all-start.4) | async-done | bytes 1146912 | tf_op jit(solution)/shard_map/all_to_all | solution.py:725
  173.8 1.1 copy-done.1
  174.9 3.2 %shard_map.118 = (f32[8,128]{1,0:T(8,128)}, f32[8,128]{1,0:T(8,128)}, f32[8,1024]{1,0:T(8,128)}, f32[8,1024]{1,0:T(8,128)}) custom-call(s32[1,1]{1,0:T(1,128)} %bitcast.refs_0_.refs_8_, bf16[1024,560]{1,0:T(8,128)(2,1)} %bitcast.18, bf16[1024,128]{1,0:T(8,128)(2,1)} %get-tuple-element.67.refs_9_.refs_2_, bf16[1024,128]{1,0:T(8,128)(2,1)} %copy-done.10, ...), custom_call_target="tpu_custom_call" | custom-call | bytes 5939204 | tf_op jit(solution)/shard_map/pallas_call | solution.py:191
  (20 shorter events, 0.0 us)
Async XLA Ops:
  3.0 44.6 %all-to-all-start = ((bf16[128,8,1152]{2,1,0:T(8,128)(2,1)}), bf16[128,8,1152]{2,1,0:T(8,128)(2,1)S(1)}, u32[]{:S(2)}, u32[]{:S(2)}) async-start(bf16[128,8,1152]{2,1,0:T(8,128)(2,1)} %bitcast.13), calls=%async_computation | async-start | bytes 4718592 | tf_op jit(solution)/shard_map/all_to_all | solution.py:700
  14.5 34.3 %collective-permute-start = (bf16[1024,1024]{1,0:T(8,128)(2,1)}, bf16[1024,1024]{1,0:T(8,128)(2,1)}, u32[]{:S(2)}, u32[]{:S(2)}) collective-permute-start(bf16[1024,1024]{1,0:T(8,128)(2,1)} %refs_6_.3), channel_id=1, source_target_pairs={{0,1},{1,0},{2,3},{3,2},{4,5},{5,4},{6,7},{7,6},{8,9},{9,8},{10,11... | collective-permute-start | bytes 6291464 | tf_op jit(solution)/shard_map/ppermute | solution.py:664
  47.6 1.4 copy-start
  47.6 15.1 %collective-permute-start.2 = (bf16[1024,1152]{1,0:T(8,128)(2,1)S(1)}, bf16[1024,1152]{1,0:T(8,128)(2,1)}, u32[]{:S(2)}, u32[]{:S(2)}) collective-permute-start(bf16[1024,1152]{1,0:T(8,128)(2,1)S(1)} %bitcast.14), channel_id=1, source_target_pairs={{0,1},{1,0},{2,3},{3,2},{4,5},{5,4},{6,7},{7,6},{8,9},{9,8},{10,11... | collective-permute-start | bytes 7077896 | tf_op jit(solution)/shard_map/ppermute | solution.py:664
  48.7 13.9 %collective-permute-start.1 = (bf16[1024,1024]{1,0:T(8,128)(2,1)}, bf16[1024,1024]{1,0:T(8,128)(2,1)}, u32[]{:S(2)}, u32[]{:S(2)}) collective-permute-start(bf16[1024,1024]{1,0:T(8,128)(2,1)} %refs_6_.2), channel_id=1, source_target_pairs={{0,1},{1,0},{2,3},{3,2},{4,5},{5,4},{6,7},{7,6},{8,9},{9,8},{10,11... | collective-permute-start | bytes 6291464 | tf_op jit(solution)/shard_map/ppermute | solution.py:664
  57.7 16.8 %all-to-all-start.1 = ((bf16[64,32,128]{2,1,0:T(8,128)(2,1)}), bf16[64,32,128]{2,1,0:T(8,128)(2,1)S(1)}, u32[]{:S(2)}, u32[]{:S(2)}) async-start(bf16[64,32,128]{2,1,0:T(8,128)(2,1)} %bitcast.28), calls=%async_computation.1 | async-start | bytes 1048576 | tf_op jit(solution)/shard_map/all_to_all | solution.py:667
  74.4 0.8 copy-start.4
  80.3 16.8 %all-to-all-start.2 = ((bf16[64,16,256]{2,1,0:T(8,128)(2,1)}), bf16[64,16,256]{2,1,0:T(8,128)(2,1)S(1)}, u32[]{:S(2)}, u32[]{:S(2)}) async-start(bf16[64,16,256]{2,1,0:T(8,128)(2,1)} %bitcast.26), calls=%async_computation.2 | async-start | bytes 1048576 | tf_op jit(solution)/shard_map/all_to_all | solution.py:667
  86.0 67.5 %collective-permute-start.12 = (bf16[704,1024]{1,0:T(8,128)(2,1)}, bf16[704,1024]{1,0:T(8,128)(2,1)}, u32[]{:S(2)}, u32[]{:S(2)}) collective-permute-start(bf16[704,1024]{1,0:T(8,128)(2,1)} %get-tuple-element.56.refs_2_), channel_id=1, source_target_pairs={{0,1},{1,0},{2,3},{3,2},{4,5},{5,4},{6,7},{7,6},{8,9},{9,8},{10,11... | collective-permute-start | bytes 4325384 | tf_op jit(solution)/shard_map/ppermute | solution.py:664
  94.3 22.6 %collective-permute-start.5 = (bf16[176,1024]{1,0:T(8,128)(2,1)}, bf16[176,1024]{1,0:T(8,128)(2,1)S(1)}, u32[]{:S(2)}, u32[]{:S(2)}) collective-permute-start(bf16[176,1024]{1,0:T(8,128)(2,1)} %get-tuple-element.58), channel_id=1, source_target_pairs={{0,4},{1,5},{2,6},{3,7},{4,0},{5,1},{6,2},{7,3},{8,12},{9,13},{10,... | collective-permute-start | bytes 1081352 | tf_op jit(solution)/shard_map/ppermute | solution.py:678
  95.7 23.9 %collective-permute-start.6 = (bf16[176,1024]{1,0:T(8,128)(2,1)}, bf16[176,1024]{1,0:T(8,128)(2,1)S(1)}, u32[]{:S(2)}, u32[]{:S(2)}) collective-permute-start(bf16[176,1024]{1,0:T(8,128)(2,1)} %get-tuple-element.59), channel_id=1, source_target_pairs={{0,32},{1,33},{2,34},{3,35},{4,36},{5,37},{6,38},{7,39},{8,40},{9,... | collective-permute-start | bytes 1081352 | tf_op jit(solution)/shard_map/ppermute | solution.py:678
  96.9 23.9 %collective-permute-start.7 = (bf16[176,1024]{1,0:T(8,128)(2,1)}, bf16[176,1024]{1,0:T(8,128)(2,1)S(1)}, u32[]{:S(2)}, u32[]{:S(2)}) collective-permute-start(bf16[176,1024]{1,0:T(8,128)(2,1)} %get-tuple-element.60), channel_id=1, source_target_pairs={{0,36},{1,37},{2,38},{3,39},{4,32},{5,33},{6,34},{7,35},{8,44},{9,... | collective-permute-start | bytes 1081352 | tf_op jit(solution)/shard_map/ppermute | solution.py:678
  97.1 0.8 copy-start.3
  105.6 29.7 %all-to-all-start.3 = ((bf16[64,16,256]{2,1,0:T(8,128)(2,1)}), bf16[64,16,256]{2,1,0:T(8,128)(2,1)S(1)}, u32[]{:S(2)}, u32[]{:S(2)}) async-start(bf16[64,16,256]{2,1,0:T(8,128)(2,1)} %bitcast.27), calls=%async_computation.3 | async-start | bytes 1048576 | tf_op jit(solution)/shard_map/all_to_all | solution.py:667
  115.6 39.1 %collective-permute-start.3 = (bf16[512,1024]{1,0:T(8,128)(2,1)}, bf16[512,1024]{1,0:T(8,128)(2,1)S(1)}, u32[]{:S(2)}, u32[]{:S(2)}) collective-permute-start(bf16[512,1024]{1,0:T(8,128)(2,1)} %get-tuple-element.48), channel_id=1, source_target_pairs={{0,1},{1,0},{2,3},{3,2},{4,5},{5,4},{6,7},{7,6},{8,9},{9,8},{10,11... | collective-permute-start | bytes 3145736 | tf_op jit(solution)/shard_map/ppermute | solution.py:664
  116.9 18.4 %copy-start.5 = (bf16[176,1024]{1,0:T(8,128)(2,1)}, bf16[176,1024]{1,0:T(8,128)(2,1)S(1)}, u32[]{:S(2)}) copy-start(bf16[176,1024]{1,0:T(8,128)(2,1)S(1)} %collective-permute-done.5.refs_10_) | copy-start | bytes 1081348
  116.9 15.4 %collective-permute-start.8 = (bf16[512,256]{1,0:T(8,128)(2,1)}, bf16[512,256]{1,0:T(8,128)(2,1)S(1)}, u32[]{:S(2)}, u32[]{:S(2)}) collective-permute-start(bf16[512,256]{1,0:T(8,128)(2,1)} %get-tuple-element.62), channel_id=1, source_target_pairs={{0,96},{1,97},{2,98},{3,99},{4,100},{5,101},{6,102},{7,103},{8,104... | collective-permute-start | bytes 786440 | tf_op jit(solution)/shard_map/ppermute | solution.py:678
  119.6 15.7 %copy-start.6 = (bf16[176,1024]{1,0:T(8,128)(2,1)}, bf16[176,1024]{1,0:T(8,128)(2,1)S(1)}, u32[]{:S(2)}) copy-start(bf16[176,1024]{1,0:T(8,128)(2,1)S(1)} %collective-permute-done.6.refs_11_) | copy-start | bytes 1081348
  119.6 12.7 %collective-permute-start.9 = (bf16[512,256]{1,0:T(8,128)(2,1)}, bf16[512,256]{1,0:T(8,128)(2,1)S(1)}, u32[]{:S(2)}, u32[]{:S(2)}) collective-permute-start(bf16[512,256]{1,0:T(8,128)(2,1)} %get-tuple-element.63), channel_id=1, source_target_pairs={{0,2},{1,3},{2,0},{3,1},{4,6},{5,7},{6,4},{7,5},{8,10},{9,11},{10,... | collective-permute-start | bytes 786440 | tf_op jit(solution)/shard_map/ppermute | solution.py:678
  120.8 14.5 %copy-start.7 = (bf16[176,1024]{1,0:T(8,128)(2,1)}, bf16[176,1024]{1,0:T(8,128)(2,1)S(1)}, u32[]{:S(2)}) copy-start(bf16[176,1024]{1,0:T(8,128)(2,1)S(1)} %collective-permute-done.7.refs_12_) | copy-start | bytes 1081348
  120.8 14.4 %collective-permute-start.10 = (bf16[512,256]{1,0:T(8,128)(2,1)}, bf16[512,256]{1,0:T(8,128)(2,1)S(1)}, u32[]{:S(2)}, u32[]{:S(2)}) collective-permute-start(bf16[512,256]{1,0:T(8,128)(2,1)} %get-tuple-element.64), channel_id=1, source_target_pairs={{0,98},{1,99},{2,96},{3,97},{4,102},{5,103},{6,100},{7,101},{8,106... | collective-permute-start | bytes 786440 | tf_op jit(solution)/shard_map/ppermute | solution.py:678
  132.3 3.0 %copy-start.9 = (bf16[512,256]{1,0:T(8,128)(2,1)}, bf16[512,256]{1,0:T(8,128)(2,1)S(1)}, u32[]{:S(2)}) copy-start(bf16[512,256]{1,0:T(8,128)(2,1)S(1)} %collective-permute-done.8.refs_14_) | copy-start | bytes 786436
  132.3 3.0 %copy-start.11 = (bf16[512,256]{1,0:T(8,128)(2,1)}, bf16[512,256]{1,0:T(8,128)(2,1)S(1)}, u32[]{:S(2)}) copy-start(bf16[512,256]{1,0:T(8,128)(2,1)S(1)} %collective-permute-done.9.refs_15_) | copy-start | bytes 786436
  135.2 0.7 copy-start.12
  135.3 0.9 copy-start.2
  143.6 8.2 %copy-start.8 = (bf16[1024,128]{1,0:T(8,128)(2,1)S(1)}, bf16[1024,128]{1,0:T(8,128)(2,1)}, u32[]{:S(2)}) copy-start(bf16[1024,128]{1,0:T(8,128)(2,1)} %get-tuple-element.67.refs_9_.refs_2_) | copy-start | bytes 786436
  143.6 9.4 %copy-start.13 = (bf16[64,1024]{1,0:T(8,128)(2,1)S(1)}, bf16[64,1024]{1,0:T(8,128)(2,1)}, u32[]{:S(2)}) copy-start(bf16[64,1024]{1,0:T(8,128)(2,1)} %get-tuple-element.52.refs_5_) | copy-start | bytes 393220
  143.7 9.4 %copy-start.15 = (bf16[64,1024]{1,0:T(8,128)(2,1)S(1)}, bf16[64,1024]{1,0:T(8,128)(2,1)}, u32[]{:S(2)}) copy-start(bf16[64,1024]{1,0:T(8,128)(2,1)} %get-tuple-element.66) | copy-start | bytes 393220
  143.7 30.2 %all-to-all-start.4 = ((bf16[128,8,560]{2,1,0:T(8,128)(2,1)}), bf16[128,8,560]{2,1,0:T(8,128)(2,1)S(1)}, u32[]{:S(2)}, u32[]{:S(2)}) async-start(bf16[128,8,560]{2,1,0:T(8,128)(2,1)} %bitcast.25), calls=%async_computation.4 | async-start | bytes 2621440 | tf_op jit(solution)/shard_map/all_to_all | solution.py:725
  151.8 2.9 %collective-permute-start.13 = (bf16[1024,128]{1,0:T(8,128)(2,1)S(1)}, bf16[1024,128]{1,0:T(8,128)(2,1)S(1)}, u32[]{:S(2)}, u32[]{:S(2)}) collective-permute-start(bf16[1024,128]{1,0:T(8,128)(2,1)S(1)} %copy-done.8), channel_id=1, source_target_pairs={{0,1},{1,0},{2,3},{3,2},{4,5},{5,4},{6,7},{7,6},{8,9},{9,8},{10,11... | collective-permute-start | bytes 786440 | tf_op jit(solution)/shard_map/ppermute | solution.py:664
  153.0 1.3 collective-permute-start.4
  153.1 1.6 collective-permute-start.11
  154.3 0.6 copy-start.16
  154.7 0.6 copy-start.17
  154.7 0.7 copy-start.10
  154.7 1.1 copy-start.14
  173.8 1.1 copy-start.1
